TPU v7x, 128 devices: a whole 4x4x4 slice. The times are simulated.
128 devices in a mesh: node: 16 (over x, z), local: 8 (over y, core).
Axes of the slice: x: 4, y: 4, z: 4, core: 2. Of those that a mesh axis runs over, the one named last changes fastest.
Arguments:
- tokens: bfloat16 [2048, 7168], P(('node', 'local')), may hold values from -6 to 6
- out_grads: bfloat16 [2048, 7168], P(('node', 'local')), may hold values from -0.59765625 to 0.59765625
- routes: int32 [2048, 8], P(('node', 'local')), may hold values from 0 to 63, as said below
- gate_values: float32 [2048, 8], P(('node', 'local')), may hold values from 0.1 to 1
- gate_weight: bfloat16 [128, 7168, 512], P(('node', 'local')), may hold values from -0.0625 to 0.0625
- up_weight: bfloat16 [128, 7168, 512], P(('node', 'local')), may hold values from -0.0625 to 0.0625
- down_weight: bfloat16 [128, 512, 7168], P(('node', 'local')), may hold values from -0.1875 to 0.1875
Outputs:
- input_grads: bfloat16 [2048, 7168], P(('node', 'local'))
- gate_grads: float32 [2048, 8], P(('node', 'local'))
Inputs may be any that keep to these rules, and one draw needn't show every extreme that they name: `routes`: each row names 8 different experts, 2 from each of 4 different groups (group of e is e // 4). Among the 16 rows of one device, at most 5 rows use a given group and at most 3 rows name a given expert; in every draw some group and some expert reach these bounds from every device.
All inputs are finite; a program needn't handle non-finite values.
Results may differ from a plain program's by a relative error of at most 0.012.
Values may be sent and summed in bfloat16 or wider, within the bound.
No kernel may reach another device: no remote copies, remote signals or barrier semaphores. Data moves between devices by JAX's collectives and lax.ppermute only.
A program may use at most 128 MiB of HBM per device.

v0:
```python
import jax
import jax.numpy as jnp
from jax import lax
from jax.sharding import PartitionSpec as P

NODE_LIMIT = 4
PER_NODE = 2


def shard_terms(rows_x, rows_dy, w_gate, w_up, w_down):
    pre_gate = jnp.dot(rows_x, w_gate, preferred_element_type=jnp.float32)
    pre_up = jnp.dot(rows_x, w_up, preferred_element_type=jnp.float32)
    sigmoid_gate = jax.nn.sigmoid(pre_gate)
    activated = pre_gate * sigmoid_gate
    hidden = (activated * pre_up).astype(jnp.bfloat16)
    back_grad = lax.dot_general(
        rows_dy, w_down, (((1,), (1,)), ((), ())), preferred_element_type=jnp.float32
    )
    part_gate = jnp.sum(hidden.astype(jnp.float32) * back_grad, axis=1)
    d_gate = (back_grad * pre_up * sigmoid_gate * (1.0 + pre_gate * (1.0 - sigmoid_gate))).astype(
        jnp.bfloat16
    )
    d_up = (back_grad * activated).astype(jnp.bfloat16)
    part_dx = lax.dot_general(
        d_gate, w_gate, (((1,), (1,)), ((), ())), preferred_element_type=jnp.float32
    )
    part_dx = part_dx + lax.dot_general(
        d_up, w_up, (((1,), (1,)), ((), ())), preferred_element_type=jnp.float32
    )
    gate_high = part_gate.astype(jnp.bfloat16)
    gate_low = (part_gate - gate_high.astype(jnp.float32)).astype(jnp.bfloat16)
    return (part_dx.astype(jnp.bfloat16), jnp.stack([gate_high, gate_low], axis=-1))


def finish_slots(
    backward_input_gradient, back_gate, position, gate_values, slots, width, row_count, pick_count
):
    flat_index = position.reshape(-1)
    picked = jnp.take(backward_input_gradient.reshape(slots, width), flat_index, axis=0).reshape(
        row_count, pick_count, 2, width
    )
    weighted = jnp.sum(picked.astype(jnp.float32) * gate_values[:, :, None, None], axis=(1, 2))
    gate_parts = jnp.take(back_gate.reshape(slots, 2), flat_index, axis=0).astype(jnp.float32)
    gate_grads = jnp.sum(gate_parts.reshape(row_count, pick_count, 4), axis=2)
    return (weighted.astype(jnp.bfloat16), gate_grads)


def on_device(tokens, out_grads, routes, gate_values, gate_weight, up_weight, down_weight):
    n_node = lax.axis_size("node")
    n_local = lax.axis_size("local")
    devices = n_node * n_local
    row_count = tokens.shape[0]
    pick_count = routes.shape[1]
    width = tokens.shape[1]
    exp_node = n_local // 2
    experts = devices // 2
    node_capacity_limit = min(
        row_count, NODE_LIMIT * (row_count - 1) // (n_node - NODE_LIMIT + 1) + 1
    )
    cap_exp = min(
        node_capacity_limit, PER_NODE * (node_capacity_limit - 1) // (exp_node - PER_NODE + 1) + 1
    )
    w_gate = gate_weight[0]
    w_up = up_weight[0]
    w_down = down_weight[0]
    token_ids = jnp.arange(row_count, dtype=jnp.int32)
    half_ids = jnp.arange(2, dtype=jnp.int32)
    pick_ids = jnp.arange(pick_count, dtype=jnp.int32)
    expert_hot = routes[:, :, None] == jnp.arange(experts, dtype=jnp.int32)[None, None, :]
    per_expert = jnp.any(expert_hot, axis=1).astype(jnp.int32)
    expert_before = jnp.cumsum(per_expert, axis=0) - per_expert
    rank_e = jnp.sum(jnp.where(expert_hot, expert_before[:, None, :], 0), axis=2)
    dest_dev = 2 * routes[:, :, None] + half_ids[None, None, :]
    slots = devices * cap_exp
    node_of = routes // exp_node
    node_hot = node_of[:, :, None] == jnp.arange(n_node, dtype=jnp.int32)[None, None, :]
    per_node = jnp.any(node_hot, axis=1).astype(jnp.int32)
    node_before = jnp.cumsum(per_node, axis=0) - per_node
    node_rank = jnp.sum(jnp.where(node_hot, node_before[:, None, :], 0), axis=2)
    slot_one = (node_of * node_capacity_limit + node_rank).reshape(-1)
    same_before = (node_of[:, :, None] == node_of[:, None, :]) & (
        pick_ids[None, None, :] < pick_ids[None, :, None]
    )
    pick_slot = jnp.sum(same_before.astype(jnp.int32), axis=2).reshape(-1)
    slot_code = (1 + routes % exp_node * cap_exp + rank_e).reshape(-1)
    rows_one = n_node * node_capacity_limit
    owner_ids = jnp.broadcast_to(token_ids[:, None], routes.shape).reshape(-1)
    source_one = (
        jnp.full((rows_one,), row_count, jnp.int32).at[slot_one].set(owner_ids, mode="drop")
    )
    slot_codes = (
        jnp.zeros((rows_one, PER_NODE), jnp.float32)
        .at[slot_one, pick_slot]
        .set(slot_code.astype(jnp.float32), mode="drop")
    )
    slot_codes = slot_codes.astype(jnp.bfloat16).reshape(n_node, node_capacity_limit, PER_NODE)
    send_x = jnp.take(tokens, source_one, axis=0, mode="fill", fill_value=0).reshape(
        n_node, node_capacity_limit, width
    )
    send_dy = jnp.take(out_grads, source_one, axis=0, mode="fill", fill_value=0).reshape(
        n_node, node_capacity_limit, width
    )
    mid_x, mid_dy, mid_payload = (
        lax.all_to_all(send_x, "node", split_axis=0, concat_axis=0, tiled=True),
        lax.all_to_all(send_dy, "node", split_axis=0, concat_axis=0, tiled=True),
        lax.all_to_all(slot_codes, "node", split_axis=0, concat_axis=0, tiled=True),
    )
    mid_payload = mid_payload.reshape(rows_one, -1)
    code_int = mid_payload.astype(jnp.int32)
    is_live = code_int > 0
    local_pick = (code_int - 1) // cap_exp
    slot_rank = (code_int - 1) % cap_exp
    anchor = jnp.arange(rows_one, dtype=jnp.int32) // node_capacity_limit
    dest_two = (
        (2 * local_pick[:, :, None] + half_ids[None, None, :]) * n_node + anchor[:, None, None]
    ) * cap_exp + slot_rank[:, :, None]
    dest_two = jnp.where(is_live[:, :, None], dest_two, slots)
    mid_ids = jnp.broadcast_to(
        jnp.arange(rows_one, dtype=jnp.int32)[:, None, None], dest_two.shape
    ).reshape(-1)
    source_two = (
        jnp.full((slots,), rows_one, jnp.int32).at[dest_two.reshape(-1)].set(mid_ids, mode="drop")
    )
    out_x = jnp.take(mid_x.reshape(rows_one, width), source_two, axis=0, mode="fill", fill_value=0)
    out_dy = jnp.take(
        mid_dy.reshape(rows_one, width), source_two, axis=0, mode="fill", fill_value=0
    )
    got_x, got_dy = (
        lax.all_to_all(
            out_x.reshape(n_local, n_node * cap_exp, width),
            "local",
            split_axis=0,
            concat_axis=0,
            tiled=True,
        ),
        lax.all_to_all(
            out_dy.reshape(n_local, n_node * cap_exp, width),
            "local",
            split_axis=0,
            concat_axis=0,
            tiled=True,
        ),
    )
    part_dx, gate_pair = shard_terms(
        got_x.reshape(slots, width), got_dy.reshape(slots, width), w_gate, w_up, w_down
    )
    backward_input_gradient, back_gate = (
        lax.all_to_all(
            lax.all_to_all(
                part_dx.reshape(n_local, n_node, cap_exp, width),
                "node",
                split_axis=1,
                concat_axis=1,
                tiled=True,
            ),
            "local",
            split_axis=0,
            concat_axis=0,
            tiled=True,
        ),
        lax.all_to_all(
            lax.all_to_all(
                gate_pair.reshape(n_local, n_node, cap_exp, 2),
                "node",
                split_axis=1,
                concat_axis=1,
                tiled=True,
            ),
            "local",
            split_axis=0,
            concat_axis=0,
            tiled=True,
        ),
    )
    position = (dest_dev % n_local * n_node + dest_dev // n_local) * cap_exp + rank_e[:, :, None]
    return finish_slots(
        backward_input_gradient,
        back_gate,
        position,
        gate_values,
        slots,
        width,
        row_count,
        pick_count,
    )


def solution(mesh):
    in_specs = (
        P(("node", "local"), None),
        P(("node", "local"), None),
        P(("node", "local"), None),
        P(("node", "local"), None),
        P(("node", "local"), None, None),
        P(("node", "local"), None, None),
        P(("node", "local"), None, None),
    )
    out_specs = (P(("node", "local"), None), P(("node", "local"), None))
    return jax.shard_map(
        on_device, mesh=mesh, in_specs=in_specs, out_specs=out_specs, check_vma=False
    )
```

profile of v0, /device:TPU:0, one launch (start us, length us, event | category | flops | bytes accessed | tf_op | source)
XLA Modules:
  0.0 526.8 jit_solution(14715696645777371254)
XLA Ops:
  3.2 6.4 %scatter_fusion = f32[80,2]{0,1:T(2,128)S(1)} fusion(f32[80,2]{0,1:T(2,128)S(1)} %broadcast_in_dim.128, s32[128]{0:T(128)S(1)} %get-tuple-element.25, f32[128]{0:T(128)S(1)} %reshape.545), kind=kCustom, calls=%fused_computation.7 | custom fusion | bytes 2560 | tf_op jit(solution)/shard_map/scatter | solution.py:94
  10.3 8.0 %all-to-all-start.1 = ((bf16[16,5,2]{1,2,0:T(2,128)(2,1)}), bf16[16,5,2]{1,2,0:T(2,128)(2,1)S(1)}, u32[]{:S(2)}, u32[]{:S(2)}) async-start(bf16[16,5,2]{1,2,0:T(2,128)(2,1)} %copy.99), calls=%async_computation.1 | async-start | bytes 16384 | tf_op jit(solution)/shard_map/all_to_all | solution.py:106
  27.3 7.2 %all-to-all-start.3 = ((bf16[16,5,7168]{2,1,0:T(8,128)(2,1)}), bf16[16,5,7168]{2,1,0:T(8,128)(2,1)S(1)}, u32[]{:S(2)}, u32[]{:S(2)}) async-start(bf16[16,5,7168]{2,1,0:T(8,128)(2,1)} %reshape.477), calls=%async_computation.3 | async-start | bytes 3670016 | tf_op jit(solution)/shard_map/all_to_all | solution.py:104
  37.0 23.7 %all-to-all-done.3 = bf16[16,5,7168]{2,1,0:T(8,128)(2,1)S(1)} async-done(((bf16[16,5,7168]{2,1,0:T(8,128)(2,1)}), bf16[16,5,7168]{2,1,0:T(8,128)(2,1)S(1)}, u32[]{:S(2)}, u32[]{:S(2)}) %all-to-all-start.3) | async-done | bytes 1146912 | tf_op jit(solution)/shard_map/all_to_all | solution.py:104
  60.8 4.4 all-to-all-start
  66.4 3.4 scatter_custom_fusion.2
  70.5 6.5 %gather_fusion.5 = bf16[384,7168]{1,0:T(8,128)(2,1)} fusion(bf16[80,7168]{1,0:T(8,128)(2,1)S(1)} %reshape.478, s32[1024]{0:T(1024)S(1)} %pad_clamp_fusion.1), kind=kCustom, calls=%fused_computation.3.clone | custom fusion | bytes 11011584 | tf_op jit(solution)/shard_map/jit(_take)/gather | solution.py:124
  77.0 11.4 %all-to-all-done = bf16[16,5,7168]{2,1,0:T(8,128)(2,1)} async-done(((bf16[16,5,7168]{2,1,0:T(8,128)(2,1)}), bf16[16,5,7168]{2,1,0:T(8,128)(2,1)}, u32[]{:S(2)}, u32[]{:S(2)}) %all-to-all-start) | async-done | bytes 1146912 | tf_op jit(solution)/shard_map/all_to_all | solution.py:105
  90.1 6.5 %gather_fusion.3 = bf16[384,7168]{1,0:T(8,128)(2,1)} fusion(bf16[80,7168]{1,0:T(8,128)(2,1)S(1)} %reshape.471, s32[1024]{0:T(1024)S(1)} %pad_clamp_fusion.1), kind=kCustom, calls=%fused_computation.1.clone | custom fusion | bytes 11011584 | tf_op jit(solution)/shard_map/jit(_take)/gather | solution.py:125
  96.6 9.2 %broadcast_select_fusion.2 = (bf16[384,7168]{1,0:T(8,128)(2,1)}, bf16[384,7168]{1,0:T(8,128)(2,1)}) fusion(bf16[384,7168]{1,0:T(8,128)(2,1)} %gather_fusion.3, pred[384]{0:T(512)(128)(4,1)S(1)} %compare_and_fusion.1, bf16[384,7168]{1,0:T(8,128)(2,1)} %gather_fusion.5), kind=kLoop, calls=%fused_computation.22 | loop fusion | flops 5505024 | bytes 22020480 | tf_op jit(solution)/shard_map/jit(_take)/select_n | solution.py:125
  105.7 69.2 %all_to_all.45 = bf16[8,48,7168]{2,1,0:T(8,128)(2,1)} all-to-all(bf16[8,48,7168]{2,1,0:T(8,128)(2,1)} %bitcast.42), channel_id=1, replica_groups=mesh['node'=16,'local'=8] {'local'}, dimensions={0} | all-to-all | bytes 11010048 | tf_op jit(solution)/shard_map/all_to_all | solution.py:129
  174.9 5.1 all-to-all-start.2
  180.1 8.8 %fusion.2 = f32[384,512]{1,0:T(8,128)} fusion(bf16[384,7168]{1,0:T(8,128)(2,1)} %bitcast.45, bf16[1,7168,512]{2,1,0:T(8,128)(2,1)} %param.15), kind=kOutput, calls=%fused_computation.12 | convolution fusion | flops 2818572288 | bytes 13631488 | tf_op jit(solution)/shard_map/dot_general | solution.py:11
  188.9 3.9 fusion.5
  192.8 51.0 %all-to-all-done.2 = bf16[8,48,7168]{2,1,0:T(8,128)(2,1)} async-done(((bf16[8,48,7168]{2,1,0:T(8,128)(2,1)}), bf16[8,48,7168]{2,1,0:T(8,128)(2,1)}, u32[]{:S(2)}, u32[]{:S(2)}) %all-to-all-start.2) | async-done | bytes 5505056 | tf_op jit(solution)/shard_map/all_to_all | solution.py:136
  243.8 8.3 %multiply_reduce_fusion.1 = (f32[384]{0:T(512)S(1)}, f32[384,512]{1,0:T(8,128)S(1)}) fusion(f32[384,512]{1,0:T(8,128)} %fusion.5, f32[384,512]{1,0:T(8,128)} %fusion.2, bf16[384,7168]{1,0:T(8,128)(2,1)} %bitcast.3, bf16[1,512,7168]{2,1,0:T(8,128)(2,1)} %param.17), kind=kOutput, calls=%fused_computation.25 | convolution fusion | flops 2820341248 | bytes 15205888 | tf_op jit(solution)/shard_map/dot_general | solution.py:16
  252.1 10.6 %fusion = f32[384,7168]{1,0:T(8,128)} fusion(bf16[1,7168,512]{2,1,0:T(8,128)(2,1)} %param.15, f32[384,512]{1,0:T(8,128)S(1)} %copy-done.4, f32[384,512]{1,0:T(8,128)S(1)} %get-tuple-element.28, f32[384,512]{1,0:T(8,128)S(1)} %copy-done.5), kind=kOutput, calls=%fused_computation.10 | convolution fusion | flops 2820538368 | bytes 20709376 | tf_op jit(solution)/shard_map/dot_general | solution.py:24
  263.8 3.9 all-to-all-start.7
  267.8 11.3 %add_convert_fusion = bf16[384,7168]{1,0:T(8,128)(2,1)} fusion(f32[384,7168]{1,0:T(8,128)} %fusion, bf16[1,7168,512]{2,1,0:T(8,128)(2,1)} %param.16, f32[384,512]{1,0:T(8,128)S(1)} %get-tuple-element.28, f32[384,512]{1,0:T(8,128)S(1)} %copy-done.4), kind=kOutput, calls=%fused_computation.9 | convolution fusion | flops 2825256960 | bytes 25427968 | tf_op jit(solution)/shard_map/dot_general | solution.py:27
  279.1 12.3 %reshape.481 = bf16[8,16,3,7168]{3,2,1,0:T(4,128)(2,1)} reshape(bf16[384,7168]{1,0:T(8,128)(2,1)} %add_convert_fusion) | data formatting | bytes 11010048 | tf_op jit(solution)/shard_map/reshape | solution.py:150
  291.4 9.4 %copy.108 = bf16[8,16,3,7168]{3,0,2,1:T(8,128)(2,1)} copy(bf16[8,16,3,7168]{3,2,1,0:T(4,128)(2,1)} %reshape.481) | data formatting | bytes 11010048 | tf_op jit(solution)/shard_map/reshape | solution.py:150
  300.8 7.3 %all-to-all-start.5 = ((bf16[8,16,3,7168]{3,0,2,1:T(8,128)(2,1)}), bf16[8,16,3,7168]{3,0,2,1:T(8,128)(2,1)}, u32[]{:S(2)}, u32[]{:S(2)}) async-start(bf16[8,16,3,7168]{3,0,2,1:T(8,128)(2,1)} %copy.108), calls=%async_computation.5 | async-start | bytes 11010048 | tf_op jit(solution)/shard_map/all_to_all | solution.py:149
  308.9 83.4 %all-to-all-done.5 = bf16[8,16,3,7168]{3,0,2,1:T(8,128)(2,1)} async-done(((bf16[8,16,3,7168]{3,0,2,1:T(8,128)(2,1)}), bf16[8,16,3,7168]{3,0,2,1:T(8,128)(2,1)}, u32[]{:S(2)}, u32[]{:S(2)}) %all-to-all-start.5) | async-done | bytes 5505056 | tf_op jit(solution)/shard_map/all_to_all | solution.py:149
  392.3 3.3 all-to-all-start.8
  395.6 7.9 %copy.109 = bf16[8,16,3,7168]{3,1,2,0:T(8,128)(2,1)} copy(bf16[8,16,3,7168]{3,0,2,1:T(8,128)(2,1)} %all-to-all-done.5) | data formatting | bytes 11010048 | tf_op jit(solution)/shard_map/all_to_all | solution.py:149
  403.6 5.2 all-to-all-start.6
  412.5 60.0 %all-to-all-done.6 = bf16[8,16,3,7168]{3,1,2,0:T(8,128)(2,1)} async-done(((bf16[8,16,3,7168]{3,1,2,0:T(8,128)(2,1)}), bf16[8,16,3,7168]{3,1,2,0:T(8,128)(2,1)}, u32[]{:S(2)}, u32[]{:S(2)}) %all-to-all-start.6) | async-done | bytes 5505056 | tf_op jit(solution)/shard_map/all_to_all | solution.py:148
  472.5 10.3 %copy.110 = bf16[8,16,3,7168]{3,2,1,0:T(4,128)(2,1)} copy(bf16[8,16,3,7168]{3,1,2,0:T(8,128)(2,1)} %all-to-all-done.6) | data formatting | bytes 11010048 | tf_op jit(solution)/shard_map/all_to_all | solution.py:148
  482.8 13.5 %reshape.482 = bf16[384,7168]{1,0:T(8,128)(2,1)} reshape(bf16[8,16,3,7168]{3,2,1,0:T(4,128)(2,1)} %copy.110) | data formatting | bytes 11010048 | tf_op jit(solution)/shard_map/reshape | solution.py:39
  496.2 11.3 %gather_fusion = bf16[256,7168]{1,0:T(8,128)(2,1)} fusion(bf16[384,7168]{1,0:T(8,128)(2,1)} %reshape.482, s32[1024]{0:T(1024)S(1)} %pad_clamp_fusion), kind=kCustom, calls=%fused_computation.4 | custom fusion | bytes 7341056 | tf_op jit(solution)/shard_map/jit(_take)/gather | solution.py:39
  507.6 8.3 %gather.17 = bf16[16,8,2,7168]{3,2,1,0:T(2,128)(2,1)} reshape(bf16[256,7168]{1,0:T(8,128)(2,1)} %gather_fusion) | data formatting | bytes 7340032 | tf_op jit(solution)/shard_map/jit(_take)/gather | solution.py:39
  515.8 10.8 %multiply_reduce_fusion = bf16[16,7168]{1,0:T(8,128)(2,1)} fusion(bf16[16,8,2,7168]{3,2,1,0:T(2,128)(2,1)} %gather.17, pred[16,8,2]{2,1,0:T(8,128)(4,1)S(1)} %copy.91, f32[16,8]{1,0:T(8,128)S(1)} %copy.113), kind=kLoop, calls=%fused_computation.19 | loop fusion | flops 7225344 | bytes 3900160 | tf_op jit(solution)/shard_map/reduce_sum | solution.py:42
  (112 shorter events, 23.8 us)
Async XLA Ops:
  0.6 18.7 %copy-start = (bf16[16,7168]{1,0:T(8,128)(2,1)S(1)}, bf16[16,7168]{1,0:T(8,128)(2,1)}, u32[]{:S(2)}) copy-start(bf16[16,7168]{1,0:T(8,128)(2,1)} %param.12) | copy-start | bytes 688132
  3.2 18.5 %copy-start.2 = (bf16[16,7168]{1,0:T(8,128)(2,1)S(1)}, bf16[16,7168]{1,0:T(8,128)(2,1)}, u32[]{:S(2)}) copy-start(bf16[16,7168]{1,0:T(8,128)(2,1)} %param.11) | copy-start | bytes 688132
  10.3 17.1 %all-to-all-start.1 = ((bf16[16,5,2]{1,2,0:T(2,128)(2,1)}), bf16[16,5,2]{1,2,0:T(2,128)(2,1)S(1)}, u32[]{:S(2)}, u32[]{:S(2)}) async-start(bf16[16,5,2]{1,2,0:T(2,128)(2,1)} %copy.99), calls=%async_computation.1 | async-start | bytes 16384 | tf_op jit(solution)/shard_map/all_to_all | solution.py:106
  27.3 33.4 %all-to-all-start.3 = ((bf16[16,5,7168]{2,1,0:T(8,128)(2,1)}), bf16[16,5,7168]{2,1,0:T(8,128)(2,1)S(1)}, u32[]{:S(2)}, u32[]{:S(2)}) async-start(bf16[16,5,7168]{2,1,0:T(8,128)(2,1)} %reshape.477), calls=%async_computation.3 | async-start | bytes 3670016 | tf_op jit(solution)/shard_map/all_to_all | solution.py:104
  60.8 27.6 %all-to-all-start = ((bf16[16,5,7168]{2,1,0:T(8,128)(2,1)}), bf16[16,5,7168]{2,1,0:T(8,128)(2,1)}, u32[]{:S(2)}, u32[]{:S(2)}) async-start(bf16[16,5,7168]{2,1,0:T(8,128)(2,1)} %reshape.470), calls=%async_computation | async-start | bytes 3670016 | tf_op jit(solution)/shard_map/all_to_all | solution.py:105
  174.9 13.9 %slice-start = ((s8[7340032]{0:T(1024)(128)(4,1)}), s8[3145728]{0:T(1024)(128)(4,1)S(1)}, s32[]{:S(2)}) async-start(s8[7340032]{0:T(1024)(128)(4,1)} %bitcast.43), calls=%async_computation.9 | async-start | bytes 6291456
  174.9 68.9 %all-to-all-start.2 = ((bf16[8,48,7168]{2,1,0:T(8,128)(2,1)}), bf16[8,48,7168]{2,1,0:T(8,128)(2,1)}, u32[]{:S(2)}, u32[]{:S(2)}) async-start(bf16[8,48,7168]{2,1,0:T(8,128)(2,1)} %bitcast.41), calls=%async_computation.2 | async-start | bytes 11010048 | tf_op jit(solution)/shard_map/all_to_all | solution.py:136
  180.1 8.8 %slice-start.1 = ((s8[7340032]{0:T(1024)(128)(4,1)}), s8[4194304]{0:T(1024)(128)(4,1)S(1)}, s32[]{:S(2)}) async-start(s8[7340032]{0:T(1024)(128)(4,1)} %bitcast.43), calls=%async_computation.10 | async-start | bytes 8388608
  180.1 8.8 %copy-start.3 = (bf16[8,48,7168]{2,1,0:T(8,128)(2,1)S(1)}, bf16[8,48,7168]{2,1,0:T(8,128)(2,1)}, u32[]{:S(2)}) copy-start(bf16[8,48,7168]{2,1,0:T(8,128)(2,1)} %all_to_all.45) | copy-start | bytes 16515076
  243.8 8.3 %copy-start.4 = (f32[384,512]{1,0:T(8,128)S(1)}, f32[384,512]{1,0:T(8,128)}, u32[]{:S(2)}) copy-start(f32[384,512]{1,0:T(8,128)} %fusion.2) | copy-start | bytes 2359300
  243.8 8.3 %copy-start.5 = (f32[384,512]{1,0:T(8,128)S(1)}, f32[384,512]{1,0:T(8,128)}, u32[]{:S(2)}) copy-start(f32[384,512]{1,0:T(8,128)} %fusion.5) | copy-start | bytes 2359300
  263.8 37.0 %all-to-all-start.7 = ((bf16[8,16,3,2]{0,3,2,1:T(2,128)(2,1)}), bf16[8,16,3,2]{0,3,2,1:T(2,128)(2,1)S(1)}, u32[]{:S(2)}, u32[]{:S(2)}) async-start(bf16[8,16,3,2]{0,3,2,1:T(2,128)(2,1)} %copy.116), calls=%async_computation.7 | async-start | bytes 49152 | tf_op jit(solution)/shard_map/all_to_all | solution.py:162
  300.8 91.5 %all-to-all-start.5 = ((bf16[8,16,3,7168]{3,0,2,1:T(8,128)(2,1)}), bf16[8,16,3,7168]{3,0,2,1:T(8,128)(2,1)}, u32[]{:S(2)}, u32[]{:S(2)}) async-start(bf16[8,16,3,7168]{3,0,2,1:T(8,128)(2,1)} %copy.108), calls=%async_computation.5 | async-start | bytes 11010048 | tf_op jit(solution)/shard_map/all_to_all | solution.py:149
  392.3 11.3 %all-to-all-start.8 = ((bf16[8,16,3,2]{1,3,2,0:T(2,128)(2,1)}), bf16[8,16,3,2]{1,3,2,0:T(2,128)(2,1)S(1)}, u32[]{:S(2)}, u32[]{:S(2)}) async-start(bf16[8,16,3,2]{1,3,2,0:T(2,128)(2,1)} %copy.117), calls=%async_computation.8 | async-start | bytes 24576 | tf_op jit(solution)/shard_map/all_to_all | solution.py:161
  403.5 6.3 %copy-start.6 = (f32[16,8]{0,1:T(8,128)S(1)}, f32[16,8]{0,1:T(8,128)}, u32[]{:S(2)}) copy-start(f32[16,8]{0,1:T(8,128)} %param.14) | copy-start | bytes 1540
  403.6 68.9 %all-to-all-start.6 = ((bf16[8,16,3,7168]{3,1,2,0:T(8,128)(2,1)}), bf16[8,16,3,7168]{3,1,2,0:T(8,128)(2,1)}, u32[]{:S(2)}, u32[]{:S(2)}) async-start(bf16[8,16,3,7168]{3,1,2,0:T(8,128)(2,1)} %copy.109), calls=%async_computation.6 | async-start | bytes 11010048 | tf_op jit(solution)/shard_map/all_to_all | solution.py:148
  496.2 30.4 %copy-start.1 = (bf16[16,7168]{1,0:T(8,128)(2,1)S(1)}, bf16[16,7168]{1,0:T(8,128)(2,1)}, u32[]{:S(2)}) copy-start(bf16[16,7168]{1,0:T(8,128)(2,1)} %param.12) | copy-start | bytes 688132
where the time goes:
time: 534 us; the launch traced here: 527 us
  waiting for transfers between devices  230 us (43%)
  local copies, waits for them, and re-layouts  115 us (22%)
  blocking collectives  69.2 us (13%)
  starting transfers between devices  44.5 us (8%)
  matrix products  42.9 us (8%)
  other arithmetic  24 us (4%)
    all_to_all x1, waiting for transfers between devices, on_device(): lax.all_to_all(part_dx.reshape(n_local, n_node, cap_exp, width), 'node',...  83.4 us
    all_to_all x1, blocking collectives, on_device(): lax.all_to_all(out_x.reshape(n_local, n_node * cap_exp, width), 'local',...  69.2 us
    all_to_all x1, waiting for transfers between devices, on_device(): lax.all_to_all(lax.all_to_all(part_dx.reshape(n_local, n_node, cap_exp, w...  60 us
    all_to_all x1, waiting for transfers between devices, on_device(): lax.all_to_all(out_dy.reshape(n_local, n_node * cap_exp, width), 'local',...  51 us
    all_to_all x1, waiting for transfers between devices, on_device(): lax.all_to_all(send_x, 'node', split_axis=0, concat_axis=0, tiled=True)  23.7 us
    reshape x2, local copies, waits for them, and re-layouts, on_device(): part_dx.reshape(n_local, n_node, cap_exp, width)  21.7 us
    gather x2, local copies, waits for them, and re-layouts, finish_slots(): jnp.take(backward_input_gradient.reshape(slots, width), flat_index, axis=0)  19.6 us
    reshape x1, local copies, waits for them, and re-layouts, finish_slots(): backward_input_gradient.reshape(slots, width)  13.5 us
  transfers between devices with their start and end apart: 8, of which 5 were waited for; matrix products, arithmetic and copies ran while one was open for 15% of the time, Pallas kernels for 0%

commit v1 on v0

v1 whole, which is shorter than its diff:
```python
import functools

import jax
import jax.numpy as jnp
from jax import lax
from jax.experimental import pallas as pl
from jax.experimental.pallas import tpu as pltpu
from jax.sharding import PartitionSpec as P

BF = jnp.bfloat16
F32 = jnp.float32
I32 = jnp.int32

N_NODE = 16
N_Y = 4
TOK = 16
CAP_NODE = 5
CAP_EXP = 3
WIDTH = 7168
HALF = 512
ROWS_Y = N_NODE * CAP_EXP
SLOTS = N_Y * ROWS_Y
ROWS_N = N_NODE * 40
EXT = 128
VMEM_LIMIT = 48 * 1024 * 1024


def iota(shape, dim):
    return lax.broadcasted_iota(I32, shape, dim)


def div3(v):
    return (v * 171) >> 9


def div5(v):
    return (v * 205) >> 10


def div40(v):
    return div5(v >> 3)


def dot(a, b):
    return jnp.dot(a, b, preferred_element_type=F32)


def dot_nt(a, b):
    return lax.dot_general(a, b, (((1,), (1,)), ((), ())), preferred_element_type=F32)


def dot_tn(a, b):
    return lax.dot_general(a, b, (((0,), (0,)), ((), ())), preferred_element_type=F32)


def onehot(mask):
    return jnp.where(mask, 1.0, 0.0)


def route_tables(routes, width):
    lane = iota((TOK, width), 1) & 63
    hot = jnp.zeros((TOK, width), F32)
    for k in range(8):
        hot = hot + onehot(routes[:, k : k + 1] == lane)
    return hot


def node_codes(hot):
    width = hot.shape[1]
    row = iota((width, 128), 0)
    group = onehot((row < 64) & ((row >> 2) == iota((width, 128), 1))).astype(BF)
    used = jnp.minimum(dot(hot.astype(BF), group), 1.0)
    tri = onehot(iota((TOK, TOK), 1) < iota((TOK, TOK), 0)).astype(BF)
    return used * (dot(tri, used.astype(BF)) + 1.0)


def send_dy_kernel(routes_ref, gates_ref, dy_ref, out_ref):
    routes = routes_ref[...]
    gates = gates_ref[...]
    width = 256
    lane = iota((TOK, width), 1)
    hot = route_tables(routes, width)
    gate = jnp.zeros((TOK, width), F32)
    for k in range(8):
        gate = gate + jnp.where(routes[:, k : k + 1] == (lane & 63), gates[:, k : k + 1], 0.0)
    tri = onehot(iota((TOK, TOK), 1) < iota((TOK, TOK), 0)).astype(BF)
    code = hot * (dot(tri, hot.astype(BF)) + 1.0)
    section = lane >> 6
    meta = jnp.where(section == 0, code, jnp.where(section == 1, gate, 0.0)).astype(BF)
    meta = jnp.concatenate([meta, jnp.zeros((TOK, 1024 - width), BF)], axis=1)
    stack = jnp.concatenate([dy_ref[:, 1024 * q : 1024 * (q + 1)] for q in range(7)] + [meta], axis=0)
    ncode = node_codes(hot)
    spread = onehot((iota((TOK, 128), 1) & 15) == iota((TOK, 128), 0)).astype(BF)
    ncode_lane = dot_tn(ncode.astype(BF), spread)[:N_NODE]
    chunk = (iota((N_NODE, 128), 1) >> 4).astype(F32)
    key = jnp.where(ncode_lane > 0.0, 8.0 * chunk + ncode_lane, -1.0)
    row = iota((40, 128), 0)
    q = div5(row)
    row_key = (8 * q + (row - 5 * q) + 1).astype(F32)
    pick = jnp.concatenate([onehot(row_key == key[n : n + 1, :]) for n in range(N_NODE)], axis=0)
    out_ref[...] = dot(pick.astype(BF), stack).astype(BF)


def send_x_kernel(place_ref, x0_ref, x1_ref, x2_ref, x3_ref, out_ref):
    y = place_ref[1]
    xs = [x0_ref, x1_ref, x2_ref, x3_ref]
    routes = jnp.concatenate([r[:, WIDTH : WIDTH + EXT] for r in xs], axis=0).astype(F32)
    lane = iota((64, 128), 1)
    wanted = jnp.where(lane < N_NODE, 4 * lane + y, -1).astype(F32)
    hot = jnp.zeros((64, 128), F32)
    for k in range(8):
        hot = hot + onehot(routes[:, k : k + 1] == wanted)
    r64 = iota((64, 64), 0)
    c64 = iota((64, 64), 1)
    tri = onehot((c64 < r64) & ((c64 >> 4) == (r64 >> 4))).astype(BF)
    code = hot * (dot(tri, hot.astype(BF)) + 1.0)
    spread = onehot((lane & 63) == iota((64, 128), 0)).astype(BF)
    code_lane = dot_tn(code.astype(BF), spread)[:N_NODE]
    block = (iota((N_NODE, 128), 1) >> 4).astype(F32)
    key = jnp.where(code_lane > 0.0, 4.0 * block + code_lane, -1.0)
    row = iota((24, 128), 0)
    b = div3(row)
    row_key = (4 * b + (row - 3 * b) + 1).astype(F32)
    pick = jnp.concatenate([onehot(row_key == key[n : n + 1, :]) for n in range(N_NODE)], axis=0).astype(BF)
    for i in range(7):
        lo = 512 * i
        stack = jnp.concatenate(
            [r[:, lo : lo + 512] for r in xs] + [r[:, 3584 + lo : 3584 + lo + 512] for r in xs], axis=0
        )
        out_ref[:, lo : lo + 512] = dot(pick, stack).astype(BF)


def regroup_kernel(place_ref, rows_ref, out0_ref, out1_ref, out2_ref, out3_ref, table_ref):
    node = place_ref[0]
    y = place_ref[1]
    outs = [out0_ref, out1_ref, out2_ref, out3_ref]
    c = iota((256, 128), 1)
    want = ((c >> 2) << 6) + 4 * node + ((y + c) & 3)
    select = onehot((c < 8) & (iota((256, 128), 0) == want)).astype(BF)
    meta = rows_ref[:, :256]
    code = lax.dot_general(select, meta, (((0,), (1,)), ((), ())), preferred_element_type=F32)[:8]
    col = iota((8, ROWS_N), 1)
    n = div40(col)
    key = jnp.where((col - 40 * n >= 35) & (code > 0.0), 4.0 * n.astype(F32) + code, -1.0)
    row = iota((ROWS_Y, ROWS_N), 0)
    rn = div3(row)
    row_key = (4 * rn + (row - 3 * rn) + 1).astype(F32)
    for q in range(7):
        key_q = pltpu.roll(key, ROWS_N - (35 - 5 * q), 1)
        pick = jnp.concatenate([onehot(row_key == key_q[s : s + 1, :]) for s in range(N_Y)], axis=0)
        moved = dot(pick.astype(BF), rows_ref[...]).astype(BF)
        for s in range(N_Y):
            outs[s][:, 1024 * q : 1024 * (q + 1)] = moved[ROWS_Y * s : ROWS_Y * (s + 1)]
    picked = dot(meta, select).astype(BF)
    r = iota((ROWS_N, ROWS_N), 0)
    rn = div40(r)
    rp = r - 40 * rn
    source = 40 * rn + 35 + (rp - 5 * div5(rp))
    table_ref[...] = dot(onehot(iota((ROWS_N, ROWS_N), 1) == source).astype(BF), picked)


def back_kernel(*refs):
    pieces, down_ref, out_ref = refs[:8], refs[8], refs[9]

    @pl.when(pl.program_id(0) == 0)
    def _():
        out_ref[...] = jnp.zeros_like(out_ref)

    rows = jnp.concatenate([p[...] for p in pieces], axis=0)
    out_ref[...] += dot_nt(rows, down_ref[...])


def forward_kernel(own_ref, other_ref, gate_ref, up_ref, back_ref, dgate_ref, dup_ref, ext_ref, pg_ref, pu_ref):
    step = pl.program_id(0)

    @pl.when(step == 0)
    def _():
        pg_ref[...] = jnp.zeros_like(pg_ref)
        pu_ref[...] = jnp.zeros_like(pu_ref)

    h = jnp.where(step >= 7, 1, 0)
    row = iota((SLOTS, 384), 0)
    s = div3(row >> 4)
    rem = row - ROWS_Y * s
    n = div3(rem)
    r = rem - 3 * n
    perm = onehot(iota((SLOTS, 384), 1) == 24 * n + 12 * h + 3 * s + r).astype(BF)
    rows = jnp.concatenate(
        [dot(perm, own_ref[...]).astype(BF), dot(perm, other_ref[...]).astype(BF)], axis=0
    )
    pg_ref[...] += dot(rows, gate_ref[...])
    pu_ref[...] += dot(rows, up_ref[...])

    @pl.when(step == 13)
    def _():
        pre_gate = pg_ref[...]
        pre_up = pu_ref[...]
        back = back_ref[...]
        sig = jax.nn.sigmoid(pre_gate)
        act = pre_gate * sig
        hidden = (act * pre_up).astype(BF)
        part = jnp.sum(hidden.astype(F32) * back, axis=1, keepdims=True)
        dgate_ref[...] = (back * pre_up * sig * (1.0 + pre_gate * (1.0 - sig))).astype(BF)
        dup_ref[...] = (back * act).astype(BF)
        high = part.astype(BF).astype(F32)
        low = part - high
        slot = iota((2 * SLOTS, EXT), 0)
        slot = jnp.where(slot >= SLOTS, slot - SLOTS, slot)
        at = 2 * div3(slot >> 4)
        lane = iota((2 * SLOTS, EXT), 1)
        ext_ref[...] = jnp.where(lane == at, high, jnp.where(lane == at + 1, low, 0.0)).astype(BF)


def dx_kernel(dgate_ref, dup_ref, gate_ref, up_ref, ext_ref, own_ref, other_ref):
    step = pl.program_id(0)
    part = (dot_nt(dgate_ref[...], gate_ref[...]) + dot_nt(dup_ref[...], up_ref[...])).astype(BF)
    at = pl.multiple_of(step * 512, 512)
    own_ref[:, pl.ds(at, 512)] = part[:SLOTS]
    other_ref[:, pl.ds(at, 512)] = part[SLOTS:]

    @pl.when(step == 0)
    def _():
        own_ref[:, 3584:] = ext_ref[:SLOTS]
        other_ref[:, 3584:] = ext_ref[SLOTS:]


def add_kernel(own_ref, got_ref, *outs):
    lane = iota((ROWS_Y, EXT), 1)
    for s in range(N_Y):
        rows = slice(ROWS_Y * s, ROWS_Y * (s + 1))
        total = own_ref[rows, :3584].astype(F32) + got_ref[rows, :3584].astype(F32)
        outs[s][:, :3584] = total.astype(BF)
        term = jnp.sum(
            own_ref[rows, 3584:].astype(F32) + got_ref[rows, 3584:].astype(F32), axis=1, keepdims=True
        )
        high = term.astype(BF).astype(F32)
        low = term - high
        outs[s][:, 3584:] = jnp.where(
            lane == 2 * s, high, jnp.where(lane == 2 * s + 1, low, 0.0)
        ).astype(BF)


def combine_kernel(table_ref, p0_ref, p1_ref, p2_ref, p3_ref, out_ref):
    pieces = [p0_ref, p1_ref, p2_ref, p3_ref]
    lane = iota((ROWS_N, SLOTS), 1)
    ls = div3(lane >> 4)
    rem = lane - ROWS_Y * ls
    ln = div3(rem)
    lr = rem - 3 * ln
    row = iota((ROWS_N, SLOTS), 0)
    rn = div40(row)
    rq = div5(row - 40 * rn)
    table = table_ref[...]
    code = jnp.zeros((ROWS_N, SLOTS), F32)
    gate = jnp.zeros((ROWS_N, SLOTS), F32)
    for s in range(N_Y):
        code = jnp.where(ls == s, table[:, s : s + 1], code)
        gate = jnp.where(ls == s, table[:, 4 + s : 5 + s], gate)
    match = (rn == ln) & (code == (lr + 1).astype(F32))
    weight = jnp.where(match, gate, 0.0)
    total = jnp.zeros((ROWS_N, 512), F32)
    for q in range(7):
        rows = jnp.concatenate([p[:, 512 * q : 512 * (q + 1)] for p in pieces], axis=0)
        total = total + dot(jnp.where(rq == q, weight, 0.0).astype(BF), rows)
    ext = jnp.concatenate([p[:, 3584:] for p in pieces], axis=0)
    terms = dot(onehot(match & (rq == 7)).astype(BF), ext)
    out_ref[:, :EXT] = (total[:, :EXT] + terms).astype(BF)
    out_ref[:, EXT:] = total[:, EXT:].astype(BF)


def finish_kernel(place_ref, routes_ref, a_ref, b_ref, dx_ref, gg_ref):
    y = place_ref[1]
    routes = routes_ref[...]
    ncode = node_codes(route_tables(routes, 128))
    col = iota((128, ROWS_N), 1)
    spread = onehot(div40(col) == iota((128, ROWS_N), 0)).astype(BF)
    code = dot(ncode.astype(BF), spread)
    col = iota((TOK, ROWS_N), 1)
    cn = div40(col)
    cp = col - 40 * cn
    cq = div5(cp)
    match = code == (cp - 5 * cq + 1).astype(F32)
    for q in range(7):
        pick = onehot(match & (cq == q)).astype(BF)
        dx_ref[:, 512 * q : 512 * (q + 1)] = dot(pick, a_ref[...]).astype(BF)
        dx_ref[:, 3584 + 512 * q : 3584 + 512 * (q + 1)] = dot(pick, b_ref[...]).astype(BF)
    last = match & (cq == 7)
    masks = jnp.concatenate(
        [onehot(last & (cn == (routes[:, k : k + 1] >> 2))) for k in range(8)], axis=0
    ).astype(BF)
    terms = dot(masks, a_ref[:, :EXT])
    lane = iota((TOK, EXT), 1)
    result = jnp.zeros((TOK, EXT), F32)
    for k in range(8):
        s = ((routes[:, k : k + 1] & 3) - y) & 3
        mine = jnp.where((lane >> 1) == s, terms[TOK * k : TOK * (k + 1)], 0.0)
        result = jnp.where(lane == k, jnp.sum(mine, axis=1, keepdims=True), result)
    gg_ref[...] = result[:, :8]


SMEM = pl.BlockSpec(memory_space=pltpu.SMEM)
VM = pl.BlockSpec(memory_space=pltpu.VMEM)
PARAMS = pltpu.CompilerParams(vmem_limit_bytes=VMEM_LIMIT)


def sds(shape, dtype=BF):
    return jax.ShapeDtypeStruct(shape, dtype)


def whole(kernel, out_shape, in_specs, name):
    multi = isinstance(out_shape, (list, tuple))
    return pl.pallas_call(
        kernel,
        out_shape=out_shape,
        in_specs=in_specs,
        out_specs=[VM] * len(out_shape) if multi else VM,
        compiler_params=PARAMS,
        name=name,
    )


def shift_y(v, s):
    return lax.ppermute(v, "local", [(i, (i + 2 * s) % 8) for i in range(8)])


def swap_core(v):
    return lax.ppermute(v, "local", [(i, i ^ 1) for i in range(8)])


def node_exchange(v):
    shape = v.shape
    v = v.reshape(N_NODE, shape[0] // N_NODE, shape[1])
    return lax.all_to_all(v, "node", split_axis=0, concat_axis=0, tiled=True).reshape(shape)


def on_device(tokens, out_grads, routes, gate_values, gate_weight, up_weight, down_weight):
    w_gate = gate_weight[0]
    w_up = up_weight[0]
    w_down = down_weight[0]
    place = jnp.stack([lax.axis_index("node"), lax.axis_index("local") // 2]).astype(I32)

    x_own = jnp.concatenate([tokens, jnp.pad(routes.astype(BF), ((0, 0), (0, EXT - 8)))], axis=1)
    x_near = [x_own] + [shift_y(x_own, s) for s in (1, 2, 3)]

    dy_send = whole(send_dy_kernel, sds((ROWS_N, 1024)), [VM] * 3, "send_dy")(
        routes, gate_values, out_grads
    )
    dy_mid = node_exchange(dy_send)
    x_send = whole(send_x_kernel, sds((384, 3584)), [SMEM] + [VM] * 4, "send_x")(place, *x_near)
    x_mine = node_exchange(x_send)

    *dy_out, table = whole(
        regroup_kernel,
        [sds((ROWS_Y, WIDTH))] * 4 + [sds((ROWS_N, 128), F32)],
        [SMEM, VM],
        "regroup",
    )(place, dy_mid)
    dy_mine = [dy_out[0]] + [shift_y(dy_out[s], s) for s in (1, 2, 3)]
    dy_other = [swap_core(v) for v in dy_mine]
    x_other = swap_core(x_mine)

    back = pl.pallas_call(
        back_kernel,
        grid=(7,),
        out_shape=sds((2 * SLOTS, HALF), F32),
        in_specs=[pl.BlockSpec((ROWS_Y, 1024), lambda i: (0, i))] * 8
        + [pl.BlockSpec((HALF, 1024), lambda i: (0, i))],
        out_specs=pl.BlockSpec((2 * SLOTS, HALF), lambda i: (0, 0)),
        compiler_params=PARAMS,
        name="back",
    )(*dy_mine, *dy_other, w_down)

    full = lambda shape: pl.BlockSpec(shape, lambda i: (0, 0))
    d_gate, d_up, ext = pl.pallas_call(
        forward_kernel,
        grid=(14,),
        out_shape=[sds((2 * SLOTS, HALF)), sds((2 * SLOTS, HALF)), sds((2 * SLOTS, EXT))],
        in_specs=[pl.BlockSpec((384, 512), lambda i: (0, lax.rem(i, 7)))] * 2
        + [pl.BlockSpec((512, HALF), lambda i: (i, 0))] * 2
        + [full((2 * SLOTS, HALF))],
        out_specs=[full((2 * SLOTS, HALF)), full((2 * SLOTS, HALF)), full((2 * SLOTS, EXT))],
        scratch_shapes=[pltpu.VMEM((2 * SLOTS, HALF), F32)] * 2,
        compiler_params=PARAMS,
        name="forward",
    )(x_mine, x_other, w_gate, w_up, back)

    halves = []
    for part in range(2):
        rows = pl.BlockSpec((512, HALF), functools.partial(lambda p, i: (7 * p + i, 0), part))
        own, other = pl.pallas_call(
            dx_kernel,
            grid=(7,),
            out_shape=[sds((SLOTS, 3584 + EXT))] * 2,
            in_specs=[full((2 * SLOTS, HALF))] * 2 + [rows] * 2 + [full((2 * SLOTS, EXT))],
            out_specs=[full((SLOTS, 3584 + EXT))] * 2,
            compiler_params=PARAMS,
            name="dx",
        )(d_gate, d_up, w_gate, w_up, ext)
        got = swap_core(other)
        pieces = whole(add_kernel, [sds((ROWS_Y, 3584 + EXT))] * 4, [VM] * 2, "add_halves")(own, got)
        pieces = [pieces[0]] + [shift_y(pieces[s], -s) for s in (1, 2, 3)]
        mixed = whole(combine_kernel, sds((ROWS_N, 512)), [VM] * 5, "combine")(table, *pieces)
        halves.append(node_exchange(mixed))

    return tuple(
        whole(
            finish_kernel, [sds((TOK, WIDTH)), sds((TOK, 8), F32)], [SMEM] + [VM] * 3, "finish"
        )(place, routes, *halves)
    )


def solution(mesh):
    row = P(("node", "local"), None)
    weight = P(("node", "local"), None, None)
    return jax.shard_map(
        on_device,
        mesh=mesh,
        in_specs=(row, row, row, row, weight, weight, weight),
        out_specs=(row, row),
        check_vma=False,
    )
```

time: 534 us -> 249 us (0.47); the launches traced: 527 us -> 247 us
  waiting for transfers between devices: 230 us -> 77.2 us
  local copies, waits for them, and re-layouts: 115 us -> 2.04 us
  Pallas kernels: 0 us -> 59 us
  matrix products: 42.9 us -> 0 us
  starting transfers between devices: 44.5 us -> 21 us
  other arithmetic: 24 us -> 1.72 us
  blocking collectives: 69.2 us -> 85.6 us
    all_to_all x8 -> x1, waiting for transfers between devices: 230 us -> 0.01 us  [node_exchange(): lax.all_to_all(v, 'node', split_axis=0, concat_axis=0, tiled=True)]
    ppermute x0 -> x19, waiting for transfers between devices: none -> 77.2 us  [the longest x12 74.6 us: shift_y(): return lax.ppermute(v, 'local', [(i, (i + 2 * s) % 8) for i in range(8)])]
    pallas_call x0 -> x12, Pallas kernels: none -> 59 us  [the longest x1 17.3 us: on_device(): pl.pallas_call(forward_kernel, grid=(14,), out_shape=[sds((2 * SLOTS, HAL...]
    dot_general x5 -> x0, matrix products: 42.9 us -> none  [the longest x1 11.3 us: shard_terms(): lax.dot_general(d_up, w_up, (((1,), (1,)), ((), ())), preferred_element_t...]
    reshape x15 -> x0, local copies, waits for them, and re-layouts: 42.1 us -> none  [the longest x2 21.7 us: on_device(): part_dx.reshape(n_local, n_node, cap_exp, width)]
    all_to_all x8 -> x1, starting transfers between devices: 44.5 us -> 4.16 us  [node_exchange(): lax.all_to_all(v, 'node', split_axis=0, concat_axis=0, tiled=True)]
    gather x7 -> x0, local copies, waits for them, and re-layouts: 38 us -> none  [the longest x2 19.6 us: finish_slots(): jnp.take(backward_input_gradient.reshape(slots, width), flat_index, axis=0)]
    all_to_all x5 -> x0, local copies, waits for them, and re-layouts: 19.2 us -> none  [the longest x1 10.3 us: on_device(): lax.all_to_all(lax.all_to_all(part_dx.reshape(n_local, n_node, cap_exp, w...]
  transfers between devices with their start and end apart: 8 -> 20, of which waited for: 5 -> 12; matrix products, arithmetic and copies ran while one was open for 15% -> 0% of each run, Pallas kernels for 0% -> 12%
where the time goes in v1:
time: 249 us; the launch traced here: 247 us
  blocking collectives  85.6 us (34%)
  waiting for transfers between devices  77.2 us (31%)
  Pallas kernels  59 us (24%)
  starting transfers between devices  21 us (8%)
    all_to_all x3, blocking collectives, node_exchange(): lax.all_to_all(v, 'node', split_axis=0, concat_axis=0, tiled=True)  85.6 us
    ppermute x12, waiting for transfers between devices, shift_y(): return lax.ppermute(v, 'local', [(i, (i + 2 * s) % 8) for i in range(8)])  74.6 us
    pallas_call x1, Pallas kernels, on_device(): pl.pallas_call(forward_kernel, grid=(14,), out_shape=[sds((2 * SLOTS, HAL...  17.3 us
    ppermute x12, starting transfers between devices, shift_y(): return lax.ppermute(v, 'local', [(i, (i + 2 * s) % 8) for i in range(8)])  15.8 us
    pallas_call x2, Pallas kernels, on_device(): pl.pallas_call(dx_kernel, grid=(7,), out_shape=[sds((SLOTS, 3584 + EXT))]...  15.7 us
    pallas_call x1, Pallas kernels, on_device(): pl.pallas_call(back_kernel, grid=(7,), out_shape=sds((2 * SLOTS, HALF), F...  8.62 us
    pallas_call x2, Pallas kernels, on_device(): whole(combine_kernel, sds((ROWS_N, 512)), [VM] * 5, 'combine')  5.36 us
  transfers between devices with their start and end apart: 20, of which 12 were waited for; matrix products, arithmetic and copies ran while one was open for 0% of the time, Pallas kernels for 12%

profile of v1, /device:TPU:0, one launch (start us, length us, event | category | flops | bytes accessed | tf_op | source)
XLA Modules:
  0.0 247.4 jit_solution(5961818499327238477)
XLA Ops:
  2.4 1.7 collective-permute-start
  4.1 2.9 %collective-permute-start.1 = (bf16[16,7296]{1,0:T(8,128)(2,1)S(1)}, bf16[16,7296]{1,0:T(8,128)(2,1)S(1)}, u32[]{:S(2)}, u32[]{:S(2)}) collective-permute-start(bf16[16,7296]{1,0:T(8,128)(2,1)S(1)} %fusion.1.x0_ref), channel_id=1, source_target_pairs={{0,4},{1,5},{2,6},{3,7},{4,0},{5,1},{6,2},{7,3},{8,12},{9,13},{10,... | collective-permute-start | bytes 700424 | tf_op jit(solution)/shard_map/ppermute | solution.py:323
  7.0 1.3 collective-permute-start.2
  8.4 2.8 %collective-permute-done.x1_ref = bf16[16,7296]{1,0:T(8,128)(2,1)S(1)} collective-permute-done((bf16[16,7296]{1,0:T(8,128)(2,1)S(1)}, bf16[16,7296]{1,0:T(8,128)(2,1)S(1)}, u32[]{:S(2)}, u32[]{:S(2)}) %collective-permute-start) | collective-permute-done | bytes 233504 | tf_op jit(solution)/shard_map/ppermute | solution.py:323
  11.2 6.2 %collective-permute-done.1.x2_ref = bf16[16,7296]{1,0:T(8,128)(2,1)S(1)} collective-permute-done((bf16[16,7296]{1,0:T(8,128)(2,1)S(1)}, bf16[16,7296]{1,0:T(8,128)(2,1)S(1)}, u32[]{:S(2)}, u32[]{:S(2)}) %collective-permute-start.1) | collective-permute-done | bytes 233504 | tf_op jit(solution)/shard_map/ppermute | solution.py:323
  17.4 1.8 send_x.1
  19.3 42.2 %all_to_all.20 = bf16[16,24,3584]{2,1,0:T(8,128)(2,1)S(1)} all-to-all(bf16[16,24,3584]{2,1,0:T(8,128)(2,1)S(1)} %bitcast.15), channel_id=1, replica_groups=mesh['node'=16,'local'=8] {'node'}, dimensions={0} | all-to-all | bytes 5505024 | tf_op jit(solution)/shard_map/all_to_all | solution.py:333
  62.5 23.8 %all_to_all.21 = bf16[16,40,1024]{2,1,0:T(8,128)(2,1)S(1)} all-to-all(bf16[16,40,1024]{2,1,0:T(8,128)(2,1)S(1)} %bitcast.17), channel_id=1, replica_groups=mesh['node'=16,'local'=8] {'node'}, dimensions={0} | all-to-all | bytes 2621440 | tf_op jit(solution)/shard_map/all_to_all | solution.py:333
  86.3 3.6 %regroup.1 = (bf16[48,7168]{1,0:T(8,128)(2,1)S(1)}, bf16[48,7168]{1,0:T(8,128)(2,1)S(1)}, bf16[48,7168]{1,0:T(8,128)(2,1)S(1)}, bf16[48,7168]{1,0:T(8,128)(2,1)S(1)}, f32[640,128]{1,0:T(8,128)S(1)}) custom-call(s32[2]{0:T(128)S(1)} %pad_add_fusion.place_ref, bf16[640,1024]{1,0:T(8,128)(2,1)S(1)} %bitcast.16), custom_call_target="tpu_custom_call" | custom-call | tf_op jit(solution)/shard_map/regroup/pallas_call | solution.py:352
  89.9 3.7 %collective-permute-start.6 = (bf16[48,7168]{1,0:T(8,128)(2,1)S(1)}, bf16[48,7168]{1,0:T(8,128)(2,1)S(1)}, u32[]{:S(2)}, u32[]{:S(2)}) collective-permute-start(bf16[48,7168]{1,0:T(8,128)(2,1)S(1)} %get-tuple-element.26), channel_id=1, source_target_pairs={{0,6},{1,7},{2,0},{3,1},{4,2},{5,3},{6,4},{7,5},{8,14},{9,15},{10,... | collective-permute-start | bytes 2064392 | tf_op jit(solution)/shard_map/ppermute | solution.py:323
  93.6 1.5 collective-permute-start.5
  95.2 26.9 %collective-permute-done.6.refs_3_ = bf16[48,7168]{1,0:T(8,128)(2,1)S(1)} collective-permute-done((bf16[48,7168]{1,0:T(8,128)(2,1)S(1)}, bf16[48,7168]{1,0:T(8,128)(2,1)S(1)}, u32[]{:S(2)}, u32[]{:S(2)}) %collective-permute-start.6) | collective-permute-done | bytes 688160 | tf_op jit(solution)/shard_map/ppermute | solution.py:323
  122.1 3.4 %collective-permute-done.4.refs_1_ = bf16[48,7168]{1,0:T(8,128)(2,1)S(1)} collective-permute-done((bf16[48,7168]{1,0:T(8,128)(2,1)S(1)}, bf16[48,7168]{1,0:T(8,128)(2,1)S(1)}, u32[]{:S(2)}, u32[]{:S(2)}) %collective-permute-start.4) | collective-permute-done | bytes 688160 | tf_op jit(solution)/shard_map/ppermute | solution.py:323
  126.0 1.6 collective-permute-done.8.refs_5_
  128.6 8.6 %back.1.back_ref = f32[384,512]{1,0:T(8,128)} custom-call(bf16[48,7168]{1,0:T(8,128)(2,1)S(1)} %get-tuple-element.23.refs_0_, bf16[48,7168]{1,0:T(8,128)(2,1)S(1)} %collective-permute-done.4.refs_1_, bf16[48,7168]{1,0:T(8,128)(2,1)S(1)} %collective-permute-done.5.refs_2_, bf16[48,7168]{1,0:T(8,128)(2,1)S(1)} %collective-permute-done.6.refs_3_, ...), custom_call_target="tpu_custom_call" | custom-call | tf_op jit(solution)/shard_map/back/pallas_call | solution.py:362
  137.3 1.1 copy-done
  138.4 17.3 %forward.1 = (bf16[384,512]{1,0:T(8,128)(2,1)S(1)}, bf16[384,512]{1,0:T(8,128)(2,1)S(1)}, bf16[384,128]{1,0:T(8,128)(2,1)S(1)}) custom-call(bf16[384,3584]{1,0:T(8,128)(2,1)S(1)} %bitcast.14, bf16[384,3584]{1,0:T(8,128)(2,1)} %collective-permute-done.3.other_ref, bf16[7168,512]{1,0:T(8,128)(2,1)} %bitcast.21, bf16[7168,512]{1,0:T(8,128)(2,1)} %bitcast.24, ...), custom_call_target="tpu_custom_call" | custom-call | tf_op jit(solution)/shard_map/forward/pallas_call | solution.py:374
  155.7 7.3 %dx.3 = (bf16[192,3712]{1,0:T(8,128)(2,1)S(1)}, bf16[192,3712]{1,0:T(8,128)(2,1)S(1)}) custom-call(bf16[384,512]{1,0:T(8,128)(2,1)S(1)} %get-tuple-element.27.dgate_ref, bf16[384,512]{1,0:T(8,128)(2,1)S(1)} %get-tuple-element.28.dup_ref, bf16[7168,512]{1,0:T(8,128)(2,1)} %bitcast.22, bf16[7168,512]{1,0:T(8,128)(2,1)} %bitcast.25, ...), custom_call_target="tpu_custom_call" | custom-call | tf_op jit(solution)/shard_map/dx/pallas_call | solution.py:390
  163.3 8.4 %dx.2 = (bf16[192,3712]{1,0:T(8,128)(2,1)S(1)}, bf16[192,3712]{1,0:T(8,128)(2,1)}) custom-call(bf16[384,512]{1,0:T(8,128)(2,1)S(1)} %get-tuple-element.27.dgate_ref, bf16[384,512]{1,0:T(8,128)(2,1)S(1)} %get-tuple-element.28.dup_ref, bf16[7168,512]{1,0:T(8,128)(2,1)} %bitcast.23, bf16[7168,512]{1,0:T(8,128)(2,1)} %bitcast.26, ...), custom_call_target="tpu_custom_call" | custom-call | tf_op jit(solution)/shard_map/dx/pallas_call | solution.py:390
  172.7 1.5 collective-permute-start.16
  175.2 8.9 %collective-permute-done.16.p1_ref = bf16[48,3712]{1,0:T(8,128)(2,1)S(1)} collective-permute-done((bf16[48,3712]{1,0:T(8,128)(2,1)S(1)}, bf16[48,3712]{1,0:T(8,128)(2,1)S(1)}, u32[]{:S(2)}, u32[]{:S(2)}) %collective-permute-start.16) | collective-permute-done | bytes 356384 | tf_op jit(solution)/shard_map/ppermute | solution.py:323
  184.1 2.8 %collective-permute-done.17.p2_ref = bf16[48,3712]{1,0:T(8,128)(2,1)S(1)} collective-permute-done((bf16[48,3712]{1,0:T(8,128)(2,1)S(1)}, bf16[48,3712]{1,0:T(8,128)(2,1)S(1)}, u32[]{:S(2)}, u32[]{:S(2)}) %collective-permute-start.17) | collective-permute-done | bytes 356384 | tf_op jit(solution)/shard_map/ppermute | solution.py:323
  187.0 6.4 %collective-permute-done.18.p3_ref = bf16[48,3712]{1,0:T(8,128)(2,1)S(1)} collective-permute-done((bf16[48,3712]{1,0:T(8,128)(2,1)S(1)}, bf16[48,3712]{1,0:T(8,128)(2,1)S(1)}, u32[]{:S(2)}, u32[]{:S(2)}) %collective-permute-start.18) | collective-permute-done | bytes 356384 | tf_op jit(solution)/shard_map/ppermute | solution.py:323
  193.4 3.1 %combine.3 = bf16[640,512]{1,0:T(8,128)(2,1)} custom-call(f32[640,128]{1,0:T(8,128)S(1)} %get-tuple-element.22.table_ref, bf16[48,3712]{1,0:T(8,128)(2,1)S(1)} %get-tuple-element.38.p0_ref, bf16[48,3712]{1,0:T(8,128)(2,1)S(1)} %collective-permute-done.16.p1_ref, bf16[48,3712]{1,0:T(8,128)(2,1)S(1)} %collective-permute-done.17.p2_ref, ...), custom_call_target="tpu_custom_call" | custom-call | tf_op jit(solution)/shard_map/combine/pallas_call | solution.py:402
  196.5 4.2 %all-to-all-start.3 = ((bf16[16,40,512]{2,1,0:T(8,128)(2,1)}), bf16[16,40,512]{2,1,0:T(8,128)(2,1)S(1)}, u32[]{:S(2)}, u32[]{:S(2)}) async-start(bf16[16,40,512]{2,1,0:T(8,128)(2,1)} %bitcast.11), calls=%async_computation.3 | async-start | bytes 1310720 | tf_op jit(solution)/shard_map/all_to_all | solution.py:333
  200.7 2.0 add_halves.2
  204.8 9.2 %collective-permute-done.12.p1_ref = bf16[48,3712]{1,0:T(8,128)(2,1)S(1)} collective-permute-done((bf16[48,3712]{1,0:T(8,128)(2,1)S(1)}, bf16[48,3712]{1,0:T(8,128)(2,1)S(1)}, u32[]{:S(2)}, u32[]{:S(2)}) %collective-permute-start.12) | collective-permute-done | bytes 356384 | tf_op jit(solution)/shard_map/ppermute | solution.py:323
  214.0 2.3 collective-permute-done.13.p2_ref
  216.2 5.6 %collective-permute-done.14.p3_ref = bf16[48,3712]{1,0:T(8,128)(2,1)S(1)} collective-permute-done((bf16[48,3712]{1,0:T(8,128)(2,1)S(1)}, bf16[48,3712]{1,0:T(8,128)(2,1)S(1)}, u32[]{:S(2)}, u32[]{:S(2)}) %collective-permute-start.14) | collective-permute-done | bytes 356384 | tf_op jit(solution)/shard_map/ppermute | solution.py:323
  221.8 2.3 combine.2
  224.1 19.7 %all_to_all.22 = bf16[16,40,512]{2,1,0:T(8,128)(2,1)S(1)} all-to-all(bf16[16,40,512]{2,1,0:T(8,128)(2,1)S(1)} %bitcast.18), channel_id=1, replica_groups=mesh['node'=16,'local'=8] {'node'}, dimensions={0} | all-to-all | bytes 1310720 | tf_op jit(solution)/shard_map/all_to_all | solution.py:333
  243.8 2.9 %finish.1 = (bf16[16,7168]{1,0:T(8,128)(2,1)}, f32[16,8]{1,0:T(8,128)S(1)}) custom-call(s32[2]{0:T(128)S(1)} %pad_add_fusion.place_ref, s32[16,8]{1,0:T(8,128)S(1)} %copy.17.routes_ref, bf16[640,512]{1,0:T(8,128)(2,1)S(1)} %bitcast.20, bf16[640,512]{1,0:T(8,128)(2,1)S(1)} %bitcast.19), custom_call_target="tpu_custom_call" | custom-call | tf_op jit(solution)/shard_map/finish/pallas_call | solution.py:406
  (38 shorter events, 9.4 us)
Async XLA Ops:
  2.4 8.9 %collective-permute-start = (bf16[16,7296]{1,0:T(8,128)(2,1)S(1)}, bf16[16,7296]{1,0:T(8,128)(2,1)S(1)}, u32[]{:S(2)}, u32[]{:S(2)}) collective-permute-start(bf16[16,7296]{1,0:T(8,128)(2,1)S(1)} %fusion.1.x0_ref), channel_id=1, source_target_pairs={{0,2},{1,3},{2,4},{3,5},{4,6},{5,7},{6,0},{7,1},{8,10},{9,11},{10,... | collective-permute-start | bytes 700424 | tf_op jit(solution)/shard_map/ppermute | solution.py:323
  4.1 13.3 %collective-permute-start.1 = (bf16[16,7296]{1,0:T(8,128)(2,1)S(1)}, bf16[16,7296]{1,0:T(8,128)(2,1)S(1)}, u32[]{:S(2)}, u32[]{:S(2)}) collective-permute-start(bf16[16,7296]{1,0:T(8,128)(2,1)S(1)} %fusion.1.x0_ref), channel_id=1, source_target_pairs={{0,4},{1,5},{2,6},{3,7},{4,0},{5,1},{6,2},{7,3},{8,12},{9,13},{10,... | collective-permute-start | bytes 700424 | tf_op jit(solution)/shard_map/ppermute | solution.py:323
  7.0 10.4 %collective-permute-start.2 = (bf16[16,7296]{1,0:T(8,128)(2,1)S(1)}, bf16[16,7296]{1,0:T(8,128)(2,1)S(1)}, u32[]{:S(2)}, u32[]{:S(2)}) collective-permute-start(bf16[16,7296]{1,0:T(8,128)(2,1)S(1)} %fusion.1.x0_ref), channel_id=1, source_target_pairs={{0,6},{1,7},{2,0},{3,1},{4,2},{5,3},{6,4},{7,5},{8,14},{9,15},{10,... | collective-permute-start | bytes 700424 | tf_op jit(solution)/shard_map/ppermute | solution.py:323
  19.2 42.2 %copy-start.2 = (s32[16,8]{0,1:T(8,128)S(1)}, s32[16,8]{0,1:T(8,128)}, u32[]{:S(2)}) copy-start(s32[16,8]{0,1:T(8,128)} %param.9) | copy-start | bytes 1540
  19.2 42.3 %copy-start.3 = (f32[16,8]{0,1:T(8,128)S(1)}, f32[16,8]{0,1:T(8,128)}, u32[]{:S(2)}) copy-start(f32[16,8]{0,1:T(8,128)} %param.10) | copy-start | bytes 1540
  19.2 42.3 %copy-start.1 = (bf16[16,7168]{1,0:T(8,128)(2,1)S(1)}, bf16[16,7168]{1,0:T(8,128)(2,1)}, u32[]{:S(2)}) copy-start(bf16[16,7168]{1,0:T(8,128)(2,1)} %dy_ref.1) | copy-start | bytes 688132
  61.4 75.9 %collective-permute-start.3 = (bf16[384,3584]{1,0:T(8,128)(2,1)S(1)}, bf16[384,3584]{1,0:T(8,128)(2,1)}, u32[]{:S(2)}, u32[]{:S(2)}) collective-permute-start(bf16[384,3584]{1,0:T(8,128)(2,1)S(1)} %bitcast.13), channel_id=1, source_target_pairs={{0,1},{1,0},{2,3},{3,2},{4,5},{5,4},{6,7},{7,6},{8,9},{9,8},{10,11... | collective-permute-start | bytes 8257544 | tf_op jit(solution)/shard_map/ppermute | solution.py:327
  89.9 32.2 %collective-permute-start.6 = (bf16[48,7168]{1,0:T(8,128)(2,1)S(1)}, bf16[48,7168]{1,0:T(8,128)(2,1)S(1)}, u32[]{:S(2)}, u32[]{:S(2)}) collective-permute-start(bf16[48,7168]{1,0:T(8,128)(2,1)S(1)} %get-tuple-element.26), channel_id=1, source_target_pairs={{0,6},{1,7},{2,0},{3,1},{4,2},{5,3},{6,4},{7,5},{8,14},{9,15},{10,... | collective-permute-start | bytes 2064392 | tf_op jit(solution)/shard_map/ppermute | solution.py:323
  93.6 31.9 %collective-permute-start.4 = (bf16[48,7168]{1,0:T(8,128)(2,1)S(1)}, bf16[48,7168]{1,0:T(8,128)(2,1)S(1)}, u32[]{:S(2)}, u32[]{:S(2)}) collective-permute-start(bf16[48,7168]{1,0:T(8,128)(2,1)S(1)} %get-tuple-element.24), channel_id=1, source_target_pairs={{0,2},{1,3},{2,4},{3,5},{4,6},{5,7},{6,0},{7,1},{8,10},{9,11},{10,... | collective-permute-start | bytes 2064392 | tf_op jit(solution)/shard_map/ppermute | solution.py:323
  93.6 31.9 %collective-permute-start.5 = (bf16[48,7168]{1,0:T(8,128)(2,1)S(1)}, bf16[48,7168]{1,0:T(8,128)(2,1)S(1)}, u32[]{:S(2)}, u32[]{:S(2)}) collective-permute-start(bf16[48,7168]{1,0:T(8,128)(2,1)S(1)} %get-tuple-element.25), channel_id=1, source_target_pairs={{0,4},{1,5},{2,6},{3,7},{4,0},{5,1},{6,2},{7,3},{8,12},{9,13},{10,... | collective-permute-start | bytes 2064392 | tf_op jit(solution)/shard_map/ppermute | solution.py:323
  95.2 30.9 %collective-permute-start.7 = (bf16[48,7168]{1,0:T(8,128)(2,1)S(1)}, bf16[48,7168]{1,0:T(8,128)(2,1)S(1)}, u32[]{:S(2)}, u32[]{:S(2)}) collective-permute-start(bf16[48,7168]{1,0:T(8,128)(2,1)S(1)} %get-tuple-element.23.refs_0_), channel_id=1, source_target_pairs={{0,1},{1,0},{2,3},{3,2},{4,5},{5,4},{6,7},{7,6},{8,9},{9,8},{10,11... | collective-permute-start | bytes 2064392 | tf_op jit(solution)/shard_map/ppermute | solution.py:327
  122.1 3.9 %collective-permute-start.10 = (bf16[48,7168]{1,0:T(8,128)(2,1)S(1)}, bf16[48,7168]{1,0:T(8,128)(2,1)S(1)}, u32[]{:S(2)}, u32[]{:S(2)}) collective-permute-start(bf16[48,7168]{1,0:T(8,128)(2,1)S(1)} %collective-permute-done.6.refs_3_), channel_id=1, source_target_pairs={{0,1},{1,0},{2,3},{3,2},{4,5},{5,4},{6,7},{7,6},{8,9},{9,8},{10,11... | collective-permute-start | bytes 2064392 | tf_op jit(solution)/shard_map/ppermute | solution.py:327
  125.5 2.1 collective-permute-start.8
  125.5 3.1 %collective-permute-start.9 = (bf16[48,7168]{1,0:T(8,128)(2,1)S(1)}, bf16[48,7168]{1,0:T(8,128)(2,1)S(1)}, u32[]{:S(2)}, u32[]{:S(2)}) collective-permute-start(bf16[48,7168]{1,0:T(8,128)(2,1)S(1)} %collective-permute-done.5.refs_2_), channel_id=1, source_target_pairs={{0,1},{1,0},{2,3},{3,2},{4,5},{5,4},{6,7},{7,6},{8,9},{9,8},{10,11... | collective-permute-start | bytes 2064392 | tf_op jit(solution)/shard_map/ppermute | solution.py:327
  137.3 1.1 copy-start
  163.1 9.0 %collective-permute-start.15 = (bf16[192,3712]{1,0:T(8,128)(2,1)S(1)}, bf16[192,3712]{1,0:T(8,128)(2,1)S(1)}, u32[]{:S(2)}, u32[]{:S(2)}) collective-permute-start(bf16[192,3712]{1,0:T(8,128)(2,1)S(1)} %get-tuple-element.37), channel_id=1, source_target_pairs={{0,1},{1,0},{2,3},{3,2},{4,5},{5,4},{6,7},{7,6},{8,9},{9,8},{10,11... | collective-permute-start | bytes 4276232 | tf_op jit(solution)/shard_map/ppermute | solution.py:327
  171.7 28.9 %collective-permute-start.11 = (bf16[192,3712]{1,0:T(8,128)(2,1)}, bf16[192,3712]{1,0:T(8,128)(2,1)}, u32[]{:S(2)}, u32[]{:S(2)}) collective-permute-start(bf16[192,3712]{1,0:T(8,128)(2,1)} %get-tuple-element.31), channel_id=1, source_target_pairs={{0,1},{1,0},{2,3},{3,2},{4,5},{5,4},{6,7},{7,6},{8,9},{9,8},{10,11... | collective-permute-start | bytes 4276232 | tf_op jit(solution)/shard_map/ppermute | solution.py:327
  172.7 11.4 %collective-permute-start.16 = (bf16[48,3712]{1,0:T(8,128)(2,1)S(1)}, bf16[48,3712]{1,0:T(8,128)(2,1)S(1)}, u32[]{:S(2)}, u32[]{:S(2)}) collective-permute-start(bf16[48,3712]{1,0:T(8,128)(2,1)S(1)} %get-tuple-element.39), channel_id=1, source_target_pairs={{0,6},{1,7},{2,0},{3,1},{4,2},{5,3},{6,4},{7,5},{8,14},{9,15},{10,... | collective-permute-start | bytes 1069064 | tf_op jit(solution)/shard_map/ppermute | solution.py:323
  174.3 12.7 %collective-permute-start.17 = (bf16[48,3712]{1,0:T(8,128)(2,1)S(1)}, bf16[48,3712]{1,0:T(8,128)(2,1)S(1)}, u32[]{:S(2)}, u32[]{:S(2)}) collective-permute-start(bf16[48,3712]{1,0:T(8,128)(2,1)S(1)} %get-tuple-element.40), channel_id=1, source_target_pairs={{0,4},{1,5},{2,6},{3,7},{4,0},{5,1},{6,2},{7,3},{8,12},{9,13},{10,... | collective-permute-start | bytes 1069064 | tf_op jit(solution)/shard_map/ppermute | solution.py:323
  174.3 19.1 %collective-permute-start.18 = (bf16[48,3712]{1,0:T(8,128)(2,1)S(1)}, bf16[48,3712]{1,0:T(8,128)(2,1)S(1)}, u32[]{:S(2)}, u32[]{:S(2)}) collective-permute-start(bf16[48,3712]{1,0:T(8,128)(2,1)S(1)} %get-tuple-element.41), channel_id=1, source_target_pairs={{0,2},{1,3},{2,4},{3,5},{4,6},{5,7},{6,0},{7,1},{8,10},{9,11},{10,... | collective-permute-start | bytes 1069064 | tf_op jit(solution)/shard_map/ppermute | solution.py:323
  196.5 27.6 %all-to-all-start.3 = ((bf16[16,40,512]{2,1,0:T(8,128)(2,1)}), bf16[16,40,512]{2,1,0:T(8,128)(2,1)S(1)}, u32[]{:S(2)}, u32[]{:S(2)}) async-start(bf16[16,40,512]{2,1,0:T(8,128)(2,1)} %bitcast.11), calls=%async_computation.3 | async-start | bytes 1310720 | tf_op jit(solution)/shard_map/all_to_all | solution.py:333
  202.7 11.3 %collective-permute-start.12 = (bf16[48,3712]{1,0:T(8,128)(2,1)S(1)}, bf16[48,3712]{1,0:T(8,128)(2,1)S(1)}, u32[]{:S(2)}, u32[]{:S(2)}) collective-permute-start(bf16[48,3712]{1,0:T(8,128)(2,1)S(1)} %get-tuple-element.33), channel_id=1, source_target_pairs={{0,6},{1,7},{2,0},{3,1},{4,2},{5,3},{6,4},{7,5},{8,14},{9,15},{10,... | collective-permute-start | bytes 1069064 | tf_op jit(solution)/shard_map/ppermute | solution.py:323
  203.4 12.8 %collective-permute-start.13 = (bf16[48,3712]{1,0:T(8,128)(2,1)S(1)}, bf16[48,3712]{1,0:T(8,128)(2,1)S(1)}, u32[]{:S(2)}, u32[]{:S(2)}) collective-permute-start(bf16[48,3712]{1,0:T(8,128)(2,1)S(1)} %get-tuple-element.34), channel_id=1, source_target_pairs={{0,4},{1,5},{2,6},{3,7},{4,0},{5,1},{6,2},{7,3},{8,12},{9,13},{10,... | collective-permute-start | bytes 1069064 | tf_op jit(solution)/shard_map/ppermute | solution.py:323
  203.7 18.1 %collective-permute-start.14 = (bf16[48,3712]{1,0:T(8,128)(2,1)S(1)}, bf16[48,3712]{1,0:T(8,128)(2,1)S(1)}, u32[]{:S(2)}, u32[]{:S(2)}) collective-permute-start(bf16[48,3712]{1,0:T(8,128)(2,1)S(1)} %get-tuple-element.35), channel_id=1, source_target_pairs={{0,2},{1,3},{2,4},{3,5},{4,6},{5,7},{6,0},{7,1},{8,10},{9,11},{10,... | collective-permute-start | bytes 1069064 | tf_op jit(solution)/shard_map/ppermute | solution.py:323

commit v2 on v1

--- a/solution.py
+++ b/solution.py
@@ -22,7 +22,7 @@
 SLOTS = N_Y * ROWS_Y
 ROWS_N = N_NODE * 40
 EXT = 128
-VMEM_LIMIT = 48 * 1024 * 1024
+VMEM_LIMIT = 36 * 1024 * 1024
 
 
 def iota(shape, dim):
@@ -104,16 +104,8 @@
 def send_x_kernel(place_ref, x0_ref, x1_ref, x2_ref, x3_ref, out_ref):
     y = place_ref[1]
     xs = [x0_ref, x1_ref, x2_ref, x3_ref]
-    routes = jnp.concatenate([r[:, WIDTH : WIDTH + EXT] for r in xs], axis=0).astype(F32)
+    code, _ = near_tables(y, xs)
     lane = iota((64, 128), 1)
-    wanted = jnp.where(lane < N_NODE, 4 * lane + y, -1).astype(F32)
-    hot = jnp.zeros((64, 128), F32)
-    for k in range(8):
-        hot = hot + onehot(routes[:, k : k + 1] == wanted)
-    r64 = iota((64, 64), 0)
-    c64 = iota((64, 64), 1)
-    tri = onehot((c64 < r64) & ((c64 >> 4) == (r64 >> 4))).astype(BF)
-    code = hot * (dot(tri, hot.astype(BF)) + 1.0)
     spread = onehot((lane & 63) == iota((64, 128), 0)).astype(BF)
     code_lane = dot_tn(code.astype(BF), spread)[:N_NODE]
     block = (iota((N_NODE, 128), 1) >> 4).astype(F32)
@@ -161,65 +153,44 @@
 
 def back_kernel(*refs):
     pieces, down_ref, out_ref = refs[:8], refs[8], refs[9]
-
-    @pl.when(pl.program_id(0) == 0)
-    def _():
-        out_ref[...] = jnp.zeros_like(out_ref)
-
     rows = jnp.concatenate([p[...] for p in pieces], axis=0)
-    out_ref[...] += dot_nt(rows, down_ref[...])
-
-
-def forward_kernel(own_ref, other_ref, gate_ref, up_ref, back_ref, dgate_ref, dup_ref, ext_ref, pg_ref, pu_ref):
-    step = pl.program_id(0)
-
-    @pl.when(step == 0)
-    def _():
-        pg_ref[...] = jnp.zeros_like(pg_ref)
-        pu_ref[...] = jnp.zeros_like(pu_ref)
-
-    h = jnp.where(step >= 7, 1, 0)
+    out_ref[...] = dot_nt(rows, down_ref[...])
+
+
+def forward_kernel(own_ref, other_ref, gate_ref, up_ref, back_ref, dgate_ref, dup_ref, ext_ref, x_ref):
     row = iota((SLOTS, 384), 0)
     s = div3(row >> 4)
     rem = row - ROWS_Y * s
     n = div3(rem)
     r = rem - 3 * n
-    perm = onehot(iota((SLOTS, 384), 1) == 24 * n + 12 * h + 3 * s + r).astype(BF)
-    rows = jnp.concatenate(
-        [dot(perm, own_ref[...]).astype(BF), dot(perm, other_ref[...]).astype(BF)], axis=0
-    )
-    pg_ref[...] += dot(rows, gate_ref[...])
-    pu_ref[...] += dot(rows, up_ref[...])
-
-    @pl.when(step == 13)
-    def _():
-        pre_gate = pg_ref[...]
-        pre_up = pu_ref[...]
-        back = back_ref[...]
-        sig = jax.nn.sigmoid(pre_gate)
-        act = pre_gate * sig
-        hidden = (act * pre_up).astype(BF)
-        part = jnp.sum(hidden.astype(F32) * back, axis=1, keepdims=True)
-        dgate_ref[...] = (back * pre_up * sig * (1.0 + pre_gate * (1.0 - sig))).astype(BF)
-        dup_ref[...] = (back * act).astype(BF)
-        high = part.astype(BF).astype(F32)
-        low = part - high
-        slot = iota((2 * SLOTS, EXT), 0)
-        slot = jnp.where(slot >= SLOTS, slot - SLOTS, slot)
-        at = 2 * div3(slot >> 4)
-        lane = iota((2 * SLOTS, EXT), 1)
-        ext_ref[...] = jnp.where(lane == at, high, jnp.where(lane == at + 1, low, 0.0)).astype(BF)
-
-
-def dx_kernel(dgate_ref, dup_ref, gate_ref, up_ref, ext_ref, own_ref, other_ref):
-    step = pl.program_id(0)
-    part = (dot_nt(dgate_ref[...], gate_ref[...]) + dot_nt(dup_ref[...], up_ref[...])).astype(BF)
-    at = pl.multiple_of(step * 512, 512)
-    own_ref[:, pl.ds(at, 512)] = part[:SLOTS]
-    other_ref[:, pl.ds(at, 512)] = part[SLOTS:]
-
-    @pl.when(step == 0)
-    def _():
+    for h in range(2):
+        perm = onehot(iota((SLOTS, 384), 1) == 24 * n + 12 * h + 3 * s + r).astype(BF)
+        x_ref[:SLOTS, 3584 * h : 3584 * (h + 1)] = dot(perm, own_ref[...]).astype(BF)
+        x_ref[SLOTS:, 3584 * h : 3584 * (h + 1)] = dot(perm, other_ref[...]).astype(BF)
+    pre_gate = dot(x_ref[...], gate_ref[...])
+    pre_up = dot(x_ref[...], up_ref[...])
+    back = back_ref[...]
+    sig = jax.nn.sigmoid(pre_gate)
+    act = pre_gate * sig
+    hidden = (act * pre_up).astype(BF)
+    part = jnp.sum(hidden.astype(F32) * back, axis=1, keepdims=True)
+    dgate_ref[...] = (back * pre_up * sig * (1.0 + pre_gate * (1.0 - sig))).astype(BF)
+    dup_ref[...] = (back * act).astype(BF)
+    high = part.astype(BF).astype(F32)
+    low = part - high
+    slot = iota((2 * SLOTS, EXT), 0)
+    slot = jnp.where(slot >= SLOTS, slot - SLOTS, slot)
+    at = 2 * div3(slot >> 4)
+    lane = iota((2 * SLOTS, EXT), 1)
+    ext_ref[...] = jnp.where(lane == at, high, jnp.where(lane == at + 1, low, 0.0)).astype(BF)
+
+
+def dx_kernel(part, dgate_ref, dup_ref, gate_ref, up_ref, ext_ref, own_ref, other_ref):
+    cols = slice(3584 * part, 3584 * (part + 1))
+    out = (dot_nt(dgate_ref[...], gate_ref[cols, :]) + dot_nt(dup_ref[...], up_ref[cols, :])).astype(BF)
+    own_ref[:, :3584] = out[:SLOTS]
+    other_ref[:, :3584] = out[SLOTS:]
+    if part == 0:
         own_ref[:, 3584:] = ext_ref[:SLOTS]
         other_ref[:, 3584:] = ext_ref[SLOTS:]
 
@@ -238,6 +209,54 @@
         outs[s][:, 3584:] = jnp.where(
             lane == 2 * s, high, jnp.where(lane == 2 * s + 1, low, 0.0)
         ).astype(BF)
+
+
+def add_to_nodes_kernel(own_ref, got_ref, out_ref):
+    row = iota((384, 384), 0)
+    block = div3(row >> 3)
+    rest = row - 24 * block
+    h = jnp.where(rest >= 12, 1, 0)
+    rest = rest - 12 * h
+    s = div3(rest)
+    source = SLOTS * h + ROWS_Y * s + 3 * block + (rest - 3 * s)
+    perm = onehot(iota((384, 384), 1) == source).astype(BF)
+    total = (own_ref[...].astype(F32) + got_ref[...].astype(F32)).astype(BF)
+    out_ref[...] = dot(perm, jnp.concatenate([total[:, :1792], total[:, 1792:]], axis=0)).astype(BF)
+
+
+def near_tables(y, xs):
+    meta = jnp.concatenate([r[:, WIDTH : WIDTH + EXT] for r in xs], axis=0).astype(F32)
+    lane = iota((64, 128), 1)
+    wanted = jnp.where(lane < N_NODE, 4 * lane + y, -1).astype(F32)
+    hot = jnp.zeros((64, 128), F32)
+    gate = jnp.zeros((64, 128), F32)
+    for k in range(8):
+        here = meta[:, k : k + 1] == wanted
+        hot = hot + onehot(here)
+        gate = gate + jnp.where(here, meta[:, 8 + k : 9 + k], 0.0)
+    r64 = iota((64, 64), 0)
+    c64 = iota((64, 64), 1)
+    tri = onehot((c64 < r64) & ((c64 >> 4) == (r64 >> 4))).astype(BF)
+    return hot * (dot(tri, hot.astype(BF)) + 1.0), gate
+
+
+def combine_near_kernel(place_ref, x0_ref, x1_ref, x2_ref, x3_ref, rows_ref, *outs):
+    code, gate = near_tables(place_ref[1], [x0_ref, x1_ref, x2_ref, x3_ref])
+    col = iota((128, 384), 1)
+    spread = onehot(div3(col >> 3) == iota((128, 384), 0)).astype(BF)
+    code = dot(code.astype(BF), spread)
+    gate = dot(gate.astype(BF), spread)
+    col = iota((64, 384), 1)
+    rest = col - 24 * div3(col >> 3)
+    half = jnp.where(rest >= 12, 1, 0)
+    rest = rest - 12 * half
+    s = div3(rest)
+    match = (s == (iota((64, 384), 0) >> 4)) & (code == (rest - 3 * s + 1).astype(F32))
+    for h in range(2):
+        weight = jnp.where(match & (half == h), gate, 0.0).astype(BF)
+        total = dot(weight, rows_ref[...]).astype(BF)
+        for s in range(N_Y):
+            outs[s][:, 1792 * h : 1792 * (h + 1)] = total[TOK * s : TOK * (s + 1)]
 
 
 def combine_kernel(table_ref, p0_ref, p1_ref, p2_ref, p3_ref, out_ref):
@@ -268,7 +287,7 @@
     out_ref[:, EXT:] = total[:, EXT:].astype(BF)
 
 
-def finish_kernel(place_ref, routes_ref, a_ref, b_ref, dx_ref, gg_ref):
+def finish_kernel(place_ref, routes_ref, a_ref, b0_ref, b1_ref, b2_ref, b3_ref, dx_ref, gg_ref):
     y = place_ref[1]
     routes = routes_ref[...]
     ncode = node_codes(route_tables(routes, 128))
@@ -283,7 +302,9 @@
     for q in range(7):
         pick = onehot(match & (cq == q)).astype(BF)
         dx_ref[:, 512 * q : 512 * (q + 1)] = dot(pick, a_ref[...]).astype(BF)
-        dx_ref[:, 3584 + 512 * q : 3584 + 512 * (q + 1)] = dot(pick, b_ref[...]).astype(BF)
+    total = b0_ref[...].astype(F32) + b1_ref[...].astype(F32)
+    total = total + b2_ref[...].astype(F32) + b3_ref[...].astype(F32)
+    dx_ref[:, 3584:] = total.astype(BF)
     last = match & (cq == 7)
     masks = jnp.concatenate(
         [onehot(last & (cn == (routes[:, k : k + 1] >> 2))) for k in range(8)], axis=0
@@ -307,13 +328,14 @@
     return jax.ShapeDtypeStruct(shape, dtype)
 
 
-def whole(kernel, out_shape, in_specs, name):
+def whole(kernel, out_shape, in_specs, name, scratch=()):
     multi = isinstance(out_shape, (list, tuple))
     return pl.pallas_call(
         kernel,
         out_shape=out_shape,
         in_specs=in_specs,
         out_specs=[VM] * len(out_shape) if multi else VM,
+        scratch_shapes=list(scratch),
         compiler_params=PARAMS,
         name=name,
     )
@@ -339,73 +361,64 @@
     w_down = down_weight[0]
     place = jnp.stack([lax.axis_index("node"), lax.axis_index("local") // 2]).astype(I32)
 
-    x_own = jnp.concatenate([tokens, jnp.pad(routes.astype(BF), ((0, 0), (0, EXT - 8)))], axis=1)
-    x_near = [x_own] + [shift_y(x_own, s) for s in (1, 2, 3)]
-
     dy_send = whole(send_dy_kernel, sds((ROWS_N, 1024)), [VM] * 3, "send_dy")(
         routes, gate_values, out_grads
     )
+    dy_send, tokens = lax.optimization_barrier((dy_send, tokens))
     dy_mid = node_exchange(dy_send)
+    picks = jnp.concatenate([routes.astype(BF), gate_values.astype(BF)], axis=1)
+    x_own = jnp.concatenate([tokens, jnp.pad(picks, ((0, 0), (0, EXT - 16)))], axis=1)
+    x_near = [x_own] + [shift_y(x_own, s) for s in (1, 2, 3)]
+
     x_send = whole(send_x_kernel, sds((384, 3584)), [SMEM] + [VM] * 4, "send_x")(place, *x_near)
-    x_mine = node_exchange(x_send)
-
     *dy_out, table = whole(
         regroup_kernel,
         [sds((ROWS_Y, WIDTH))] * 4 + [sds((ROWS_N, 128), F32)],
         [SMEM, VM],
         "regroup",
     )(place, dy_mid)
+    x_send, table = lax.optimization_barrier((x_send, table))
+    x_mine = node_exchange(x_send)
     dy_mine = [dy_out[0]] + [shift_y(dy_out[s], s) for s in (1, 2, 3)]
     dy_other = [swap_core(v) for v in dy_mine]
+
+    back = whole(back_kernel, sds((2 * SLOTS, HALF), F32), [VM] * 9, "back")(
+        *dy_mine, *dy_other, w_down
+    )
+    x_mine, back = lax.optimization_barrier((x_mine, back))
     x_other = swap_core(x_mine)
-
-    back = pl.pallas_call(
-        back_kernel,
-        grid=(7,),
-        out_shape=sds((2 * SLOTS, HALF), F32),
-        in_specs=[pl.BlockSpec((ROWS_Y, 1024), lambda i: (0, i))] * 8
-        + [pl.BlockSpec((HALF, 1024), lambda i: (0, i))],
-        out_specs=pl.BlockSpec((2 * SLOTS, HALF), lambda i: (0, 0)),
-        compiler_params=PARAMS,
-        name="back",
-    )(*dy_mine, *dy_other, w_down)
-
-    full = lambda shape: pl.BlockSpec(shape, lambda i: (0, 0))
-    d_gate, d_up, ext = pl.pallas_call(
+    d_gate, d_up, ext = whole(
         forward_kernel,
-        grid=(14,),
-        out_shape=[sds((2 * SLOTS, HALF)), sds((2 * SLOTS, HALF)), sds((2 * SLOTS, EXT))],
-        in_specs=[pl.BlockSpec((384, 512), lambda i: (0, lax.rem(i, 7)))] * 2
-        + [pl.BlockSpec((512, HALF), lambda i: (i, 0))] * 2
-        + [full((2 * SLOTS, HALF))],
-        out_specs=[full((2 * SLOTS, HALF)), full((2 * SLOTS, HALF)), full((2 * SLOTS, EXT))],
-        scratch_shapes=[pltpu.VMEM((2 * SLOTS, HALF), F32)] * 2,
-        compiler_params=PARAMS,
-        name="forward",
+        [sds((2 * SLOTS, HALF)), sds((2 * SLOTS, HALF)), sds((2 * SLOTS, EXT))],
+        [VM] * 5,
+        "forward",
+        [pltpu.VMEM((2 * SLOTS, WIDTH), BF)],
     )(x_mine, x_other, w_gate, w_up, back)
 
-    halves = []
-    for part in range(2):
-        rows = pl.BlockSpec((512, HALF), functools.partial(lambda p, i: (7 * p + i, 0), part))
-        own, other = pl.pallas_call(
-            dx_kernel,
-            grid=(7,),
-            out_shape=[sds((SLOTS, 3584 + EXT))] * 2,
-            in_specs=[full((2 * SLOTS, HALF))] * 2 + [rows] * 2 + [full((2 * SLOTS, EXT))],
-            out_specs=[full((SLOTS, 3584 + EXT))] * 2,
-            compiler_params=PARAMS,
-            name="dx",
+    def dx(part, width):
+        return whole(
+            functools.partial(dx_kernel, part), [sds((SLOTS, width))] * 2, [VM] * 5, "dx"
         )(d_gate, d_up, w_gate, w_up, ext)
-        got = swap_core(other)
-        pieces = whole(add_kernel, [sds((ROWS_Y, 3584 + EXT))] * 4, [VM] * 2, "add_halves")(own, got)
-        pieces = [pieces[0]] + [shift_y(pieces[s], -s) for s in (1, 2, 3)]
-        mixed = whole(combine_kernel, sds((ROWS_N, 512)), [VM] * 5, "combine")(table, *pieces)
-        halves.append(node_exchange(mixed))
-
+
+    own_a, other_a = dx(0, 3584 + EXT)
+    own_b, other_b = dx(1, 3584)
+    got_a = swap_core(other_a)
+    got_b = swap_core(other_b)
+    pieces = whole(add_kernel, [sds((ROWS_Y, 3584 + EXT))] * 4, [VM] * 2, "add_halves")(own_a, got_a)
+    pieces = [pieces[0]] + [shift_y(pieces[s], -s) for s in (1, 2, 3)]
+    sent_b = whole(add_to_nodes_kernel, sds((384, 1792)), [VM] * 2, "add_to_nodes")(own_b, got_b)
+    back_b = node_exchange(sent_b)
+    mixed = whole(combine_kernel, sds((ROWS_N, 512)), [VM] * 5, "combine")(table, *pieces)
+    mixed, back_b = lax.optimization_barrier((mixed, back_b))
+    back_a = node_exchange(mixed)
+    near = whole(combine_near_kernel, [sds((TOK, 3584))] * 4, [SMEM] + [VM] * 5, "combine_near")(
+        place, *x_near, back_b
+    )
+    near = [near[0]] + [shift_y(near[s], -s) for s in (1, 2, 3)]
     return tuple(
         whole(
-            finish_kernel, [sds((TOK, WIDTH)), sds((TOK, 8), F32)], [SMEM] + [VM] * 3, "finish"
-        )(place, routes, *halves)
+            finish_kernel, [sds((TOK, WIDTH)), sds((TOK, 8), F32)], [SMEM] + [VM] * 6, "finish"
+        )(place, routes, back_a, *near)
     )
 
 

time: 249 us -> 184 us (0.74)
  blocking collectives: 85.6 us -> 0 us
  starting transfers between devices: 21 us -> 42.5 us
  local copies, waits for them, and re-layouts: 2.04 us -> 18.1 us
  Pallas kernels: 59 us -> 43.6 us
    all_to_all x3 -> x0, blocking collectives: 85.6 us -> none  [node_exchange(): lax.all_to_all(v, 'node', split_axis=0, concat_axis=0, tiled=True)]
    all_to_all x1 -> x4, starting transfers between devices: 4.16 us -> 28.3 us  [node_exchange(): lax.all_to_all(v, 'node', split_axis=0, concat_axis=0, tiled=True)]
    unnamed x10 -> x54, local copies, waits for them, and re-layouts: 1.29 us -> 17.3 us
    pallas_call x4 -> x6, Pallas kernels: 41.7 us -> 27 us  [the longest x1 13.1 us: on_device(): whole(forward_kernel, [sds((2 * SLOTS, HALF)), sds((2 * SLOTS, HALF)), sd...]
    ppermute x12, waiting for transfers between devices: 74.6 us -> 65.5 us  [shift_y(): return lax.ppermute(v, 'local', [(i, (i + 2 * s) % 8) for i in range(8)])]
    ppermute x7, waiting for transfers between devices: 2.62 us -> 8.69 us  [swap_core(): return lax.ppermute(v, 'local', [(i, i ^ 1) for i in range(8)])]
    all_to_all x1 -> x4, waiting for transfers between devices: 0.01 us -> 3.28 us  [node_exchange(): lax.all_to_all(v, 'node', split_axis=0, concat_axis=0, tiled=True)]
    ppermute x12, starting transfers between devices: 15.8 us -> 12.9 us  [shift_y(): return lax.ppermute(v, 'local', [(i, (i + 2 * s) % 8) for i in range(8)])]
  transfers between devices with their start and end apart: 20 -> 23, of which waited for: 12 -> 16; matrix products, arithmetic and copies ran while one was open for 0% -> 0% of each run, Pallas kernels for 12% -> 11%
where the time goes in v2:
time: 184 us; the launch traced here: 183 us
  waiting for transfers between devices  77.5 us (42%)
  Pallas kernels  43.6 us (24%)
  starting transfers between devices  42.5 us (23%)
  local copies, waits for them, and re-layouts  18.1 us (10%)
    ppermute x12, waiting for transfers between devices, shift_y(): return lax.ppermute(v, 'local', [(i, (i + 2 * s) % 8) for i in range(8)])  65.5 us
    all_to_all x4, starting transfers between devices, node_exchange(): lax.all_to_all(v, 'node', split_axis=0, concat_axis=0, tiled=True)  28.3 us
    unnamed x54, local copies, waits for them, and re-layouts  17.3 us
    pallas_call x1, Pallas kernels, on_device(): whole(forward_kernel, [sds((2 * SLOTS, HALF)), sds((2 * SLOTS, HALF)), sd...  13.1 us
    ppermute x12, starting transfers between devices, shift_y(): return lax.ppermute(v, 'local', [(i, (i + 2 * s) % 8) for i in range(8)])  12.9 us
    ppermute x7, waiting for transfers between devices, swap_core(): return lax.ppermute(v, 'local', [(i, i ^ 1) for i in range(8)])  8.69 us
    pallas_call x2, Pallas kernels, dx(): whole(functools.partial(dx_kernel, part), [sds((SLOTS, width))] * 2, [VM]...  7.21 us
  transfers between devices with their start and end apart: 23, of which 16 were waited for; matrix products, arithmetic and copies ran while one was open for 0% of the time, Pallas kernels for 11%

profile of v2, /device:TPU:0, one launch (start us, length us, event | category | flops | bytes accessed | tf_op | source)
XLA Modules:
  0.0 182.8 jit_solution(8323786891727400482)
XLA Ops:
  3.1 2.0 %send_dy.1 = bf16[640,1024]{1,0:T(8,128)(2,1)} custom-call(s32[16,8]{1,0:T(8,128)S(1)} %copy.19.routes_ref, f32[16,8]{1,0:T(8,128)S(1)} %copy.16.gates_ref, bf16[16,7168]{1,0:T(8,128)(2,1)S(1)} %copy-done.17), custom_call_target="tpu_custom_call" | custom-call | tf_op jit(solution)/shard_map/send_dy/pallas_call | solution.py:364
  5.1 8.1 %all-to-all-start = ((bf16[16,40,1024]{2,1,0:T(8,128)(2,1)}), bf16[16,40,1024]{2,1,0:T(8,128)(2,1)S(1)}, u32[]{:S(2)}, u32[]{:S(2)}) async-start(bf16[16,40,1024]{2,1,0:T(8,128)(2,1)} %bitcast.2), calls=%async_computation | async-start | bytes 2621440 | tf_op jit(solution)/shard_map/all_to_all | solution.py:355
  13.6 3.1 %collective-permute-start.2 = (bf16[16,7296]{1,0:T(8,128)(2,1)S(1)}, bf16[16,7296]{1,0:T(8,128)(2,1)S(1)}, u32[]{:S(2)}, u32[]{:S(2)}) collective-permute-start(bf16[16,7296]{1,0:T(8,128)(2,1)S(1)} %pad_maximum_fusion.x0_ref), channel_id=1, source_target_pairs={{0,6},{1,7},{2,0},{3,1},{4,2},{5,3},{6,4},{7,5},{8,14},{9,15},{10,... | collective-permute-start | bytes 700424 | tf_op jit(solution)/shard_map/ppermute | solution.py:345
  18.3 8.0 %collective-permute-done.2.x3_ref = bf16[16,7296]{1,0:T(8,128)(2,1)S(1)} collective-permute-done((bf16[16,7296]{1,0:T(8,128)(2,1)S(1)}, bf16[16,7296]{1,0:T(8,128)(2,1)S(1)}, u32[]{:S(2)}, u32[]{:S(2)}) %collective-permute-start.2) | collective-permute-done | bytes 233504 | tf_op jit(solution)/shard_map/ppermute | solution.py:345
  26.8 3.2 %collective-permute-done.x1_ref = bf16[16,7296]{1,0:T(8,128)(2,1)S(1)} collective-permute-done((bf16[16,7296]{1,0:T(8,128)(2,1)S(1)}, bf16[16,7296]{1,0:T(8,128)(2,1)S(1)}, u32[]{:S(2)}, u32[]{:S(2)}) %collective-permute-start) | collective-permute-done | bytes 233504 | tf_op jit(solution)/shard_map/ppermute | solution.py:345
  30.0 3.3 %send_x.1 = bf16[384,3584]{1,0:T(8,128)(2,1)} custom-call(s32[2]{0:T(128)S(1)} %pad_add_fusion.place_ref, bf16[16,7296]{1,0:T(8,128)(2,1)S(1)} %pad_maximum_fusion.x0_ref, bf16[16,7296]{1,0:T(8,128)(2,1)S(1)} %collective-permute-done.x1_ref, bf16[16,7296]{1,0:T(8,128)(2,1)S(1)} %collective-permute-done.1.x2_ref, ...), custom_call_target="tpu_custom_call" | custom-call | tf_op jit(solution)/shard_map/send_x/pallas_call | solution.py:373
  34.0 3.6 %regroup.1 = (bf16[48,7168]{1,0:T(8,128)(2,1)S(1)}, bf16[48,7168]{1,0:T(8,128)(2,1)S(1)}, bf16[48,7168]{1,0:T(8,128)(2,1)S(1)}, bf16[48,7168]{1,0:T(8,128)(2,1)S(1)}, f32[640,128]{1,0:T(8,128)S(1)}) custom-call(s32[2]{0:T(128)S(1)} %pad_add_fusion.place_ref, bf16[640,1024]{1,0:T(8,128)(2,1)S(1)} %bitcast.23), custom_call_target="tpu_custom_call" | custom-call | tf_op jit(solution)/shard_map/regroup/pallas_call | solution.py:374
  40.1 6.3 %all-to-all-start.1 = ((bf16[16,24,3584]{2,1,0:T(8,128)(2,1)}), bf16[16,24,3584]{2,1,0:T(8,128)(2,1)}, u32[]{:S(2)}, u32[]{:S(2)}) async-start(bf16[16,24,3584]{2,1,0:T(8,128)(2,1)} %bitcast.4), calls=%async_computation.1 | async-start | bytes 5505024 | tf_op jit(solution)/shard_map/all_to_all | solution.py:355
  46.5 2.6 %collective-permute-start.4 = (bf16[48,7168]{1,0:T(8,128)(2,1)S(1)}, bf16[48,7168]{1,0:T(8,128)(2,1)S(1)}, u32[]{:S(2)}, u32[]{:S(2)}) collective-permute-start(bf16[48,7168]{1,0:T(8,128)(2,1)S(1)} %copy-done.19), channel_id=1, source_target_pairs={{0,4},{1,5},{2,6},{3,7},{4,0},{5,1},{6,2},{7,3},{8,12},{9,13},{10,... | collective-permute-start | bytes 2064392 | tf_op jit(solution)/shard_map/ppermute | solution.py:345
  50.4 29.3 %collective-permute-done.3.refs_1_ = bf16[48,7168]{1,0:T(8,128)(2,1)S(1)} collective-permute-done((bf16[48,7168]{1,0:T(8,128)(2,1)}, bf16[48,7168]{1,0:T(8,128)(2,1)S(1)}, u32[]{:S(2)}, u32[]{:S(2)}) %collective-permute-start.3) | collective-permute-done | bytes 688160 | tf_op jit(solution)/shard_map/ppermute | solution.py:345
  80.3 1.5 collective-permute-done.7.refs_5_
  83.8 3.1 %copy-done.2 = bf16[1,512,7168]{2,1,0:T(8,128)(2,1)S(1)} copy-done((bf16[1,512,7168]{2,1,0:T(8,128)(2,1)S(1)}, bf16[1,512,7168]{2,1,0:T(8,128)(2,1)}, u32[]{:S(2)}) %copy-start.2) | copy-done | bytes 7340056
  88.0 3.0 %back.1.back_ref = f32[384,512]{1,0:T(8,128)S(1)} custom-call(bf16[48,7168]{1,0:T(8,128)(2,1)S(1)} %copy-done.14, bf16[48,7168]{1,0:T(8,128)(2,1)S(1)} %collective-permute-done.3.refs_1_, bf16[48,7168]{1,0:T(8,128)(2,1)S(1)} %collective-permute-done.4.refs_2_, bf16[48,7168]{1,0:T(8,128)(2,1)S(1)} %collective-permute-done.5.refs_3_, ...), custom_call_target="tpu_custom_call" | custom-call | tf_op jit(solution)/shard_map/back/pallas_call | solution.py:385
  92.1 5.2 %collective-permute-done.10.other_ref = bf16[384,3584]{1,0:T(8,128)(2,1)S(1)} collective-permute-done((bf16[384,3584]{1,0:T(8,128)(2,1)}, bf16[384,3584]{1,0:T(8,128)(2,1)S(1)}, u32[]{:S(2)}, u32[]{:S(2)}) %collective-permute-start.10) | collective-permute-done | bytes 2752544 | tf_op jit(solution)/shard_map/ppermute | solution.py:349
  97.2 3.1 %copy-done = bf16[1,7168,512]{2,1,0:T(8,128)(2,1)S(1)} copy-done((bf16[1,7168,512]{2,1,0:T(8,128)(2,1)S(1)}, bf16[1,7168,512]{2,1,0:T(8,128)(2,1)}, u32[]{:S(2)}) %copy-start) | copy-done | bytes 7340056
  101.5 13.1 %forward.1 = (bf16[384,512]{1,0:T(8,128)(2,1)S(1)}, bf16[384,512]{1,0:T(8,128)(2,1)S(1)}, bf16[384,128]{1,0:T(8,128)(2,1)S(1)}) custom-call(bf16[384,3584]{1,0:T(8,128)(2,1)} %bitcast.5.own_ref, bf16[384,3584]{1,0:T(8,128)(2,1)S(1)} %collective-permute-done.10.other_ref, bf16[7168,512]{1,0:T(8,128)(2,1)S(1)} %bitcast.13, bf16[7168,512]{1,0:T(8,128)(2,1)} %bitcast.18, ...), custom_call_target="tpu_custom_call" | custom-call | tf_op jit(solution)/shard_map/forward/pallas_call | solution.py:390
  114.6 3.1 %copy-done.1 = bf16[1,7168,512]{2,1,0:T(8,128)(2,1)S(1)} copy-done((bf16[1,7168,512]{2,1,0:T(8,128)(2,1)S(1)}, bf16[1,7168,512]{2,1,0:T(8,128)(2,1)}, u32[]{:S(2)}) %copy-start.1) | copy-done | bytes 7340056
  117.6 3.0 %dx.3 = (bf16[192,3584]{1,0:T(8,128)(2,1)S(1)}, bf16[192,3584]{1,0:T(8,128)(2,1)S(1)}) custom-call(bf16[384,512]{1,0:T(8,128)(2,1)S(1)} %get-tuple-element.41.dgate_ref, bf16[384,512]{1,0:T(8,128)(2,1)S(1)} %get-tuple-element.42.dup_ref, bf16[7168,512]{1,0:T(8,128)(2,1)S(1)} %bitcast.16, bf16[7168,512]{1,0:T(8,128)(2,1)S(1)} %bitcast.19, ...), custom_call_target="tpu_custom_call" | custom-call | tf_op jit(solution)/shard_map/dx/pallas_call | solution.py:399
  120.9 4.2 %dx.2 = (bf16[192,3712]{1,0:T(8,128)(2,1)S(1)}, bf16[192,3712]{1,0:T(8,128)(2,1)}) custom-call(bf16[384,512]{1,0:T(8,128)(2,1)S(1)} %get-tuple-element.41.dgate_ref, bf16[384,512]{1,0:T(8,128)(2,1)S(1)} %get-tuple-element.42.dup_ref, bf16[7168,512]{1,0:T(8,128)(2,1)S(1)} %bitcast.17, bf16[7168,512]{1,0:T(8,128)(2,1)S(1)} %bitcast.20, ...), custom_call_target="tpu_custom_call" | custom-call | tf_op jit(solution)/shard_map/dx/pallas_call | solution.py:399
  125.5 2.2 %add_to_nodes.1 = bf16[384,1792]{1,0:T(8,128)(2,1)} custom-call(bf16[192,3584]{1,0:T(8,128)(2,1)S(1)} %get-tuple-element.50.own_ref, bf16[192,3584]{1,0:T(8,128)(2,1)S(1)} %collective-permute-done.15.got_ref), custom_call_target="tpu_custom_call" | custom-call | tf_op jit(solution)/shard_map/add_to_nodes/pallas_call | solution.py:409
  127.6 7.0 %all-to-all-start.2 = ((bf16[16,24,1792]{2,1,0:T(8,128)(2,1)}), bf16[16,24,1792]{2,1,0:T(8,128)(2,1)S(1)}, u32[]{:S(2)}, u32[]{:S(2)}) async-start(bf16[16,24,1792]{2,1,0:T(8,128)(2,1)} %bitcast.9), calls=%async_computation.2 | async-start | bytes 2752512 | tf_op jit(solution)/shard_map/all_to_all | solution.py:355
  134.6 2.0 %add_halves.1 = (bf16[48,3712]{1,0:T(8,128)(2,1)S(1)}, bf16[48,3712]{1,0:T(8,128)(2,1)S(1)}, bf16[48,3712]{1,0:T(8,128)(2,1)S(1)}, bf16[48,3712]{1,0:T(8,128)(2,1)S(1)}) custom-call(bf16[192,3712]{1,0:T(8,128)(2,1)S(1)} %copy-done.6, bf16[192,3712]{1,0:T(8,128)(2,1)} %collective-permute-done.11.got_ref), custom_call_target="tpu_custom_call" | custom-call | tf_op jit(solution)/shard_map/add_halves/pallas_call | solution.py:407
  138.7 9.2 %collective-permute-done.12.p1_ref = bf16[48,3712]{1,0:T(8,128)(2,1)S(1)} collective-permute-done((bf16[48,3712]{1,0:T(8,128)(2,1)S(1)}, bf16[48,3712]{1,0:T(8,128)(2,1)S(1)}, u32[]{:S(2)}, u32[]{:S(2)}) %collective-permute-start.12) | collective-permute-done | bytes 356384 | tf_op jit(solution)/shard_map/ppermute | solution.py:345
  147.9 2.4 %collective-permute-done.13.p2_ref = bf16[48,3712]{1,0:T(8,128)(2,1)S(1)} collective-permute-done((bf16[48,3712]{1,0:T(8,128)(2,1)S(1)}, bf16[48,3712]{1,0:T(8,128)(2,1)S(1)}, u32[]{:S(2)}, u32[]{:S(2)}) %collective-permute-start.13) | collective-permute-done | bytes 356384 | tf_op jit(solution)/shard_map/ppermute | solution.py:345
  150.3 6.1 %collective-permute-done.14.p3_ref = bf16[48,3712]{1,0:T(8,128)(2,1)S(1)} collective-permute-done((bf16[48,3712]{1,0:T(8,128)(2,1)S(1)}, bf16[48,3712]{1,0:T(8,128)(2,1)S(1)}, u32[]{:S(2)}, u32[]{:S(2)}) %collective-permute-start.14) | collective-permute-done | bytes 356384 | tf_op jit(solution)/shard_map/ppermute | solution.py:345
  156.5 3.1 %combine.1 = bf16[640,512]{1,0:T(8,128)(2,1)} custom-call(f32[640,128]{1,0:T(8,128)S(1)} %copy-done.16, bf16[48,3712]{1,0:T(8,128)(2,1)S(1)} %get-tuple-element.46.p0_ref, bf16[48,3712]{1,0:T(8,128)(2,1)S(1)} %collective-permute-done.12.p1_ref, bf16[48,3712]{1,0:T(8,128)(2,1)S(1)} %collective-permute-done.13.p2_ref, ...), custom_call_target="tpu_custom_call" | custom-call | tf_op jit(solution)/shard_map/combine/pallas_call | solution.py:411
  159.6 6.9 %all-to-all-start.3 = ((bf16[16,40,512]{2,1,0:T(8,128)(2,1)}), bf16[16,40,512]{2,1,0:T(8,128)(2,1)S(1)}, u32[]{:S(2)}, u32[]{:S(2)}) async-start(bf16[16,40,512]{2,1,0:T(8,128)(2,1)} %bitcast.11), calls=%async_computation.3 | async-start | bytes 1310720 | tf_op jit(solution)/shard_map/all_to_all | solution.py:355
  166.6 1.5 combine_near.1
  170.2 4.0 %collective-permute-done.16.b1_ref = bf16[16,3584]{1,0:T(8,128)(2,1)S(1)} collective-permute-done((bf16[16,3584]{1,0:T(8,128)(2,1)S(1)}, bf16[16,3584]{1,0:T(8,128)(2,1)S(1)}, u32[]{:S(2)}, u32[]{:S(2)}) %collective-permute-start.16) | collective-permute-done | bytes 114720 | tf_op jit(solution)/shard_map/ppermute | solution.py:345
  174.2 2.0 %collective-permute-done.17.b2_ref = bf16[16,3584]{1,0:T(8,128)(2,1)S(1)} collective-permute-done((bf16[16,3584]{1,0:T(8,128)(2,1)S(1)}, bf16[16,3584]{1,0:T(8,128)(2,1)S(1)}, u32[]{:S(2)}, u32[]{:S(2)}) %collective-permute-start.17) | collective-permute-done | bytes 114720 | tf_op jit(solution)/shard_map/ppermute | solution.py:345
  177.0 2.6 %all-to-all-done.3 = bf16[16,40,512]{2,1,0:T(8,128)(2,1)S(1)} async-done(((bf16[16,40,512]{2,1,0:T(8,128)(2,1)}), bf16[16,40,512]{2,1,0:T(8,128)(2,1)S(1)}, u32[]{:S(2)}, u32[]{:S(2)}) %all-to-all-start.3) | async-done | bytes 655392 | tf_op jit(solution)/shard_map/all_to_all | solution.py:355
  179.6 2.5 %finish.1 = (bf16[16,7168]{1,0:T(8,128)(2,1)}, f32[16,8]{1,0:T(8,128)S(1)}) custom-call(s32[2]{0:T(128)S(1)} %pad_add_fusion.place_ref, s32[16,8]{1,0:T(8,128)S(1)} %copy.19.routes_ref, bf16[640,512]{1,0:T(8,128)(2,1)S(1)} %bitcast.24, bf16[16,3584]{1,0:T(8,128)(2,1)S(1)} %get-tuple-element.54.b0_ref, bf16[16,3584]{1,0:T(8,128)(2,1)S(1)} %collective-permute-done.16.b1_ref, ...), custom_call_target="tpu_custom_call" | custom-call | tf_op jit(solution)/shard_map/finish/pallas_call | solution.py:419
  (89 shorter events, 21.5 us)
Async XLA Ops:
  5.1 8.1 %copy-start.23 = (f32[16,8]{0,1:T(8,128)S(1)}, f32[16,8]{0,1:T(8,128)}, u32[]{:S(2)}) copy-start(f32[16,8]{0,1:T(8,128)} %param.10) | copy-start | bytes 1540
  5.1 8.4 %copy-start.21 = (bf16[16,7168]{1,0:T(8,128)(2,1)S(1)}, bf16[16,7168]{1,0:T(8,128)(2,1)}, u32[]{:S(2)}) copy-start(bf16[16,7168]{1,0:T(8,128)(2,1)} %param.7) | copy-start | bytes 688132
  5.1 28.9 %all-to-all-start = ((bf16[16,40,1024]{2,1,0:T(8,128)(2,1)}), bf16[16,40,1024]{2,1,0:T(8,128)(2,1)S(1)}, u32[]{:S(2)}, u32[]{:S(2)}) async-start(bf16[16,40,1024]{2,1,0:T(8,128)(2,1)} %bitcast.2), calls=%async_computation | async-start | bytes 2621440 | tf_op jit(solution)/shard_map/all_to_all | solution.py:355
  13.6 12.8 %collective-permute-start.2 = (bf16[16,7296]{1,0:T(8,128)(2,1)S(1)}, bf16[16,7296]{1,0:T(8,128)(2,1)S(1)}, u32[]{:S(2)}, u32[]{:S(2)}) collective-permute-start(bf16[16,7296]{1,0:T(8,128)(2,1)S(1)} %pad_maximum_fusion.x0_ref), channel_id=1, source_target_pairs={{0,6},{1,7},{2,0},{3,1},{4,2},{5,3},{6,4},{7,5},{8,14},{9,15},{10,... | collective-permute-start | bytes 700424 | tf_op jit(solution)/shard_map/ppermute | solution.py:345
  16.6 10.2 %collective-permute-start.1 = (bf16[16,7296]{1,0:T(8,128)(2,1)S(1)}, bf16[16,7296]{1,0:T(8,128)(2,1)S(1)}, u32[]{:S(2)}, u32[]{:S(2)}) collective-permute-start(bf16[16,7296]{1,0:T(8,128)(2,1)S(1)} %pad_maximum_fusion.x0_ref), channel_id=1, source_target_pairs={{0,4},{1,5},{2,6},{3,7},{4,0},{5,1},{6,2},{7,3},{8,12},{9,13},{10,... | collective-permute-start | bytes 700424 | tf_op jit(solution)/shard_map/ppermute | solution.py:345
  17.3 12.8 %collective-permute-start = (bf16[16,7296]{1,0:T(8,128)(2,1)S(1)}, bf16[16,7296]{1,0:T(8,128)(2,1)S(1)}, u32[]{:S(2)}, u32[]{:S(2)}) collective-permute-start(bf16[16,7296]{1,0:T(8,128)(2,1)S(1)} %pad_maximum_fusion.x0_ref), channel_id=1, source_target_pairs={{0,2},{1,3},{2,4},{3,5},{4,6},{5,7},{6,0},{7,1},{8,10},{9,11},{10,... | collective-permute-start | bytes 700424 | tf_op jit(solution)/shard_map/ppermute | solution.py:345
  39.3 11.1 %copy-start.13 = (bf16[48,7168]{1,0:T(8,128)(2,1)}, bf16[48,7168]{1,0:T(8,128)(2,1)S(1)}, u32[]{:S(2)}) copy-start(bf16[48,7168]{1,0:T(8,128)(2,1)S(1)} %get-tuple-element.35.refs_0_) | copy-start | bytes 2064388
  40.1 51.9 %all-to-all-start.1 = ((bf16[16,24,3584]{2,1,0:T(8,128)(2,1)}), bf16[16,24,3584]{2,1,0:T(8,128)(2,1)}, u32[]{:S(2)}, u32[]{:S(2)}) async-start(bf16[16,24,3584]{2,1,0:T(8,128)(2,1)} %bitcast.4), calls=%async_computation.1 | async-start | bytes 5505024 | tf_op jit(solution)/shard_map/all_to_all | solution.py:355
  46.4 33.3 %collective-permute-start.3 = (bf16[48,7168]{1,0:T(8,128)(2,1)}, bf16[48,7168]{1,0:T(8,128)(2,1)S(1)}, u32[]{:S(2)}, u32[]{:S(2)}) collective-permute-start(bf16[48,7168]{1,0:T(8,128)(2,1)} %copy-done.20), channel_id=1, source_target_pairs={{0,2},{1,3},{2,4},{3,5},{4,6},{5,7},{6,0},{7,1},{8,10},{9,11},{10,... | collective-permute-start | bytes 2064392 | tf_op jit(solution)/shard_map/ppermute | solution.py:345
  46.5 33.2 %collective-permute-start.4 = (bf16[48,7168]{1,0:T(8,128)(2,1)S(1)}, bf16[48,7168]{1,0:T(8,128)(2,1)S(1)}, u32[]{:S(2)}, u32[]{:S(2)}) collective-permute-start(bf16[48,7168]{1,0:T(8,128)(2,1)S(1)} %copy-done.19), channel_id=1, source_target_pairs={{0,4},{1,5},{2,6},{3,7},{4,0},{5,1},{6,2},{7,3},{8,12},{9,13},{10,... | collective-permute-start | bytes 2064392 | tf_op jit(solution)/shard_map/ppermute | solution.py:345
  49.1 31.1 %collective-permute-start.5 = (bf16[48,7168]{1,0:T(8,128)(2,1)S(1)}, bf16[48,7168]{1,0:T(8,128)(2,1)S(1)}, u32[]{:S(2)}, u32[]{:S(2)}) collective-permute-start(bf16[48,7168]{1,0:T(8,128)(2,1)S(1)} %get-tuple-element.38), channel_id=1, source_target_pairs={{0,6},{1,7},{2,0},{3,1},{4,2},{5,3},{6,4},{7,5},{8,14},{9,15},{10,... | collective-permute-start | bytes 2064392 | tf_op jit(solution)/shard_map/ppermute | solution.py:345
  50.4 29.9 %collective-permute-start.6 = (bf16[48,7168]{1,0:T(8,128)(2,1)S(1)}, bf16[48,7168]{1,0:T(8,128)(2,1)S(1)}, u32[]{:S(2)}, u32[]{:S(2)}) collective-permute-start(bf16[48,7168]{1,0:T(8,128)(2,1)S(1)} %get-tuple-element.35.refs_0_), channel_id=1, source_target_pairs={{0,1},{1,0},{2,3},{3,2},{4,5},{5,4},{6,7},{7,6},{8,9},{9,8},{10,11... | collective-permute-start | bytes 2064392 | tf_op jit(solution)/shard_map/ppermute | solution.py:349
  79.7 2.1 %collective-permute-start.7 = (bf16[48,7168]{1,0:T(8,128)(2,1)S(1)}, bf16[48,7168]{1,0:T(8,128)(2,1)S(1)}, u32[]{:S(2)}, u32[]{:S(2)}) collective-permute-start(bf16[48,7168]{1,0:T(8,128)(2,1)S(1)} %collective-permute-done.3.refs_1_), channel_id=1, source_target_pairs={{0,1},{1,0},{2,3},{3,2},{4,5},{5,4},{6,7},{7,6},{8,9},{9,8},{10,11... | collective-permute-start | bytes 2064392 | tf_op jit(solution)/shard_map/ppermute | solution.py:349
  79.7 3.1 %collective-permute-start.8 = (bf16[48,7168]{1,0:T(8,128)(2,1)S(1)}, bf16[48,7168]{1,0:T(8,128)(2,1)S(1)}, u32[]{:S(2)}, u32[]{:S(2)}) collective-permute-start(bf16[48,7168]{1,0:T(8,128)(2,1)S(1)} %collective-permute-done.4.refs_2_), channel_id=1, source_target_pairs={{0,1},{1,0},{2,3},{3,2},{4,5},{5,4},{6,7},{7,6},{8,9},{9,8},{10,11... | collective-permute-start | bytes 2064392 | tf_op jit(solution)/shard_map/ppermute | solution.py:349
  80.2 3.6 %collective-permute-start.9 = (bf16[48,7168]{1,0:T(8,128)(2,1)S(1)}, bf16[48,7168]{1,0:T(8,128)(2,1)S(1)}, u32[]{:S(2)}, u32[]{:S(2)}) collective-permute-start(bf16[48,7168]{1,0:T(8,128)(2,1)S(1)} %collective-permute-done.5.refs_3_), channel_id=1, source_target_pairs={{0,1},{1,0},{2,3},{3,2},{4,5},{5,4},{6,7},{7,6},{8,9},{9,8},{10,11... | collective-permute-start | bytes 2064392 | tf_op jit(solution)/shard_map/ppermute | solution.py:349
  88.0 26.5 %slice-start = ((s8[7340032]{0:T(1024)(128)(4,1)}), s8[3145728]{0:T(1024)(128)(4,1)S(1)}, s32[]{:S(2)}) async-start(s8[7340032]{0:T(1024)(128)(4,1)} %bitcast.14), calls=%async_computation.4 | async-start | bytes 6291456
  91.9 5.3 %collective-permute-start.10 = (bf16[384,3584]{1,0:T(8,128)(2,1)}, bf16[384,3584]{1,0:T(8,128)(2,1)S(1)}, u32[]{:S(2)}, u32[]{:S(2)}) collective-permute-start(bf16[384,3584]{1,0:T(8,128)(2,1)} %bitcast.5.own_ref), channel_id=1, source_target_pairs={{0,1},{1,0},{2,3},{3,2},{4,5},{5,4},{6,7},{7,6},{8,9},{9,8},{10,11... | collective-permute-start | bytes 8257544 | tf_op jit(solution)/shard_map/ppermute | solution.py:349
  101.5 13.1 %slice-start.1 = ((s8[7340032]{0:T(1024)(128)(4,1)}), s8[4194304]{0:T(1024)(128)(4,1)S(1)}, s32[]{:S(2)}) async-start(s8[7340032]{0:T(1024)(128)(4,1)} %bitcast.14), calls=%async_computation.5 | async-start | bytes 8388608
  120.7 4.8 %collective-permute-start.15 = (bf16[192,3584]{1,0:T(8,128)(2,1)S(1)}, bf16[192,3584]{1,0:T(8,128)(2,1)S(1)}, u32[]{:S(2)}, u32[]{:S(2)}) collective-permute-start(bf16[192,3584]{1,0:T(8,128)(2,1)S(1)} %get-tuple-element.51), channel_id=1, source_target_pairs={{0,1},{1,0},{2,3},{3,2},{4,5},{5,4},{6,7},{7,6},{8,9},{9,8},{10,11... | collective-permute-start | bytes 4128776 | tf_op jit(solution)/shard_map/ppermute | solution.py:349
  125.1 9.5 %collective-permute-start.11 = (bf16[192,3712]{1,0:T(8,128)(2,1)}, bf16[192,3712]{1,0:T(8,128)(2,1)}, u32[]{:S(2)}, u32[]{:S(2)}) collective-permute-start(bf16[192,3712]{1,0:T(8,128)(2,1)} %get-tuple-element.45), channel_id=1, source_target_pairs={{0,1},{1,0},{2,3},{3,2},{4,5},{5,4},{6,7},{7,6},{8,9},{9,8},{10,11... | collective-permute-start | bytes 4276232 | tf_op jit(solution)/shard_map/ppermute | solution.py:349
  127.6 32.0 %all-to-all-start.2 = ((bf16[16,24,1792]{2,1,0:T(8,128)(2,1)}), bf16[16,24,1792]{2,1,0:T(8,128)(2,1)S(1)}, u32[]{:S(2)}, u32[]{:S(2)}) async-start(bf16[16,24,1792]{2,1,0:T(8,128)(2,1)} %bitcast.9), calls=%async_computation.2 | async-start | bytes 2752512 | tf_op jit(solution)/shard_map/all_to_all | solution.py:355
  134.6 21.9 %copy-start.16 = (f32[640,128]{1,0:T(8,128)S(1)}, f32[640,128]{1,0:T(8,128)}, u32[]{:S(2)}) copy-start(f32[640,128]{1,0:T(8,128)} %copy-done.15) | copy-start | bytes 983044
  136.6 11.3 %collective-permute-start.12 = (bf16[48,3712]{1,0:T(8,128)(2,1)S(1)}, bf16[48,3712]{1,0:T(8,128)(2,1)S(1)}, u32[]{:S(2)}, u32[]{:S(2)}) collective-permute-start(bf16[48,3712]{1,0:T(8,128)(2,1)S(1)} %get-tuple-element.47), channel_id=1, source_target_pairs={{0,6},{1,7},{2,0},{3,1},{4,2},{5,3},{6,4},{7,5},{8,14},{9,15},{10,... | collective-permute-start | bytes 1069064 | tf_op jit(solution)/shard_map/ppermute | solution.py:345
  137.5 12.8 %collective-permute-start.13 = (bf16[48,3712]{1,0:T(8,128)(2,1)S(1)}, bf16[48,3712]{1,0:T(8,128)(2,1)S(1)}, u32[]{:S(2)}, u32[]{:S(2)}) collective-permute-start(bf16[48,3712]{1,0:T(8,128)(2,1)S(1)} %get-tuple-element.48), channel_id=1, source_target_pairs={{0,4},{1,5},{2,6},{3,7},{4,0},{5,1},{6,2},{7,3},{8,12},{9,13},{10,... | collective-permute-start | bytes 1069064 | tf_op jit(solution)/shard_map/ppermute | solution.py:345
  137.5 18.9 %collective-permute-start.14 = (bf16[48,3712]{1,0:T(8,128)(2,1)S(1)}, bf16[48,3712]{1,0:T(8,128)(2,1)S(1)}, u32[]{:S(2)}, u32[]{:S(2)}) collective-permute-start(bf16[48,3712]{1,0:T(8,128)(2,1)S(1)} %get-tuple-element.49), channel_id=1, source_target_pairs={{0,2},{1,3},{2,4},{3,5},{4,6},{5,7},{6,0},{7,1},{8,10},{9,11},{10,... | collective-permute-start | bytes 1069064 | tf_op jit(solution)/shard_map/ppermute | solution.py:345
  156.5 10.1 %copy-start.8 = (bf16[16,7296]{1,0:T(8,128)(2,1)S(1)}, bf16[16,7296]{1,0:T(8,128)(2,1)}, u32[]{:S(2)}) copy-start(bf16[16,7296]{1,0:T(8,128)(2,1)} %copy-done.7) | copy-start | bytes 700420
  156.5 10.1 %copy-start.10 = (bf16[16,7296]{1,0:T(8,128)(2,1)S(1)}, bf16[16,7296]{1,0:T(8,128)(2,1)}, u32[]{:S(2)}) copy-start(bf16[16,7296]{1,0:T(8,128)(2,1)} %copy-done.9) | copy-start | bytes 700420
  156.5 10.1 %copy-start.12 = (bf16[16,7296]{1,0:T(8,128)(2,1)S(1)}, bf16[16,7296]{1,0:T(8,128)(2,1)}, u32[]{:S(2)}) copy-start(bf16[16,7296]{1,0:T(8,128)(2,1)} %copy-done.11) | copy-start | bytes 700420
  159.6 20.0 %all-to-all-start.3 = ((bf16[16,40,512]{2,1,0:T(8,128)(2,1)}), bf16[16,40,512]{2,1,0:T(8,128)(2,1)S(1)}, u32[]{:S(2)}, u32[]{:S(2)}) async-start(bf16[16,40,512]{2,1,0:T(8,128)(2,1)} %bitcast.11), calls=%async_computation.3 | async-start | bytes 1310720 | tf_op jit(solution)/shard_map/all_to_all | solution.py:355
  168.1 6.1 %collective-permute-start.16 = (bf16[16,3584]{1,0:T(8,128)(2,1)S(1)}, bf16[16,3584]{1,0:T(8,128)(2,1)S(1)}, u32[]{:S(2)}, u32[]{:S(2)}) collective-permute-start(bf16[16,3584]{1,0:T(8,128)(2,1)S(1)} %get-tuple-element.55), channel_id=1, source_target_pairs={{0,6},{1,7},{2,0},{3,1},{4,2},{5,3},{6,4},{7,5},{8,14},{9,15},{10,... | collective-permute-start | bytes 344072 | tf_op jit(solution)/shard_map/ppermute | solution.py:345
  168.9 7.4 %collective-permute-start.17 = (bf16[16,3584]{1,0:T(8,128)(2,1)S(1)}, bf16[16,3584]{1,0:T(8,128)(2,1)S(1)}, u32[]{:S(2)}, u32[]{:S(2)}) collective-permute-start(bf16[16,3584]{1,0:T(8,128)(2,1)S(1)} %get-tuple-element.56), channel_id=1, source_target_pairs={{0,4},{1,5},{2,6},{3,7},{4,0},{5,1},{6,2},{7,3},{8,12},{9,13},{10,... | collective-permute-start | bytes 344072 | tf_op jit(solution)/shard_map/ppermute | solution.py:345
  169.1 7.9 %collective-permute-start.18 = (bf16[16,3584]{1,0:T(8,128)(2,1)S(1)}, bf16[16,3584]{1,0:T(8,128)(2,1)S(1)}, u32[]{:S(2)}, u32[]{:S(2)}) collective-permute-start(bf16[16,3584]{1,0:T(8,128)(2,1)S(1)} %get-tuple-element.57), channel_id=1, source_target_pairs={{0,2},{1,3},{2,4},{3,5},{4,6},{5,7},{6,0},{7,1},{8,10},{9,11},{10,... | collective-permute-start | bytes 344072 | tf_op jit(solution)/shard_map/ppermute | solution.py:345
  (17 other events, 57.4 us)

commit v3 on v2

--- a/solution.py
+++ b/solution.py
@@ -22,7 +22,8 @@
 SLOTS = N_Y * ROWS_Y
 ROWS_N = N_NODE * 40
 EXT = 128
-VMEM_LIMIT = 36 * 1024 * 1024
+MIB = 1024 * 1024
+VMEM_LIMITS = {"back": 20, "forward_own": 30, "forward": 30, "dx": 24}
 
 
 def iota(shape, dim):
@@ -57,8 +58,12 @@
     return jnp.where(mask, 1.0, 0.0)
 
 
+def by_token(v):
+    return dot_tn(v.astype(F32).astype(BF), onehot(iota((8, 128), 0) == iota((8, 128), 1)).astype(BF))
+
+
 def route_tables(routes, width):
-    lane = iota((TOK, width), 1) & 63
+    lane = (iota((TOK, width), 1) & 63).astype(F32)
     hot = jnp.zeros((TOK, width), F32)
     for k in range(8):
         hot = hot + onehot(routes[:, k : k + 1] == lane)
@@ -75,14 +80,15 @@
 
 
 def send_dy_kernel(routes_ref, gates_ref, dy_ref, out_ref):
-    routes = routes_ref[...]
-    gates = gates_ref[...]
+    routes = by_token(routes_ref[...])
+    gates = by_token(gates_ref[...])
     width = 256
     lane = iota((TOK, width), 1)
+    expert = (lane & 63).astype(F32)
     hot = route_tables(routes, width)
     gate = jnp.zeros((TOK, width), F32)
     for k in range(8):
-        gate = gate + jnp.where(routes[:, k : k + 1] == (lane & 63), gates[:, k : k + 1], 0.0)
+        gate = gate + jnp.where(routes[:, k : k + 1] == expert, gates[:, k : k + 1], 0.0)
     tri = onehot(iota((TOK, TOK), 1) < iota((TOK, TOK), 0)).astype(BF)
     code = hot * (dot(tri, hot.astype(BF)) + 1.0)
     section = lane >> 6
@@ -122,7 +128,7 @@
         out_ref[:, lo : lo + 512] = dot(pick, stack).astype(BF)
 
 
-def regroup_kernel(place_ref, rows_ref, out0_ref, out1_ref, out2_ref, out3_ref, table_ref):
+def regroup_kernel(place_ref, rows_ref, out0_ref, out1_ref, out2_ref, out3_ref, table_ref, mark_ref):
     node = place_ref[0]
     y = place_ref[1]
     outs = [out0_ref, out1_ref, out2_ref, out3_ref]
@@ -130,6 +136,7 @@
     want = ((c >> 2) << 6) + 4 * node + ((y + c) & 3)
     select = onehot((c < 8) & (iota((256, 128), 0) == want)).astype(BF)
     meta = rows_ref[:, :256]
+    mark_ref[...] = jnp.zeros_like(mark_ref)
     code = lax.dot_general(select, meta, (((0,), (1,)), ((), ())), preferred_element_type=F32)[:8]
     col = iota((8, ROWS_N), 1)
     n = div40(col)
@@ -151,24 +158,68 @@
     table_ref[...] = dot(onehot(iota((ROWS_N, ROWS_N), 1) == source).astype(BF), picked)
 
 
+def copy_parts(source, target, sems, first, rows):
+    copies = []
+    step = rows // sems.shape[0]
+    for i in range(sems.shape[0]):
+        at = pl.ds(first + step * i, step)
+        copies.append(pltpu.make_async_copy(source.at[at], target.at[at], sems.at[i]))
+        copies[-1].start()
+    return copies
+
+
+def wait_all(copies):
+    for copy in copies:
+        copy.wait()
+
+
+def stage_kernel(source_ref, mark_ref, out_ref, sems):
+    wait_all(copy_parts(source_ref, out_ref, sems, 0, source_ref.shape[0]))
+
+
 def back_kernel(*refs):
     pieces, down_ref, out_ref = refs[:8], refs[8], refs[9]
     rows = jnp.concatenate([p[...] for p in pieces], axis=0)
     out_ref[...] = dot_nt(rows, down_ref[...])
 
 
-def forward_kernel(own_ref, other_ref, gate_ref, up_ref, back_ref, dgate_ref, dup_ref, ext_ref, x_ref):
+def slot_order(h):
     row = iota((SLOTS, 384), 0)
     s = div3(row >> 4)
     rem = row - ROWS_Y * s
     n = div3(rem)
     r = rem - 3 * n
+    return onehot(iota((SLOTS, 384), 1) == 24 * n + 12 * h + 3 * s + r).astype(BF)
+
+
+def forward_own_kernel(x_ref, gate_hbm, up_hbm, mark_ref, pg_ref, pu_ref, gate_ref, up_ref, sems):
+    loads = []
     for h in range(2):
-        perm = onehot(iota((SLOTS, 384), 1) == 24 * n + 12 * h + 3 * s + r).astype(BF)
-        x_ref[:SLOTS, 3584 * h : 3584 * (h + 1)] = dot(perm, own_ref[...]).astype(BF)
-        x_ref[SLOTS:, 3584 * h : 3584 * (h + 1)] = dot(perm, other_ref[...]).astype(BF)
-    pre_gate = dot(x_ref[...], gate_ref[...])
-    pre_up = dot(x_ref[...], up_ref[...])
+        loads.append(copy_parts(gate_hbm, gate_ref, sems.at[2 * h], 3584 * h, 3584))
+        loads.append(copy_parts(up_hbm, up_ref, sems.at[2 * h + 1], 3584 * h, 3584))
+    for h in range(2):
+        rows = dot(slot_order(h), x_ref[...]).astype(BF)
+        at = slice(3584 * h, 3584 * (h + 1))
+        wait_all(loads[2 * h])
+        gate = dot(rows, gate_ref[at, :])
+        wait_all(loads[2 * h + 1])
+        up = dot(rows, up_ref[at, :])
+        pg_ref[...] = gate if h == 0 else pg_ref[...] + gate
+        pu_ref[...] = up if h == 0 else pu_ref[...] + up
+
+
+def forward_kernel(
+    x_ref, gate_ref, up_ref, back_ref, pg_ref, pu_ref, dgate_ref, dup_ref, ext_ref
+):
+    pre_gate = jnp.zeros((SLOTS, HALF), F32)
+    pre_up = jnp.zeros((SLOTS, HALF), F32)
+    for h in range(2):
+        rows = dot(slot_order(h), x_ref[...]).astype(BF)
+        at = slice(3584 * h, 3584 * (h + 1))
+        pre_gate = pre_gate + dot(rows, gate_ref[at, :])
+        pre_up = pre_up + dot(rows, up_ref[at, :])
+    pre_gate = jnp.concatenate([pg_ref[...], pre_gate], axis=0)
+    pre_up = jnp.concatenate([pu_ref[...], pre_up], axis=0)
     back = back_ref[...]
     sig = jax.nn.sigmoid(pre_gate)
     act = pre_gate * sig
@@ -196,6 +247,7 @@
 
 
 def add_kernel(own_ref, got_ref, *outs):
+    outs[4][...] = jnp.zeros_like(outs[4])
     lane = iota((ROWS_Y, EXT), 1)
     for s in range(N_Y):
         rows = slice(ROWS_Y * s, ROWS_Y * (s + 1))
@@ -211,7 +263,7 @@
         ).astype(BF)
 
 
-def add_to_nodes_kernel(own_ref, got_ref, out_ref):
+def add_to_nodes_kernel(own_ref, got_ref, mark_ref, out_ref):
     row = iota((384, 384), 0)
     block = div3(row >> 3)
     rest = row - 24 * block
@@ -289,7 +341,7 @@
 
 def finish_kernel(place_ref, routes_ref, a_ref, b0_ref, b1_ref, b2_ref, b3_ref, dx_ref, gg_ref):
     y = place_ref[1]
-    routes = routes_ref[...]
+    routes = by_token(routes_ref[...])
     ncode = node_codes(route_tables(routes, 128))
     col = iota((128, ROWS_N), 1)
     spread = onehot(div40(col) == iota((128, ROWS_N), 0)).astype(BF)
@@ -306,22 +358,22 @@
     total = total + b2_ref[...].astype(F32) + b3_ref[...].astype(F32)
     dx_ref[:, 3584:] = total.astype(BF)
     last = match & (cq == 7)
+    picks = routes.astype(I32)
     masks = jnp.concatenate(
-        [onehot(last & (cn == (routes[:, k : k + 1] >> 2))) for k in range(8)], axis=0
+        [onehot(last & (cn == (picks[:, k : k + 1] >> 2))) for k in range(8)], axis=0
     ).astype(BF)
     terms = dot(masks, a_ref[:, :EXT])
     lane = iota((TOK, EXT), 1)
     result = jnp.zeros((TOK, EXT), F32)
     for k in range(8):
-        s = ((routes[:, k : k + 1] & 3) - y) & 3
+        s = ((picks[:, k : k + 1] & 3) - y) & 3
         mine = jnp.where((lane >> 1) == s, terms[TOK * k : TOK * (k + 1)], 0.0)
         result = jnp.where(lane == k, jnp.sum(mine, axis=1, keepdims=True), result)
-    gg_ref[...] = result[:, :8]
+    gg_ref[...] = result.T[:8]
 
 
 SMEM = pl.BlockSpec(memory_space=pltpu.SMEM)
 VM = pl.BlockSpec(memory_space=pltpu.VMEM)
-PARAMS = pltpu.CompilerParams(vmem_limit_bytes=VMEM_LIMIT)
 
 
 def sds(shape, dtype=BF):
@@ -336,7 +388,7 @@
         in_specs=in_specs,
         out_specs=[VM] * len(out_shape) if multi else VM,
         scratch_shapes=list(scratch),
-        compiler_params=PARAMS,
+        compiler_params=pltpu.CompilerParams(vmem_limit_bytes=VMEM_LIMITS.get(name, 14) * MIB),
         name=name,
     )
 
@@ -362,7 +414,7 @@
     place = jnp.stack([lax.axis_index("node"), lax.axis_index("local") // 2]).astype(I32)
 
     dy_send = whole(send_dy_kernel, sds((ROWS_N, 1024)), [VM] * 3, "send_dy")(
-        routes, gate_values, out_grads
+        routes.T, gate_values.T, out_grads
     )
     dy_send, tokens = lax.optimization_barrier((dy_send, tokens))
     dy_mid = node_exchange(dy_send)
@@ -371,42 +423,64 @@
     x_near = [x_own] + [shift_y(x_own, s) for s in (1, 2, 3)]
 
     x_send = whole(send_x_kernel, sds((384, 3584)), [SMEM] + [VM] * 4, "send_x")(place, *x_near)
-    *dy_out, table = whole(
+    *dy_out, table, mark = whole(
         regroup_kernel,
-        [sds((ROWS_Y, WIDTH))] * 4 + [sds((ROWS_N, 128), F32)],
+        [sds((ROWS_Y, WIDTH))] * 4 + [sds((ROWS_N, 128), F32), sds((8, 128), F32)],
         [SMEM, VM],
         "regroup",
     )(place, dy_mid)
-    x_send, table = lax.optimization_barrier((x_send, table))
     x_mine = node_exchange(x_send)
     dy_mine = [dy_out[0]] + [shift_y(dy_out[s], s) for s in (1, 2, 3)]
     dy_other = [swap_core(v) for v in dy_mine]
-
+    hbm = pl.BlockSpec(memory_space=pl.ANY)
+    down_near = whole(
+        stage_kernel,
+        sds((HALF, WIDTH)),
+        [hbm, VM],
+        "stage",
+        [pltpu.SemaphoreType.DMA((8,))],
+    )(w_down, mark)
     back = whole(back_kernel, sds((2 * SLOTS, HALF), F32), [VM] * 9, "back")(
-        *dy_mine, *dy_other, w_down
+        *dy_mine, *dy_other, down_near
     )
     x_mine, back = lax.optimization_barrier((x_mine, back))
     x_other = swap_core(x_mine)
+    pre_gate, pre_up, gate_near, up_near = whole(
+        forward_own_kernel,
+        [sds((SLOTS, HALF), F32)] * 2 + [sds((WIDTH, HALF))] * 2,
+        [VM, hbm, hbm, hbm],
+        "forward_own",
+        [pltpu.SemaphoreType.DMA((4, 4))],
+    )(x_mine, w_gate, w_up, back)
     d_gate, d_up, ext = whole(
         forward_kernel,
         [sds((2 * SLOTS, HALF)), sds((2 * SLOTS, HALF)), sds((2 * SLOTS, EXT))],
-        [VM] * 5,
+        [VM] * 6,
         "forward",
-        [pltpu.VMEM((2 * SLOTS, WIDTH), BF)],
-    )(x_mine, x_other, w_gate, w_up, back)
+    )(x_other, gate_near, up_near, back, pre_gate, pre_up)
 
     def dx(part, width):
         return whole(
-            functools.partial(dx_kernel, part), [sds((SLOTS, width))] * 2, [VM] * 5, "dx"
-        )(d_gate, d_up, w_gate, w_up, ext)
+            functools.partial(dx_kernel, part),
+            [sds((SLOTS, width))] * 2,
+            [VM] * 5,
+            "dx",
+        )(d_gate, d_up, gate_near, up_near, ext)
 
     own_a, other_a = dx(0, 3584 + EXT)
     own_b, other_b = dx(1, 3584)
     got_a = swap_core(other_a)
     got_b = swap_core(other_b)
-    pieces = whole(add_kernel, [sds((ROWS_Y, 3584 + EXT))] * 4, [VM] * 2, "add_halves")(own_a, got_a)
+    *pieces, mark = whole(
+        add_kernel,
+        [sds((ROWS_Y, 3584 + EXT))] * 4 + [sds((8, 128), F32)],
+        [VM] * 2,
+        "add_halves",
+    )(own_a, got_a)
     pieces = [pieces[0]] + [shift_y(pieces[s], -s) for s in (1, 2, 3)]
-    sent_b = whole(add_to_nodes_kernel, sds((384, 1792)), [VM] * 2, "add_to_nodes")(own_b, got_b)
+    sent_b = whole(add_to_nodes_kernel, sds((384, 1792)), [VM] * 3, "add_to_nodes")(
+        own_b, got_b, mark
+    )
     back_b = node_exchange(sent_b)
     mixed = whole(combine_kernel, sds((ROWS_N, 512)), [VM] * 5, "combine")(table, *pieces)
     mixed, back_b = lax.optimization_barrier((mixed, back_b))
@@ -415,11 +489,10 @@
         place, *x_near, back_b
     )
     near = [near[0]] + [shift_y(near[s], -s) for s in (1, 2, 3)]
-    return tuple(
-        whole(
-            finish_kernel, [sds((TOK, WIDTH)), sds((TOK, 8), F32)], [SMEM] + [VM] * 6, "finish"
-        )(place, routes, back_a, *near)
-    )
+    input_grads, gate_grads = whole(
+        finish_kernel, [sds((TOK, WIDTH)), sds((8, TOK), F32)], [SMEM] + [VM] * 6, "finish"
+    )(place, routes.T, back_a, *near)
+    return input_grads, gate_grads.T
 
 
 def solution(mesh):

time: 184 us -> 167 us (0.908)
  local copies, waits for them, and re-layouts: 18.1 us -> 6.33 us
  waiting for transfers between devices: 77.5 us -> 70.4 us
  starting transfers between devices: 42.5 us -> 44.6 us
    unnamed x54 -> x34, local copies, waits for them, and re-layouts: 17.3 us -> 6.17 us
    pallas_call x3 -> x5, Pallas kernels: 6.7 us -> 15.9 us  [the longest x1 8.43 us: on_device(): whole(forward_own_kernel, [sds((SLOTS, HALF), F32)] * 2 + [sds((WIDTH, HA...]
    pallas_call x1, Pallas kernels: 13.1 us -> 4.76 us  [on_device(): whole(forward_kernel, [sds((2 * SLOTS, HALF)), sds((2 * SLOTS, HALF)), sd...]
    ppermute x7, waiting for transfers between devices: 8.69 us -> 2.12 us  [swap_core(): return lax.ppermute(v, 'local', [(i, i ^ 1) for i in range(8)])]
  transfers between devices with their start and end apart: 23 -> 23, of which waited for: 16 -> 13; matrix products, arithmetic and copies ran while one was open for 0% -> 0% of each run, Pallas kernels for 11% -> 17%
where the time goes in v3:
time: 167 us; the launch traced here: 166 us
  waiting for transfers between devices  70.4 us (42%)
  starting transfers between devices  44.6 us (27%)
  Pallas kernels  43.6 us (26%)
  local copies, waits for them, and re-layouts  6.33 us (4%)
    ppermute x12, waiting for transfers between devices, shift_y(): return lax.ppermute(v, 'local', [(i, (i + 2 * s) % 8) for i in range(8)])  65.3 us
    all_to_all x4, starting transfers between devices, node_exchange(): lax.all_to_all(v, 'node', split_axis=0, concat_axis=0, tiled=True)  28.3 us
    ppermute x12, starting transfers between devices, shift_y(): return lax.ppermute(v, 'local', [(i, (i + 2 * s) % 8) for i in range(8)])  14.1 us
    pallas_call x1, Pallas kernels, on_device(): whole(forward_own_kernel, [sds((SLOTS, HALF), F32)] * 2 + [sds((WIDTH, HA...  8.43 us
    unnamed x34, local copies, waits for them, and re-layouts  6.17 us
    pallas_call x2, Pallas kernels, dx(): whole(functools.partial(dx_kernel, part), [sds((SLOTS, width))] * 2, [VM]...  6.08 us
    pallas_call x1, Pallas kernels, on_device(): whole(forward_kernel, [sds((2 * SLOTS, HALF)), sds((2 * SLOTS, HALF)), sd...  4.76 us
    pallas_call x1, Pallas kernels, on_device(): whole(regroup_kernel, [sds((ROWS_Y, WIDTH))] * 4 + [sds((ROWS_N, 128), F3...  3.59 us
  transfers between devices with their start and end apart: 23, of which 13 were waited for; matrix products, arithmetic and copies ran while one was open for 0% of the time, Pallas kernels for 17%

profile of v3, /device:TPU:0, one launch (start us, length us, event | category | flops | bytes accessed | tf_op | source)
XLA Modules:
  0.0 165.9 jit_solution(7773323699295498351)
XLA Ops:
  2.9 2.2 %send_dy.1 = bf16[640,1024]{1,0:T(8,128)(2,1)} custom-call(s32[8,16]{1,0:T(8,128)S(1)} %bitcast.20, f32[8,16]{1,0:T(8,128)S(1)} %bitcast.22, bf16[16,7168]{1,0:T(8,128)(2,1)S(1)} %copy-done.11), custom_call_target="tpu_custom_call" | custom-call | tf_op jit(solution)/shard_map/send_dy/pallas_call | solution.py:416
  5.2 8.1 %all-to-all-start = ((bf16[16,40,1024]{2,1,0:T(8,128)(2,1)}), bf16[16,40,1024]{2,1,0:T(8,128)(2,1)S(1)}, u32[]{:S(2)}, u32[]{:S(2)}) async-start(bf16[16,40,1024]{2,1,0:T(8,128)(2,1)} %bitcast.4), calls=%async_computation | async-start | bytes 2621440 | tf_op jit(solution)/shard_map/all_to_all | solution.py:407
  13.6 3.1 %collective-permute-start.2 = (bf16[16,7296]{1,0:T(8,128)(2,1)S(1)}, bf16[16,7296]{1,0:T(8,128)(2,1)S(1)}, u32[]{:S(2)}, u32[]{:S(2)}) collective-permute-start(bf16[16,7296]{1,0:T(8,128)(2,1)S(1)} %pad_maximum_fusion.x0_ref), channel_id=1, source_target_pairs={{0,6},{1,7},{2,0},{3,1},{4,2},{5,3},{6,4},{7,5},{8,14},{9,15},{10,... | collective-permute-start | bytes 700424 | tf_op jit(solution)/shard_map/ppermute | solution.py:397
  17.3 1.0 collective-permute-start
  18.4 8.0 %collective-permute-done.2.x3_ref = bf16[16,7296]{1,0:T(8,128)(2,1)S(1)} collective-permute-done((bf16[16,7296]{1,0:T(8,128)(2,1)S(1)}, bf16[16,7296]{1,0:T(8,128)(2,1)S(1)}, u32[]{:S(2)}, u32[]{:S(2)}) %collective-permute-start.2) | collective-permute-done | bytes 233504 | tf_op jit(solution)/shard_map/ppermute | solution.py:397
  26.9 3.2 %collective-permute-done.x1_ref = bf16[16,7296]{1,0:T(8,128)(2,1)S(1)} collective-permute-done((bf16[16,7296]{1,0:T(8,128)(2,1)S(1)}, bf16[16,7296]{1,0:T(8,128)(2,1)S(1)}, u32[]{:S(2)}, u32[]{:S(2)}) %collective-permute-start) | collective-permute-done | bytes 233504 | tf_op jit(solution)/shard_map/ppermute | solution.py:397
  30.1 3.3 %send_x.1 = bf16[384,3584]{1,0:T(8,128)(2,1)} custom-call(s32[2]{0:T(128)S(1)} %pad_add_fusion.place_ref, bf16[16,7296]{1,0:T(8,128)(2,1)S(1)} %pad_maximum_fusion.x0_ref, bf16[16,7296]{1,0:T(8,128)(2,1)S(1)} %collective-permute-done.x1_ref, bf16[16,7296]{1,0:T(8,128)(2,1)S(1)} %collective-permute-done.1.x2_ref, ...), custom_call_target="tpu_custom_call" | custom-call | tf_op jit(solution)/shard_map/send_x/pallas_call | solution.py:425
  34.1 6.3 %all-to-all-start.1 = ((bf16[16,24,3584]{2,1,0:T(8,128)(2,1)}), bf16[16,24,3584]{2,1,0:T(8,128)(2,1)}, u32[]{:S(2)}, u32[]{:S(2)}) async-start(bf16[16,24,3584]{2,1,0:T(8,128)(2,1)} %bitcast.6), calls=%async_computation.1 | async-start | bytes 5505024 | tf_op jit(solution)/shard_map/all_to_all | solution.py:407
  40.4 3.6 %regroup.1 = (bf16[48,7168]{1,0:T(8,128)(2,1)S(1)}, bf16[48,7168]{1,0:T(8,128)(2,1)S(1)}, bf16[48,7168]{1,0:T(8,128)(2,1)S(1)}, bf16[48,7168]{1,0:T(8,128)(2,1)S...) custom-call(s32[2]{0:T(128)S(1)} %pad_add_fusion.place_ref, bf16[640,1024]{1,0:T(8,128)(2,1)S(1)} %bitcast.18), custom_call_target="tpu_custom_call" | custom-call | tf_op jit(solution)/shard_map/regroup/pallas_call | solution.py:426
  44.8 2.6 %collective-permute-start.4 = (bf16[48,7168]{1,0:T(8,128)(2,1)S(1)}, bf16[48,7168]{1,0:T(8,128)(2,1)S(1)}, u32[]{:S(2)}, u32[]{:S(2)}) collective-permute-start(bf16[48,7168]{1,0:T(8,128)(2,1)S(1)} %get-tuple-element.41), channel_id=1, source_target_pairs={{0,4},{1,5},{2,6},{3,7},{4,0},{5,1},{6,2},{7,3},{8,12},{9,13},{10,... | collective-permute-start | bytes 2064392 | tf_op jit(solution)/shard_map/ppermute | solution.py:397
  47.3 1.3 collective-permute-start.5
  48.7 29.1 %collective-permute-done.3.refs_1_ = bf16[48,7168]{1,0:T(8,128)(2,1)S(1)} collective-permute-done((bf16[48,7168]{1,0:T(8,128)(2,1)S(1)}, bf16[48,7168]{1,0:T(8,128)(2,1)S(1)}, u32[]{:S(2)}, u32[]{:S(2)}) %collective-permute-start.3) | collective-permute-done | bytes 688160 | tf_op jit(solution)/shard_map/ppermute | solution.py:397
  78.4 3.1 %copy-done = bf16[1,512,7168]{2,1,0:T(8,128)(2,1)S(1)} copy-done((bf16[1,512,7168]{2,1,0:T(8,128)(2,1)S(1)}, bf16[1,512,7168]{2,1,0:T(8,128)(2,1)}, u32[]{:S(2)}) %copy-start) | copy-done | bytes 7340056
  81.5 1.9 %stage.1.refs_8_ = bf16[512,7168]{1,0:T(8,128)(2,1)S(1)} custom-call(bf16[512,7168]{1,0:T(8,128)(2,1)S(1)} %bitcast.16, f32[8,128]{1,0:T(8,128)S(1)} %get-tuple-element.43.mark_ref), custom_call_target="tpu_custom_call" | custom-call | tf_op jit(solution)/shard_map/stage/pallas_call | solution.py:436
  83.4 3.1 %back.1.mark_ref.back_ref = f32[384,512]{1,0:T(8,128)S(1)} custom-call(bf16[48,7168]{1,0:T(8,128)(2,1)S(1)} %get-tuple-element.39.refs_0_, bf16[48,7168]{1,0:T(8,128)(2,1)S(1)} %collective-permute-done.3.refs_1_, bf16[48,7168]{1,0:T(8,128)(2,1)S(1)} %collective-permute-done.4.refs_2_, bf16[48,7168]{1,0:T(8,128)(2,1)S(1)} %collective-permute-done.5.refs_3_, ...), custom_call_target="tpu_custom_call" | custom-call | tf_op jit(solution)/shard_map/back/pallas_call | solution.py:443
  87.3 8.4 %forward_own.1 = (f32[192,512]{1,0:T(8,128)S(1)}, f32[192,512]{1,0:T(8,128)S(1)}, bf16[7168,512]{1,0:T(8,128)(2,1)S(1)}, bf16[7168,512]{1,0:T(8,128)(2,1)S(1)}) custom-call(bf16[384,3584]{1,0:T(8,128)(2,1)} %bitcast.7.x_ref, bf16[7168,512]{1,0:T(8,128)(2,1)} %bitcast.23, bf16[7168,512]{1,0:T(8,128)(2,1)} %bitcast.24, f32[384,512]{1,0:T(8,128)S(1)} %back.1.mark_ref.back_ref), custom_call_target="tpu_custom_call" | custom-call | tf_op jit(solution)/shard_map/forward_own/pallas_call | solution.py:448
  95.7 4.8 %forward.1 = (bf16[384,512]{1,0:T(8,128)(2,1)S(1)}, bf16[384,512]{1,0:T(8,128)(2,1)S(1)}, bf16[384,128]{1,0:T(8,128)(2,1)S(1)}) custom-call(bf16[384,3584]{1,0:T(8,128)(2,1)S(1)} %collective-permute-done.10.x_ref, bf16[7168,512]{1,0:T(8,128)(2,1)S(1)} %get-tuple-element.46.gate_ref, bf16[7168,512]{1,0:T(8,128)(2,1)S(1)} %get-tuple-element.47.up_ref, ...), custom_call_target="tpu_custom_call" | custom-call | tf_op jit(solution)/shard_map/forward/pallas_call | solution.py:455
  100.5 3.0 %dx.2 = (bf16[192,3712]{1,0:T(8,128)(2,1)S(1)}, bf16[192,3712]{1,0:T(8,128)(2,1)S(1)}) custom-call(bf16[384,512]{1,0:T(8,128)(2,1)S(1)} %get-tuple-element.50.dgate_ref, bf16[384,512]{1,0:T(8,128)(2,1)S(1)} %get-tuple-element.51.dup_ref, bf16[7168,512]{1,0:T(8,128)(2,1)S(1)} %get-tuple-element.46.gate_ref, bf16[7168,512]{1,0:T(8,128)(2,1)S(1)} %get-tuple-element.47.up_ref, ...), custom_call_target="tpu_custom_call" | custom-call | tf_op jit(solution)/shard_map/dx/pallas_call | solution.py:463
  103.6 3.0 %dx.3 = (bf16[192,3584]{1,0:T(8,128)(2,1)S(1)}, bf16[192,3584]{1,0:T(8,128)(2,1)S(1)}) custom-call(bf16[384,512]{1,0:T(8,128)(2,1)S(1)} %get-tuple-element.50.dgate_ref, bf16[384,512]{1,0:T(8,128)(2,1)S(1)} %get-tuple-element.51.dup_ref, bf16[7168,512]{1,0:T(8,128)(2,1)S(1)} %get-tuple-element.46.gate_ref, bf16[7168,512]{1,0:T(8,128)(2,1)S(1)} %get-tuple-element.47.up_ref, ...), custom_call_target="tpu_custom_call" | custom-call | tf_op jit(solution)/shard_map/dx/pallas_call | solution.py:463
  108.1 2.1 %collective-permute-done.15.got_ref = bf16[192,3584]{1,0:T(8,128)(2,1)S(1)} collective-permute-done((bf16[192,3584]{1,0:T(8,128)(2,1)S(1)}, bf16[192,3584]{1,0:T(8,128)(2,1)S(1)}, u32[]{:S(2)}, u32[]{:S(2)}) %collective-permute-start.15) | collective-permute-done | bytes 1376288 | tf_op jit(solution)/shard_map/ppermute | solution.py:401
  110.2 2.2 %add_to_nodes.1 = bf16[384,1792]{1,0:T(8,128)(2,1)} custom-call(bf16[192,3584]{1,0:T(8,128)(2,1)S(1)} %get-tuple-element.59.own_ref, bf16[192,3584]{1,0:T(8,128)(2,1)S(1)} %collective-permute-done.15.got_ref, f32[8,128]{1,0:T(8,128)S(1)} %get-tuple-element.61.mark_ref), custom_call_target="tpu_custom_call" | custom-call | tf_op jit(solution)/shard_map/add_to_nodes/pallas_call | solution.py:481
  112.4 7.0 %all-to-all-start.2 = ((bf16[16,24,1792]{2,1,0:T(8,128)(2,1)}), bf16[16,24,1792]{2,1,0:T(8,128)(2,1)S(1)}, u32[]{:S(2)}, u32[]{:S(2)}) async-start(bf16[16,24,1792]{2,1,0:T(8,128)(2,1)} %bitcast.11), calls=%async_computation.2 | async-start | bytes 2752512 | tf_op jit(solution)/shard_map/all_to_all | solution.py:407
  119.5 2.4 %collective-permute-start.12 = (bf16[48,3712]{1,0:T(8,128)(2,1)S(1)}, bf16[48,3712]{1,0:T(8,128)(2,1)S(1)}, u32[]{:S(2)}, u32[]{:S(2)}) collective-permute-start(bf16[48,3712]{1,0:T(8,128)(2,1)S(1)} %get-tuple-element.56), channel_id=1, source_target_pairs={{0,6},{1,7},{2,0},{3,1},{4,2},{5,3},{6,4},{7,5},{8,14},{9,15},{10,... | collective-permute-start | bytes 1069064 | tf_op jit(solution)/shard_map/ppermute | solution.py:397
  122.8 14.5 %collective-permute-done.12.p1_ref = bf16[48,3712]{1,0:T(8,128)(2,1)S(1)} collective-permute-done((bf16[48,3712]{1,0:T(8,128)(2,1)S(1)}, bf16[48,3712]{1,0:T(8,128)(2,1)S(1)}, u32[]{:S(2)}, u32[]{:S(2)}) %collective-permute-start.12) | collective-permute-done | bytes 356384 | tf_op jit(solution)/shard_map/ppermute | solution.py:397
  137.4 3.4 %collective-permute-done.14.p3_ref = bf16[48,3712]{1,0:T(8,128)(2,1)S(1)} collective-permute-done((bf16[48,3712]{1,0:T(8,128)(2,1)S(1)}, bf16[48,3712]{1,0:T(8,128)(2,1)S(1)}, u32[]{:S(2)}, u32[]{:S(2)}) %collective-permute-start.14) | collective-permute-done | bytes 356384 | tf_op jit(solution)/shard_map/ppermute | solution.py:397
  140.8 3.1 %combine.1 = bf16[640,512]{1,0:T(8,128)(2,1)} custom-call(f32[640,128]{1,0:T(8,128)S(1)} %copy-done.10, bf16[48,3712]{1,0:T(8,128)(2,1)S(1)} %get-tuple-element.55.p0_ref, bf16[48,3712]{1,0:T(8,128)(2,1)S(1)} %collective-permute-done.12.p1_ref, bf16[48,3712]{1,0:T(8,128)(2,1)S(1)} %collective-permute-done.13.p2_ref, ...), custom_call_target="tpu_custom_call" | custom-call | tf_op jit(solution)/shard_map/combine/pallas_call | solution.py:485
  143.9 6.9 %all-to-all-start.3 = ((bf16[16,40,512]{2,1,0:T(8,128)(2,1)}), bf16[16,40,512]{2,1,0:T(8,128)(2,1)S(1)}, u32[]{:S(2)}, u32[]{:S(2)}) async-start(bf16[16,40,512]{2,1,0:T(8,128)(2,1)} %bitcast.13), calls=%async_computation.3 | async-start | bytes 1310720 | tf_op jit(solution)/shard_map/all_to_all | solution.py:407
  150.8 1.5 combine_near.1
  154.4 3.6 %collective-permute-done.16.b1_ref = bf16[16,3584]{1,0:T(8,128)(2,1)S(1)} collective-permute-done((bf16[16,3584]{1,0:T(8,128)(2,1)S(1)}, bf16[16,3584]{1,0:T(8,128)(2,1)S(1)}, u32[]{:S(2)}, u32[]{:S(2)}) %collective-permute-start.16) | collective-permute-done | bytes 114720 | tf_op jit(solution)/shard_map/ppermute | solution.py:397
  158.1 2.4 %collective-permute-done.17.b2_ref = bf16[16,3584]{1,0:T(8,128)(2,1)S(1)} collective-permute-done((bf16[16,3584]{1,0:T(8,128)(2,1)S(1)}, bf16[16,3584]{1,0:T(8,128)(2,1)S(1)}, u32[]{:S(2)}, u32[]{:S(2)}) %collective-permute-start.17) | collective-permute-done | bytes 114720 | tf_op jit(solution)/shard_map/ppermute | solution.py:397
  160.9 2.3 %all-to-all-done.3 = bf16[16,40,512]{2,1,0:T(8,128)(2,1)S(1)} async-done(((bf16[16,40,512]{2,1,0:T(8,128)(2,1)}), bf16[16,40,512]{2,1,0:T(8,128)(2,1)S(1)}, u32[]{:S(2)}, u32[]{:S(2)}) %all-to-all-start.3) | async-done | bytes 655392 | tf_op jit(solution)/shard_map/all_to_all | solution.py:407
  163.2 2.8 %finish.1 = (bf16[16,7168]{1,0:T(8,128)(2,1)}, f32[8,16]{1,0:T(8,128)}) custom-call(s32[2]{0:T(128)S(1)} %pad_add_fusion.place_ref, s32[8,16]{1,0:T(8,128)S(1)} %bitcast.21, bf16[640,512]{1,0:T(8,128)(2,1)S(1)} %bitcast.19, bf16[16,3584]{1,0:T(8,128)(2,1)S(1)} %get-tuple-element.64.b0_ref, bf16[16,3584]{1,0:T(8,128)(2,1)S(1)} %collective-permute-done.16.b1_ref, ...), custom_call_target="tpu_custom_call" | custom-call | tf_op jit(solution)/shard_map/finish/pallas_call | solution.py:492
  (69 shorter events, 11.7 us)
Async XLA Ops:
  5.2 8.1 %copy-start.13 = (s32[16,8]{0,1:T(8,128)S(1)}, s32[16,8]{0,1:T(8,128)}, u32[]{:S(2)}) copy-start(s32[16,8]{0,1:T(8,128)} %param.9) | copy-start | bytes 1540
  5.2 8.1 %copy-start.15 = (f32[16,8]{0,1:T(8,128)S(1)}, f32[16,8]{0,1:T(8,128)}, u32[]{:S(2)}) copy-start(f32[16,8]{0,1:T(8,128)} %param.10) | copy-start | bytes 1540
  5.2 8.4 %copy-start.16 = (bf16[16,7168]{1,0:T(8,128)(2,1)S(1)}, bf16[16,7168]{1,0:T(8,128)(2,1)}, u32[]{:S(2)}) copy-start(bf16[16,7168]{1,0:T(8,128)(2,1)} %param.7) | copy-start | bytes 688132
  5.2 28.9 %all-to-all-start = ((bf16[16,40,1024]{2,1,0:T(8,128)(2,1)}), bf16[16,40,1024]{2,1,0:T(8,128)(2,1)S(1)}, u32[]{:S(2)}, u32[]{:S(2)}) async-start(bf16[16,40,1024]{2,1,0:T(8,128)(2,1)} %bitcast.4), calls=%async_computation | async-start | bytes 2621440 | tf_op jit(solution)/shard_map/all_to_all | solution.py:407
  13.6 19.8 %copy-start.1 = (bf16[16,7296]{1,0:T(8,128)(2,1)}, bf16[16,7296]{1,0:T(8,128)(2,1)S(1)}, u32[]{:S(2)}) copy-start(bf16[16,7296]{1,0:T(8,128)(2,1)S(1)} %pad_maximum_fusion.x0_ref) | copy-start | bytes 700420
  13.6 12.8 %collective-permute-start.2 = (bf16[16,7296]{1,0:T(8,128)(2,1)S(1)}, bf16[16,7296]{1,0:T(8,128)(2,1)S(1)}, u32[]{:S(2)}, u32[]{:S(2)}) collective-permute-start(bf16[16,7296]{1,0:T(8,128)(2,1)S(1)} %pad_maximum_fusion.x0_ref), channel_id=1, source_target_pairs={{0,6},{1,7},{2,0},{3,1},{4,2},{5,3},{6,4},{7,5},{8,14},{9,15},{10,... | collective-permute-start | bytes 700424 | tf_op jit(solution)/shard_map/ppermute | solution.py:397
  16.7 10.2 %collective-permute-start.1 = (bf16[16,7296]{1,0:T(8,128)(2,1)S(1)}, bf16[16,7296]{1,0:T(8,128)(2,1)S(1)}, u32[]{:S(2)}, u32[]{:S(2)}) collective-permute-start(bf16[16,7296]{1,0:T(8,128)(2,1)S(1)} %pad_maximum_fusion.x0_ref), channel_id=1, source_target_pairs={{0,4},{1,5},{2,6},{3,7},{4,0},{5,1},{6,2},{7,3},{8,12},{9,13},{10,... | collective-permute-start | bytes 700424 | tf_op jit(solution)/shard_map/ppermute | solution.py:397
  17.3 12.8 %collective-permute-start = (bf16[16,7296]{1,0:T(8,128)(2,1)S(1)}, bf16[16,7296]{1,0:T(8,128)(2,1)S(1)}, u32[]{:S(2)}, u32[]{:S(2)}) collective-permute-start(bf16[16,7296]{1,0:T(8,128)(2,1)S(1)} %pad_maximum_fusion.x0_ref), channel_id=1, source_target_pairs={{0,2},{1,3},{2,4},{3,5},{4,6},{5,7},{6,0},{7,1},{8,10},{9,11},{10,... | collective-permute-start | bytes 700424 | tf_op jit(solution)/shard_map/ppermute | solution.py:397
  34.1 52.4 %all-to-all-start.1 = ((bf16[16,24,3584]{2,1,0:T(8,128)(2,1)}), bf16[16,24,3584]{2,1,0:T(8,128)(2,1)}, u32[]{:S(2)}, u32[]{:S(2)}) async-start(bf16[16,24,3584]{2,1,0:T(8,128)(2,1)} %bitcast.6), calls=%async_computation.1 | async-start | bytes 5505024 | tf_op jit(solution)/shard_map/all_to_all | solution.py:407
  44.8 33.0 %collective-permute-start.3 = (bf16[48,7168]{1,0:T(8,128)(2,1)S(1)}, bf16[48,7168]{1,0:T(8,128)(2,1)S(1)}, u32[]{:S(2)}, u32[]{:S(2)}) collective-permute-start(bf16[48,7168]{1,0:T(8,128)(2,1)S(1)} %get-tuple-element.40), channel_id=1, source_target_pairs={{0,2},{1,3},{2,4},{3,5},{4,6},{5,7},{6,0},{7,1},{8,10},{9,11},{10,... | collective-permute-start | bytes 2064392 | tf_op jit(solution)/shard_map/ppermute | solution.py:397
  44.8 33.0 %collective-permute-start.4 = (bf16[48,7168]{1,0:T(8,128)(2,1)S(1)}, bf16[48,7168]{1,0:T(8,128)(2,1)S(1)}, u32[]{:S(2)}, u32[]{:S(2)}) collective-permute-start(bf16[48,7168]{1,0:T(8,128)(2,1)S(1)} %get-tuple-element.41), channel_id=1, source_target_pairs={{0,4},{1,5},{2,6},{3,7},{4,0},{5,1},{6,2},{7,3},{8,12},{9,13},{10,... | collective-permute-start | bytes 2064392 | tf_op jit(solution)/shard_map/ppermute | solution.py:397
  47.3 31.1 %collective-permute-start.5 = (bf16[48,7168]{1,0:T(8,128)(2,1)S(1)}, bf16[48,7168]{1,0:T(8,128)(2,1)S(1)}, u32[]{:S(2)}, u32[]{:S(2)}) collective-permute-start(bf16[48,7168]{1,0:T(8,128)(2,1)S(1)} %get-tuple-element.42), channel_id=1, source_target_pairs={{0,6},{1,7},{2,0},{3,1},{4,2},{5,3},{6,4},{7,5},{8,14},{9,15},{10,... | collective-permute-start | bytes 2064392 | tf_op jit(solution)/shard_map/ppermute | solution.py:397
  48.7 34.7 %collective-permute-start.6 = (bf16[48,7168]{1,0:T(8,128)(2,1)S(1)}, bf16[48,7168]{1,0:T(8,128)(2,1)S(1)}, u32[]{:S(2)}, u32[]{:S(2)}) collective-permute-start(bf16[48,7168]{1,0:T(8,128)(2,1)S(1)} %get-tuple-element.39.refs_0_), channel_id=1, source_target_pairs={{0,1},{1,0},{2,3},{3,2},{4,5},{5,4},{6,7},{7,6},{8,9},{9,8},{10,11... | collective-permute-start | bytes 2064392 | tf_op jit(solution)/shard_map/ppermute | solution.py:401
  77.8 5.6 %collective-permute-start.7 = (bf16[48,7168]{1,0:T(8,128)(2,1)S(1)}, bf16[48,7168]{1,0:T(8,128)(2,1)S(1)}, u32[]{:S(2)}, u32[]{:S(2)}) collective-permute-start(bf16[48,7168]{1,0:T(8,128)(2,1)S(1)} %collective-permute-done.3.refs_1_), channel_id=1, source_target_pairs={{0,1},{1,0},{2,3},{3,2},{4,5},{5,4},{6,7},{7,6},{8,9},{9,8},{10,11... | collective-permute-start | bytes 2064392 | tf_op jit(solution)/shard_map/ppermute | solution.py:401
  77.8 5.6 %collective-permute-start.8 = (bf16[48,7168]{1,0:T(8,128)(2,1)S(1)}, bf16[48,7168]{1,0:T(8,128)(2,1)S(1)}, u32[]{:S(2)}, u32[]{:S(2)}) collective-permute-start(bf16[48,7168]{1,0:T(8,128)(2,1)S(1)} %collective-permute-done.4.refs_2_), channel_id=1, source_target_pairs={{0,1},{1,0},{2,3},{3,2},{4,5},{5,4},{6,7},{7,6},{8,9},{9,8},{10,11... | collective-permute-start | bytes 2064392 | tf_op jit(solution)/shard_map/ppermute | solution.py:401
  78.4 5.0 %collective-permute-start.9 = (bf16[48,7168]{1,0:T(8,128)(2,1)S(1)}, bf16[48,7168]{1,0:T(8,128)(2,1)S(1)}, u32[]{:S(2)}, u32[]{:S(2)}) collective-permute-start(bf16[48,7168]{1,0:T(8,128)(2,1)S(1)} %collective-permute-done.5.refs_3_), channel_id=1, source_target_pairs={{0,1},{1,0},{2,3},{3,2},{4,5},{5,4},{6,7},{7,6},{8,9},{9,8},{10,11... | collective-permute-start | bytes 2064392 | tf_op jit(solution)/shard_map/ppermute | solution.py:401
  86.5 9.2 %collective-permute-start.10 = (bf16[384,3584]{1,0:T(8,128)(2,1)}, bf16[384,3584]{1,0:T(8,128)(2,1)S(1)}, u32[]{:S(2)}, u32[]{:S(2)}) collective-permute-start(bf16[384,3584]{1,0:T(8,128)(2,1)} %bitcast.7.x_ref), channel_id=1, source_target_pairs={{0,1},{1,0},{2,3},{3,2},{4,5},{5,4},{6,7},{7,6},{8,9},{9,8},{10,11... | collective-permute-start | bytes 8257544 | tf_op jit(solution)/shard_map/ppermute | solution.py:401
  103.5 3.9 %collective-permute-start.11 = (bf16[192,3712]{1,0:T(8,128)(2,1)S(1)}, bf16[192,3712]{1,0:T(8,128)(2,1)S(1)}, u32[]{:S(2)}, u32[]{:S(2)}) collective-permute-start(bf16[192,3712]{1,0:T(8,128)(2,1)S(1)} %get-tuple-element.54), channel_id=1, source_target_pairs={{0,1},{1,0},{2,3},{3,2},{4,5},{5,4},{6,7},{7,6},{8,9},{9,8},{10,11... | collective-permute-start | bytes 4276232 | tf_op jit(solution)/shard_map/ppermute | solution.py:401
  106.7 3.5 %collective-permute-start.15 = (bf16[192,3584]{1,0:T(8,128)(2,1)S(1)}, bf16[192,3584]{1,0:T(8,128)(2,1)S(1)}, u32[]{:S(2)}, u32[]{:S(2)}) collective-permute-start(bf16[192,3584]{1,0:T(8,128)(2,1)S(1)} %get-tuple-element.60), channel_id=1, source_target_pairs={{0,1},{1,0},{2,3},{3,2},{4,5},{5,4},{6,7},{7,6},{8,9},{9,8},{10,11... | collective-permute-start | bytes 4128776 | tf_op jit(solution)/shard_map/ppermute | solution.py:401
  112.4 28.3 %copy-start.10 = (f32[640,128]{1,0:T(8,128)S(1)}, f32[640,128]{1,0:T(8,128)}, u32[]{:S(2)}) copy-start(f32[640,128]{1,0:T(8,128)} %copy-done.9) | copy-start | bytes 983044
  112.4 31.5 %all-to-all-start.2 = ((bf16[16,24,1792]{2,1,0:T(8,128)(2,1)}), bf16[16,24,1792]{2,1,0:T(8,128)(2,1)S(1)}, u32[]{:S(2)}, u32[]{:S(2)}) async-start(bf16[16,24,1792]{2,1,0:T(8,128)(2,1)} %bitcast.11), calls=%async_computation.2 | async-start | bytes 2752512 | tf_op jit(solution)/shard_map/all_to_all | solution.py:407
  119.5 17.9 %collective-permute-start.12 = (bf16[48,3712]{1,0:T(8,128)(2,1)S(1)}, bf16[48,3712]{1,0:T(8,128)(2,1)S(1)}, u32[]{:S(2)}, u32[]{:S(2)}) collective-permute-start(bf16[48,3712]{1,0:T(8,128)(2,1)S(1)} %get-tuple-element.56), channel_id=1, source_target_pairs={{0,6},{1,7},{2,0},{3,1},{4,2},{5,3},{6,4},{7,5},{8,14},{9,15},{10,... | collective-permute-start | bytes 1069064 | tf_op jit(solution)/shard_map/ppermute | solution.py:397
  121.9 15.5 %collective-permute-start.13 = (bf16[48,3712]{1,0:T(8,128)(2,1)S(1)}, bf16[48,3712]{1,0:T(8,128)(2,1)S(1)}, u32[]{:S(2)}, u32[]{:S(2)}) collective-permute-start(bf16[48,3712]{1,0:T(8,128)(2,1)S(1)} %get-tuple-element.57), channel_id=1, source_target_pairs={{0,4},{1,5},{2,6},{3,7},{4,0},{5,1},{6,2},{7,3},{8,12},{9,13},{10,... | collective-permute-start | bytes 1069064 | tf_op jit(solution)/shard_map/ppermute | solution.py:397
  121.9 18.9 %collective-permute-start.14 = (bf16[48,3712]{1,0:T(8,128)(2,1)S(1)}, bf16[48,3712]{1,0:T(8,128)(2,1)S(1)}, u32[]{:S(2)}, u32[]{:S(2)}) collective-permute-start(bf16[48,3712]{1,0:T(8,128)(2,1)S(1)} %get-tuple-element.58), channel_id=1, source_target_pairs={{0,2},{1,3},{2,4},{3,5},{4,6},{5,7},{6,0},{7,1},{8,10},{9,11},{10,... | collective-permute-start | bytes 1069064 | tf_op jit(solution)/shard_map/ppermute | solution.py:397
  140.7 10.0 %copy-start.2 = (bf16[16,7296]{1,0:T(8,128)(2,1)S(1)}, bf16[16,7296]{1,0:T(8,128)(2,1)}, u32[]{:S(2)}) copy-start(bf16[16,7296]{1,0:T(8,128)(2,1)} %copy-done.1) | copy-start | bytes 700420
  140.7 10.0 %copy-start.4 = (bf16[16,7296]{1,0:T(8,128)(2,1)S(1)}, bf16[16,7296]{1,0:T(8,128)(2,1)}, u32[]{:S(2)}) copy-start(bf16[16,7296]{1,0:T(8,128)(2,1)} %copy-done.3) | copy-start | bytes 700420
  140.7 10.0 %copy-start.6 = (bf16[16,7296]{1,0:T(8,128)(2,1)S(1)}, bf16[16,7296]{1,0:T(8,128)(2,1)}, u32[]{:S(2)}) copy-start(bf16[16,7296]{1,0:T(8,128)(2,1)} %copy-done.5) | copy-start | bytes 700420
  140.8 10.0 %copy-start.8 = (bf16[16,7296]{1,0:T(8,128)(2,1)S(1)}, bf16[16,7296]{1,0:T(8,128)(2,1)}, u32[]{:S(2)}) copy-start(bf16[16,7296]{1,0:T(8,128)(2,1)} %copy-done.7) | copy-start | bytes 700420
  143.9 19.3 %all-to-all-start.3 = ((bf16[16,40,512]{2,1,0:T(8,128)(2,1)}), bf16[16,40,512]{2,1,0:T(8,128)(2,1)S(1)}, u32[]{:S(2)}, u32[]{:S(2)}) async-start(bf16[16,40,512]{2,1,0:T(8,128)(2,1)} %bitcast.13), calls=%async_computation.3 | async-start | bytes 1310720 | tf_op jit(solution)/shard_map/all_to_all | solution.py:407
  152.3 5.7 %collective-permute-start.16 = (bf16[16,3584]{1,0:T(8,128)(2,1)S(1)}, bf16[16,3584]{1,0:T(8,128)(2,1)S(1)}, u32[]{:S(2)}, u32[]{:S(2)}) collective-permute-start(bf16[16,3584]{1,0:T(8,128)(2,1)S(1)} %get-tuple-element.65), channel_id=1, source_target_pairs={{0,6},{1,7},{2,0},{3,1},{4,2},{5,3},{6,4},{7,5},{8,14},{9,15},{10,... | collective-permute-start | bytes 344072 | tf_op jit(solution)/shard_map/ppermute | solution.py:397
  153.3 7.2 %collective-permute-start.17 = (bf16[16,3584]{1,0:T(8,128)(2,1)S(1)}, bf16[16,3584]{1,0:T(8,128)(2,1)S(1)}, u32[]{:S(2)}, u32[]{:S(2)}) collective-permute-start(bf16[16,3584]{1,0:T(8,128)(2,1)S(1)} %get-tuple-element.66), channel_id=1, source_target_pairs={{0,4},{1,5},{2,6},{3,7},{4,0},{5,1},{6,2},{7,3},{8,12},{9,13},{10,... | collective-permute-start | bytes 344072 | tf_op jit(solution)/shard_map/ppermute | solution.py:397
  153.6 7.3 %collective-permute-start.18 = (bf16[16,3584]{1,0:T(8,128)(2,1)S(1)}, bf16[16,3584]{1,0:T(8,128)(2,1)S(1)}, u32[]{:S(2)}, u32[]{:S(2)}) collective-permute-start(bf16[16,3584]{1,0:T(8,128)(2,1)S(1)} %get-tuple-element.67), channel_id=1, source_target_pairs={{0,2},{1,3},{2,4},{3,5},{4,6},{5,7},{6,0},{7,1},{8,10},{9,11},{10,... | collective-permute-start | bytes 344072 | tf_op jit(solution)/shard_map/ppermute | solution.py:397
  (8 other events, 23.1 us)

commit v4 on v3

--- a/solution.py
+++ b/solution.py
@@ -23,7 +23,7 @@
 ROWS_N = N_NODE * 40
 EXT = 128
 MIB = 1024 * 1024
-VMEM_LIMITS = {"back": 20, "forward_own": 30, "forward": 30, "dx": 24}
+VMEM_LIMITS = {"send_dy": 60, "back": 20, "forward_own": 30, "forward": 30, "dx": 24}
 
 
 def iota(shape, dim):
@@ -128,7 +128,7 @@
         out_ref[:, lo : lo + 512] = dot(pick, stack).astype(BF)
 
 
-def regroup_kernel(place_ref, rows_ref, out0_ref, out1_ref, out2_ref, out3_ref, table_ref, mark_ref):
+def regroup_kernel(place_ref, rows_ref, out0_ref, out1_ref, out2_ref, out3_ref, meta_ref, mark_ref):
     node = place_ref[0]
     y = place_ref[1]
     outs = [out0_ref, out1_ref, out2_ref, out3_ref]
@@ -136,6 +136,7 @@
     want = ((c >> 2) << 6) + 4 * node + ((y + c) & 3)
     select = onehot((c < 8) & (iota((256, 128), 0) == want)).astype(BF)
     meta = rows_ref[:, :256]
+    meta_ref[...] = meta
     mark_ref[...] = jnp.zeros_like(mark_ref)
     code = lax.dot_general(select, meta, (((0,), (1,)), ((), ())), preferred_element_type=F32)[:8]
     col = iota((8, ROWS_N), 1)
@@ -150,12 +151,17 @@
         moved = dot(pick.astype(BF), rows_ref[...]).astype(BF)
         for s in range(N_Y):
             outs[s][:, 1024 * q : 1024 * (q + 1)] = moved[ROWS_Y * s : ROWS_Y * (s + 1)]
-    picked = dot(meta, select).astype(BF)
-    r = iota((ROWS_N, ROWS_N), 0)
-    rn = div40(r)
-    rp = r - 40 * rn
-    source = 40 * rn + 35 + (rp - 5 * div5(rp))
-    table_ref[...] = dot(onehot(iota((ROWS_N, ROWS_N), 1) == source).astype(BF), picked)
+
+
+def table_kernel(place_ref, meta_ref, table_ref):
+    c = iota((256, 128), 1)
+    want = ((c >> 2) << 6) + 4 * place_ref[0] + ((place_ref[1] + c) & 3)
+    select = onehot((c < 8) & (iota((256, 128), 0) == want)).astype(BF)
+    picked = dot(meta_ref[...], select).astype(BF)
+    r = iota((128, ROWS_N), 0)
+    j = r & 7
+    source = jnp.where(j < CAP_NODE, 40 * (r >> 3) + 35 + j, -1)
+    table_ref[...] = dot(onehot(iota((128, ROWS_N), 1) == source).astype(BF), picked)
 
 
 def copy_parts(source, target, sems, first, rows):
@@ -311,32 +317,32 @@
             outs[s][:, 1792 * h : 1792 * (h + 1)] = total[TOK * s : TOK * (s + 1)]
 
 
-def combine_kernel(table_ref, p0_ref, p1_ref, p2_ref, p3_ref, out_ref):
+def combine_kernel(table_ref, p0_ref, p1_ref, p2_ref, p3_ref, out_ref, rows_ref):
     pieces = [p0_ref, p1_ref, p2_ref, p3_ref]
-    lane = iota((ROWS_N, SLOTS), 1)
+    lane = iota((128, SLOTS), 1)
     ls = div3(lane >> 4)
     rem = lane - ROWS_Y * ls
     ln = div3(rem)
     lr = rem - 3 * ln
-    row = iota((ROWS_N, SLOTS), 0)
-    rn = div40(row)
-    rq = div5(row - 40 * rn)
     table = table_ref[...]
-    code = jnp.zeros((ROWS_N, SLOTS), F32)
-    gate = jnp.zeros((ROWS_N, SLOTS), F32)
+    code = jnp.zeros((128, SLOTS), F32)
+    gate = jnp.zeros((128, SLOTS), F32)
     for s in range(N_Y):
         code = jnp.where(ls == s, table[:, s : s + 1], code)
         gate = jnp.where(ls == s, table[:, 4 + s : 5 + s], gate)
-    match = (rn == ln) & (code == (lr + 1).astype(F32))
-    weight = jnp.where(match, gate, 0.0)
-    total = jnp.zeros((ROWS_N, 512), F32)
+    match = ((iota((128, SLOTS), 0) >> 3) == ln) & (code == (lr + 1).astype(F32))
+    weight = jnp.where(match, gate, 0.0).astype(BF)
+    ext = jnp.concatenate([p[:, 3584:] for p in pieces], axis=0)
+    terms = dot(onehot(match).astype(BF), ext)
+    terms = jnp.concatenate([terms, jnp.zeros((128, 512 - EXT), F32)], axis=1)
     for q in range(7):
-        rows = jnp.concatenate([p[:, 512 * q : 512 * (q + 1)] for p in pieces], axis=0)
-        total = total + dot(jnp.where(rq == q, weight, 0.0).astype(BF), rows)
-    ext = jnp.concatenate([p[:, 3584:] for p in pieces], axis=0)
-    terms = dot(onehot(match & (rq == 7)).astype(BF), ext)
-    out_ref[:, :EXT] = (total[:, :EXT] + terms).astype(BF)
-    out_ref[:, EXT:] = total[:, EXT:].astype(BF)
+        total = dot(weight, jnp.concatenate([p[:, 512 * q : 512 * (q + 1)] for p in pieces], axis=0))
+        for n in range(N_NODE):
+            at = 40 * n + 5 * q
+            rows_ref[at : at + 8, :] = total[8 * n : 8 * n + 8]
+    for n in range(N_NODE):
+        rows_ref[40 * n + 35 : 40 * n + 40, :] = terms[8 * n : 8 * n + 5]
+    out_ref[...] = rows_ref[...].astype(BF)
 
 
 def finish_kernel(place_ref, routes_ref, a_ref, b0_ref, b1_ref, b2_ref, b3_ref, dx_ref, gg_ref):
@@ -351,9 +357,10 @@
     cp = col - 40 * cn
     cq = div5(cp)
     match = code == (cp - 5 * cq + 1).astype(F32)
+    pick = jnp.concatenate([onehot(match & (cq == q)) for q in range(7)], axis=0).astype(BF)
+    total = dot(pick, a_ref[...]).astype(BF)
     for q in range(7):
-        pick = onehot(match & (cq == q)).astype(BF)
-        dx_ref[:, 512 * q : 512 * (q + 1)] = dot(pick, a_ref[...]).astype(BF)
+        dx_ref[:, 512 * q : 512 * (q + 1)] = total[TOK * q : TOK * (q + 1)]
     total = b0_ref[...].astype(F32) + b1_ref[...].astype(F32)
     total = total + b2_ref[...].astype(F32) + b3_ref[...].astype(F32)
     dx_ref[:, 3584:] = total.astype(BF)
@@ -423,9 +430,9 @@
     x_near = [x_own] + [shift_y(x_own, s) for s in (1, 2, 3)]
 
     x_send = whole(send_x_kernel, sds((384, 3584)), [SMEM] + [VM] * 4, "send_x")(place, *x_near)
-    *dy_out, table, mark = whole(
+    *dy_out, meta, mark = whole(
         regroup_kernel,
-        [sds((ROWS_Y, WIDTH))] * 4 + [sds((ROWS_N, 128), F32), sds((8, 128), F32)],
+        [sds((ROWS_Y, WIDTH))] * 4 + [sds((ROWS_N, 256)), sds((8, 128), F32)],
         [SMEM, VM],
         "regroup",
     )(place, dy_mid)
@@ -440,6 +447,7 @@
         "stage",
         [pltpu.SemaphoreType.DMA((8,))],
     )(w_down, mark)
+    table = whole(table_kernel, sds((128, 128), F32), [SMEM, VM], "table")(place, meta)
     back = whole(back_kernel, sds((2 * SLOTS, HALF), F32), [VM] * 9, "back")(
         *dy_mine, *dy_other, down_near
     )
@@ -482,7 +490,13 @@
         own_b, got_b, mark
     )
     back_b = node_exchange(sent_b)
-    mixed = whole(combine_kernel, sds((ROWS_N, 512)), [VM] * 5, "combine")(table, *pieces)
+    mixed = whole(
+        combine_kernel,
+        sds((ROWS_N, 512)),
+        [VM] * 5,
+        "combine",
+        [pltpu.VMEM((ROWS_N, 512), F32)],
+    )(table, *pieces)
     mixed, back_b = lax.optimization_barrier((mixed, back_b))
     back_a = node_exchange(mixed)
     near = whole(combine_near_kernel, [sds((TOK, 3584))] * 4, [SMEM] + [VM] * 5, "combine_near")(

time: 167 us -> 163 us (0.976)
  local copies, waits for them, and re-layouts: 6.33 us -> 4.01 us
    unnamed x34 -> x28, local copies, waits for them, and re-layouts: 6.17 us -> 3.85 us
    pallas_call x2 -> x3, Pallas kernels: 6.7 us -> 5.74 us  [the longest x1 3.14 us: on_device(): whole(regroup_kernel, [sds((ROWS_Y, WIDTH))] * 4 + [sds((ROWS_N, 256)), s...]
where the time goes in v4:
time: 163 us; the launch traced here: 162 us
  waiting for transfers between devices  69.3 us (43%)
  starting transfers between devices  44.6 us (27%)
  Pallas kernels  43.1 us (26%)
  local copies, waits for them, and re-layouts  4.01 us (2%)
    ppermute x12, waiting for transfers between devices, shift_y(): return lax.ppermute(v, 'local', [(i, (i + 2 * s) % 8) for i in range(8)])  64.3 us
    all_to_all x4, starting transfers between devices, node_exchange(): lax.all_to_all(v, 'node', split_axis=0, concat_axis=0, tiled=True)  28.3 us
    ppermute x12, starting transfers between devices, shift_y(): return lax.ppermute(v, 'local', [(i, (i + 2 * s) % 8) for i in range(8)])  14.1 us
    pallas_call x1, Pallas kernels, on_device(): whole(forward_own_kernel, [sds((SLOTS, HALF), F32)] * 2 + [sds((WIDTH, HA...  8.43 us
    pallas_call x2, Pallas kernels, dx(): whole(functools.partial(dx_kernel, part), [sds((SLOTS, width))] * 2, [VM]...  6.09 us
    pallas_call x1, Pallas kernels, on_device(): whole(forward_kernel, [sds((2 * SLOTS, HALF)), sds((2 * SLOTS, HALF)), sd...  4.82 us
    unnamed x28, local copies, waits for them, and re-layouts  3.85 us
    pallas_call x1, Pallas kernels, on_device(): whole(send_x_kernel, sds((384, 3584)), [SMEM] + [VM] * 4, 'send_x')  3.32 us
  transfers between devices with their start and end apart: 23, of which 13 were waited for; matrix products, arithmetic and copies ran while one was open for 0% of the time, Pallas kernels for 17%

profile of v4, /device:TPU:0, one launch (start us, length us, event | category | flops | bytes accessed | tf_op | source)
XLA Modules:
  0.0 162.2 jit_solution(10937967266348153224)
XLA Ops:
  0.6 3.2 %send_dy.1 = bf16[640,1024]{1,0:T(8,128)(2,1)} custom-call(s32[8,16]{1,0:T(8,128)} %bitcast.20, f32[8,16]{1,0:T(8,128)} %bitcast.25, bf16[16,7168]{1,0:T(8,128)(2,1)} %dy_ref.1), custom_call_target="tpu_custom_call" | custom-call | tf_op jit(solution)/shard_map/send_dy/pallas_call | solution.py:423
  3.8 8.1 %all-to-all-start = ((bf16[16,40,1024]{2,1,0:T(8,128)(2,1)}), bf16[16,40,1024]{2,1,0:T(8,128)(2,1)S(1)}, u32[]{:S(2)}, u32[]{:S(2)}) async-start(bf16[16,40,1024]{2,1,0:T(8,128)(2,1)} %bitcast.24), calls=%async_computation | async-start | bytes 2621440 | tf_op jit(solution)/shard_map/all_to_all | solution.py:414
  12.3 3.1 %collective-permute-start.2 = (bf16[16,7296]{1,0:T(8,128)(2,1)S(1)}, bf16[16,7296]{1,0:T(8,128)(2,1)S(1)}, u32[]{:S(2)}, u32[]{:S(2)}) collective-permute-start(bf16[16,7296]{1,0:T(8,128)(2,1)S(1)} %pad_maximum_fusion.x0_ref), channel_id=1, source_target_pairs={{0,6},{1,7},{2,0},{3,1},{4,2},{5,3},{6,4},{7,5},{8,14},{9,15},{10,... | collective-permute-start | bytes 700424 | tf_op jit(solution)/shard_map/ppermute | solution.py:404
  17.0 8.0 %collective-permute-done.2.x3_ref = bf16[16,7296]{1,0:T(8,128)(2,1)S(1)} collective-permute-done((bf16[16,7296]{1,0:T(8,128)(2,1)S(1)}, bf16[16,7296]{1,0:T(8,128)(2,1)S(1)}, u32[]{:S(2)}, u32[]{:S(2)}) %collective-permute-start.2) | collective-permute-done | bytes 233504 | tf_op jit(solution)/shard_map/ppermute | solution.py:404
  25.5 3.2 %collective-permute-done.x1_ref = bf16[16,7296]{1,0:T(8,128)(2,1)S(1)} collective-permute-done((bf16[16,7296]{1,0:T(8,128)(2,1)S(1)}, bf16[16,7296]{1,0:T(8,128)(2,1)S(1)}, u32[]{:S(2)}, u32[]{:S(2)}) %collective-permute-start) | collective-permute-done | bytes 233504 | tf_op jit(solution)/shard_map/ppermute | solution.py:404
  28.7 3.3 %send_x.1 = bf16[384,3584]{1,0:T(8,128)(2,1)} custom-call(s32[2]{0:T(128)S(1)} %pad_add_fusion.place_ref, bf16[16,7296]{1,0:T(8,128)(2,1)S(1)} %pad_maximum_fusion.x0_ref, bf16[16,7296]{1,0:T(8,128)(2,1)S(1)} %collective-permute-done.x1_ref, bf16[16,7296]{1,0:T(8,128)(2,1)S(1)} %collective-permute-done.1.x2_ref, ...), custom_call_target="tpu_custom_call" | custom-call | tf_op jit(solution)/shard_map/send_x/pallas_call | solution.py:432
  32.7 6.3 %all-to-all-start.1 = ((bf16[16,24,3584]{2,1,0:T(8,128)(2,1)}), bf16[16,24,3584]{2,1,0:T(8,128)(2,1)}, u32[]{:S(2)}, u32[]{:S(2)}) async-start(bf16[16,24,3584]{2,1,0:T(8,128)(2,1)} %bitcast.6), calls=%async_computation.1 | async-start | bytes 5505024 | tf_op jit(solution)/shard_map/all_to_all | solution.py:414
  39.1 3.1 %regroup.1 = (bf16[48,7168]{1,0:T(8,128)(2,1)S(1)}, bf16[48,7168]{1,0:T(8,128)(2,1)S(1)}, bf16[48,7168]{1,0:T(8,128)(2,1)S(1)}, bf16[48,7168]{1,0:T(8,128)(2,1)S...) custom-call(s32[2]{0:T(128)S(1)} %pad_add_fusion.place_ref, bf16[640,1024]{1,0:T(8,128)(2,1)S(1)} %bitcast.18), custom_call_target="tpu_custom_call" | custom-call | tf_op jit(solution)/shard_map/regroup/pallas_call | solution.py:433
  43.0 2.6 %collective-permute-start.4 = (bf16[48,7168]{1,0:T(8,128)(2,1)S(1)}, bf16[48,7168]{1,0:T(8,128)(2,1)S(1)}, u32[]{:S(2)}, u32[]{:S(2)}) collective-permute-start(bf16[48,7168]{1,0:T(8,128)(2,1)S(1)} %get-tuple-element.41), channel_id=1, source_target_pairs={{0,4},{1,5},{2,6},{3,7},{4,0},{5,1},{6,2},{7,3},{8,12},{9,13},{10,... | collective-permute-start | bytes 2064392 | tf_op jit(solution)/shard_map/ppermute | solution.py:404
  45.6 1.3 collective-permute-start.5
  46.9 29.1 %collective-permute-done.3.refs_1_ = bf16[48,7168]{1,0:T(8,128)(2,1)S(1)} collective-permute-done((bf16[48,7168]{1,0:T(8,128)(2,1)S(1)}, bf16[48,7168]{1,0:T(8,128)(2,1)S(1)}, u32[]{:S(2)}, u32[]{:S(2)}) %collective-permute-start.3) | collective-permute-done | bytes 688160 | tf_op jit(solution)/shard_map/ppermute | solution.py:404
  76.6 3.1 %copy-done = bf16[1,512,7168]{2,1,0:T(8,128)(2,1)S(1)} copy-done((bf16[1,512,7168]{2,1,0:T(8,128)(2,1)S(1)}, bf16[1,512,7168]{2,1,0:T(8,128)(2,1)}, u32[]{:S(2)}) %copy-start) | copy-done | bytes 7340056
  79.7 1.9 %stage.1.refs_8_ = bf16[512,7168]{1,0:T(8,128)(2,1)S(1)} custom-call(bf16[512,7168]{1,0:T(8,128)(2,1)S(1)} %bitcast.16, f32[8,128]{1,0:T(8,128)S(1)} %get-tuple-element.43.mark_ref), custom_call_target="tpu_custom_call" | custom-call | tf_op jit(solution)/shard_map/stage/pallas_call | solution.py:443
  81.6 3.0 %back.1.mark_ref.back_ref = f32[384,512]{1,0:T(8,128)S(1)} custom-call(bf16[48,7168]{1,0:T(8,128)(2,1)S(1)} %get-tuple-element.39.refs_0_, bf16[48,7168]{1,0:T(8,128)(2,1)S(1)} %collective-permute-done.3.refs_1_, bf16[48,7168]{1,0:T(8,128)(2,1)S(1)} %collective-permute-done.4.refs_2_, bf16[48,7168]{1,0:T(8,128)(2,1)S(1)} %collective-permute-done.5.refs_3_, ...), custom_call_target="tpu_custom_call" | custom-call | tf_op jit(solution)/shard_map/back/pallas_call | solution.py:451
  85.4 8.4 %forward_own.1 = (f32[192,512]{1,0:T(8,128)S(1)}, f32[192,512]{1,0:T(8,128)S(1)}, bf16[7168,512]{1,0:T(8,128)(2,1)S(1)}, bf16[7168,512]{1,0:T(8,128)(2,1)S(1)}) custom-call(bf16[384,3584]{1,0:T(8,128)(2,1)} %bitcast.7.x_ref, bf16[7168,512]{1,0:T(8,128)(2,1)} %bitcast.22, bf16[7168,512]{1,0:T(8,128)(2,1)} %bitcast.23, f32[384,512]{1,0:T(8,128)S(1)} %back.1.mark_ref.back_ref), custom_call_target="tpu_custom_call" | custom-call | tf_op jit(solution)/shard_map/forward_own/pallas_call | solution.py:456
  93.9 4.8 %forward.1 = (bf16[384,512]{1,0:T(8,128)(2,1)S(1)}, bf16[384,512]{1,0:T(8,128)(2,1)S(1)}, bf16[384,128]{1,0:T(8,128)(2,1)S(1)}) custom-call(bf16[384,3584]{1,0:T(8,128)(2,1)S(1)} %collective-permute-done.10.x_ref, bf16[7168,512]{1,0:T(8,128)(2,1)S(1)} %get-tuple-element.46.gate_ref, bf16[7168,512]{1,0:T(8,128)(2,1)S(1)} %get-tuple-element.47.up_ref, ...), custom_call_target="tpu_custom_call" | custom-call | tf_op jit(solution)/shard_map/forward/pallas_call | solution.py:463
  98.7 3.0 %dx.2 = (bf16[192,3712]{1,0:T(8,128)(2,1)S(1)}, bf16[192,3712]{1,0:T(8,128)(2,1)S(1)}) custom-call(bf16[384,512]{1,0:T(8,128)(2,1)S(1)} %get-tuple-element.50.dgate_ref, bf16[384,512]{1,0:T(8,128)(2,1)S(1)} %get-tuple-element.51.dup_ref, bf16[7168,512]{1,0:T(8,128)(2,1)S(1)} %get-tuple-element.46.gate_ref, bf16[7168,512]{1,0:T(8,128)(2,1)S(1)} %get-tuple-element.47.up_ref, ...), custom_call_target="tpu_custom_call" | custom-call | tf_op jit(solution)/shard_map/dx/pallas_call | solution.py:471
  101.8 3.0 %dx.3 = (bf16[192,3584]{1,0:T(8,128)(2,1)S(1)}, bf16[192,3584]{1,0:T(8,128)(2,1)S(1)}) custom-call(bf16[384,512]{1,0:T(8,128)(2,1)S(1)} %get-tuple-element.50.dgate_ref, bf16[384,512]{1,0:T(8,128)(2,1)S(1)} %get-tuple-element.51.dup_ref, bf16[7168,512]{1,0:T(8,128)(2,1)S(1)} %get-tuple-element.46.gate_ref, bf16[7168,512]{1,0:T(8,128)(2,1)S(1)} %get-tuple-element.47.up_ref, ...), custom_call_target="tpu_custom_call" | custom-call | tf_op jit(solution)/shard_map/dx/pallas_call | solution.py:471
  106.3 2.1 %collective-permute-done.15.got_ref = bf16[192,3584]{1,0:T(8,128)(2,1)S(1)} collective-permute-done((bf16[192,3584]{1,0:T(8,128)(2,1)S(1)}, bf16[192,3584]{1,0:T(8,128)(2,1)S(1)}, u32[]{:S(2)}, u32[]{:S(2)}) %collective-permute-start.15) | collective-permute-done | bytes 1376288 | tf_op jit(solution)/shard_map/ppermute | solution.py:408
  108.4 2.2 %add_to_nodes.1 = bf16[384,1792]{1,0:T(8,128)(2,1)} custom-call(bf16[192,3584]{1,0:T(8,128)(2,1)S(1)} %get-tuple-element.59.own_ref, bf16[192,3584]{1,0:T(8,128)(2,1)S(1)} %collective-permute-done.15.got_ref, f32[8,128]{1,0:T(8,128)S(1)} %get-tuple-element.61.mark_ref), custom_call_target="tpu_custom_call" | custom-call | tf_op jit(solution)/shard_map/add_to_nodes/pallas_call | solution.py:489
  110.6 7.0 %all-to-all-start.2 = ((bf16[16,24,1792]{2,1,0:T(8,128)(2,1)}), bf16[16,24,1792]{2,1,0:T(8,128)(2,1)S(1)}, u32[]{:S(2)}, u32[]{:S(2)}) async-start(bf16[16,24,1792]{2,1,0:T(8,128)(2,1)} %bitcast.11), calls=%async_computation.2 | async-start | bytes 2752512 | tf_op jit(solution)/shard_map/all_to_all | solution.py:414
  117.6 2.4 %collective-permute-start.12 = (bf16[48,3712]{1,0:T(8,128)(2,1)S(1)}, bf16[48,3712]{1,0:T(8,128)(2,1)S(1)}, u32[]{:S(2)}, u32[]{:S(2)}) collective-permute-start(bf16[48,3712]{1,0:T(8,128)(2,1)S(1)} %get-tuple-element.56), channel_id=1, source_target_pairs={{0,6},{1,7},{2,0},{3,1},{4,2},{5,3},{6,4},{7,5},{8,14},{9,15},{10,... | collective-permute-start | bytes 1069064 | tf_op jit(solution)/shard_map/ppermute | solution.py:404
  121.0 1.0 table.1.table_ref
  122.0 13.5 %collective-permute-done.12.p1_ref = bf16[48,3712]{1,0:T(8,128)(2,1)S(1)} collective-permute-done((bf16[48,3712]{1,0:T(8,128)(2,1)S(1)}, bf16[48,3712]{1,0:T(8,128)(2,1)S(1)}, u32[]{:S(2)}, u32[]{:S(2)}) %collective-permute-start.12) | collective-permute-done | bytes 356384 | tf_op jit(solution)/shard_map/ppermute | solution.py:404
  135.6 3.4 %collective-permute-done.14.p3_ref = bf16[48,3712]{1,0:T(8,128)(2,1)S(1)} collective-permute-done((bf16[48,3712]{1,0:T(8,128)(2,1)S(1)}, bf16[48,3712]{1,0:T(8,128)(2,1)S(1)}, u32[]{:S(2)}, u32[]{:S(2)}) %collective-permute-start.14) | collective-permute-done | bytes 356384 | tf_op jit(solution)/shard_map/ppermute | solution.py:404
  139.0 1.6 combine.1
  140.6 6.9 %all-to-all-start.3 = ((bf16[16,40,512]{2,1,0:T(8,128)(2,1)}), bf16[16,40,512]{2,1,0:T(8,128)(2,1)S(1)}, u32[]{:S(2)}, u32[]{:S(2)}) async-start(bf16[16,40,512]{2,1,0:T(8,128)(2,1)} %bitcast.13), calls=%async_computation.3 | async-start | bytes 1310720 | tf_op jit(solution)/shard_map/all_to_all | solution.py:414
  147.5 1.5 combine_near.1
  151.1 3.6 %collective-permute-done.16.b1_ref = bf16[16,3584]{1,0:T(8,128)(2,1)S(1)} collective-permute-done((bf16[16,3584]{1,0:T(8,128)(2,1)S(1)}, bf16[16,3584]{1,0:T(8,128)(2,1)S(1)}, u32[]{:S(2)}, u32[]{:S(2)}) %collective-permute-start.16) | collective-permute-done | bytes 114720 | tf_op jit(solution)/shard_map/ppermute | solution.py:404
  154.8 2.4 %collective-permute-done.17.b2_ref = bf16[16,3584]{1,0:T(8,128)(2,1)S(1)} collective-permute-done((bf16[16,3584]{1,0:T(8,128)(2,1)S(1)}, bf16[16,3584]{1,0:T(8,128)(2,1)S(1)}, u32[]{:S(2)}, u32[]{:S(2)}) %collective-permute-start.17) | collective-permute-done | bytes 114720 | tf_op jit(solution)/shard_map/ppermute | solution.py:404
  157.6 2.3 %all-to-all-done.3 = bf16[16,40,512]{2,1,0:T(8,128)(2,1)S(1)} async-done(((bf16[16,40,512]{2,1,0:T(8,128)(2,1)}), bf16[16,40,512]{2,1,0:T(8,128)(2,1)S(1)}, u32[]{:S(2)}, u32[]{:S(2)}) %all-to-all-start.3) | async-done | bytes 655392 | tf_op jit(solution)/shard_map/all_to_all | solution.py:414
  159.9 2.3 %finish.1 = (bf16[16,7168]{1,0:T(8,128)(2,1)}, f32[8,16]{1,0:T(8,128)}) custom-call(s32[2]{0:T(128)S(1)} %pad_add_fusion.place_ref, s32[8,16]{1,0:T(8,128)S(1)} %bitcast.21, bf16[640,512]{1,0:T(8,128)(2,1)S(1)} %bitcast.19, bf16[16,3584]{1,0:T(8,128)(2,1)S(1)} %get-tuple-element.64.b0_ref, bf16[16,3584]{1,0:T(8,128)(2,1)S(1)} %collective-permute-done.16.b1_ref, ...), custom_call_target="tpu_custom_call" | custom-call | tf_op jit(solution)/shard_map/finish/pallas_call | solution.py:506
  (64 shorter events, 10.3 us)
Async XLA Ops:
  3.8 8.1 %copy-start.11 = (s32[16,8]{0,1:T(8,128)S(1)}, s32[16,8]{0,1:T(8,128)}, u32[]{:S(2)}) copy-start(s32[16,8]{0,1:T(8,128)} %param.9) | copy-start | bytes 1540
  3.8 8.1 %copy-start.13 = (f32[16,8]{0,1:T(8,128)S(1)}, f32[16,8]{0,1:T(8,128)}, u32[]{:S(2)}) copy-start(f32[16,8]{0,1:T(8,128)} %param.10) | copy-start | bytes 1540
  3.8 8.4 %copy-start.12 = (bf16[16,7168]{1,0:T(8,128)(2,1)S(1)}, bf16[16,7168]{1,0:T(8,128)(2,1)}, u32[]{:S(2)}) copy-start(bf16[16,7168]{1,0:T(8,128)(2,1)} %param.7) | copy-start | bytes 688132
  3.8 28.9 %all-to-all-start = ((bf16[16,40,1024]{2,1,0:T(8,128)(2,1)}), bf16[16,40,1024]{2,1,0:T(8,128)(2,1)S(1)}, u32[]{:S(2)}, u32[]{:S(2)}) async-start(bf16[16,40,1024]{2,1,0:T(8,128)(2,1)} %bitcast.24), calls=%async_computation | async-start | bytes 2621440 | tf_op jit(solution)/shard_map/all_to_all | solution.py:414
  12.3 19.8 %copy-start.1 = (bf16[16,7296]{1,0:T(8,128)(2,1)}, bf16[16,7296]{1,0:T(8,128)(2,1)S(1)}, u32[]{:S(2)}) copy-start(bf16[16,7296]{1,0:T(8,128)(2,1)S(1)} %pad_maximum_fusion.x0_ref) | copy-start | bytes 700420
  12.3 12.8 %collective-permute-start.2 = (bf16[16,7296]{1,0:T(8,128)(2,1)S(1)}, bf16[16,7296]{1,0:T(8,128)(2,1)S(1)}, u32[]{:S(2)}, u32[]{:S(2)}) collective-permute-start(bf16[16,7296]{1,0:T(8,128)(2,1)S(1)} %pad_maximum_fusion.x0_ref), channel_id=1, source_target_pairs={{0,6},{1,7},{2,0},{3,1},{4,2},{5,3},{6,4},{7,5},{8,14},{9,15},{10,... | collective-permute-start | bytes 700424 | tf_op jit(solution)/shard_map/ppermute | solution.py:404
  15.4 10.2 %collective-permute-start.1 = (bf16[16,7296]{1,0:T(8,128)(2,1)S(1)}, bf16[16,7296]{1,0:T(8,128)(2,1)S(1)}, u32[]{:S(2)}, u32[]{:S(2)}) collective-permute-start(bf16[16,7296]{1,0:T(8,128)(2,1)S(1)} %pad_maximum_fusion.x0_ref), channel_id=1, source_target_pairs={{0,4},{1,5},{2,6},{3,7},{4,0},{5,1},{6,2},{7,3},{8,12},{9,13},{10,... | collective-permute-start | bytes 700424 | tf_op jit(solution)/shard_map/ppermute | solution.py:404
  16.0 12.7 %collective-permute-start = (bf16[16,7296]{1,0:T(8,128)(2,1)S(1)}, bf16[16,7296]{1,0:T(8,128)(2,1)S(1)}, u32[]{:S(2)}, u32[]{:S(2)}) collective-permute-start(bf16[16,7296]{1,0:T(8,128)(2,1)S(1)} %pad_maximum_fusion.x0_ref), channel_id=1, source_target_pairs={{0,2},{1,3},{2,4},{3,5},{4,6},{5,7},{6,0},{7,1},{8,10},{9,11},{10,... | collective-permute-start | bytes 700424 | tf_op jit(solution)/shard_map/ppermute | solution.py:404
  32.7 51.9 %all-to-all-start.1 = ((bf16[16,24,3584]{2,1,0:T(8,128)(2,1)}), bf16[16,24,3584]{2,1,0:T(8,128)(2,1)}, u32[]{:S(2)}, u32[]{:S(2)}) async-start(bf16[16,24,3584]{2,1,0:T(8,128)(2,1)} %bitcast.6), calls=%async_computation.1 | async-start | bytes 5505024 | tf_op jit(solution)/shard_map/all_to_all | solution.py:414
  43.0 33.0 %collective-permute-start.3 = (bf16[48,7168]{1,0:T(8,128)(2,1)S(1)}, bf16[48,7168]{1,0:T(8,128)(2,1)S(1)}, u32[]{:S(2)}, u32[]{:S(2)}) collective-permute-start(bf16[48,7168]{1,0:T(8,128)(2,1)S(1)} %get-tuple-element.40), channel_id=1, source_target_pairs={{0,2},{1,3},{2,4},{3,5},{4,6},{5,7},{6,0},{7,1},{8,10},{9,11},{10,... | collective-permute-start | bytes 2064392 | tf_op jit(solution)/shard_map/ppermute | solution.py:404
  43.0 33.0 %collective-permute-start.4 = (bf16[48,7168]{1,0:T(8,128)(2,1)S(1)}, bf16[48,7168]{1,0:T(8,128)(2,1)S(1)}, u32[]{:S(2)}, u32[]{:S(2)}) collective-permute-start(bf16[48,7168]{1,0:T(8,128)(2,1)S(1)} %get-tuple-element.41), channel_id=1, source_target_pairs={{0,4},{1,5},{2,6},{3,7},{4,0},{5,1},{6,2},{7,3},{8,12},{9,13},{10,... | collective-permute-start | bytes 2064392 | tf_op jit(solution)/shard_map/ppermute | solution.py:404
  45.6 31.1 %collective-permute-start.5 = (bf16[48,7168]{1,0:T(8,128)(2,1)S(1)}, bf16[48,7168]{1,0:T(8,128)(2,1)S(1)}, u32[]{:S(2)}, u32[]{:S(2)}) collective-permute-start(bf16[48,7168]{1,0:T(8,128)(2,1)S(1)} %get-tuple-element.42), channel_id=1, source_target_pairs={{0,6},{1,7},{2,0},{3,1},{4,2},{5,3},{6,4},{7,5},{8,14},{9,15},{10,... | collective-permute-start | bytes 2064392 | tf_op jit(solution)/shard_map/ppermute | solution.py:404
  46.9 34.7 %collective-permute-start.6 = (bf16[48,7168]{1,0:T(8,128)(2,1)S(1)}, bf16[48,7168]{1,0:T(8,128)(2,1)S(1)}, u32[]{:S(2)}, u32[]{:S(2)}) collective-permute-start(bf16[48,7168]{1,0:T(8,128)(2,1)S(1)} %get-tuple-element.39.refs_0_), channel_id=1, source_target_pairs={{0,1},{1,0},{2,3},{3,2},{4,5},{5,4},{6,7},{7,6},{8,9},{9,8},{10,11... | collective-permute-start | bytes 2064392 | tf_op jit(solution)/shard_map/ppermute | solution.py:408
  76.0 5.6 %collective-permute-start.7 = (bf16[48,7168]{1,0:T(8,128)(2,1)S(1)}, bf16[48,7168]{1,0:T(8,128)(2,1)S(1)}, u32[]{:S(2)}, u32[]{:S(2)}) collective-permute-start(bf16[48,7168]{1,0:T(8,128)(2,1)S(1)} %collective-permute-done.3.refs_1_), channel_id=1, source_target_pairs={{0,1},{1,0},{2,3},{3,2},{4,5},{5,4},{6,7},{7,6},{8,9},{9,8},{10,11... | collective-permute-start | bytes 2064392 | tf_op jit(solution)/shard_map/ppermute | solution.py:408
  76.0 5.6 %collective-permute-start.8 = (bf16[48,7168]{1,0:T(8,128)(2,1)S(1)}, bf16[48,7168]{1,0:T(8,128)(2,1)S(1)}, u32[]{:S(2)}, u32[]{:S(2)}) collective-permute-start(bf16[48,7168]{1,0:T(8,128)(2,1)S(1)} %collective-permute-done.4.refs_2_), channel_id=1, source_target_pairs={{0,1},{1,0},{2,3},{3,2},{4,5},{5,4},{6,7},{7,6},{8,9},{9,8},{10,11... | collective-permute-start | bytes 2064392 | tf_op jit(solution)/shard_map/ppermute | solution.py:408
  76.6 5.0 %collective-permute-start.9 = (bf16[48,7168]{1,0:T(8,128)(2,1)S(1)}, bf16[48,7168]{1,0:T(8,128)(2,1)S(1)}, u32[]{:S(2)}, u32[]{:S(2)}) collective-permute-start(bf16[48,7168]{1,0:T(8,128)(2,1)S(1)} %collective-permute-done.5.refs_3_), channel_id=1, source_target_pairs={{0,1},{1,0},{2,3},{3,2},{4,5},{5,4},{6,7},{7,6},{8,9},{9,8},{10,11... | collective-permute-start | bytes 2064392 | tf_op jit(solution)/shard_map/ppermute | solution.py:408
  84.7 9.2 %collective-permute-start.10 = (bf16[384,3584]{1,0:T(8,128)(2,1)}, bf16[384,3584]{1,0:T(8,128)(2,1)S(1)}, u32[]{:S(2)}, u32[]{:S(2)}) collective-permute-start(bf16[384,3584]{1,0:T(8,128)(2,1)} %bitcast.7.x_ref), channel_id=1, source_target_pairs={{0,1},{1,0},{2,3},{3,2},{4,5},{5,4},{6,7},{7,6},{8,9},{9,8},{10,11... | collective-permute-start | bytes 8257544 | tf_op jit(solution)/shard_map/ppermute | solution.py:408
  101.7 3.9 %collective-permute-start.11 = (bf16[192,3712]{1,0:T(8,128)(2,1)S(1)}, bf16[192,3712]{1,0:T(8,128)(2,1)S(1)}, u32[]{:S(2)}, u32[]{:S(2)}) collective-permute-start(bf16[192,3712]{1,0:T(8,128)(2,1)S(1)} %get-tuple-element.54), channel_id=1, source_target_pairs={{0,1},{1,0},{2,3},{3,2},{4,5},{5,4},{6,7},{7,6},{8,9},{9,8},{10,11... | collective-permute-start | bytes 4276232 | tf_op jit(solution)/shard_map/ppermute | solution.py:408
  104.9 3.5 %collective-permute-start.15 = (bf16[192,3584]{1,0:T(8,128)(2,1)S(1)}, bf16[192,3584]{1,0:T(8,128)(2,1)S(1)}, u32[]{:S(2)}, u32[]{:S(2)}) collective-permute-start(bf16[192,3584]{1,0:T(8,128)(2,1)S(1)} %get-tuple-element.60), channel_id=1, source_target_pairs={{0,1},{1,0},{2,3},{3,2},{4,5},{5,4},{6,7},{7,6},{8,9},{9,8},{10,11... | collective-permute-start | bytes 4128776 | tf_op jit(solution)/shard_map/ppermute | solution.py:408
  110.6 10.4 %copy-start.10 = (bf16[640,256]{1,0:T(8,128)(2,1)S(1)}, bf16[640,256]{1,0:T(8,128)(2,1)}, u32[]{:S(2)}) copy-start(bf16[640,256]{1,0:T(8,128)(2,1)} %copy-done.9) | copy-start | bytes 983044
  110.6 30.0 %all-to-all-start.2 = ((bf16[16,24,1792]{2,1,0:T(8,128)(2,1)}), bf16[16,24,1792]{2,1,0:T(8,128)(2,1)S(1)}, u32[]{:S(2)}, u32[]{:S(2)}) async-start(bf16[16,24,1792]{2,1,0:T(8,128)(2,1)} %bitcast.11), calls=%async_computation.2 | async-start | bytes 2752512 | tf_op jit(solution)/shard_map/all_to_all | solution.py:414
  117.6 17.9 %collective-permute-start.12 = (bf16[48,3712]{1,0:T(8,128)(2,1)S(1)}, bf16[48,3712]{1,0:T(8,128)(2,1)S(1)}, u32[]{:S(2)}, u32[]{:S(2)}) collective-permute-start(bf16[48,3712]{1,0:T(8,128)(2,1)S(1)} %get-tuple-element.56), channel_id=1, source_target_pairs={{0,6},{1,7},{2,0},{3,1},{4,2},{5,3},{6,4},{7,5},{8,14},{9,15},{10,... | collective-permute-start | bytes 1069064 | tf_op jit(solution)/shard_map/ppermute | solution.py:404
  120.1 15.5 %collective-permute-start.13 = (bf16[48,3712]{1,0:T(8,128)(2,1)S(1)}, bf16[48,3712]{1,0:T(8,128)(2,1)S(1)}, u32[]{:S(2)}, u32[]{:S(2)}) collective-permute-start(bf16[48,3712]{1,0:T(8,128)(2,1)S(1)} %get-tuple-element.57), channel_id=1, source_target_pairs={{0,4},{1,5},{2,6},{3,7},{4,0},{5,1},{6,2},{7,3},{8,12},{9,13},{10,... | collective-permute-start | bytes 1069064 | tf_op jit(solution)/shard_map/ppermute | solution.py:404
  120.1 18.9 %collective-permute-start.14 = (bf16[48,3712]{1,0:T(8,128)(2,1)S(1)}, bf16[48,3712]{1,0:T(8,128)(2,1)S(1)}, u32[]{:S(2)}, u32[]{:S(2)}) collective-permute-start(bf16[48,3712]{1,0:T(8,128)(2,1)S(1)} %get-tuple-element.58), channel_id=1, source_target_pairs={{0,2},{1,3},{2,4},{3,5},{4,6},{5,7},{6,0},{7,1},{8,10},{9,11},{10,... | collective-permute-start | bytes 1069064 | tf_op jit(solution)/shard_map/ppermute | solution.py:404
  138.9 8.5 %copy-start.2 = (bf16[16,7296]{1,0:T(8,128)(2,1)S(1)}, bf16[16,7296]{1,0:T(8,128)(2,1)}, u32[]{:S(2)}) copy-start(bf16[16,7296]{1,0:T(8,128)(2,1)} %copy-done.1) | copy-start | bytes 700420
  138.9 8.5 %copy-start.4 = (bf16[16,7296]{1,0:T(8,128)(2,1)S(1)}, bf16[16,7296]{1,0:T(8,128)(2,1)}, u32[]{:S(2)}) copy-start(bf16[16,7296]{1,0:T(8,128)(2,1)} %copy-done.3) | copy-start | bytes 700420
  138.9 8.5 %copy-start.6 = (bf16[16,7296]{1,0:T(8,128)(2,1)S(1)}, bf16[16,7296]{1,0:T(8,128)(2,1)}, u32[]{:S(2)}) copy-start(bf16[16,7296]{1,0:T(8,128)(2,1)} %copy-done.5) | copy-start | bytes 700420
  138.9 8.5 %copy-start.8 = (bf16[16,7296]{1,0:T(8,128)(2,1)S(1)}, bf16[16,7296]{1,0:T(8,128)(2,1)}, u32[]{:S(2)}) copy-start(bf16[16,7296]{1,0:T(8,128)(2,1)} %copy-done.7) | copy-start | bytes 700420
  140.6 19.3 %all-to-all-start.3 = ((bf16[16,40,512]{2,1,0:T(8,128)(2,1)}), bf16[16,40,512]{2,1,0:T(8,128)(2,1)S(1)}, u32[]{:S(2)}, u32[]{:S(2)}) async-start(bf16[16,40,512]{2,1,0:T(8,128)(2,1)} %bitcast.13), calls=%async_computation.3 | async-start | bytes 1310720 | tf_op jit(solution)/shard_map/all_to_all | solution.py:414
  149.0 5.7 %collective-permute-start.16 = (bf16[16,3584]{1,0:T(8,128)(2,1)S(1)}, bf16[16,3584]{1,0:T(8,128)(2,1)S(1)}, u32[]{:S(2)}, u32[]{:S(2)}) collective-permute-start(bf16[16,3584]{1,0:T(8,128)(2,1)S(1)} %get-tuple-element.65), channel_id=1, source_target_pairs={{0,6},{1,7},{2,0},{3,1},{4,2},{5,3},{6,4},{7,5},{8,14},{9,15},{10,... | collective-permute-start | bytes 344072 | tf_op jit(solution)/shard_map/ppermute | solution.py:404
  150.0 7.2 %collective-permute-start.17 = (bf16[16,3584]{1,0:T(8,128)(2,1)S(1)}, bf16[16,3584]{1,0:T(8,128)(2,1)S(1)}, u32[]{:S(2)}, u32[]{:S(2)}) collective-permute-start(bf16[16,3584]{1,0:T(8,128)(2,1)S(1)} %get-tuple-element.66), channel_id=1, source_target_pairs={{0,4},{1,5},{2,6},{3,7},{4,0},{5,1},{6,2},{7,3},{8,12},{9,13},{10,... | collective-permute-start | bytes 344072 | tf_op jit(solution)/shard_map/ppermute | solution.py:404
  150.3 7.3 %collective-permute-start.18 = (bf16[16,3584]{1,0:T(8,128)(2,1)S(1)}, bf16[16,3584]{1,0:T(8,128)(2,1)S(1)}, u32[]{:S(2)}, u32[]{:S(2)}) collective-permute-start(bf16[16,3584]{1,0:T(8,128)(2,1)S(1)} %get-tuple-element.67), channel_id=1, source_target_pairs={{0,2},{1,3},{2,4},{3,5},{4,6},{5,7},{6,0},{7,1},{8,10},{9,11},{10,... | collective-permute-start | bytes 344072 | tf_op jit(solution)/shard_map/ppermute | solution.py:404
  (5 other events, 20.7 us)

commit v5 on v4

--- a/solution.py
+++ b/solution.py
@@ -23,7 +23,7 @@
 ROWS_N = N_NODE * 40
 EXT = 128
 MIB = 1024 * 1024
-VMEM_LIMITS = {"send_dy": 60, "back": 20, "forward_own": 30, "forward": 30, "dx": 24}
+VMEM_LIMITS = {"send_dy": 60, "regroup_own": 24, "back": 20, "forward_own": 30, "forward": 30, "dx": 24}
 
 
 def iota(shape, dim):
@@ -128,17 +128,28 @@
         out_ref[:, lo : lo + 512] = dot(pick, stack).astype(BF)
 
 
-def regroup_kernel(place_ref, rows_ref, out0_ref, out1_ref, out2_ref, out3_ref, meta_ref, mark_ref):
-    node = place_ref[0]
-    y = place_ref[1]
-    outs = [out0_ref, out1_ref, out2_ref, out3_ref]
+def copy_parts(source, target, sems, first, rows):
+    copies = []
+    step = rows // sems.shape[0]
+    for i in range(sems.shape[0]):
+        at = pl.ds(first + step * i, step)
+        copies.append(pltpu.make_async_copy(source.at[at], target.at[at], sems.at[i]))
+        copies[-1].start()
+    return copies
+
+
+def wait_all(copies):
+    for copy in copies:
+        copy.wait()
+
+
+def regroup(shifts, place_ref, rows_ref, outs):
     c = iota((256, 128), 1)
-    want = ((c >> 2) << 6) + 4 * node + ((y + c) & 3)
+    want = ((c >> 2) << 6) + 4 * place_ref[0] + ((place_ref[1] + c) & 3)
     select = onehot((c < 8) & (iota((256, 128), 0) == want)).astype(BF)
-    meta = rows_ref[:, :256]
-    meta_ref[...] = meta
-    mark_ref[...] = jnp.zeros_like(mark_ref)
-    code = lax.dot_general(select, meta, (((0,), (1,)), ((), ())), preferred_element_type=F32)[:8]
+    code = lax.dot_general(
+        select, rows_ref[:, :256], (((0,), (1,)), ((), ())), preferred_element_type=F32
+    )[:8]
     col = iota((8, ROWS_N), 1)
     n = div40(col)
     key = jnp.where((col - 40 * n >= 35) & (code > 0.0), 4.0 * n.astype(F32) + code, -1.0)
@@ -147,10 +158,21 @@
     row_key = (4 * rn + (row - 3 * rn) + 1).astype(F32)
     for q in range(7):
         key_q = pltpu.roll(key, ROWS_N - (35 - 5 * q), 1)
-        pick = jnp.concatenate([onehot(row_key == key_q[s : s + 1, :]) for s in range(N_Y)], axis=0)
+        pick = jnp.concatenate([onehot(row_key == key_q[s : s + 1, :]) for s in shifts], axis=0)
         moved = dot(pick.astype(BF), rows_ref[...]).astype(BF)
-        for s in range(N_Y):
-            outs[s][:, 1024 * q : 1024 * (q + 1)] = moved[ROWS_Y * s : ROWS_Y * (s + 1)]
+        for i, out in enumerate(outs):
+            out[:, 1024 * q : 1024 * (q + 1)] = moved[ROWS_Y * i : ROWS_Y * (i + 1)]
+
+
+def regroup_far_kernel(place_ref, rows_ref, out1_ref, out2_ref, out3_ref, meta_ref):
+    meta_ref[...] = rows_ref[:, :256]
+    regroup((1, 2, 3), place_ref, rows_ref, [out1_ref, out2_ref, out3_ref])
+
+
+def regroup_own_kernel(place_ref, rows_ref, down_hbm, out_ref, down_ref, sems):
+    loads = copy_parts(down_hbm, down_ref, sems, 0, HALF)
+    regroup((0,), place_ref, rows_ref, [out_ref])
+    wait_all(loads)
 
 
 def table_kernel(place_ref, meta_ref, table_ref):
@@ -162,25 +184,6 @@
     j = r & 7
     source = jnp.where(j < CAP_NODE, 40 * (r >> 3) + 35 + j, -1)
     table_ref[...] = dot(onehot(iota((128, ROWS_N), 1) == source).astype(BF), picked)
-
-
-def copy_parts(source, target, sems, first, rows):
-    copies = []
-    step = rows // sems.shape[0]
-    for i in range(sems.shape[0]):
-        at = pl.ds(first + step * i, step)
-        copies.append(pltpu.make_async_copy(source.at[at], target.at[at], sems.at[i]))
-        copies[-1].start()
-    return copies
-
-
-def wait_all(copies):
-    for copy in copies:
-        copy.wait()
-
-
-def stage_kernel(source_ref, mark_ref, out_ref, sems):
-    wait_all(copy_parts(source_ref, out_ref, sems, 0, source_ref.shape[0]))
 
 
 def back_kernel(*refs):
@@ -430,23 +433,23 @@
     x_near = [x_own] + [shift_y(x_own, s) for s in (1, 2, 3)]
 
     x_send = whole(send_x_kernel, sds((384, 3584)), [SMEM] + [VM] * 4, "send_x")(place, *x_near)
-    *dy_out, meta, mark = whole(
-        regroup_kernel,
-        [sds((ROWS_Y, WIDTH))] * 4 + [sds((ROWS_N, 256)), sds((8, 128), F32)],
+    hbm = pl.BlockSpec(memory_space=pl.ANY)
+    *dy_far, meta = whole(
+        regroup_far_kernel,
+        [sds((ROWS_Y, WIDTH))] * 3 + [sds((ROWS_N, 256))],
         [SMEM, VM],
         "regroup",
     )(place, dy_mid)
+    dy_own, down_near = whole(
+        regroup_own_kernel,
+        [sds((ROWS_Y, WIDTH)), sds((HALF, WIDTH))],
+        [SMEM, VM, hbm],
+        "regroup_own",
+        [pltpu.SemaphoreType.DMA((8,))],
+    )(place, dy_mid, w_down)
     x_mine = node_exchange(x_send)
-    dy_mine = [dy_out[0]] + [shift_y(dy_out[s], s) for s in (1, 2, 3)]
+    dy_mine = [dy_own] + [shift_y(dy_far[s - 1], s) for s in (1, 2, 3)]
     dy_other = [swap_core(v) for v in dy_mine]
-    hbm = pl.BlockSpec(memory_space=pl.ANY)
-    down_near = whole(
-        stage_kernel,
-        sds((HALF, WIDTH)),
-        [hbm, VM],
-        "stage",
-        [pltpu.SemaphoreType.DMA((8,))],
-    )(w_down, mark)
     table = whole(table_kernel, sds((128, 128), F32), [SMEM, VM], "table")(place, meta)
     back = whole(back_kernel, sds((2 * SLOTS, HALF), F32), [VM] * 9, "back")(
         *dy_mine, *dy_other, down_near

time: 163 us -> 159 us (0.975)
  waiting for transfers between devices: 69.3 us -> 66.6 us
  starting transfers between devices: 44.6 us -> 42.9 us
    ppermute x12, waiting for transfers between devices: 64.3 us -> 57.4 us  [shift_y(): return lax.ppermute(v, 'local', [(i, (i + 2 * s) % 8) for i in range(8)])]
    ppermute x7, waiting for transfers between devices: 2.12 us -> 5.81 us  [swap_core(): return lax.ppermute(v, 'local', [(i, i ^ 1) for i in range(8)])]
    pallas_call x2, Pallas kernels: 4.99 us -> 6.73 us  [the longest x1 4.1 us: on_device(): whole(regroup_own_kernel, [sds((ROWS_Y, WIDTH)), sds((HALF, WIDTH))], [SM...]
    unnamed x28 -> x14, local copies, waits for them, and re-layouts: 3.85 us -> 4.62 us
  transfers between devices with their start and end apart: 23 -> 23, of which waited for: 13 -> 18; matrix products, arithmetic and copies ran while one was open for 0% -> 0% of each run, Pallas kernels for 17% -> 18%
where the time goes in v5:
time: 159 us
  waiting for transfers between devices  66.6 us (42%)
  Pallas kernels  43.3 us (27%)
  starting transfers between devices  42.9 us (27%)
  local copies, waits for them, and re-layouts  4.79 us (3%)
    ppermute x12, waiting for transfers between devices, shift_y(): return lax.ppermute(v, 'local', [(i, (i + 2 * s) % 8) for i in range(8)])  57.4 us
    all_to_all x4, starting transfers between devices, node_exchange(): lax.all_to_all(v, 'node', split_axis=0, concat_axis=0, tiled=True)  28.1 us
    ppermute x12, starting transfers between devices, shift_y(): return lax.ppermute(v, 'local', [(i, (i + 2 * s) % 8) for i in range(8)])  12.9 us
    pallas_call x1, Pallas kernels, on_device(): whole(forward_own_kernel, [sds((SLOTS, HALF), F32)] * 2 + [sds((WIDTH, HA...  8.43 us
    pallas_call x2, Pallas kernels, dx(): whole(functools.partial(dx_kernel, part), [sds((SLOTS, width))] * 2, [VM]...  6.08 us
    ppermute x7, waiting for transfers between devices, swap_core(): return lax.ppermute(v, 'local', [(i, i ^ 1) for i in range(8)])  5.81 us
    pallas_call x1, Pallas kernels, on_device(): whole(forward_kernel, [sds((2 * SLOTS, HALF)), sds((2 * SLOTS, HALF)), sd...  4.82 us
    unnamed x14, local copies, waits for them, and re-layouts  4.62 us
  transfers between devices with their start and end apart: 23, of which 18 were waited for; matrix products, arithmetic and copies ran while one was open for 0% of the time, Pallas kernels for 18%

profile of v5, /device:TPU:0, one launch (start us, length us, event | category | flops | bytes accessed | tf_op | source)
XLA Modules:
  0.0 158.6 jit_solution(9656192692604087297)
XLA Ops:
  0.6 3.2 %send_dy.1 = bf16[640,1024]{1,0:T(8,128)(2,1)} custom-call(s32[8,16]{1,0:T(8,128)} %bitcast.22, f32[8,16]{1,0:T(8,128)} %bitcast.27, bf16[16,7168]{1,0:T(8,128)(2,1)} %dy_ref.1), custom_call_target="tpu_custom_call" | custom-call | tf_op jit(solution)/shard_map/send_dy/pallas_call | solution.py:426
  3.8 8.1 %all-to-all-start = ((bf16[16,40,1024]{2,1,0:T(8,128)(2,1)}), bf16[16,40,1024]{2,1,0:T(8,128)(2,1)S(1)}, u32[]{:S(2)}, u32[]{:S(2)}) async-start(bf16[16,40,1024]{2,1,0:T(8,128)(2,1)} %bitcast.26), calls=%async_computation | async-start | bytes 2621440 | tf_op jit(solution)/shard_map/all_to_all | solution.py:417
  12.2 3.1 %collective-permute-start.2 = (bf16[16,7296]{1,0:T(8,128)(2,1)S(1)}, bf16[16,7296]{1,0:T(8,128)(2,1)S(1)}, u32[]{:S(2)}, u32[]{:S(2)}) collective-permute-start(bf16[16,7296]{1,0:T(8,128)(2,1)S(1)} %pad_maximum_fusion.x0_ref), channel_id=1, source_target_pairs={{0,6},{1,7},{2,0},{3,1},{4,2},{5,3},{6,4},{7,5},{8,14},{9,15},{10,... | collective-permute-start | bytes 700424 | tf_op jit(solution)/shard_map/ppermute | solution.py:407
  17.0 8.0 %collective-permute-done.2.x3_ref = bf16[16,7296]{1,0:T(8,128)(2,1)S(1)} collective-permute-done((bf16[16,7296]{1,0:T(8,128)(2,1)S(1)}, bf16[16,7296]{1,0:T(8,128)(2,1)S(1)}, u32[]{:S(2)}, u32[]{:S(2)}) %collective-permute-start.2) | collective-permute-done | bytes 233504 | tf_op jit(solution)/shard_map/ppermute | solution.py:407
  25.5 3.2 %collective-permute-done.x1_ref = bf16[16,7296]{1,0:T(8,128)(2,1)S(1)} collective-permute-done((bf16[16,7296]{1,0:T(8,128)(2,1)S(1)}, bf16[16,7296]{1,0:T(8,128)(2,1)S(1)}, u32[]{:S(2)}, u32[]{:S(2)}) %collective-permute-start) | collective-permute-done | bytes 233504 | tf_op jit(solution)/shard_map/ppermute | solution.py:407
  28.7 1.8 %send_x.1 = bf16[384,3584]{1,0:T(8,128)(2,1)S(1)} custom-call(s32[2]{0:T(128)S(1)} %pad_add_fusion.place_ref, bf16[16,7296]{1,0:T(8,128)(2,1)S(1)} %pad_maximum_fusion.x0_ref, bf16[16,7296]{1,0:T(8,128)(2,1)S(1)} %collective-permute-done.x1_ref, bf16[16,7296]{1,0:T(8,128)(2,1)S(1)} %collective-permute-done.1.x2_ref, ...), custom_call_target="tpu_custom_call" | custom-call | tf_op jit(solution)/shard_map/send_x/pallas_call | solution.py:435
  30.5 1.5 copy-done
  32.7 6.3 %all-to-all-start.1 = ((bf16[16,24,3584]{2,1,0:T(8,128)(2,1)}), bf16[16,24,3584]{2,1,0:T(8,128)(2,1)}, u32[]{:S(2)}, u32[]{:S(2)}) async-start(bf16[16,24,3584]{2,1,0:T(8,128)(2,1)} %bitcast.18), calls=%async_computation.1 | async-start | bytes 5505024 | tf_op jit(solution)/shard_map/all_to_all | solution.py:417
  39.0 2.6 %regroup.1 = (bf16[48,7168]{1,0:T(8,128)(2,1)S(1)}, bf16[48,7168]{1,0:T(8,128)(2,1)S(1)}, bf16[48,7168]{1,0:T(8,128)(2,1)S(1)}, bf16[640,256]{1,0:T(8,128)(2,1)S(1)}) custom-call(s32[2]{0:T(128)S(1)} %pad_add_fusion.place_ref, bf16[640,1024]{1,0:T(8,128)(2,1)S(1)} %bitcast.16), custom_call_target="tpu_custom_call" | custom-call | tf_op jit(solution)/shard_map/regroup/pallas_call | solution.py:437
  41.7 2.6 %collective-permute-start.4 = (bf16[48,7168]{1,0:T(8,128)(2,1)S(1)}, bf16[48,7168]{1,0:T(8,128)(2,1)S(1)}, u32[]{:S(2)}, u32[]{:S(2)}) collective-permute-start(bf16[48,7168]{1,0:T(8,128)(2,1)S(1)} %get-tuple-element.41), channel_id=1, source_target_pairs={{0,4},{1,5},{2,6},{3,7},{4,0},{5,1},{6,2},{7,3},{8,12},{9,13},{10,... | collective-permute-start | bytes 2064392 | tf_op jit(solution)/shard_map/ppermute | solution.py:407
  45.7 3.1 %copy-done.1 = bf16[1,512,7168]{2,1,0:T(8,128)(2,1)S(1)} copy-done((bf16[1,512,7168]{2,1,0:T(8,128)(2,1)S(1)}, bf16[1,512,7168]{2,1,0:T(8,128)(2,1)}, u32[]{:S(2)}) %copy-start.1) | copy-done | bytes 7340056
  48.8 4.1 %regroup_own.1 = (bf16[48,7168]{1,0:T(8,128)(2,1)S(1)}, bf16[512,7168]{1,0:T(8,128)(2,1)S(1)}) custom-call(s32[2]{0:T(128)S(1)} %pad_add_fusion.place_ref, bf16[640,1024]{1,0:T(8,128)(2,1)S(1)} %bitcast.17, bf16[512,7168]{1,0:T(8,128)(2,1)S(1)} %bitcast.19), custom_call_target="tpu_custom_call" | custom-call | tf_op jit(solution)/shard_map/regroup_own/pallas_call | solution.py:443
  53.0 21.7 %collective-permute-done.3.refs_1_ = bf16[48,7168]{1,0:T(8,128)(2,1)S(1)} collective-permute-done((bf16[48,7168]{1,0:T(8,128)(2,1)S(1)}, bf16[48,7168]{1,0:T(8,128)(2,1)S(1)}, u32[]{:S(2)}, u32[]{:S(2)}) %collective-permute-start.3) | collective-permute-done | bytes 688160 | tf_op jit(solution)/shard_map/ppermute | solution.py:407
  75.4 1.5 collective-permute-done.7.refs_5_
  78.9 3.0 %back.1.mark_ref.back_ref = f32[384,512]{1,0:T(8,128)S(1)} custom-call(bf16[48,7168]{1,0:T(8,128)(2,1)S(1)} %get-tuple-element.39.refs_0_, bf16[48,7168]{1,0:T(8,128)(2,1)S(1)} %collective-permute-done.3.refs_1_, bf16[48,7168]{1,0:T(8,128)(2,1)S(1)} %collective-permute-done.4.refs_2_, bf16[48,7168]{1,0:T(8,128)(2,1)S(1)} %collective-permute-done.5.refs_3_, ...), custom_call_target="tpu_custom_call" | custom-call | tf_op jit(solution)/shard_map/back/pallas_call | solution.py:454
  82.3 8.4 %forward_own.1 = (f32[192,512]{1,0:T(8,128)S(1)}, f32[192,512]{1,0:T(8,128)S(1)}, bf16[7168,512]{1,0:T(8,128)(2,1)S(1)}, bf16[7168,512]{1,0:T(8,128)(2,1)S(1)}) custom-call(bf16[384,3584]{1,0:T(8,128)(2,1)} %bitcast.7.x_ref, bf16[7168,512]{1,0:T(8,128)(2,1)} %bitcast.24, bf16[7168,512]{1,0:T(8,128)(2,1)} %bitcast.25, f32[384,512]{1,0:T(8,128)S(1)} %back.1.mark_ref.back_ref), custom_call_target="tpu_custom_call" | custom-call | tf_op jit(solution)/shard_map/forward_own/pallas_call | solution.py:459
  90.8 4.8 %forward.1 = (bf16[384,512]{1,0:T(8,128)(2,1)S(1)}, bf16[384,512]{1,0:T(8,128)(2,1)S(1)}, bf16[384,128]{1,0:T(8,128)(2,1)S(1)}) custom-call(bf16[384,3584]{1,0:T(8,128)(2,1)S(1)} %collective-permute-done.10.x_ref, bf16[7168,512]{1,0:T(8,128)(2,1)S(1)} %get-tuple-element.46.gate_ref, bf16[7168,512]{1,0:T(8,128)(2,1)S(1)} %get-tuple-element.47.up_ref, ...), custom_call_target="tpu_custom_call" | custom-call | tf_op jit(solution)/shard_map/forward/pallas_call | solution.py:466
  95.6 3.0 %dx.2 = (bf16[192,3712]{1,0:T(8,128)(2,1)S(1)}, bf16[192,3712]{1,0:T(8,128)(2,1)S(1)}) custom-call(bf16[384,512]{1,0:T(8,128)(2,1)S(1)} %get-tuple-element.50.dgate_ref, bf16[384,512]{1,0:T(8,128)(2,1)S(1)} %get-tuple-element.51.dup_ref, bf16[7168,512]{1,0:T(8,128)(2,1)S(1)} %get-tuple-element.46.gate_ref, bf16[7168,512]{1,0:T(8,128)(2,1)S(1)} %get-tuple-element.47.up_ref, ...), custom_call_target="tpu_custom_call" | custom-call | tf_op jit(solution)/shard_map/dx/pallas_call | solution.py:474
  99.1 3.0 %dx.3 = (bf16[192,3584]{1,0:T(8,128)(2,1)S(1)}, bf16[192,3584]{1,0:T(8,128)(2,1)S(1)}) custom-call(bf16[384,512]{1,0:T(8,128)(2,1)S(1)} %get-tuple-element.50.dgate_ref, bf16[384,512]{1,0:T(8,128)(2,1)S(1)} %get-tuple-element.51.dup_ref, bf16[7168,512]{1,0:T(8,128)(2,1)S(1)} %get-tuple-element.46.gate_ref, bf16[7168,512]{1,0:T(8,128)(2,1)S(1)} %get-tuple-element.47.up_ref, ...), custom_call_target="tpu_custom_call" | custom-call | tf_op jit(solution)/shard_map/dx/pallas_call | solution.py:474
  103.2 2.3 %collective-permute-done.15.got_ref = bf16[192,3584]{1,0:T(8,128)(2,1)S(1)} collective-permute-done((bf16[192,3584]{1,0:T(8,128)(2,1)S(1)}, bf16[192,3584]{1,0:T(8,128)(2,1)S(1)}, u32[]{:S(2)}, u32[]{:S(2)}) %collective-permute-start.15) | collective-permute-done | bytes 1376288 | tf_op jit(solution)/shard_map/ppermute | solution.py:411
  105.6 2.2 %add_to_nodes.1 = bf16[384,1792]{1,0:T(8,128)(2,1)} custom-call(bf16[192,3584]{1,0:T(8,128)(2,1)S(1)} %get-tuple-element.59.own_ref, bf16[192,3584]{1,0:T(8,128)(2,1)S(1)} %collective-permute-done.15.got_ref, f32[8,128]{1,0:T(8,128)S(1)} %get-tuple-element.61.mark_ref), custom_call_target="tpu_custom_call" | custom-call | tf_op jit(solution)/shard_map/add_to_nodes/pallas_call | solution.py:492
  107.8 6.9 %all-to-all-start.2 = ((bf16[16,24,1792]{2,1,0:T(8,128)(2,1)}), bf16[16,24,1792]{2,1,0:T(8,128)(2,1)S(1)}, u32[]{:S(2)}, u32[]{:S(2)}) async-start(bf16[16,24,1792]{2,1,0:T(8,128)(2,1)} %bitcast.11), calls=%async_computation.2 | async-start | bytes 2752512 | tf_op jit(solution)/shard_map/all_to_all | solution.py:417
  117.8 8.4 %collective-permute-done.12.p1_ref = bf16[48,3712]{1,0:T(8,128)(2,1)S(1)} collective-permute-done((bf16[48,3712]{1,0:T(8,128)(2,1)}, bf16[48,3712]{1,0:T(8,128)(2,1)S(1)}, u32[]{:S(2)}, u32[]{:S(2)}) %collective-permute-start.12) | collective-permute-done | bytes 356384 | tf_op jit(solution)/shard_map/ppermute | solution.py:407
  126.2 2.5 %collective-permute-done.13.p2_ref = bf16[48,3712]{1,0:T(8,128)(2,1)S(1)} collective-permute-done((bf16[48,3712]{1,0:T(8,128)(2,1)}, bf16[48,3712]{1,0:T(8,128)(2,1)S(1)}, u32[]{:S(2)}, u32[]{:S(2)}) %collective-permute-start.13) | collective-permute-done | bytes 356384 | tf_op jit(solution)/shard_map/ppermute | solution.py:407
  128.7 6.2 %collective-permute-done.14.p3_ref = bf16[48,3712]{1,0:T(8,128)(2,1)S(1)} collective-permute-done((bf16[48,3712]{1,0:T(8,128)(2,1)S(1)}, bf16[48,3712]{1,0:T(8,128)(2,1)S(1)}, u32[]{:S(2)}, u32[]{:S(2)}) %collective-permute-start.14) | collective-permute-done | bytes 356384 | tf_op jit(solution)/shard_map/ppermute | solution.py:407
  134.9 1.6 combine.1
  136.5 6.8 %all-to-all-start.3 = ((bf16[16,40,512]{2,1,0:T(8,128)(2,1)}), bf16[16,40,512]{2,1,0:T(8,128)(2,1)S(1)}, u32[]{:S(2)}, u32[]{:S(2)}) async-start(bf16[16,40,512]{2,1,0:T(8,128)(2,1)} %bitcast.13), calls=%async_computation.3 | async-start | bytes 1310720 | tf_op jit(solution)/shard_map/all_to_all | solution.py:417
  143.3 1.5 combine_near.1
  147.0 4.0 %collective-permute-done.16.b1_ref = bf16[16,3584]{1,0:T(8,128)(2,1)S(1)} collective-permute-done((bf16[16,3584]{1,0:T(8,128)(2,1)S(1)}, bf16[16,3584]{1,0:T(8,128)(2,1)S(1)}, u32[]{:S(2)}, u32[]{:S(2)}) %collective-permute-start.16) | collective-permute-done | bytes 114720 | tf_op jit(solution)/shard_map/ppermute | solution.py:407
  150.9 2.0 %collective-permute-done.17.b2_ref = bf16[16,3584]{1,0:T(8,128)(2,1)S(1)} collective-permute-done((bf16[16,3584]{1,0:T(8,128)(2,1)S(1)}, bf16[16,3584]{1,0:T(8,128)(2,1)S(1)}, u32[]{:S(2)}, u32[]{:S(2)}) %collective-permute-start.17) | collective-permute-done | bytes 114720 | tf_op jit(solution)/shard_map/ppermute | solution.py:407
  153.7 2.6 %all-to-all-done.3 = bf16[16,40,512]{2,1,0:T(8,128)(2,1)S(1)} async-done(((bf16[16,40,512]{2,1,0:T(8,128)(2,1)}), bf16[16,40,512]{2,1,0:T(8,128)(2,1)S(1)}, u32[]{:S(2)}, u32[]{:S(2)}) %all-to-all-start.3) | async-done | bytes 655392 | tf_op jit(solution)/shard_map/all_to_all | solution.py:417
  156.4 2.3 %finish.1 = (bf16[16,7168]{1,0:T(8,128)(2,1)}, f32[8,16]{1,0:T(8,128)}) custom-call(s32[2]{0:T(128)S(1)} %pad_add_fusion.place_ref, s32[8,16]{1,0:T(8,128)S(1)} %bitcast.23, bf16[640,512]{1,0:T(8,128)(2,1)S(1)} %bitcast.21, bf16[16,3584]{1,0:T(8,128)(2,1)S(1)} %get-tuple-element.64.b0_ref, bf16[16,3584]{1,0:T(8,128)(2,1)S(1)} %collective-permute-done.16.b1_ref, ...), custom_call_target="tpu_custom_call" | custom-call | tf_op jit(solution)/shard_map/finish/pallas_call | solution.py:509
  (50 shorter events, 15.3 us)
Async XLA Ops:
  3.8 8.1 %copy-start.2 = (s32[16,8]{0,1:T(8,128)S(1)}, s32[16,8]{0,1:T(8,128)}, u32[]{:S(2)}) copy-start(s32[16,8]{0,1:T(8,128)} %param.9) | copy-start | bytes 1540
  3.8 8.1 %copy-start.6 = (f32[16,8]{0,1:T(8,128)S(1)}, f32[16,8]{0,1:T(8,128)}, u32[]{:S(2)}) copy-start(f32[16,8]{0,1:T(8,128)} %param.10) | copy-start | bytes 1540
  3.8 8.4 %copy-start.5 = (bf16[16,7168]{1,0:T(8,128)(2,1)S(1)}, bf16[16,7168]{1,0:T(8,128)(2,1)}, u32[]{:S(2)}) copy-start(bf16[16,7168]{1,0:T(8,128)(2,1)} %param.7) | copy-start | bytes 688132
  3.8 28.9 %all-to-all-start = ((bf16[16,40,1024]{2,1,0:T(8,128)(2,1)}), bf16[16,40,1024]{2,1,0:T(8,128)(2,1)S(1)}, u32[]{:S(2)}, u32[]{:S(2)}) async-start(bf16[16,40,1024]{2,1,0:T(8,128)(2,1)} %bitcast.26), calls=%async_computation | async-start | bytes 2621440 | tf_op jit(solution)/shard_map/all_to_all | solution.py:417
  12.2 12.8 %collective-permute-start.2 = (bf16[16,7296]{1,0:T(8,128)(2,1)S(1)}, bf16[16,7296]{1,0:T(8,128)(2,1)S(1)}, u32[]{:S(2)}, u32[]{:S(2)}) collective-permute-start(bf16[16,7296]{1,0:T(8,128)(2,1)S(1)} %pad_maximum_fusion.x0_ref), channel_id=1, source_target_pairs={{0,6},{1,7},{2,0},{3,1},{4,2},{5,3},{6,4},{7,5},{8,14},{9,15},{10,... | collective-permute-start | bytes 700424 | tf_op jit(solution)/shard_map/ppermute | solution.py:407
  15.3 10.2 %collective-permute-start.1 = (bf16[16,7296]{1,0:T(8,128)(2,1)S(1)}, bf16[16,7296]{1,0:T(8,128)(2,1)S(1)}, u32[]{:S(2)}, u32[]{:S(2)}) collective-permute-start(bf16[16,7296]{1,0:T(8,128)(2,1)S(1)} %pad_maximum_fusion.x0_ref), channel_id=1, source_target_pairs={{0,4},{1,5},{2,6},{3,7},{4,0},{5,1},{6,2},{7,3},{8,12},{9,13},{10,... | collective-permute-start | bytes 700424 | tf_op jit(solution)/shard_map/ppermute | solution.py:407
  16.0 12.7 %collective-permute-start = (bf16[16,7296]{1,0:T(8,128)(2,1)S(1)}, bf16[16,7296]{1,0:T(8,128)(2,1)S(1)}, u32[]{:S(2)}, u32[]{:S(2)}) collective-permute-start(bf16[16,7296]{1,0:T(8,128)(2,1)S(1)} %pad_maximum_fusion.x0_ref), channel_id=1, source_target_pairs={{0,2},{1,3},{2,4},{3,5},{4,6},{5,7},{6,0},{7,1},{8,10},{9,11},{10,... | collective-permute-start | bytes 700424 | tf_op jit(solution)/shard_map/ppermute | solution.py:407
  30.5 1.5 copy-start
  32.7 49.2 %all-to-all-start.1 = ((bf16[16,24,3584]{2,1,0:T(8,128)(2,1)}), bf16[16,24,3584]{2,1,0:T(8,128)(2,1)}, u32[]{:S(2)}, u32[]{:S(2)}) async-start(bf16[16,24,3584]{2,1,0:T(8,128)(2,1)} %bitcast.18), calls=%async_computation.1 | async-start | bytes 5505024 | tf_op jit(solution)/shard_map/all_to_all | solution.py:417
  41.7 33.1 %collective-permute-start.3 = (bf16[48,7168]{1,0:T(8,128)(2,1)S(1)}, bf16[48,7168]{1,0:T(8,128)(2,1)S(1)}, u32[]{:S(2)}, u32[]{:S(2)}) collective-permute-start(bf16[48,7168]{1,0:T(8,128)(2,1)S(1)} %get-tuple-element.40), channel_id=1, source_target_pairs={{0,2},{1,3},{2,4},{3,5},{4,6},{5,7},{6,0},{7,1},{8,10},{9,11},{10,... | collective-permute-start | bytes 2064392 | tf_op jit(solution)/shard_map/ppermute | solution.py:407
  41.7 33.0 %collective-permute-start.4 = (bf16[48,7168]{1,0:T(8,128)(2,1)S(1)}, bf16[48,7168]{1,0:T(8,128)(2,1)S(1)}, u32[]{:S(2)}, u32[]{:S(2)}) collective-permute-start(bf16[48,7168]{1,0:T(8,128)(2,1)S(1)} %get-tuple-element.41), channel_id=1, source_target_pairs={{0,4},{1,5},{2,6},{3,7},{4,0},{5,1},{6,2},{7,3},{8,12},{9,13},{10,... | collective-permute-start | bytes 2064392 | tf_op jit(solution)/shard_map/ppermute | solution.py:407
  44.4 31.0 %collective-permute-start.5 = (bf16[48,7168]{1,0:T(8,128)(2,1)S(1)}, bf16[48,7168]{1,0:T(8,128)(2,1)S(1)}, u32[]{:S(2)}, u32[]{:S(2)}) collective-permute-start(bf16[48,7168]{1,0:T(8,128)(2,1)S(1)} %get-tuple-element.42), channel_id=1, source_target_pairs={{0,6},{1,7},{2,0},{3,1},{4,2},{5,3},{6,4},{7,5},{8,14},{9,15},{10,... | collective-permute-start | bytes 2064392 | tf_op jit(solution)/shard_map/ppermute | solution.py:407
  45.7 3.1 %copy-start.1 = (bf16[1,512,7168]{2,1,0:T(8,128)(2,1)S(1)}, bf16[1,512,7168]{2,1,0:T(8,128)(2,1)}, u32[]{:S(2)}) copy-start(bf16[1,512,7168]{2,1,0:T(8,128)(2,1)} %param.13) | copy-start | bytes 22020100
  52.9 22.5 %collective-permute-start.6 = (bf16[48,7168]{1,0:T(8,128)(2,1)S(1)}, bf16[48,7168]{1,0:T(8,128)(2,1)S(1)}, u32[]{:S(2)}, u32[]{:S(2)}) collective-permute-start(bf16[48,7168]{1,0:T(8,128)(2,1)S(1)} %get-tuple-element.39.refs_0_), channel_id=1, source_target_pairs={{0,1},{1,0},{2,3},{3,2},{4,5},{5,4},{6,7},{7,6},{8,9},{9,8},{10,11... | collective-permute-start | bytes 2064392 | tf_op jit(solution)/shard_map/ppermute | solution.py:411
  74.8 2.1 %collective-permute-start.7 = (bf16[48,7168]{1,0:T(8,128)(2,1)S(1)}, bf16[48,7168]{1,0:T(8,128)(2,1)S(1)}, u32[]{:S(2)}, u32[]{:S(2)}) collective-permute-start(bf16[48,7168]{1,0:T(8,128)(2,1)S(1)} %collective-permute-done.3.refs_1_), channel_id=1, source_target_pairs={{0,1},{1,0},{2,3},{3,2},{4,5},{5,4},{6,7},{7,6},{8,9},{9,8},{10,11... | collective-permute-start | bytes 2064392 | tf_op jit(solution)/shard_map/ppermute | solution.py:411
  74.8 3.1 %collective-permute-start.8 = (bf16[48,7168]{1,0:T(8,128)(2,1)S(1)}, bf16[48,7168]{1,0:T(8,128)(2,1)S(1)}, u32[]{:S(2)}, u32[]{:S(2)}) collective-permute-start(bf16[48,7168]{1,0:T(8,128)(2,1)S(1)} %collective-permute-done.4.refs_2_), channel_id=1, source_target_pairs={{0,1},{1,0},{2,3},{3,2},{4,5},{5,4},{6,7},{7,6},{8,9},{9,8},{10,11... | collective-permute-start | bytes 2064392 | tf_op jit(solution)/shard_map/ppermute | solution.py:411
  75.4 3.5 %collective-permute-start.9 = (bf16[48,7168]{1,0:T(8,128)(2,1)S(1)}, bf16[48,7168]{1,0:T(8,128)(2,1)S(1)}, u32[]{:S(2)}, u32[]{:S(2)}) collective-permute-start(bf16[48,7168]{1,0:T(8,128)(2,1)S(1)} %collective-permute-done.5.refs_3_), channel_id=1, source_target_pairs={{0,1},{1,0},{2,3},{3,2},{4,5},{5,4},{6,7},{7,6},{8,9},{9,8},{10,11... | collective-permute-start | bytes 2064392 | tf_op jit(solution)/shard_map/ppermute | solution.py:411
  81.9 8.8 %collective-permute-start.10 = (bf16[384,3584]{1,0:T(8,128)(2,1)}, bf16[384,3584]{1,0:T(8,128)(2,1)S(1)}, u32[]{:S(2)}, u32[]{:S(2)}) collective-permute-start(bf16[384,3584]{1,0:T(8,128)(2,1)} %bitcast.7.x_ref), channel_id=1, source_target_pairs={{0,1},{1,0},{2,3},{3,2},{4,5},{5,4},{6,7},{7,6},{8,9},{9,8},{10,11... | collective-permute-start | bytes 8257544 | tf_op jit(solution)/shard_map/ppermute | solution.py:411
  98.6 3.9 %collective-permute-start.11 = (bf16[192,3712]{1,0:T(8,128)(2,1)S(1)}, bf16[192,3712]{1,0:T(8,128)(2,1)S(1)}, u32[]{:S(2)}, u32[]{:S(2)}) collective-permute-start(bf16[192,3712]{1,0:T(8,128)(2,1)S(1)} %get-tuple-element.54), channel_id=1, source_target_pairs={{0,1},{1,0},{2,3},{3,2},{4,5},{5,4},{6,7},{7,6},{8,9},{9,8},{10,11... | collective-permute-start | bytes 4276232 | tf_op jit(solution)/shard_map/ppermute | solution.py:411
  102.1 3.4 %collective-permute-start.15 = (bf16[192,3584]{1,0:T(8,128)(2,1)S(1)}, bf16[192,3584]{1,0:T(8,128)(2,1)S(1)}, u32[]{:S(2)}, u32[]{:S(2)}) collective-permute-start(bf16[192,3584]{1,0:T(8,128)(2,1)S(1)} %get-tuple-element.60), channel_id=1, source_target_pairs={{0,1},{1,0},{2,3},{3,2},{4,5},{5,4},{6,7},{7,6},{8,9},{9,8},{10,11... | collective-permute-start | bytes 4128776 | tf_op jit(solution)/shard_map/ppermute | solution.py:411
  103.2 4.5 %copy-start.3 = (bf16[48,3712]{1,0:T(8,128)(2,1)}, bf16[48,3712]{1,0:T(8,128)(2,1)S(1)}, u32[]{:S(2)}) copy-start(bf16[48,3712]{1,0:T(8,128)(2,1)S(1)} %get-tuple-element.57) | copy-start | bytes 1069060
  103.2 4.5 %copy-start.4 = (bf16[48,3712]{1,0:T(8,128)(2,1)}, bf16[48,3712]{1,0:T(8,128)(2,1)S(1)}, u32[]{:S(2)}) copy-start(bf16[48,3712]{1,0:T(8,128)(2,1)S(1)} %get-tuple-element.56) | copy-start | bytes 1069060
  107.8 28.8 %all-to-all-start.2 = ((bf16[16,24,1792]{2,1,0:T(8,128)(2,1)}), bf16[16,24,1792]{2,1,0:T(8,128)(2,1)S(1)}, u32[]{:S(2)}, u32[]{:S(2)}) async-start(bf16[16,24,1792]{2,1,0:T(8,128)(2,1)} %bitcast.11), calls=%async_computation.2 | async-start | bytes 2752512 | tf_op jit(solution)/shard_map/all_to_all | solution.py:417
  114.7 11.5 %collective-permute-start.12 = (bf16[48,3712]{1,0:T(8,128)(2,1)}, bf16[48,3712]{1,0:T(8,128)(2,1)S(1)}, u32[]{:S(2)}, u32[]{:S(2)}) collective-permute-start(bf16[48,3712]{1,0:T(8,128)(2,1)} %copy-done.4), channel_id=1, source_target_pairs={{0,6},{1,7},{2,0},{3,1},{4,2},{5,3},{6,4},{7,5},{8,14},{9,15},{10,... | collective-permute-start | bytes 1069064 | tf_op jit(solution)/shard_map/ppermute | solution.py:407
  115.7 13.0 %collective-permute-start.13 = (bf16[48,3712]{1,0:T(8,128)(2,1)}, bf16[48,3712]{1,0:T(8,128)(2,1)S(1)}, u32[]{:S(2)}, u32[]{:S(2)}) collective-permute-start(bf16[48,3712]{1,0:T(8,128)(2,1)} %copy-done.3), channel_id=1, source_target_pairs={{0,4},{1,5},{2,6},{3,7},{4,0},{5,1},{6,2},{7,3},{8,12},{9,13},{10,... | collective-permute-start | bytes 1069064 | tf_op jit(solution)/shard_map/ppermute | solution.py:407
  115.7 19.1 %collective-permute-start.14 = (bf16[48,3712]{1,0:T(8,128)(2,1)S(1)}, bf16[48,3712]{1,0:T(8,128)(2,1)S(1)}, u32[]{:S(2)}, u32[]{:S(2)}) collective-permute-start(bf16[48,3712]{1,0:T(8,128)(2,1)S(1)} %get-tuple-element.58), channel_id=1, source_target_pairs={{0,2},{1,3},{2,4},{3,5},{4,6},{5,7},{6,0},{7,1},{8,10},{9,11},{10,... | collective-permute-start | bytes 1069064 | tf_op jit(solution)/shard_map/ppermute | solution.py:407
  136.5 19.8 %all-to-all-start.3 = ((bf16[16,40,512]{2,1,0:T(8,128)(2,1)}), bf16[16,40,512]{2,1,0:T(8,128)(2,1)S(1)}, u32[]{:S(2)}, u32[]{:S(2)}) async-start(bf16[16,40,512]{2,1,0:T(8,128)(2,1)} %bitcast.13), calls=%async_computation.3 | async-start | bytes 1310720 | tf_op jit(solution)/shard_map/all_to_all | solution.py:417
  144.9 6.1 %collective-permute-start.16 = (bf16[16,3584]{1,0:T(8,128)(2,1)S(1)}, bf16[16,3584]{1,0:T(8,128)(2,1)S(1)}, u32[]{:S(2)}, u32[]{:S(2)}) collective-permute-start(bf16[16,3584]{1,0:T(8,128)(2,1)S(1)} %get-tuple-element.65), channel_id=1, source_target_pairs={{0,6},{1,7},{2,0},{3,1},{4,2},{5,3},{6,4},{7,5},{8,14},{9,15},{10,... | collective-permute-start | bytes 344072 | tf_op jit(solution)/shard_map/ppermute | solution.py:407
  145.6 7.4 %collective-permute-start.17 = (bf16[16,3584]{1,0:T(8,128)(2,1)S(1)}, bf16[16,3584]{1,0:T(8,128)(2,1)S(1)}, u32[]{:S(2)}, u32[]{:S(2)}) collective-permute-start(bf16[16,3584]{1,0:T(8,128)(2,1)S(1)} %get-tuple-element.66), channel_id=1, source_target_pairs={{0,4},{1,5},{2,6},{3,7},{4,0},{5,1},{6,2},{7,3},{8,12},{9,13},{10,... | collective-permute-start | bytes 344072 | tf_op jit(solution)/shard_map/ppermute | solution.py:407
  145.9 7.9 %collective-permute-start.18 = (bf16[16,3584]{1,0:T(8,128)(2,1)S(1)}, bf16[16,3584]{1,0:T(8,128)(2,1)S(1)}, u32[]{:S(2)}, u32[]{:S(2)}) collective-permute-start(bf16[16,3584]{1,0:T(8,128)(2,1)S(1)} %get-tuple-element.67), channel_id=1, source_target_pairs={{0,2},{1,3},{2,4},{3,5},{4,6},{5,7},{6,0},{7,1},{8,10},{9,11},{10,... | collective-permute-start | bytes 344072 | tf_op jit(solution)/shard_map/ppermute | solution.py:407

commit v6 on v5

--- a/solution.py
+++ b/solution.py
@@ -390,7 +390,7 @@
     return jax.ShapeDtypeStruct(shape, dtype)
 
 
-def whole(kernel, out_shape, in_specs, name, scratch=()):
+def whole(kernel, out_shape, in_specs, name, scratch=(), cost=None):
     multi = isinstance(out_shape, (list, tuple))
     return pl.pallas_call(
         kernel,
@@ -399,6 +399,7 @@
         out_specs=[VM] * len(out_shape) if multi else VM,
         scratch_shapes=list(scratch),
         compiler_params=pltpu.CompilerParams(vmem_limit_bytes=VMEM_LIMITS.get(name, 14) * MIB),
+        cost_estimate=cost,
         name=name,
     )
 
@@ -499,6 +500,7 @@
         [VM] * 5,
         "combine",
         [pltpu.VMEM((ROWS_N, 512), F32)],
+        pl.CostEstimate(flops=20_000_000_000, bytes_accessed=70_000_000, transcendentals=0),
     )(table, *pieces)
     mixed, back_b = lax.optimization_barrier((mixed, back_b))
     back_a = node_exchange(mixed)

time: 159 us -> 156 us (0.981)
  waiting for transfers between devices: 66.6 us -> 61.4 us
    ppermute x12, waiting for transfers between devices: 57.4 us -> 47.1 us  [shift_y(): return lax.ppermute(v, 'local', [(i, (i + 2 * s) % 8) for i in range(8)])]
    all_to_all x4, waiting for transfers between devices: 3.38 us -> 10.8 us  [node_exchange(): lax.all_to_all(v, 'node', split_axis=0, concat_axis=0, tiled=True)]
    all_to_all x4, starting transfers between devices: 28.1 us -> 24.9 us  [node_exchange(): lax.all_to_all(v, 'node', split_axis=0, concat_axis=0, tiled=True)]
    ppermute x12, starting transfers between devices: 12.9 us -> 16.1 us  [shift_y(): return lax.ppermute(v, 'local', [(i, (i + 2 * s) % 8) for i in range(8)])]
    ppermute x7, waiting for transfers between devices: 5.81 us -> 3.5 us  [swap_core(): return lax.ppermute(v, 'local', [(i, i ^ 1) for i in range(8)])]
    unnamed x14 -> x12, local copies, waits for them, and re-layouts: 4.62 us -> 5.45 us
  transfers between devices with their start and end apart: 23 -> 23, of which waited for: 18 -> 14; matrix products, arithmetic and copies ran while one was open for 0% -> 0% of each run, Pallas kernels for 18% -> 20%
where the time goes in v6:
time: 156 us; the launch traced here: 155 us
  waiting for transfers between devices  61.4 us (39%)
  Pallas kernels  44.2 us (28%)
  starting transfers between devices  42.9 us (28%)
  local copies, waits for them, and re-layouts  5.61 us (4%)
    ppermute x12, waiting for transfers between devices, shift_y(): return lax.ppermute(v, 'local', [(i, (i + 2 * s) % 8) for i in range(8)])  47.1 us
    all_to_all x4, starting transfers between devices, node_exchange(): lax.all_to_all(v, 'node', split_axis=0, concat_axis=0, tiled=True)  24.9 us
    ppermute x12, starting transfers between devices, shift_y(): return lax.ppermute(v, 'local', [(i, (i + 2 * s) % 8) for i in range(8)])  16.1 us
    all_to_all x4, waiting for transfers between devices, node_exchange(): lax.all_to_all(v, 'node', split_axis=0, concat_axis=0, tiled=True)  10.8 us
    pallas_call x1, Pallas kernels, on_device(): whole(forward_own_kernel, [sds((SLOTS, HALF), F32)] * 2 + [sds((WIDTH, HA...  8.42 us
    pallas_call x2, Pallas kernels, dx(): whole(functools.partial(dx_kernel, part), [sds((SLOTS, width))] * 2, [VM]...  6.08 us
    unnamed x12, local copies, waits for them, and re-layouts  5.45 us
    pallas_call x1, Pallas kernels, on_device(): whole(forward_kernel, [sds((2 * SLOTS, HALF)), sds((2 * SLOTS, HALF)), sd...  4.81 us
  transfers between devices with their start and end apart: 23, of which 14 were waited for; matrix products, arithmetic and copies ran while one was open for 0% of the time, Pallas kernels for 20%

profile of v6, /device:TPU:0, one launch (start us, length us, event | category | flops | bytes accessed | tf_op | source)
XLA Modules:
  0.0 155.2 jit_solution(9126354269627686493)
XLA Ops:
  0.6 3.2 %send_dy.1 = bf16[640,1024]{1,0:T(8,128)(2,1)} custom-call(s32[8,16]{1,0:T(8,128)} %bitcast.23, f32[8,16]{1,0:T(8,128)} %bitcast.28, bf16[16,7168]{1,0:T(8,128)(2,1)} %dy_ref.1), custom_call_target="tpu_custom_call" | custom-call | tf_op jit(solution)/shard_map/send_dy/pallas_call | solution.py:427
  3.8 8.1 %all-to-all-start = ((bf16[16,40,1024]{2,1,0:T(8,128)(2,1)}), bf16[16,40,1024]{2,1,0:T(8,128)(2,1)S(1)}, u32[]{:S(2)}, u32[]{:S(2)}) async-start(bf16[16,40,1024]{2,1,0:T(8,128)(2,1)} %bitcast.27), calls=%async_computation | async-start | bytes 2621440 | tf_op jit(solution)/shard_map/all_to_all | solution.py:418
  12.2 3.1 %collective-permute-start.2 = (bf16[16,7296]{1,0:T(8,128)(2,1)S(1)}, bf16[16,7296]{1,0:T(8,128)(2,1)S(1)}, u32[]{:S(2)}, u32[]{:S(2)}) collective-permute-start(bf16[16,7296]{1,0:T(8,128)(2,1)S(1)} %pad_maximum_fusion.x0_ref), channel_id=1, source_target_pairs={{0,6},{1,7},{2,0},{3,1},{4,2},{5,3},{6,4},{7,5},{8,14},{9,15},{10,... | collective-permute-start | bytes 700424 | tf_op jit(solution)/shard_map/ppermute | solution.py:408
  17.0 8.0 %collective-permute-done.2.x3_ref = bf16[16,7296]{1,0:T(8,128)(2,1)S(1)} collective-permute-done((bf16[16,7296]{1,0:T(8,128)(2,1)S(1)}, bf16[16,7296]{1,0:T(8,128)(2,1)S(1)}, u32[]{:S(2)}, u32[]{:S(2)}) %collective-permute-start.2) | collective-permute-done | bytes 233504 | tf_op jit(solution)/shard_map/ppermute | solution.py:408
  25.5 3.2 %collective-permute-done.x1_ref = bf16[16,7296]{1,0:T(8,128)(2,1)S(1)} collective-permute-done((bf16[16,7296]{1,0:T(8,128)(2,1)S(1)}, bf16[16,7296]{1,0:T(8,128)(2,1)S(1)}, u32[]{:S(2)}, u32[]{:S(2)}) %collective-permute-start) | collective-permute-done | bytes 233504 | tf_op jit(solution)/shard_map/ppermute | solution.py:408
  28.7 1.8 %send_x.1 = bf16[384,3584]{1,0:T(8,128)(2,1)S(1)} custom-call(s32[2]{0:T(128)S(1)} %pad_add_fusion.place_ref, bf16[16,7296]{1,0:T(8,128)(2,1)S(1)} %pad_maximum_fusion.x0_ref, bf16[16,7296]{1,0:T(8,128)(2,1)S(1)} %collective-permute-done.x1_ref, bf16[16,7296]{1,0:T(8,128)(2,1)S(1)} %collective-permute-done.1.x2_ref, ...), custom_call_target="tpu_custom_call" | custom-call | tf_op jit(solution)/shard_map/send_x/pallas_call | solution.py:436
  30.5 1.5 copy-done
  32.7 6.3 %all-to-all-start.1 = ((bf16[16,24,3584]{2,1,0:T(8,128)(2,1)}), bf16[16,24,3584]{2,1,0:T(8,128)(2,1)}, u32[]{:S(2)}, u32[]{:S(2)}) async-start(bf16[16,24,3584]{2,1,0:T(8,128)(2,1)} %bitcast.18), calls=%async_computation.1 | async-start | bytes 5505024 | tf_op jit(solution)/shard_map/all_to_all | solution.py:418
  39.0 2.6 %regroup.1 = (bf16[48,7168]{1,0:T(8,128)(2,1)S(1)}, bf16[48,7168]{1,0:T(8,128)(2,1)S(1)}, bf16[48,7168]{1,0:T(8,128)(2,1)S(1)}, bf16[640,256]{1,0:T(8,128)(2,1)S(1)}) custom-call(s32[2]{0:T(128)S(1)} %pad_add_fusion.place_ref, bf16[640,1024]{1,0:T(8,128)(2,1)S(1)} %bitcast.16), custom_call_target="tpu_custom_call" | custom-call | tf_op jit(solution)/shard_map/regroup/pallas_call | solution.py:438
  41.7 2.6 %collective-permute-start.4 = (bf16[48,7168]{1,0:T(8,128)(2,1)S(1)}, bf16[48,7168]{1,0:T(8,128)(2,1)S(1)}, u32[]{:S(2)}, u32[]{:S(2)}) collective-permute-start(bf16[48,7168]{1,0:T(8,128)(2,1)S(1)} %get-tuple-element.41), channel_id=1, source_target_pairs={{0,4},{1,5},{2,6},{3,7},{4,0},{5,1},{6,2},{7,3},{8,12},{9,13},{10,... | collective-permute-start | bytes 2064392 | tf_op jit(solution)/shard_map/ppermute | solution.py:408
  44.4 1.3 collective-permute-start.5
  45.7 3.1 %copy-done.1 = bf16[1,512,7168]{2,1,0:T(8,128)(2,1)S(1)} copy-done((bf16[1,512,7168]{2,1,0:T(8,128)(2,1)S(1)}, bf16[1,512,7168]{2,1,0:T(8,128)(2,1)}, u32[]{:S(2)}) %copy-start.1) | copy-done | bytes 7340056
  48.8 4.1 %regroup_own.1 = (bf16[48,7168]{1,0:T(8,128)(2,1)S(1)}, bf16[512,7168]{1,0:T(8,128)(2,1)S(1)}) custom-call(s32[2]{0:T(128)S(1)} %pad_add_fusion.place_ref, bf16[640,1024]{1,0:T(8,128)(2,1)S(1)} %bitcast.17, bf16[512,7168]{1,0:T(8,128)(2,1)S(1)} %bitcast.19), custom_call_target="tpu_custom_call" | custom-call | tf_op jit(solution)/shard_map/regroup_own/pallas_call | solution.py:444
  53.0 21.8 %collective-permute-done.3.refs_1_ = bf16[48,7168]{1,0:T(8,128)(2,1)S(1)} collective-permute-done((bf16[48,7168]{1,0:T(8,128)(2,1)S(1)}, bf16[48,7168]{1,0:T(8,128)(2,1)S(1)}, u32[]{:S(2)}, u32[]{:S(2)}) %collective-permute-start.3) | collective-permute-done | bytes 688160 | tf_op jit(solution)/shard_map/ppermute | solution.py:408
  75.4 1.5 collective-permute-done.7.refs_5_
  78.9 3.0 %back.1.mark_ref.back_ref = f32[384,512]{1,0:T(8,128)S(1)} custom-call(bf16[48,7168]{1,0:T(8,128)(2,1)S(1)} %get-tuple-element.39.refs_0_, bf16[48,7168]{1,0:T(8,128)(2,1)S(1)} %collective-permute-done.3.refs_1_, bf16[48,7168]{1,0:T(8,128)(2,1)S(1)} %collective-permute-done.4.refs_2_, bf16[48,7168]{1,0:T(8,128)(2,1)S(1)} %collective-permute-done.5.refs_3_, ...), custom_call_target="tpu_custom_call" | custom-call | tf_op jit(solution)/shard_map/back/pallas_call | solution.py:455
  82.3 8.4 %forward_own.1 = (f32[192,512]{1,0:T(8,128)S(1)}, f32[192,512]{1,0:T(8,128)S(1)}, bf16[7168,512]{1,0:T(8,128)(2,1)S(1)}, bf16[7168,512]{1,0:T(8,128)(2,1)S(1)}) custom-call(bf16[384,3584]{1,0:T(8,128)(2,1)} %bitcast.7.x_ref, bf16[7168,512]{1,0:T(8,128)(2,1)} %bitcast.25, bf16[7168,512]{1,0:T(8,128)(2,1)} %bitcast.26, f32[384,512]{1,0:T(8,128)S(1)} %back.1.mark_ref.back_ref), custom_call_target="tpu_custom_call" | custom-call | tf_op jit(solution)/shard_map/forward_own/pallas_call | solution.py:460
  90.8 4.8 %forward.1 = (bf16[384,512]{1,0:T(8,128)(2,1)S(1)}, bf16[384,512]{1,0:T(8,128)(2,1)S(1)}, bf16[384,128]{1,0:T(8,128)(2,1)S(1)}) custom-call(bf16[384,3584]{1,0:T(8,128)(2,1)S(1)} %collective-permute-done.10.x_ref, bf16[7168,512]{1,0:T(8,128)(2,1)S(1)} %get-tuple-element.46.gate_ref, bf16[7168,512]{1,0:T(8,128)(2,1)S(1)} %get-tuple-element.47.up_ref, ...), custom_call_target="tpu_custom_call" | custom-call | tf_op jit(solution)/shard_map/forward/pallas_call | solution.py:467
  95.6 3.0 %dx.2 = (bf16[192,3712]{1,0:T(8,128)(2,1)S(1)}, bf16[192,3712]{1,0:T(8,128)(2,1)S(1)}) custom-call(bf16[384,512]{1,0:T(8,128)(2,1)S(1)} %get-tuple-element.50.dgate_ref, bf16[384,512]{1,0:T(8,128)(2,1)S(1)} %get-tuple-element.51.dup_ref, bf16[7168,512]{1,0:T(8,128)(2,1)S(1)} %get-tuple-element.46.gate_ref, bf16[7168,512]{1,0:T(8,128)(2,1)S(1)} %get-tuple-element.47.up_ref, ...), custom_call_target="tpu_custom_call" | custom-call | tf_op jit(solution)/shard_map/dx/pallas_call | solution.py:475
  99.1 3.0 %dx.3 = (bf16[192,3584]{1,0:T(8,128)(2,1)S(1)}, bf16[192,3584]{1,0:T(8,128)(2,1)S(1)}) custom-call(bf16[384,512]{1,0:T(8,128)(2,1)S(1)} %get-tuple-element.50.dgate_ref, bf16[384,512]{1,0:T(8,128)(2,1)S(1)} %get-tuple-element.51.dup_ref, bf16[7168,512]{1,0:T(8,128)(2,1)S(1)} %get-tuple-element.46.gate_ref, bf16[7168,512]{1,0:T(8,128)(2,1)S(1)} %get-tuple-element.47.up_ref, ...), custom_call_target="tpu_custom_call" | custom-call | tf_op jit(solution)/shard_map/dx/pallas_call | solution.py:475
  106.9 2.2 %add_to_nodes.1 = bf16[384,1792]{1,0:T(8,128)(2,1)} custom-call(bf16[192,3584]{1,0:T(8,128)(2,1)S(1)} %get-tuple-element.59.own_ref, bf16[192,3584]{1,0:T(8,128)(2,1)S(1)} %collective-permute-done.15.got_ref, f32[8,128]{1,0:T(8,128)S(1)} %get-tuple-element.61.mark_ref), custom_call_target="tpu_custom_call" | custom-call | tf_op jit(solution)/shard_map/add_to_nodes/pallas_call | solution.py:493
  109.1 6.9 %all-to-all-start.2 = ((bf16[16,24,1792]{2,1,0:T(8,128)(2,1)}), bf16[16,24,1792]{2,1,0:T(8,128)(2,1)S(1)}, u32[]{:S(2)}, u32[]{:S(2)}) async-start(bf16[16,24,1792]{2,1,0:T(8,128)(2,1)} %bitcast.11), calls=%async_computation.2 | async-start | bytes 2752512 | tf_op jit(solution)/shard_map/all_to_all | solution.py:418
  116.0 1.9 %collective-permute-done.13.p2_ref = bf16[48,3712]{1,0:T(8,128)(2,1)} collective-permute-done((bf16[48,3712]{1,0:T(8,128)(2,1)}, bf16[48,3712]{1,0:T(8,128)(2,1)}, u32[]{:S(2)}, u32[]{:S(2)}) %collective-permute-start.13) | collective-permute-done | bytes 356384 | tf_op jit(solution)/shard_map/ppermute | solution.py:408
  117.9 6.7 %collective-permute-done.14.p3_ref = bf16[48,3712]{1,0:T(8,128)(2,1)} collective-permute-done((bf16[48,3712]{1,0:T(8,128)(2,1)S(1)}, bf16[48,3712]{1,0:T(8,128)(2,1)}, u32[]{:S(2)}, u32[]{:S(2)}) %collective-permute-start.14) | collective-permute-done | bytes 356384 | tf_op jit(solution)/shard_map/ppermute | solution.py:408
  124.6 1.9 %combine.1 = bf16[640,512]{1,0:T(8,128)(2,1)S(1)} custom-call(f32[128,128]{1,0:T(8,128)S(1)} %table.1.table_ref, bf16[48,3712]{1,0:T(8,128)(2,1)S(1)} %get-tuple-element.55.p0_ref, bf16[48,3712]{1,0:T(8,128)(2,1)} %collective-permute-done.12.p1_ref, bf16[48,3712]{1,0:T(8,128)(2,1)} %collective-permute-done.13.p2_ref, ...), custom_call_target="tpu_custom_call" | custom-call | flops 20000000000 | bytes 70000000 | tf_op jit(solution)/shard_map/combine/pallas_call | solution.py:497
  127.3 10.1 %all-to-all-done.2 = bf16[16,24,1792]{2,1,0:T(8,128)(2,1)S(1)} async-done(((bf16[16,24,1792]{2,1,0:T(8,128)(2,1)}), bf16[16,24,1792]{2,1,0:T(8,128)(2,1)S(1)}, u32[]{:S(2)}, u32[]{:S(2)}) %all-to-all-start.2) | async-done | bytes 1376288 | tf_op jit(solution)/shard_map/all_to_all | solution.py:418
  137.5 3.6 %all-to-all-start.3 = ((bf16[16,40,512]{2,1,0:T(8,128)(2,1)}), bf16[16,40,512]{2,1,0:T(8,128)(2,1)S(1)}, u32[]{:S(2)}, u32[]{:S(2)}) async-start(bf16[16,40,512]{2,1,0:T(8,128)(2,1)} %bitcast.22), calls=%async_computation.3 | async-start | bytes 1310720 | tf_op jit(solution)/shard_map/all_to_all | solution.py:418
  141.1 1.5 combine_near.1
  142.6 2.7 %collective-permute-start.16 = (bf16[16,3584]{1,0:T(8,128)(2,1)S(1)}, bf16[16,3584]{1,0:T(8,128)(2,1)S(1)}, u32[]{:S(2)}, u32[]{:S(2)}) collective-permute-start(bf16[16,3584]{1,0:T(8,128)(2,1)S(1)} %get-tuple-element.65), channel_id=1, source_target_pairs={{0,6},{1,7},{2,0},{3,1},{4,2},{5,3},{6,4},{7,5},{8,14},{9,15},{10,... | collective-permute-start | bytes 344072 | tf_op jit(solution)/shard_map/ppermute | solution.py:408
  145.3 1.6 %collective-permute-start.17 = (bf16[16,3584]{1,0:T(8,128)(2,1)S(1)}, bf16[16,3584]{1,0:T(8,128)(2,1)S(1)}, u32[]{:S(2)}, u32[]{:S(2)}) collective-permute-start(bf16[16,3584]{1,0:T(8,128)(2,1)S(1)} %get-tuple-element.66), channel_id=1, source_target_pairs={{0,4},{1,5},{2,6},{3,7},{4,0},{5,1},{6,2},{7,3},{8,12},{9,13},{10,... | collective-permute-start | bytes 344072 | tf_op jit(solution)/shard_map/ppermute | solution.py:408
  147.9 3.7 %collective-permute-done.17.b2_ref = bf16[16,3584]{1,0:T(8,128)(2,1)S(1)} collective-permute-done((bf16[16,3584]{1,0:T(8,128)(2,1)S(1)}, bf16[16,3584]{1,0:T(8,128)(2,1)S(1)}, u32[]{:S(2)}, u32[]{:S(2)}) %collective-permute-start.17) | collective-permute-done | bytes 114720 | tf_op jit(solution)/shard_map/ppermute | solution.py:408
  152.9 2.3 %finish.1 = (bf16[16,7168]{1,0:T(8,128)(2,1)}, f32[8,16]{1,0:T(8,128)}) custom-call(s32[2]{0:T(128)S(1)} %pad_add_fusion.place_ref, s32[8,16]{1,0:T(8,128)S(1)} %bitcast.24, bf16[640,512]{1,0:T(8,128)(2,1)S(1)} %bitcast.21, bf16[16,3584]{1,0:T(8,128)(2,1)S(1)} %get-tuple-element.64.b0_ref, bf16[16,3584]{1,0:T(8,128)(2,1)S(1)} %collective-permute-done.16.b1_ref, ...), custom_call_target="tpu_custom_call" | custom-call | tf_op jit(solution)/shard_map/finish/pallas_call | solution.py:511
  (48 shorter events, 14.6 us)
Async XLA Ops:
  3.8 8.1 %copy-start.3 = (s32[16,8]{0,1:T(8,128)S(1)}, s32[16,8]{0,1:T(8,128)}, u32[]{:S(2)}) copy-start(s32[16,8]{0,1:T(8,128)} %param.9) | copy-start | bytes 1540
  3.8 8.1 %copy-start.5 = (f32[16,8]{0,1:T(8,128)S(1)}, f32[16,8]{0,1:T(8,128)}, u32[]{:S(2)}) copy-start(f32[16,8]{0,1:T(8,128)} %param.10) | copy-start | bytes 1540
  3.8 8.4 %copy-start.4 = (bf16[16,7168]{1,0:T(8,128)(2,1)S(1)}, bf16[16,7168]{1,0:T(8,128)(2,1)}, u32[]{:S(2)}) copy-start(bf16[16,7168]{1,0:T(8,128)(2,1)} %param.7) | copy-start | bytes 688132
  3.8 28.9 %all-to-all-start = ((bf16[16,40,1024]{2,1,0:T(8,128)(2,1)}), bf16[16,40,1024]{2,1,0:T(8,128)(2,1)S(1)}, u32[]{:S(2)}, u32[]{:S(2)}) async-start(bf16[16,40,1024]{2,1,0:T(8,128)(2,1)} %bitcast.27), calls=%async_computation | async-start | bytes 2621440 | tf_op jit(solution)/shard_map/all_to_all | solution.py:418
  12.2 12.8 %collective-permute-start.2 = (bf16[16,7296]{1,0:T(8,128)(2,1)S(1)}, bf16[16,7296]{1,0:T(8,128)(2,1)S(1)}, u32[]{:S(2)}, u32[]{:S(2)}) collective-permute-start(bf16[16,7296]{1,0:T(8,128)(2,1)S(1)} %pad_maximum_fusion.x0_ref), channel_id=1, source_target_pairs={{0,6},{1,7},{2,0},{3,1},{4,2},{5,3},{6,4},{7,5},{8,14},{9,15},{10,... | collective-permute-start | bytes 700424 | tf_op jit(solution)/shard_map/ppermute | solution.py:408
  15.3 10.2 %collective-permute-start.1 = (bf16[16,7296]{1,0:T(8,128)(2,1)S(1)}, bf16[16,7296]{1,0:T(8,128)(2,1)S(1)}, u32[]{:S(2)}, u32[]{:S(2)}) collective-permute-start(bf16[16,7296]{1,0:T(8,128)(2,1)S(1)} %pad_maximum_fusion.x0_ref), channel_id=1, source_target_pairs={{0,4},{1,5},{2,6},{3,7},{4,0},{5,1},{6,2},{7,3},{8,12},{9,13},{10,... | collective-permute-start | bytes 700424 | tf_op jit(solution)/shard_map/ppermute | solution.py:408
  16.0 12.7 %collective-permute-start = (bf16[16,7296]{1,0:T(8,128)(2,1)S(1)}, bf16[16,7296]{1,0:T(8,128)(2,1)S(1)}, u32[]{:S(2)}, u32[]{:S(2)}) collective-permute-start(bf16[16,7296]{1,0:T(8,128)(2,1)S(1)} %pad_maximum_fusion.x0_ref), channel_id=1, source_target_pairs={{0,2},{1,3},{2,4},{3,5},{4,6},{5,7},{6,0},{7,1},{8,10},{9,11},{10,... | collective-permute-start | bytes 700424 | tf_op jit(solution)/shard_map/ppermute | solution.py:408
  30.5 1.5 copy-start
  32.7 49.2 %all-to-all-start.1 = ((bf16[16,24,3584]{2,1,0:T(8,128)(2,1)}), bf16[16,24,3584]{2,1,0:T(8,128)(2,1)}, u32[]{:S(2)}, u32[]{:S(2)}) async-start(bf16[16,24,3584]{2,1,0:T(8,128)(2,1)} %bitcast.18), calls=%async_computation.1 | async-start | bytes 5505024 | tf_op jit(solution)/shard_map/all_to_all | solution.py:418
  41.7 33.1 %collective-permute-start.3 = (bf16[48,7168]{1,0:T(8,128)(2,1)S(1)}, bf16[48,7168]{1,0:T(8,128)(2,1)S(1)}, u32[]{:S(2)}, u32[]{:S(2)}) collective-permute-start(bf16[48,7168]{1,0:T(8,128)(2,1)S(1)} %get-tuple-element.40), channel_id=1, source_target_pairs={{0,2},{1,3},{2,4},{3,5},{4,6},{5,7},{6,0},{7,1},{8,10},{9,11},{10,... | collective-permute-start | bytes 2064392 | tf_op jit(solution)/shard_map/ppermute | solution.py:408
  41.7 33.0 %collective-permute-start.4 = (bf16[48,7168]{1,0:T(8,128)(2,1)S(1)}, bf16[48,7168]{1,0:T(8,128)(2,1)S(1)}, u32[]{:S(2)}, u32[]{:S(2)}) collective-permute-start(bf16[48,7168]{1,0:T(8,128)(2,1)S(1)} %get-tuple-element.41), channel_id=1, source_target_pairs={{0,4},{1,5},{2,6},{3,7},{4,0},{5,1},{6,2},{7,3},{8,12},{9,13},{10,... | collective-permute-start | bytes 2064392 | tf_op jit(solution)/shard_map/ppermute | solution.py:408
  44.4 31.0 %collective-permute-start.5 = (bf16[48,7168]{1,0:T(8,128)(2,1)S(1)}, bf16[48,7168]{1,0:T(8,128)(2,1)S(1)}, u32[]{:S(2)}, u32[]{:S(2)}) collective-permute-start(bf16[48,7168]{1,0:T(8,128)(2,1)S(1)} %get-tuple-element.42), channel_id=1, source_target_pairs={{0,6},{1,7},{2,0},{3,1},{4,2},{5,3},{6,4},{7,5},{8,14},{9,15},{10,... | collective-permute-start | bytes 2064392 | tf_op jit(solution)/shard_map/ppermute | solution.py:408
  45.7 3.1 %copy-start.1 = (bf16[1,512,7168]{2,1,0:T(8,128)(2,1)S(1)}, bf16[1,512,7168]{2,1,0:T(8,128)(2,1)}, u32[]{:S(2)}) copy-start(bf16[1,512,7168]{2,1,0:T(8,128)(2,1)} %param.13) | copy-start | bytes 22020100
  52.9 22.5 %collective-permute-start.6 = (bf16[48,7168]{1,0:T(8,128)(2,1)S(1)}, bf16[48,7168]{1,0:T(8,128)(2,1)S(1)}, u32[]{:S(2)}, u32[]{:S(2)}) collective-permute-start(bf16[48,7168]{1,0:T(8,128)(2,1)S(1)} %get-tuple-element.39.refs_0_), channel_id=1, source_target_pairs={{0,1},{1,0},{2,3},{3,2},{4,5},{5,4},{6,7},{7,6},{8,9},{9,8},{10,11... | collective-permute-start | bytes 2064392 | tf_op jit(solution)/shard_map/ppermute | solution.py:412
  74.8 2.1 %collective-permute-start.7 = (bf16[48,7168]{1,0:T(8,128)(2,1)S(1)}, bf16[48,7168]{1,0:T(8,128)(2,1)S(1)}, u32[]{:S(2)}, u32[]{:S(2)}) collective-permute-start(bf16[48,7168]{1,0:T(8,128)(2,1)S(1)} %collective-permute-done.3.refs_1_), channel_id=1, source_target_pairs={{0,1},{1,0},{2,3},{3,2},{4,5},{5,4},{6,7},{7,6},{8,9},{9,8},{10,11... | collective-permute-start | bytes 2064392 | tf_op jit(solution)/shard_map/ppermute | solution.py:412
  74.8 3.1 %collective-permute-start.8 = (bf16[48,7168]{1,0:T(8,128)(2,1)S(1)}, bf16[48,7168]{1,0:T(8,128)(2,1)S(1)}, u32[]{:S(2)}, u32[]{:S(2)}) collective-permute-start(bf16[48,7168]{1,0:T(8,128)(2,1)S(1)} %collective-permute-done.4.refs_2_), channel_id=1, source_target_pairs={{0,1},{1,0},{2,3},{3,2},{4,5},{5,4},{6,7},{7,6},{8,9},{9,8},{10,11... | collective-permute-start | bytes 2064392 | tf_op jit(solution)/shard_map/ppermute | solution.py:412
  75.4 3.5 %collective-permute-start.9 = (bf16[48,7168]{1,0:T(8,128)(2,1)S(1)}, bf16[48,7168]{1,0:T(8,128)(2,1)S(1)}, u32[]{:S(2)}, u32[]{:S(2)}) collective-permute-start(bf16[48,7168]{1,0:T(8,128)(2,1)S(1)} %collective-permute-done.5.refs_3_), channel_id=1, source_target_pairs={{0,1},{1,0},{2,3},{3,2},{4,5},{5,4},{6,7},{7,6},{8,9},{9,8},{10,11... | collective-permute-start | bytes 2064392 | tf_op jit(solution)/shard_map/ppermute | solution.py:412
  81.9 8.8 %collective-permute-start.10 = (bf16[384,3584]{1,0:T(8,128)(2,1)}, bf16[384,3584]{1,0:T(8,128)(2,1)S(1)}, u32[]{:S(2)}, u32[]{:S(2)}) collective-permute-start(bf16[384,3584]{1,0:T(8,128)(2,1)} %bitcast.7.x_ref), channel_id=1, source_target_pairs={{0,1},{1,0},{2,3},{3,2},{4,5},{5,4},{6,7},{7,6},{8,9},{9,8},{10,11... | collective-permute-start | bytes 8257544 | tf_op jit(solution)/shard_map/ppermute | solution.py:412
  98.6 3.9 %collective-permute-start.11 = (bf16[192,3712]{1,0:T(8,128)(2,1)S(1)}, bf16[192,3712]{1,0:T(8,128)(2,1)S(1)}, u32[]{:S(2)}, u32[]{:S(2)}) collective-permute-start(bf16[192,3712]{1,0:T(8,128)(2,1)S(1)} %get-tuple-element.54), channel_id=1, source_target_pairs={{0,1},{1,0},{2,3},{3,2},{4,5},{5,4},{6,7},{7,6},{8,9},{9,8},{10,11... | collective-permute-start | bytes 4276232 | tf_op jit(solution)/shard_map/ppermute | solution.py:412
  102.1 4.7 %collective-permute-start.15 = (bf16[192,3584]{1,0:T(8,128)(2,1)S(1)}, bf16[192,3584]{1,0:T(8,128)(2,1)S(1)}, u32[]{:S(2)}, u32[]{:S(2)}) collective-permute-start(bf16[192,3584]{1,0:T(8,128)(2,1)S(1)} %get-tuple-element.60), channel_id=1, source_target_pairs={{0,1},{1,0},{2,3},{3,2},{4,5},{5,4},{6,7},{7,6},{8,9},{9,8},{10,11... | collective-permute-start | bytes 4128776 | tf_op jit(solution)/shard_map/ppermute | solution.py:412
  103.8 12.1 %collective-permute-start.12 = (bf16[48,3712]{1,0:T(8,128)(2,1)}, bf16[48,3712]{1,0:T(8,128)(2,1)}, u32[]{:S(2)}, u32[]{:S(2)}) collective-permute-start(bf16[48,3712]{1,0:T(8,128)(2,1)} %get-tuple-element.56), channel_id=1, source_target_pairs={{0,6},{1,7},{2,0},{3,1},{4,2},{5,3},{6,4},{7,5},{8,14},{9,15},{10,... | collective-permute-start | bytes 1069064 | tf_op jit(solution)/shard_map/ppermute | solution.py:408
  104.8 13.0 %collective-permute-start.13 = (bf16[48,3712]{1,0:T(8,128)(2,1)}, bf16[48,3712]{1,0:T(8,128)(2,1)}, u32[]{:S(2)}, u32[]{:S(2)}) collective-permute-start(bf16[48,3712]{1,0:T(8,128)(2,1)} %get-tuple-element.57), channel_id=1, source_target_pairs={{0,4},{1,5},{2,6},{3,7},{4,0},{5,1},{6,2},{7,3},{8,12},{9,13},{10,... | collective-permute-start | bytes 1069064 | tf_op jit(solution)/shard_map/ppermute | solution.py:408
  104.8 19.7 %collective-permute-start.14 = (bf16[48,3712]{1,0:T(8,128)(2,1)S(1)}, bf16[48,3712]{1,0:T(8,128)(2,1)}, u32[]{:S(2)}, u32[]{:S(2)}) collective-permute-start(bf16[48,3712]{1,0:T(8,128)(2,1)S(1)} %get-tuple-element.58), channel_id=1, source_target_pairs={{0,2},{1,3},{2,4},{3,5},{4,6},{5,7},{6,0},{7,1},{8,10},{9,11},{10,... | collective-permute-start | bytes 1069064 | tf_op jit(solution)/shard_map/ppermute | solution.py:408
  109.1 28.4 %all-to-all-start.2 = ((bf16[16,24,1792]{2,1,0:T(8,128)(2,1)}), bf16[16,24,1792]{2,1,0:T(8,128)(2,1)S(1)}, u32[]{:S(2)}, u32[]{:S(2)}) async-start(bf16[16,24,1792]{2,1,0:T(8,128)(2,1)} %bitcast.11), calls=%async_computation.2 | async-start | bytes 2752512 | tf_op jit(solution)/shard_map/all_to_all | solution.py:418
  126.5 0.8 copy-start.2
  137.5 15.5 %all-to-all-start.3 = ((bf16[16,40,512]{2,1,0:T(8,128)(2,1)}), bf16[16,40,512]{2,1,0:T(8,128)(2,1)S(1)}, u32[]{:S(2)}, u32[]{:S(2)}) async-start(bf16[16,40,512]{2,1,0:T(8,128)(2,1)} %bitcast.22), calls=%async_computation.3 | async-start | bytes 1310720 | tf_op jit(solution)/shard_map/all_to_all | solution.py:418
  142.6 5.3 %collective-permute-start.16 = (bf16[16,3584]{1,0:T(8,128)(2,1)S(1)}, bf16[16,3584]{1,0:T(8,128)(2,1)S(1)}, u32[]{:S(2)}, u32[]{:S(2)}) collective-permute-start(bf16[16,3584]{1,0:T(8,128)(2,1)S(1)} %get-tuple-element.65), channel_id=1, source_target_pairs={{0,6},{1,7},{2,0},{3,1},{4,2},{5,3},{6,4},{7,5},{8,14},{9,15},{10,... | collective-permute-start | bytes 344072 | tf_op jit(solution)/shard_map/ppermute | solution.py:408
  145.3 6.3 %collective-permute-start.17 = (bf16[16,3584]{1,0:T(8,128)(2,1)S(1)}, bf16[16,3584]{1,0:T(8,128)(2,1)S(1)}, u32[]{:S(2)}, u32[]{:S(2)}) collective-permute-start(bf16[16,3584]{1,0:T(8,128)(2,1)S(1)} %get-tuple-element.66), channel_id=1, source_target_pairs={{0,4},{1,5},{2,6},{3,7},{4,0},{5,1},{6,2},{7,3},{8,12},{9,13},{10,... | collective-permute-start | bytes 344072 | tf_op jit(solution)/shard_map/ppermute | solution.py:408
  146.9 6.0 %collective-permute-start.18 = (bf16[16,3584]{1,0:T(8,128)(2,1)S(1)}, bf16[16,3584]{1,0:T(8,128)(2,1)S(1)}, u32[]{:S(2)}, u32[]{:S(2)}) collective-permute-start(bf16[16,3584]{1,0:T(8,128)(2,1)S(1)} %get-tuple-element.67), channel_id=1, source_target_pairs={{0,2},{1,3},{2,4},{3,5},{4,6},{5,7},{6,0},{7,1},{8,10},{9,11},{10,... | collective-permute-start | bytes 344072 | tf_op jit(solution)/shard_map/ppermute | solution.py:408

commit v7 on v6

--- a/solution.py
+++ b/solution.py
@@ -175,7 +175,7 @@
     wait_all(loads)
 
 
-def table_kernel(place_ref, meta_ref, table_ref):
+def table_kernel(place_ref, meta_ref, mark_ref, table_ref):
     c = iota((256, 128), 1)
     want = ((c >> 2) << 6) + 4 * place_ref[0] + ((place_ref[1] + c) & 3)
     select = onehot((c < 8) & (iota((256, 128), 0) == want)).astype(BF)
@@ -272,7 +272,8 @@
         ).astype(BF)
 
 
-def add_to_nodes_kernel(own_ref, got_ref, mark_ref, out_ref):
+def add_to_nodes_kernel(own_ref, got_ref, mark_ref, out_ref, mark_out):
+    mark_out[...] = mark_ref[...]
     row = iota((384, 384), 0)
     block = div3(row >> 3)
     rest = row - 24 * block
@@ -451,7 +452,6 @@
     x_mine = node_exchange(x_send)
     dy_mine = [dy_own] + [shift_y(dy_far[s - 1], s) for s in (1, 2, 3)]
     dy_other = [swap_core(v) for v in dy_mine]
-    table = whole(table_kernel, sds((128, 128), F32), [SMEM, VM], "table")(place, meta)
     back = whole(back_kernel, sds((2 * SLOTS, HALF), F32), [VM] * 9, "back")(
         *dy_mine, *dy_other, down_near
     )
@@ -490,9 +490,10 @@
         "add_halves",
     )(own_a, got_a)
     pieces = [pieces[0]] + [shift_y(pieces[s], -s) for s in (1, 2, 3)]
-    sent_b = whole(add_to_nodes_kernel, sds((384, 1792)), [VM] * 3, "add_to_nodes")(
-        own_b, got_b, mark
-    )
+    sent_b, mark = whole(
+        add_to_nodes_kernel, [sds((384, 1792)), sds((8, 128), F32)], [VM] * 3, "add_to_nodes"
+    )(own_b, got_b, mark)
+    table = whole(table_kernel, sds((128, 128), F32), [SMEM, VM, VM], "table")(place, meta, mark)
     back_b = node_exchange(sent_b)
     mixed = whole(
         combine_kernel,

time: 156 us -> 155 us (level)
  no operation moved by 1% of the time
where the time goes in v7:
time: 155 us; the launch traced here: 154 us
  waiting for transfers between devices  60.4 us (39%)
  Pallas kernels  44.2 us (29%)
  starting transfers between devices  42.9 us (28%)
  local copies, waits for them, and re-layouts  5.62 us (4%)
    ppermute x12, waiting for transfers between devices, shift_y(): return lax.ppermute(v, 'local', [(i, (i + 2 * s) % 8) for i in range(8)])  47.1 us
    all_to_all x4, starting transfers between devices, node_exchange(): lax.all_to_all(v, 'node', split_axis=0, concat_axis=0, tiled=True)  24.9 us
    ppermute x12, starting transfers between devices, shift_y(): return lax.ppermute(v, 'local', [(i, (i + 2 * s) % 8) for i in range(8)])  16.1 us
    all_to_all x4, waiting for transfers between devices, node_exchange(): lax.all_to_all(v, 'node', split_axis=0, concat_axis=0, tiled=True)  9.83 us
    pallas_call x1, Pallas kernels, on_device(): whole(forward_own_kernel, [sds((SLOTS, HALF), F32)] * 2 + [sds((WIDTH, HA...  8.43 us
    pallas_call x2, Pallas kernels, dx(): whole(functools.partial(dx_kernel, part), [sds((SLOTS, width))] * 2, [VM]...  6.08 us
    unnamed x12, local copies, waits for them, and re-layouts  5.45 us
    pallas_call x1, Pallas kernels, on_device(): whole(forward_kernel, [sds((2 * SLOTS, HALF)), sds((2 * SLOTS, HALF)), sd...  4.82 us
  transfers between devices with their start and end apart: 23, of which 14 were waited for; matrix products, arithmetic and copies ran while one was open for 0% of the time, Pallas kernels for 20%

profile of v7, /device:TPU:0, one launch (start us, length us, event | category | flops | bytes accessed | tf_op | source)
XLA Modules:
  0.0 154.2 jit_solution(5086705036475948375)
XLA Ops:
  0.6 3.2 %send_dy.1 = bf16[640,1024]{1,0:T(8,128)(2,1)} custom-call(s32[8,16]{1,0:T(8,128)} %bitcast.23, f32[8,16]{1,0:T(8,128)} %bitcast.28, bf16[16,7168]{1,0:T(8,128)(2,1)} %dy_ref.1), custom_call_target="tpu_custom_call" | custom-call | tf_op jit(solution)/shard_map/send_dy/pallas_call | solution.py:428
  3.8 8.1 %all-to-all-start = ((bf16[16,40,1024]{2,1,0:T(8,128)(2,1)}), bf16[16,40,1024]{2,1,0:T(8,128)(2,1)S(1)}, u32[]{:S(2)}, u32[]{:S(2)}) async-start(bf16[16,40,1024]{2,1,0:T(8,128)(2,1)} %bitcast.27), calls=%async_computation | async-start | bytes 2621440 | tf_op jit(solution)/shard_map/all_to_all | solution.py:419
  12.2 3.1 %collective-permute-start.2 = (bf16[16,7296]{1,0:T(8,128)(2,1)S(1)}, bf16[16,7296]{1,0:T(8,128)(2,1)S(1)}, u32[]{:S(2)}, u32[]{:S(2)}) collective-permute-start(bf16[16,7296]{1,0:T(8,128)(2,1)S(1)} %pad_maximum_fusion.x0_ref), channel_id=1, source_target_pairs={{0,6},{1,7},{2,0},{3,1},{4,2},{5,3},{6,4},{7,5},{8,14},{9,15},{10,... | collective-permute-start | bytes 700424 | tf_op jit(solution)/shard_map/ppermute | solution.py:409
  17.0 8.0 %collective-permute-done.2.x3_ref = bf16[16,7296]{1,0:T(8,128)(2,1)S(1)} collective-permute-done((bf16[16,7296]{1,0:T(8,128)(2,1)S(1)}, bf16[16,7296]{1,0:T(8,128)(2,1)S(1)}, u32[]{:S(2)}, u32[]{:S(2)}) %collective-permute-start.2) | collective-permute-done | bytes 233504 | tf_op jit(solution)/shard_map/ppermute | solution.py:409
  25.5 3.2 %collective-permute-done.x1_ref = bf16[16,7296]{1,0:T(8,128)(2,1)S(1)} collective-permute-done((bf16[16,7296]{1,0:T(8,128)(2,1)S(1)}, bf16[16,7296]{1,0:T(8,128)(2,1)S(1)}, u32[]{:S(2)}, u32[]{:S(2)}) %collective-permute-start) | collective-permute-done | bytes 233504 | tf_op jit(solution)/shard_map/ppermute | solution.py:409
  28.7 1.8 %send_x.1 = bf16[384,3584]{1,0:T(8,128)(2,1)S(1)} custom-call(s32[2]{0:T(128)S(1)} %pad_add_fusion.place_ref, bf16[16,7296]{1,0:T(8,128)(2,1)S(1)} %pad_maximum_fusion.x0_ref, bf16[16,7296]{1,0:T(8,128)(2,1)S(1)} %collective-permute-done.x1_ref, bf16[16,7296]{1,0:T(8,128)(2,1)S(1)} %collective-permute-done.1.x2_ref, ...), custom_call_target="tpu_custom_call" | custom-call | tf_op jit(solution)/shard_map/send_x/pallas_call | solution.py:437
  30.5 1.5 copy-done
  32.7 6.3 %all-to-all-start.1 = ((bf16[16,24,3584]{2,1,0:T(8,128)(2,1)}), bf16[16,24,3584]{2,1,0:T(8,128)(2,1)}, u32[]{:S(2)}, u32[]{:S(2)}) async-start(bf16[16,24,3584]{2,1,0:T(8,128)(2,1)} %bitcast.18), calls=%async_computation.1 | async-start | bytes 5505024 | tf_op jit(solution)/shard_map/all_to_all | solution.py:419
  39.0 2.6 %regroup.1 = (bf16[48,7168]{1,0:T(8,128)(2,1)S(1)}, bf16[48,7168]{1,0:T(8,128)(2,1)S(1)}, bf16[48,7168]{1,0:T(8,128)(2,1)S(1)}, bf16[640,256]{1,0:T(8,128)(2,1)S(1)}) custom-call(s32[2]{0:T(128)S(1)} %pad_add_fusion.place_ref, bf16[640,1024]{1,0:T(8,128)(2,1)S(1)} %bitcast.16), custom_call_target="tpu_custom_call" | custom-call | tf_op jit(solution)/shard_map/regroup/pallas_call | solution.py:439
  41.7 2.6 %collective-permute-start.4 = (bf16[48,7168]{1,0:T(8,128)(2,1)S(1)}, bf16[48,7168]{1,0:T(8,128)(2,1)S(1)}, u32[]{:S(2)}, u32[]{:S(2)}) collective-permute-start(bf16[48,7168]{1,0:T(8,128)(2,1)S(1)} %get-tuple-element.43), channel_id=1, source_target_pairs={{0,4},{1,5},{2,6},{3,7},{4,0},{5,1},{6,2},{7,3},{8,12},{9,13},{10,... | collective-permute-start | bytes 2064392 | tf_op jit(solution)/shard_map/ppermute | solution.py:409
  44.4 1.3 collective-permute-start.5
  45.7 3.1 %copy-done.1 = bf16[1,512,7168]{2,1,0:T(8,128)(2,1)S(1)} copy-done((bf16[1,512,7168]{2,1,0:T(8,128)(2,1)S(1)}, bf16[1,512,7168]{2,1,0:T(8,128)(2,1)}, u32[]{:S(2)}) %copy-start.1) | copy-done | bytes 7340056
  48.8 4.1 %regroup_own.1 = (bf16[48,7168]{1,0:T(8,128)(2,1)S(1)}, bf16[512,7168]{1,0:T(8,128)(2,1)S(1)}) custom-call(s32[2]{0:T(128)S(1)} %pad_add_fusion.place_ref, bf16[640,1024]{1,0:T(8,128)(2,1)S(1)} %bitcast.17, bf16[512,7168]{1,0:T(8,128)(2,1)S(1)} %bitcast.19), custom_call_target="tpu_custom_call" | custom-call | tf_op jit(solution)/shard_map/regroup_own/pallas_call | solution.py:445
  53.0 21.7 %collective-permute-done.3.refs_1_ = bf16[48,7168]{1,0:T(8,128)(2,1)S(1)} collective-permute-done((bf16[48,7168]{1,0:T(8,128)(2,1)S(1)}, bf16[48,7168]{1,0:T(8,128)(2,1)S(1)}, u32[]{:S(2)}, u32[]{:S(2)}) %collective-permute-start.3) | collective-permute-done | bytes 688160 | tf_op jit(solution)/shard_map/ppermute | solution.py:409
  75.4 1.5 collective-permute-done.7.refs_5_
  78.9 3.0 %back.1.mark_ref.back_ref = f32[384,512]{1,0:T(8,128)S(1)} custom-call(bf16[48,7168]{1,0:T(8,128)(2,1)S(1)} %get-tuple-element.41.refs_0_, bf16[48,7168]{1,0:T(8,128)(2,1)S(1)} %collective-permute-done.3.refs_1_, bf16[48,7168]{1,0:T(8,128)(2,1)S(1)} %collective-permute-done.4.refs_2_, bf16[48,7168]{1,0:T(8,128)(2,1)S(1)} %collective-permute-done.5.refs_3_, ...), custom_call_target="tpu_custom_call" | custom-call | tf_op jit(solution)/shard_map/back/pallas_call | solution.py:455
  82.3 8.4 %forward_own.1 = (f32[192,512]{1,0:T(8,128)S(1)}, f32[192,512]{1,0:T(8,128)S(1)}, bf16[7168,512]{1,0:T(8,128)(2,1)S(1)}, bf16[7168,512]{1,0:T(8,128)(2,1)S(1)}) custom-call(bf16[384,3584]{1,0:T(8,128)(2,1)} %bitcast.7.x_ref, bf16[7168,512]{1,0:T(8,128)(2,1)} %bitcast.25, bf16[7168,512]{1,0:T(8,128)(2,1)} %bitcast.26, f32[384,512]{1,0:T(8,128)S(1)} %back.1.mark_ref.back_ref), custom_call_target="tpu_custom_call" | custom-call | tf_op jit(solution)/shard_map/forward_own/pallas_call | solution.py:460
  90.8 4.8 %forward.1 = (bf16[384,512]{1,0:T(8,128)(2,1)S(1)}, bf16[384,512]{1,0:T(8,128)(2,1)S(1)}, bf16[384,128]{1,0:T(8,128)(2,1)S(1)}) custom-call(bf16[384,3584]{1,0:T(8,128)(2,1)S(1)} %collective-permute-done.10.x_ref, bf16[7168,512]{1,0:T(8,128)(2,1)S(1)} %get-tuple-element.48.gate_ref, bf16[7168,512]{1,0:T(8,128)(2,1)S(1)} %get-tuple-element.49.up_ref, ...), custom_call_target="tpu_custom_call" | custom-call | tf_op jit(solution)/shard_map/forward/pallas_call | solution.py:467
  95.6 3.0 %dx.3 = (bf16[192,3712]{1,0:T(8,128)(2,1)S(1)}, bf16[192,3712]{1,0:T(8,128)(2,1)S(1)}) custom-call(bf16[384,512]{1,0:T(8,128)(2,1)S(1)} %get-tuple-element.52.dgate_ref, bf16[384,512]{1,0:T(8,128)(2,1)S(1)} %get-tuple-element.53.dup_ref, bf16[7168,512]{1,0:T(8,128)(2,1)S(1)} %get-tuple-element.48.gate_ref, bf16[7168,512]{1,0:T(8,128)(2,1)S(1)} %get-tuple-element.49.up_ref, ...), custom_call_target="tpu_custom_call" | custom-call | tf_op jit(solution)/shard_map/dx/pallas_call | solution.py:475
  99.1 3.0 %dx.2 = (bf16[192,3584]{1,0:T(8,128)(2,1)S(1)}, bf16[192,3584]{1,0:T(8,128)(2,1)S(1)}) custom-call(bf16[384,512]{1,0:T(8,128)(2,1)S(1)} %get-tuple-element.52.dgate_ref, bf16[384,512]{1,0:T(8,128)(2,1)S(1)} %get-tuple-element.53.dup_ref, bf16[7168,512]{1,0:T(8,128)(2,1)S(1)} %get-tuple-element.48.gate_ref, bf16[7168,512]{1,0:T(8,128)(2,1)S(1)} %get-tuple-element.49.up_ref, ...), custom_call_target="tpu_custom_call" | custom-call | tf_op jit(solution)/shard_map/dx/pallas_call | solution.py:475
  105.9 2.2 %add_to_nodes.1 = (bf16[384,1792]{1,0:T(8,128)(2,1)}, f32[8,128]{1,0:T(8,128)S(1)}) custom-call(bf16[192,3584]{1,0:T(8,128)(2,1)S(1)} %get-tuple-element.55.own_ref, bf16[192,3584]{1,0:T(8,128)(2,1)S(1)} %collective-permute-done.11.got_ref, f32[8,128]{1,0:T(8,128)S(1)} %get-tuple-element.59.mark_ref), custom_call_target="tpu_custom_call" | custom-call | tf_op jit(solution)/shard_map/add_to_nodes/pallas_call | solution.py:493
  108.1 6.9 %all-to-all-start.2 = ((bf16[16,24,1792]{2,1,0:T(8,128)(2,1)}), bf16[16,24,1792]{2,1,0:T(8,128)(2,1)S(1)}, u32[]{:S(2)}, u32[]{:S(2)}) async-start(bf16[16,24,1792]{2,1,0:T(8,128)(2,1)} %bitcast.11), calls=%async_computation.2 | async-start | bytes 2752512 | tf_op jit(solution)/shard_map/all_to_all | solution.py:419
  116.0 1.9 %collective-permute-done.14.p2_ref = bf16[48,3712]{1,0:T(8,128)(2,1)} collective-permute-done((bf16[48,3712]{1,0:T(8,128)(2,1)}, bf16[48,3712]{1,0:T(8,128)(2,1)}, u32[]{:S(2)}, u32[]{:S(2)}) %collective-permute-start.14) | collective-permute-done | bytes 356384 | tf_op jit(solution)/shard_map/ppermute | solution.py:409
  117.9 6.7 %collective-permute-done.15.p3_ref = bf16[48,3712]{1,0:T(8,128)(2,1)} collective-permute-done((bf16[48,3712]{1,0:T(8,128)(2,1)S(1)}, bf16[48,3712]{1,0:T(8,128)(2,1)}, u32[]{:S(2)}, u32[]{:S(2)}) %collective-permute-start.15) | collective-permute-done | bytes 356384 | tf_op jit(solution)/shard_map/ppermute | solution.py:409
  124.6 1.9 %combine.1 = bf16[640,512]{1,0:T(8,128)(2,1)S(1)} custom-call(f32[128,128]{1,0:T(8,128)S(1)} %table.1.table_ref, bf16[48,3712]{1,0:T(8,128)(2,1)S(1)} %get-tuple-element.61.p0_ref, bf16[48,3712]{1,0:T(8,128)(2,1)} %collective-permute-done.13.p1_ref, bf16[48,3712]{1,0:T(8,128)(2,1)} %collective-permute-done.14.p2_ref, ...), custom_call_target="tpu_custom_call" | custom-call | flops 20000000000 | bytes 70000000 | tf_op jit(solution)/shard_map/combine/pallas_call | solution.py:498
  127.3 9.1 %all-to-all-done.2 = bf16[16,24,1792]{2,1,0:T(8,128)(2,1)S(1)} async-done(((bf16[16,24,1792]{2,1,0:T(8,128)(2,1)}), bf16[16,24,1792]{2,1,0:T(8,128)(2,1)S(1)}, u32[]{:S(2)}, u32[]{:S(2)}) %all-to-all-start.2) | async-done | bytes 1376288 | tf_op jit(solution)/shard_map/all_to_all | solution.py:419
  136.5 3.6 %all-to-all-start.3 = ((bf16[16,40,512]{2,1,0:T(8,128)(2,1)}), bf16[16,40,512]{2,1,0:T(8,128)(2,1)S(1)}, u32[]{:S(2)}, u32[]{:S(2)}) async-start(bf16[16,40,512]{2,1,0:T(8,128)(2,1)} %bitcast.22), calls=%async_computation.3 | async-start | bytes 1310720 | tf_op jit(solution)/shard_map/all_to_all | solution.py:419
  140.1 1.5 combine_near.1
  141.6 2.7 %collective-permute-start.16 = (bf16[16,3584]{1,0:T(8,128)(2,1)S(1)}, bf16[16,3584]{1,0:T(8,128)(2,1)S(1)}, u32[]{:S(2)}, u32[]{:S(2)}) collective-permute-start(bf16[16,3584]{1,0:T(8,128)(2,1)S(1)} %get-tuple-element.69), channel_id=1, source_target_pairs={{0,6},{1,7},{2,0},{3,1},{4,2},{5,3},{6,4},{7,5},{8,14},{9,15},{10,... | collective-permute-start | bytes 344072 | tf_op jit(solution)/shard_map/ppermute | solution.py:409
  144.3 1.6 %collective-permute-start.17 = (bf16[16,3584]{1,0:T(8,128)(2,1)S(1)}, bf16[16,3584]{1,0:T(8,128)(2,1)S(1)}, u32[]{:S(2)}, u32[]{:S(2)}) collective-permute-start(bf16[16,3584]{1,0:T(8,128)(2,1)S(1)} %get-tuple-element.70), channel_id=1, source_target_pairs={{0,4},{1,5},{2,6},{3,7},{4,0},{5,1},{6,2},{7,3},{8,12},{9,13},{10,... | collective-permute-start | bytes 344072 | tf_op jit(solution)/shard_map/ppermute | solution.py:409
  146.9 3.7 %collective-permute-done.17.b2_ref = bf16[16,3584]{1,0:T(8,128)(2,1)S(1)} collective-permute-done((bf16[16,3584]{1,0:T(8,128)(2,1)S(1)}, bf16[16,3584]{1,0:T(8,128)(2,1)S(1)}, u32[]{:S(2)}, u32[]{:S(2)}) %collective-permute-start.17) | collective-permute-done | bytes 114720 | tf_op jit(solution)/shard_map/ppermute | solution.py:409
  151.9 2.3 %finish.1 = (bf16[16,7168]{1,0:T(8,128)(2,1)}, f32[8,16]{1,0:T(8,128)}) custom-call(s32[2]{0:T(128)S(1)} %pad_add_fusion.place_ref, s32[8,16]{1,0:T(8,128)S(1)} %bitcast.24, bf16[640,512]{1,0:T(8,128)(2,1)S(1)} %bitcast.21, bf16[16,3584]{1,0:T(8,128)(2,1)S(1)} %get-tuple-element.68.b0_ref, bf16[16,3584]{1,0:T(8,128)(2,1)S(1)} %collective-permute-done.16.b1_ref, ...), custom_call_target="tpu_custom_call" | custom-call | tf_op jit(solution)/shard_map/finish/pallas_call | solution.py:512
  (48 shorter events, 14.6 us)
Async XLA Ops:
  3.8 8.1 %copy-start.3 = (s32[16,8]{0,1:T(8,128)S(1)}, s32[16,8]{0,1:T(8,128)}, u32[]{:S(2)}) copy-start(s32[16,8]{0,1:T(8,128)} %param.9) | copy-start | bytes 1540
  3.8 8.1 %copy-start.5 = (f32[16,8]{0,1:T(8,128)S(1)}, f32[16,8]{0,1:T(8,128)}, u32[]{:S(2)}) copy-start(f32[16,8]{0,1:T(8,128)} %param.10) | copy-start | bytes 1540
  3.8 8.4 %copy-start.4 = (bf16[16,7168]{1,0:T(8,128)(2,1)S(1)}, bf16[16,7168]{1,0:T(8,128)(2,1)}, u32[]{:S(2)}) copy-start(bf16[16,7168]{1,0:T(8,128)(2,1)} %param.7) | copy-start | bytes 688132
  3.8 28.9 %all-to-all-start = ((bf16[16,40,1024]{2,1,0:T(8,128)(2,1)}), bf16[16,40,1024]{2,1,0:T(8,128)(2,1)S(1)}, u32[]{:S(2)}, u32[]{:S(2)}) async-start(bf16[16,40,1024]{2,1,0:T(8,128)(2,1)} %bitcast.27), calls=%async_computation | async-start | bytes 2621440 | tf_op jit(solution)/shard_map/all_to_all | solution.py:419
  12.2 12.8 %collective-permute-start.2 = (bf16[16,7296]{1,0:T(8,128)(2,1)S(1)}, bf16[16,7296]{1,0:T(8,128)(2,1)S(1)}, u32[]{:S(2)}, u32[]{:S(2)}) collective-permute-start(bf16[16,7296]{1,0:T(8,128)(2,1)S(1)} %pad_maximum_fusion.x0_ref), channel_id=1, source_target_pairs={{0,6},{1,7},{2,0},{3,1},{4,2},{5,3},{6,4},{7,5},{8,14},{9,15},{10,... | collective-permute-start | bytes 700424 | tf_op jit(solution)/shard_map/ppermute | solution.py:409
  15.3 10.2 %collective-permute-start.1 = (bf16[16,7296]{1,0:T(8,128)(2,1)S(1)}, bf16[16,7296]{1,0:T(8,128)(2,1)S(1)}, u32[]{:S(2)}, u32[]{:S(2)}) collective-permute-start(bf16[16,7296]{1,0:T(8,128)(2,1)S(1)} %pad_maximum_fusion.x0_ref), channel_id=1, source_target_pairs={{0,4},{1,5},{2,6},{3,7},{4,0},{5,1},{6,2},{7,3},{8,12},{9,13},{10,... | collective-permute-start | bytes 700424 | tf_op jit(solution)/shard_map/ppermute | solution.py:409
  16.0 12.7 %collective-permute-start = (bf16[16,7296]{1,0:T(8,128)(2,1)S(1)}, bf16[16,7296]{1,0:T(8,128)(2,1)S(1)}, u32[]{:S(2)}, u32[]{:S(2)}) collective-permute-start(bf16[16,7296]{1,0:T(8,128)(2,1)S(1)} %pad_maximum_fusion.x0_ref), channel_id=1, source_target_pairs={{0,2},{1,3},{2,4},{3,5},{4,6},{5,7},{6,0},{7,1},{8,10},{9,11},{10,... | collective-permute-start | bytes 700424 | tf_op jit(solution)/shard_map/ppermute | solution.py:409
  30.5 1.5 copy-start
  32.7 49.2 %all-to-all-start.1 = ((bf16[16,24,3584]{2,1,0:T(8,128)(2,1)}), bf16[16,24,3584]{2,1,0:T(8,128)(2,1)}, u32[]{:S(2)}, u32[]{:S(2)}) async-start(bf16[16,24,3584]{2,1,0:T(8,128)(2,1)} %bitcast.18), calls=%async_computation.1 | async-start | bytes 5505024 | tf_op jit(solution)/shard_map/all_to_all | solution.py:419
  41.7 33.1 %collective-permute-start.3 = (bf16[48,7168]{1,0:T(8,128)(2,1)S(1)}, bf16[48,7168]{1,0:T(8,128)(2,1)S(1)}, u32[]{:S(2)}, u32[]{:S(2)}) collective-permute-start(bf16[48,7168]{1,0:T(8,128)(2,1)S(1)} %get-tuple-element.42), channel_id=1, source_target_pairs={{0,2},{1,3},{2,4},{3,5},{4,6},{5,7},{6,0},{7,1},{8,10},{9,11},{10,... | collective-permute-start | bytes 2064392 | tf_op jit(solution)/shard_map/ppermute | solution.py:409
  41.7 33.0 %collective-permute-start.4 = (bf16[48,7168]{1,0:T(8,128)(2,1)S(1)}, bf16[48,7168]{1,0:T(8,128)(2,1)S(1)}, u32[]{:S(2)}, u32[]{:S(2)}) collective-permute-start(bf16[48,7168]{1,0:T(8,128)(2,1)S(1)} %get-tuple-element.43), channel_id=1, source_target_pairs={{0,4},{1,5},{2,6},{3,7},{4,0},{5,1},{6,2},{7,3},{8,12},{9,13},{10,... | collective-permute-start | bytes 2064392 | tf_op jit(solution)/shard_map/ppermute | solution.py:409
  44.4 31.0 %collective-permute-start.5 = (bf16[48,7168]{1,0:T(8,128)(2,1)S(1)}, bf16[48,7168]{1,0:T(8,128)(2,1)S(1)}, u32[]{:S(2)}, u32[]{:S(2)}) collective-permute-start(bf16[48,7168]{1,0:T(8,128)(2,1)S(1)} %get-tuple-element.44), channel_id=1, source_target_pairs={{0,6},{1,7},{2,0},{3,1},{4,2},{5,3},{6,4},{7,5},{8,14},{9,15},{10,... | collective-permute-start | bytes 2064392 | tf_op jit(solution)/shard_map/ppermute | solution.py:409
  45.7 3.1 %copy-start.1 = (bf16[1,512,7168]{2,1,0:T(8,128)(2,1)S(1)}, bf16[1,512,7168]{2,1,0:T(8,128)(2,1)}, u32[]{:S(2)}) copy-start(bf16[1,512,7168]{2,1,0:T(8,128)(2,1)} %param.13) | copy-start | bytes 22020100
  52.9 22.5 %collective-permute-start.6 = (bf16[48,7168]{1,0:T(8,128)(2,1)S(1)}, bf16[48,7168]{1,0:T(8,128)(2,1)S(1)}, u32[]{:S(2)}, u32[]{:S(2)}) collective-permute-start(bf16[48,7168]{1,0:T(8,128)(2,1)S(1)} %get-tuple-element.41.refs_0_), channel_id=1, source_target_pairs={{0,1},{1,0},{2,3},{3,2},{4,5},{5,4},{6,7},{7,6},{8,9},{9,8},{10,11... | collective-permute-start | bytes 2064392 | tf_op jit(solution)/shard_map/ppermute | solution.py:413
  74.8 2.1 %collective-permute-start.7 = (bf16[48,7168]{1,0:T(8,128)(2,1)S(1)}, bf16[48,7168]{1,0:T(8,128)(2,1)S(1)}, u32[]{:S(2)}, u32[]{:S(2)}) collective-permute-start(bf16[48,7168]{1,0:T(8,128)(2,1)S(1)} %collective-permute-done.3.refs_1_), channel_id=1, source_target_pairs={{0,1},{1,0},{2,3},{3,2},{4,5},{5,4},{6,7},{7,6},{8,9},{9,8},{10,11... | collective-permute-start | bytes 2064392 | tf_op jit(solution)/shard_map/ppermute | solution.py:413
  74.8 3.1 %collective-permute-start.8 = (bf16[48,7168]{1,0:T(8,128)(2,1)S(1)}, bf16[48,7168]{1,0:T(8,128)(2,1)S(1)}, u32[]{:S(2)}, u32[]{:S(2)}) collective-permute-start(bf16[48,7168]{1,0:T(8,128)(2,1)S(1)} %collective-permute-done.4.refs_2_), channel_id=1, source_target_pairs={{0,1},{1,0},{2,3},{3,2},{4,5},{5,4},{6,7},{7,6},{8,9},{9,8},{10,11... | collective-permute-start | bytes 2064392 | tf_op jit(solution)/shard_map/ppermute | solution.py:413
  75.4 3.5 %collective-permute-start.9 = (bf16[48,7168]{1,0:T(8,128)(2,1)S(1)}, bf16[48,7168]{1,0:T(8,128)(2,1)S(1)}, u32[]{:S(2)}, u32[]{:S(2)}) collective-permute-start(bf16[48,7168]{1,0:T(8,128)(2,1)S(1)} %collective-permute-done.5.refs_3_), channel_id=1, source_target_pairs={{0,1},{1,0},{2,3},{3,2},{4,5},{5,4},{6,7},{7,6},{8,9},{9,8},{10,11... | collective-permute-start | bytes 2064392 | tf_op jit(solution)/shard_map/ppermute | solution.py:413
  81.9 8.8 %collective-permute-start.10 = (bf16[384,3584]{1,0:T(8,128)(2,1)}, bf16[384,3584]{1,0:T(8,128)(2,1)S(1)}, u32[]{:S(2)}, u32[]{:S(2)}) collective-permute-start(bf16[384,3584]{1,0:T(8,128)(2,1)} %bitcast.7.x_ref), channel_id=1, source_target_pairs={{0,1},{1,0},{2,3},{3,2},{4,5},{5,4},{6,7},{7,6},{8,9},{9,8},{10,11... | collective-permute-start | bytes 8257544 | tf_op jit(solution)/shard_map/ppermute | solution.py:413
  98.6 3.9 %collective-permute-start.12 = (bf16[192,3712]{1,0:T(8,128)(2,1)S(1)}, bf16[192,3712]{1,0:T(8,128)(2,1)S(1)}, u32[]{:S(2)}, u32[]{:S(2)}) collective-permute-start(bf16[192,3712]{1,0:T(8,128)(2,1)S(1)} %get-tuple-element.58), channel_id=1, source_target_pairs={{0,1},{1,0},{2,3},{3,2},{4,5},{5,4},{6,7},{7,6},{8,9},{9,8},{10,11... | collective-permute-start | bytes 4276232 | tf_op jit(solution)/shard_map/ppermute | solution.py:413
  102.1 3.7 %collective-permute-start.11 = (bf16[192,3584]{1,0:T(8,128)(2,1)S(1)}, bf16[192,3584]{1,0:T(8,128)(2,1)S(1)}, u32[]{:S(2)}, u32[]{:S(2)}) collective-permute-start(bf16[192,3584]{1,0:T(8,128)(2,1)S(1)} %get-tuple-element.56), channel_id=1, source_target_pairs={{0,1},{1,0},{2,3},{3,2},{4,5},{5,4},{6,7},{7,6},{8,9},{9,8},{10,11... | collective-permute-start | bytes 4128776 | tf_op jit(solution)/shard_map/ppermute | solution.py:413
  103.8 12.1 %collective-permute-start.13 = (bf16[48,3712]{1,0:T(8,128)(2,1)}, bf16[48,3712]{1,0:T(8,128)(2,1)}, u32[]{:S(2)}, u32[]{:S(2)}) collective-permute-start(bf16[48,3712]{1,0:T(8,128)(2,1)} %get-tuple-element.62), channel_id=1, source_target_pairs={{0,6},{1,7},{2,0},{3,1},{4,2},{5,3},{6,4},{7,5},{8,14},{9,15},{10,... | collective-permute-start | bytes 1069064 | tf_op jit(solution)/shard_map/ppermute | solution.py:409
  104.8 13.0 %collective-permute-start.14 = (bf16[48,3712]{1,0:T(8,128)(2,1)}, bf16[48,3712]{1,0:T(8,128)(2,1)}, u32[]{:S(2)}, u32[]{:S(2)}) collective-permute-start(bf16[48,3712]{1,0:T(8,128)(2,1)} %get-tuple-element.63), channel_id=1, source_target_pairs={{0,4},{1,5},{2,6},{3,7},{4,0},{5,1},{6,2},{7,3},{8,12},{9,13},{10,... | collective-permute-start | bytes 1069064 | tf_op jit(solution)/shard_map/ppermute | solution.py:409
  104.8 19.7 %collective-permute-start.15 = (bf16[48,3712]{1,0:T(8,128)(2,1)S(1)}, bf16[48,3712]{1,0:T(8,128)(2,1)}, u32[]{:S(2)}, u32[]{:S(2)}) collective-permute-start(bf16[48,3712]{1,0:T(8,128)(2,1)S(1)} %get-tuple-element.64), channel_id=1, source_target_pairs={{0,2},{1,3},{2,4},{3,5},{4,6},{5,7},{6,0},{7,1},{8,10},{9,11},{10,... | collective-permute-start | bytes 1069064 | tf_op jit(solution)/shard_map/ppermute | solution.py:409
  108.1 28.4 %all-to-all-start.2 = ((bf16[16,24,1792]{2,1,0:T(8,128)(2,1)}), bf16[16,24,1792]{2,1,0:T(8,128)(2,1)S(1)}, u32[]{:S(2)}, u32[]{:S(2)}) async-start(bf16[16,24,1792]{2,1,0:T(8,128)(2,1)} %bitcast.11), calls=%async_computation.2 | async-start | bytes 2752512 | tf_op jit(solution)/shard_map/all_to_all | solution.py:419
  126.5 0.8 copy-start.2
  136.5 15.4 %all-to-all-start.3 = ((bf16[16,40,512]{2,1,0:T(8,128)(2,1)}), bf16[16,40,512]{2,1,0:T(8,128)(2,1)S(1)}, u32[]{:S(2)}, u32[]{:S(2)}) async-start(bf16[16,40,512]{2,1,0:T(8,128)(2,1)} %bitcast.22), calls=%async_computation.3 | async-start | bytes 1310720 | tf_op jit(solution)/shard_map/all_to_all | solution.py:419
  141.6 5.3 %collective-permute-start.16 = (bf16[16,3584]{1,0:T(8,128)(2,1)S(1)}, bf16[16,3584]{1,0:T(8,128)(2,1)S(1)}, u32[]{:S(2)}, u32[]{:S(2)}) collective-permute-start(bf16[16,3584]{1,0:T(8,128)(2,1)S(1)} %get-tuple-element.69), channel_id=1, source_target_pairs={{0,6},{1,7},{2,0},{3,1},{4,2},{5,3},{6,4},{7,5},{8,14},{9,15},{10,... | collective-permute-start | bytes 344072 | tf_op jit(solution)/shard_map/ppermute | solution.py:409
  144.3 6.3 %collective-permute-start.17 = (bf16[16,3584]{1,0:T(8,128)(2,1)S(1)}, bf16[16,3584]{1,0:T(8,128)(2,1)S(1)}, u32[]{:S(2)}, u32[]{:S(2)}) collective-permute-start(bf16[16,3584]{1,0:T(8,128)(2,1)S(1)} %get-tuple-element.70), channel_id=1, source_target_pairs={{0,4},{1,5},{2,6},{3,7},{4,0},{5,1},{6,2},{7,3},{8,12},{9,13},{10,... | collective-permute-start | bytes 344072 | tf_op jit(solution)/shard_map/ppermute | solution.py:409
  145.9 6.0 %collective-permute-start.18 = (bf16[16,3584]{1,0:T(8,128)(2,1)S(1)}, bf16[16,3584]{1,0:T(8,128)(2,1)S(1)}, u32[]{:S(2)}, u32[]{:S(2)}) collective-permute-start(bf16[16,3584]{1,0:T(8,128)(2,1)S(1)} %get-tuple-element.71), channel_id=1, source_target_pairs={{0,2},{1,3},{2,4},{3,5},{4,6},{5,7},{6,0},{7,1},{8,10},{9,11},{10,... | collective-permute-start | bytes 344072 | tf_op jit(solution)/shard_map/ppermute | solution.py:409

commit v8 on v7

--- a/solution.py
+++ b/solution.py
@@ -22,6 +22,13 @@
 SLOTS = N_Y * ROWS_Y
 ROWS_N = N_NODE * 40
 EXT = 128
+A_PARTS = 15
+A_CHUNK = 256
+A_WIDTH = A_PARTS * A_CHUNK
+A_BLOCK = 5 * (A_PARTS + 1)
+ROWS_A = N_NODE * A_BLOCK
+B_WIDTH = WIDTH - A_WIDTH
+B_HALF = B_WIDTH // 2
 MIB = 1024 * 1024
 VMEM_LIMITS = {"send_dy": 60, "regroup_own": 24, "back": 20, "forward_own": 30, "forward": 30, "dx": 24}
 
@@ -246,13 +253,14 @@
 
 
 def dx_kernel(part, dgate_ref, dup_ref, gate_ref, up_ref, ext_ref, own_ref, other_ref):
-    cols = slice(3584 * part, 3584 * (part + 1))
+    cols = slice(A_WIDTH, WIDTH) if part else slice(0, A_WIDTH)
+    width = cols.stop - cols.start
     out = (dot_nt(dgate_ref[...], gate_ref[cols, :]) + dot_nt(dup_ref[...], up_ref[cols, :])).astype(BF)
-    own_ref[:, :3584] = out[:SLOTS]
-    other_ref[:, :3584] = out[SLOTS:]
+    own_ref[:, :width] = out[:SLOTS]
+    other_ref[:, :width] = out[SLOTS:]
     if part == 0:
-        own_ref[:, 3584:] = ext_ref[:SLOTS]
-        other_ref[:, 3584:] = ext_ref[SLOTS:]
+        own_ref[:, A_WIDTH:] = ext_ref[:SLOTS]
+        other_ref[:, A_WIDTH:] = ext_ref[SLOTS:]
 
 
 def add_kernel(own_ref, got_ref, *outs):
@@ -260,14 +268,14 @@
     lane = iota((ROWS_Y, EXT), 1)
     for s in range(N_Y):
         rows = slice(ROWS_Y * s, ROWS_Y * (s + 1))
-        total = own_ref[rows, :3584].astype(F32) + got_ref[rows, :3584].astype(F32)
-        outs[s][:, :3584] = total.astype(BF)
+        total = own_ref[rows, :A_WIDTH].astype(F32) + got_ref[rows, :A_WIDTH].astype(F32)
+        outs[s][:, :A_WIDTH] = total.astype(BF)
         term = jnp.sum(
-            own_ref[rows, 3584:].astype(F32) + got_ref[rows, 3584:].astype(F32), axis=1, keepdims=True
+            own_ref[rows, A_WIDTH:].astype(F32) + got_ref[rows, A_WIDTH:].astype(F32), axis=1, keepdims=True
         )
         high = term.astype(BF).astype(F32)
         low = term - high
-        outs[s][:, 3584:] = jnp.where(
+        outs[s][:, A_WIDTH:] = jnp.where(
             lane == 2 * s, high, jnp.where(lane == 2 * s + 1, low, 0.0)
         ).astype(BF)
 
@@ -283,7 +291,7 @@
     source = SLOTS * h + ROWS_Y * s + 3 * block + (rest - 3 * s)
     perm = onehot(iota((384, 384), 1) == source).astype(BF)
     total = (own_ref[...].astype(F32) + got_ref[...].astype(F32)).astype(BF)
-    out_ref[...] = dot(perm, jnp.concatenate([total[:, :1792], total[:, 1792:]], axis=0)).astype(BF)
+    out_ref[...] = dot(perm, jnp.concatenate([total[:, :B_HALF], total[:, B_HALF:]], axis=0)).astype(BF)
 
 
 def near_tables(y, xs):
@@ -318,7 +326,7 @@
         weight = jnp.where(match & (half == h), gate, 0.0).astype(BF)
         total = dot(weight, rows_ref[...]).astype(BF)
         for s in range(N_Y):
-            outs[s][:, 1792 * h : 1792 * (h + 1)] = total[TOK * s : TOK * (s + 1)]
+            outs[s][:, B_HALF * h : B_HALF * (h + 1)] = total[TOK * s : TOK * (s + 1)]
 
 
 def combine_kernel(table_ref, p0_ref, p1_ref, p2_ref, p3_ref, out_ref, rows_ref):
@@ -336,16 +344,16 @@
         gate = jnp.where(ls == s, table[:, 4 + s : 5 + s], gate)
     match = ((iota((128, SLOTS), 0) >> 3) == ln) & (code == (lr + 1).astype(F32))
     weight = jnp.where(match, gate, 0.0).astype(BF)
-    ext = jnp.concatenate([p[:, 3584:] for p in pieces], axis=0)
+    ext = jnp.concatenate([p[:, A_WIDTH:] for p in pieces], axis=0)
     terms = dot(onehot(match).astype(BF), ext)
-    terms = jnp.concatenate([terms, jnp.zeros((128, 512 - EXT), F32)], axis=1)
-    for q in range(7):
-        total = dot(weight, jnp.concatenate([p[:, 512 * q : 512 * (q + 1)] for p in pieces], axis=0))
+    terms = jnp.concatenate([terms, jnp.zeros((128, A_CHUNK - EXT), F32)], axis=1)
+    for q in range(A_PARTS):
+        total = dot(weight, jnp.concatenate([p[:, A_CHUNK * q : A_CHUNK * (q + 1)] for p in pieces], axis=0))
         for n in range(N_NODE):
-            at = 40 * n + 5 * q
+            at = A_BLOCK * n + 5 * q
             rows_ref[at : at + 8, :] = total[8 * n : 8 * n + 8]
     for n in range(N_NODE):
-        rows_ref[40 * n + 35 : 40 * n + 40, :] = terms[8 * n : 8 * n + 5]
+        rows_ref[A_BLOCK * (n + 1) - 5 : A_BLOCK * (n + 1), :] = terms[8 * n : 8 * n + 5]
     out_ref[...] = rows_ref[...].astype(BF)
 
 
@@ -353,22 +361,22 @@
     y = place_ref[1]
     routes = by_token(routes_ref[...])
     ncode = node_codes(route_tables(routes, 128))
-    col = iota((128, ROWS_N), 1)
-    spread = onehot(div40(col) == iota((128, ROWS_N), 0)).astype(BF)
+    col = iota((128, ROWS_A), 1)
+    spread = onehot(div5(col >> 4) == iota((128, ROWS_A), 0)).astype(BF)
     code = dot(ncode.astype(BF), spread)
-    col = iota((TOK, ROWS_N), 1)
-    cn = div40(col)
-    cp = col - 40 * cn
+    col = iota((TOK, ROWS_A), 1)
+    cn = div5(col >> 4)
+    cp = col - A_BLOCK * cn
     cq = div5(cp)
     match = code == (cp - 5 * cq + 1).astype(F32)
-    pick = jnp.concatenate([onehot(match & (cq == q)) for q in range(7)], axis=0).astype(BF)
+    pick = jnp.concatenate([onehot(match & (cq == q)) for q in range(A_PARTS)], axis=0).astype(BF)
     total = dot(pick, a_ref[...]).astype(BF)
-    for q in range(7):
-        dx_ref[:, 512 * q : 512 * (q + 1)] = total[TOK * q : TOK * (q + 1)]
+    for q in range(A_PARTS):
+        dx_ref[:, A_CHUNK * q : A_CHUNK * (q + 1)] = total[TOK * q : TOK * (q + 1)]
     total = b0_ref[...].astype(F32) + b1_ref[...].astype(F32)
     total = total + b2_ref[...].astype(F32) + b3_ref[...].astype(F32)
-    dx_ref[:, 3584:] = total.astype(BF)
-    last = match & (cq == 7)
+    dx_ref[:, A_WIDTH:] = total.astype(BF)
+    last = match & (cq == A_PARTS)
     picks = routes.astype(I32)
     masks = jnp.concatenate(
         [onehot(last & (cn == (picks[:, k : k + 1] >> 2))) for k in range(8)], axis=0
@@ -479,33 +487,33 @@
             "dx",
         )(d_gate, d_up, gate_near, up_near, ext)
 
-    own_a, other_a = dx(0, 3584 + EXT)
-    own_b, other_b = dx(1, 3584)
+    own_a, other_a = dx(0, A_WIDTH + EXT)
+    own_b, other_b = dx(1, B_WIDTH)
     got_a = swap_core(other_a)
     got_b = swap_core(other_b)
     *pieces, mark = whole(
         add_kernel,
-        [sds((ROWS_Y, 3584 + EXT))] * 4 + [sds((8, 128), F32)],
+        [sds((ROWS_Y, A_WIDTH + EXT))] * 4 + [sds((8, 128), F32)],
         [VM] * 2,
         "add_halves",
     )(own_a, got_a)
     pieces = [pieces[0]] + [shift_y(pieces[s], -s) for s in (1, 2, 3)]
     sent_b, mark = whole(
-        add_to_nodes_kernel, [sds((384, 1792)), sds((8, 128), F32)], [VM] * 3, "add_to_nodes"
+        add_to_nodes_kernel, [sds((384, B_HALF)), sds((8, 128), F32)], [VM] * 3, "add_to_nodes"
     )(own_b, got_b, mark)
     table = whole(table_kernel, sds((128, 128), F32), [SMEM, VM, VM], "table")(place, meta, mark)
     back_b = node_exchange(sent_b)
     mixed = whole(
         combine_kernel,
-        sds((ROWS_N, 512)),
+        sds((ROWS_A, A_CHUNK)),
         [VM] * 5,
         "combine",
-        [pltpu.VMEM((ROWS_N, 512), F32)],
+        [pltpu.VMEM((ROWS_A, A_CHUNK), F32)],
         pl.CostEstimate(flops=20_000_000_000, bytes_accessed=70_000_000, transcendentals=0),
     )(table, *pieces)
     mixed, back_b = lax.optimization_barrier((mixed, back_b))
     back_a = node_exchange(mixed)
-    near = whole(combine_near_kernel, [sds((TOK, 3584))] * 4, [SMEM] + [VM] * 5, "combine_near")(
+    near = whole(combine_near_kernel, [sds((TOK, B_WIDTH))] * 4, [SMEM] + [VM] * 5, "combine_near")(
         place, *x_near, back_b
     )
     near = [near[0]] + [shift_y(near[s], -s) for s in (1, 2, 3)]

time: 155 us -> 154 us (level)
    all_to_all x4, waiting for transfers between devices: 9.83 us -> 7.45 us  [node_exchange(): lax.all_to_all(v, 'node', split_axis=0, concat_axis=0, tiled=True)]
    unnamed x12 -> x10, local copies, waits for them, and re-layouts: 5.45 us -> 4.62 us
  transfers between devices with their start and end apart: 23 -> 23, of which waited for: 14 -> 14; matrix products, arithmetic and copies ran while one was open for 0% -> 0% of each run, Pallas kernels for 20% -> 21%
where the time goes in v8:
time: 154 us; the launch traced here: 153 us
  waiting for transfers between devices  59.2 us (38%)
  Pallas kernels  45.3 us (29%)
  starting transfers between devices  42.8 us (28%)
  local copies, waits for them, and re-layouts  4.79 us (3%)
    ppermute x12, waiting for transfers between devices, shift_y(): return lax.ppermute(v, 'local', [(i, (i + 2 * s) % 8) for i in range(8)])  48.2 us
    all_to_all x4, starting transfers between devices, node_exchange(): lax.all_to_all(v, 'node', split_axis=0, concat_axis=0, tiled=True)  24.9 us
    ppermute x12, starting transfers between devices, shift_y(): return lax.ppermute(v, 'local', [(i, (i + 2 * s) % 8) for i in range(8)])  16.1 us
    pallas_call x1, Pallas kernels, on_device(): whole(forward_own_kernel, [sds((SLOTS, HALF), F32)] * 2 + [sds((WIDTH, HA...  8.42 us
    all_to_all x4, waiting for transfers between devices, node_exchange(): lax.all_to_all(v, 'node', split_axis=0, concat_axis=0, tiled=True)  7.45 us
    pallas_call x2, Pallas kernels, dx(): whole(functools.partial(dx_kernel, part), [sds((SLOTS, width))] * 2, [VM]...  6.09 us
    pallas_call x1, Pallas kernels, on_device(): whole(forward_kernel, [sds((2 * SLOTS, HALF)), sds((2 * SLOTS, HALF)), sd...  4.81 us
    unnamed x10, local copies, waits for them, and re-layouts  4.62 us
  transfers between devices with their start and end apart: 23, of which 14 were waited for; matrix products, arithmetic and copies ran while one was open for 0% of the time, Pallas kernels for 21%

profile of v8, /device:TPU:0, one launch (start us, length us, event | category | flops | bytes accessed | tf_op | source)
XLA Modules:
  0.0 153.2 jit_solution(6241407316816207387)
XLA Ops:
  0.6 3.2 %send_dy.1 = bf16[640,1024]{1,0:T(8,128)(2,1)} custom-call(s32[8,16]{1,0:T(8,128)} %bitcast.22, f32[8,16]{1,0:T(8,128)} %bitcast.27, bf16[16,7168]{1,0:T(8,128)(2,1)} %dy_ref.1), custom_call_target="tpu_custom_call" | custom-call | tf_op jit(solution)/shard_map/send_dy/pallas_call | solution.py:436
  3.8 8.1 %all-to-all-start = ((bf16[16,40,1024]{2,1,0:T(8,128)(2,1)}), bf16[16,40,1024]{2,1,0:T(8,128)(2,1)S(1)}, u32[]{:S(2)}, u32[]{:S(2)}) async-start(bf16[16,40,1024]{2,1,0:T(8,128)(2,1)} %bitcast.26), calls=%async_computation | async-start | bytes 2621440 | tf_op jit(solution)/shard_map/all_to_all | solution.py:427
  12.2 3.1 %collective-permute-start.2 = (bf16[16,7296]{1,0:T(8,128)(2,1)S(1)}, bf16[16,7296]{1,0:T(8,128)(2,1)S(1)}, u32[]{:S(2)}, u32[]{:S(2)}) collective-permute-start(bf16[16,7296]{1,0:T(8,128)(2,1)S(1)} %pad_maximum_fusion.x0_ref), channel_id=1, source_target_pairs={{0,6},{1,7},{2,0},{3,1},{4,2},{5,3},{6,4},{7,5},{8,14},{9,15},{10,... | collective-permute-start | bytes 700424 | tf_op jit(solution)/shard_map/ppermute | solution.py:417
  17.0 8.0 %collective-permute-done.2.x3_ref = bf16[16,7296]{1,0:T(8,128)(2,1)S(1)} collective-permute-done((bf16[16,7296]{1,0:T(8,128)(2,1)S(1)}, bf16[16,7296]{1,0:T(8,128)(2,1)S(1)}, u32[]{:S(2)}, u32[]{:S(2)}) %collective-permute-start.2) | collective-permute-done | bytes 233504 | tf_op jit(solution)/shard_map/ppermute | solution.py:417
  25.5 3.2 %collective-permute-done.x1_ref = bf16[16,7296]{1,0:T(8,128)(2,1)S(1)} collective-permute-done((bf16[16,7296]{1,0:T(8,128)(2,1)S(1)}, bf16[16,7296]{1,0:T(8,128)(2,1)S(1)}, u32[]{:S(2)}, u32[]{:S(2)}) %collective-permute-start) | collective-permute-done | bytes 233504 | tf_op jit(solution)/shard_map/ppermute | solution.py:417
  28.7 1.8 %send_x.1 = bf16[384,3584]{1,0:T(8,128)(2,1)S(1)} custom-call(s32[2]{0:T(128)S(1)} %pad_add_fusion.place_ref, bf16[16,7296]{1,0:T(8,128)(2,1)S(1)} %pad_maximum_fusion.x0_ref, bf16[16,7296]{1,0:T(8,128)(2,1)S(1)} %collective-permute-done.x1_ref, bf16[16,7296]{1,0:T(8,128)(2,1)S(1)} %collective-permute-done.1.x2_ref, ...), custom_call_target="tpu_custom_call" | custom-call | tf_op jit(solution)/shard_map/send_x/pallas_call | solution.py:445
  30.5 1.5 copy-done
  32.7 6.3 %all-to-all-start.1 = ((bf16[16,24,3584]{2,1,0:T(8,128)(2,1)}), bf16[16,24,3584]{2,1,0:T(8,128)(2,1)}, u32[]{:S(2)}, u32[]{:S(2)}) async-start(bf16[16,24,3584]{2,1,0:T(8,128)(2,1)} %bitcast.18), calls=%async_computation.1 | async-start | bytes 5505024 | tf_op jit(solution)/shard_map/all_to_all | solution.py:427
  39.0 2.6 %regroup.1 = (bf16[48,7168]{1,0:T(8,128)(2,1)S(1)}, bf16[48,7168]{1,0:T(8,128)(2,1)S(1)}, bf16[48,7168]{1,0:T(8,128)(2,1)S(1)}, bf16[640,256]{1,0:T(8,128)(2,1)S(1)}) custom-call(s32[2]{0:T(128)S(1)} %pad_add_fusion.place_ref, bf16[640,1024]{1,0:T(8,128)(2,1)S(1)} %bitcast.16), custom_call_target="tpu_custom_call" | custom-call | tf_op jit(solution)/shard_map/regroup/pallas_call | solution.py:447
  41.7 2.6 %collective-permute-start.4 = (bf16[48,7168]{1,0:T(8,128)(2,1)S(1)}, bf16[48,7168]{1,0:T(8,128)(2,1)S(1)}, u32[]{:S(2)}, u32[]{:S(2)}) collective-permute-start(bf16[48,7168]{1,0:T(8,128)(2,1)S(1)} %get-tuple-element.43), channel_id=1, source_target_pairs={{0,4},{1,5},{2,6},{3,7},{4,0},{5,1},{6,2},{7,3},{8,12},{9,13},{10,... | collective-permute-start | bytes 2064392 | tf_op jit(solution)/shard_map/ppermute | solution.py:417
  45.7 3.1 %copy-done.1 = bf16[1,512,7168]{2,1,0:T(8,128)(2,1)S(1)} copy-done((bf16[1,512,7168]{2,1,0:T(8,128)(2,1)S(1)}, bf16[1,512,7168]{2,1,0:T(8,128)(2,1)}, u32[]{:S(2)}) %copy-start.1) | copy-done | bytes 7340056
  48.8 4.1 %regroup_own.1 = (bf16[48,7168]{1,0:T(8,128)(2,1)S(1)}, bf16[512,7168]{1,0:T(8,128)(2,1)S(1)}) custom-call(s32[2]{0:T(128)S(1)} %pad_add_fusion.place_ref, bf16[640,1024]{1,0:T(8,128)(2,1)S(1)} %bitcast.17, bf16[512,7168]{1,0:T(8,128)(2,1)S(1)} %bitcast.19), custom_call_target="tpu_custom_call" | custom-call | tf_op jit(solution)/shard_map/regroup_own/pallas_call | solution.py:453
  53.0 21.8 %collective-permute-done.3.refs_1_ = bf16[48,7168]{1,0:T(8,128)(2,1)S(1)} collective-permute-done((bf16[48,7168]{1,0:T(8,128)(2,1)S(1)}, bf16[48,7168]{1,0:T(8,128)(2,1)S(1)}, u32[]{:S(2)}, u32[]{:S(2)}) %collective-permute-start.3) | collective-permute-done | bytes 688160 | tf_op jit(solution)/shard_map/ppermute | solution.py:417
  75.4 1.5 collective-permute-done.7.refs_5_
  78.9 3.0 %back.1.mark_ref.back_ref = f32[384,512]{1,0:T(8,128)S(1)} custom-call(bf16[48,7168]{1,0:T(8,128)(2,1)S(1)} %get-tuple-element.41.refs_0_, bf16[48,7168]{1,0:T(8,128)(2,1)S(1)} %collective-permute-done.3.refs_1_, bf16[48,7168]{1,0:T(8,128)(2,1)S(1)} %collective-permute-done.4.refs_2_, bf16[48,7168]{1,0:T(8,128)(2,1)S(1)} %collective-permute-done.5.refs_3_, ...), custom_call_target="tpu_custom_call" | custom-call | tf_op jit(solution)/shard_map/back/pallas_call | solution.py:463
  82.3 8.4 %forward_own.1 = (f32[192,512]{1,0:T(8,128)S(1)}, f32[192,512]{1,0:T(8,128)S(1)}, bf16[7168,512]{1,0:T(8,128)(2,1)S(1)}, bf16[7168,512]{1,0:T(8,128)(2,1)S(1)}) custom-call(bf16[384,3584]{1,0:T(8,128)(2,1)} %bitcast.7.x_ref, bf16[7168,512]{1,0:T(8,128)(2,1)} %bitcast.24, bf16[7168,512]{1,0:T(8,128)(2,1)} %bitcast.25, f32[384,512]{1,0:T(8,128)S(1)} %back.1.mark_ref.back_ref), custom_call_target="tpu_custom_call" | custom-call | tf_op jit(solution)/shard_map/forward_own/pallas_call | solution.py:468
  90.8 4.8 %forward.1 = (bf16[384,512]{1,0:T(8,128)(2,1)S(1)}, bf16[384,512]{1,0:T(8,128)(2,1)S(1)}, bf16[384,128]{1,0:T(8,128)(2,1)S(1)}) custom-call(bf16[384,3584]{1,0:T(8,128)(2,1)S(1)} %collective-permute-done.10.x_ref, bf16[7168,512]{1,0:T(8,128)(2,1)S(1)} %get-tuple-element.48.gate_ref, bf16[7168,512]{1,0:T(8,128)(2,1)S(1)} %get-tuple-element.49.up_ref, ...), custom_call_target="tpu_custom_call" | custom-call | tf_op jit(solution)/shard_map/forward/pallas_call | solution.py:475
  95.6 3.3 %dx.3 = (bf16[192,3968]{1,0:T(8,128)(2,1)S(1)}, bf16[192,3968]{1,0:T(8,128)(2,1)S(1)}) custom-call(bf16[384,512]{1,0:T(8,128)(2,1)S(1)} %get-tuple-element.52.dgate_ref, bf16[384,512]{1,0:T(8,128)(2,1)S(1)} %get-tuple-element.53.dup_ref, bf16[7168,512]{1,0:T(8,128)(2,1)S(1)} %get-tuple-element.48.gate_ref, bf16[7168,512]{1,0:T(8,128)(2,1)S(1)} %get-tuple-element.49.up_ref, ...), custom_call_target="tpu_custom_call" | custom-call | tf_op jit(solution)/shard_map/dx/pallas_call | solution.py:483
  99.3 2.8 %dx.2 = (bf16[192,3328]{1,0:T(8,128)(2,1)S(1)}, bf16[192,3328]{1,0:T(8,128)(2,1)S(1)}) custom-call(bf16[384,512]{1,0:T(8,128)(2,1)S(1)} %get-tuple-element.52.dgate_ref, bf16[384,512]{1,0:T(8,128)(2,1)S(1)} %get-tuple-element.53.dup_ref, bf16[7168,512]{1,0:T(8,128)(2,1)S(1)} %get-tuple-element.48.gate_ref, bf16[7168,512]{1,0:T(8,128)(2,1)S(1)} %get-tuple-element.49.up_ref, ...), custom_call_target="tpu_custom_call" | custom-call | tf_op jit(solution)/shard_map/dx/pallas_call | solution.py:483
  102.6 1.4 add_halves.1
  106.1 2.1 %add_to_nodes.1 = (bf16[384,1664]{1,0:T(8,128)(2,1)}, f32[8,128]{1,0:T(8,128)S(1)}) custom-call(bf16[192,3328]{1,0:T(8,128)(2,1)S(1)} %get-tuple-element.55.own_ref, bf16[192,3328]{1,0:T(8,128)(2,1)S(1)} %collective-permute-done.11.got_ref, f32[8,128]{1,0:T(8,128)S(1)} %get-tuple-element.59.mark_ref), custom_call_target="tpu_custom_call" | custom-call | tf_op jit(solution)/shard_map/add_to_nodes/pallas_call | solution.py:501
  108.2 6.9 %all-to-all-start.2 = ((bf16[16,24,1664]{2,1,0:T(8,128)(2,1)}), bf16[16,24,1664]{2,1,0:T(8,128)(2,1)S(1)}, u32[]{:S(2)}, u32[]{:S(2)}) async-start(bf16[16,24,1664]{2,1,0:T(8,128)(2,1)} %bitcast.11), calls=%async_computation.2 | async-start | bytes 2555904 | tf_op jit(solution)/shard_map/all_to_all | solution.py:427
  116.1 2.5 %collective-permute-done.14.p2_ref = bf16[48,3968]{1,0:T(8,128)(2,1)} collective-permute-done((bf16[48,3968]{1,0:T(8,128)(2,1)}, bf16[48,3968]{1,0:T(8,128)(2,1)}, u32[]{:S(2)}, u32[]{:S(2)}) %collective-permute-start.14) | collective-permute-done | bytes 380960 | tf_op jit(solution)/shard_map/ppermute | solution.py:417
  118.6 7.3 %collective-permute-done.15.p3_ref = bf16[48,3968]{1,0:T(8,128)(2,1)} collective-permute-done((bf16[48,3968]{1,0:T(8,128)(2,1)}, bf16[48,3968]{1,0:T(8,128)(2,1)}, u32[]{:S(2)}, u32[]{:S(2)}) %collective-permute-start.15) | collective-permute-done | bytes 380960 | tf_op jit(solution)/shard_map/ppermute | solution.py:417
  125.9 2.8 %combine.1 = bf16[1280,256]{1,0:T(8,128)(2,1)} custom-call(f32[128,128]{1,0:T(8,128)S(1)} %table.1.table_ref, bf16[48,3968]{1,0:T(8,128)(2,1)S(1)} %get-tuple-element.61.p0_ref, bf16[48,3968]{1,0:T(8,128)(2,1)} %collective-permute-done.13.p1_ref, bf16[48,3968]{1,0:T(8,128)(2,1)} %collective-permute-done.14.p2_ref, ...), custom_call_target="tpu_custom_call" | custom-call | flops 20000000000 | bytes 70000000 | tf_op jit(solution)/shard_map/combine/pallas_call | solution.py:506
  128.7 6.8 %all-to-all-done.2 = bf16[16,24,1664]{2,1,0:T(8,128)(2,1)S(1)} async-done(((bf16[16,24,1664]{2,1,0:T(8,128)(2,1)}), bf16[16,24,1664]{2,1,0:T(8,128)(2,1)S(1)}, u32[]{:S(2)}, u32[]{:S(2)}) %all-to-all-start.2) | async-done | bytes 1277984 | tf_op jit(solution)/shard_map/all_to_all | solution.py:427
  135.5 3.6 %all-to-all-start.3 = ((bf16[16,80,256]{2,1,0:T(8,128)(2,1)}), bf16[16,80,256]{2,1,0:T(8,128)(2,1)S(1)}, u32[]{:S(2)}, u32[]{:S(2)}) async-start(bf16[16,80,256]{2,1,0:T(8,128)(2,1)} %bitcast.13), calls=%async_computation.3 | async-start | bytes 1310720 | tf_op jit(solution)/shard_map/all_to_all | solution.py:427
  139.1 1.5 combine_near.1
  140.6 2.7 %collective-permute-start.16 = (bf16[16,3328]{1,0:T(8,128)(2,1)S(1)}, bf16[16,3328]{1,0:T(8,128)(2,1)S(1)}, u32[]{:S(2)}, u32[]{:S(2)}) collective-permute-start(bf16[16,3328]{1,0:T(8,128)(2,1)S(1)} %get-tuple-element.69), channel_id=1, source_target_pairs={{0,6},{1,7},{2,0},{3,1},{4,2},{5,3},{6,4},{7,5},{8,14},{9,15},{10,... | collective-permute-start | bytes 319496 | tf_op jit(solution)/shard_map/ppermute | solution.py:417
  143.3 1.5 collective-permute-start.17
  145.9 3.7 %collective-permute-done.17.b2_ref = bf16[16,3328]{1,0:T(8,128)(2,1)S(1)} collective-permute-done((bf16[16,3328]{1,0:T(8,128)(2,1)S(1)}, bf16[16,3328]{1,0:T(8,128)(2,1)S(1)}, u32[]{:S(2)}, u32[]{:S(2)}) %collective-permute-start.17) | collective-permute-done | bytes 106528 | tf_op jit(solution)/shard_map/ppermute | solution.py:417
  150.8 2.4 %finish.1 = (bf16[16,7168]{1,0:T(8,128)(2,1)}, f32[8,16]{1,0:T(8,128)}) custom-call(s32[2]{0:T(128)S(1)} %pad_add_fusion.place_ref, s32[8,16]{1,0:T(8,128)S(1)} %bitcast.23, bf16[1280,256]{1,0:T(8,128)(2,1)S(1)} %bitcast.21, bf16[16,3328]{1,0:T(8,128)(2,1)S(1)} %get-tuple-element.68.b0_ref, bf16[16,3328]{1,0:T(8,128)(2,1)S(1)} %collective-permute-done.16.b1_ref, ...), custom_call_target="tpu_custom_call" | custom-call | tf_op jit(solution)/shard_map/finish/pallas_call | solution.py:520
  (46 shorter events, 13.8 us)
Async XLA Ops:
  3.8 8.1 %copy-start.2 = (s32[16,8]{0,1:T(8,128)S(1)}, s32[16,8]{0,1:T(8,128)}, u32[]{:S(2)}) copy-start(s32[16,8]{0,1:T(8,128)} %param.9) | copy-start | bytes 1540
  3.8 8.1 %copy-start.4 = (f32[16,8]{0,1:T(8,128)S(1)}, f32[16,8]{0,1:T(8,128)}, u32[]{:S(2)}) copy-start(f32[16,8]{0,1:T(8,128)} %param.10) | copy-start | bytes 1540
  3.8 8.4 %copy-start.3 = (bf16[16,7168]{1,0:T(8,128)(2,1)S(1)}, bf16[16,7168]{1,0:T(8,128)(2,1)}, u32[]{:S(2)}) copy-start(bf16[16,7168]{1,0:T(8,128)(2,1)} %param.7) | copy-start | bytes 688132
  3.8 28.9 %all-to-all-start = ((bf16[16,40,1024]{2,1,0:T(8,128)(2,1)}), bf16[16,40,1024]{2,1,0:T(8,128)(2,1)S(1)}, u32[]{:S(2)}, u32[]{:S(2)}) async-start(bf16[16,40,1024]{2,1,0:T(8,128)(2,1)} %bitcast.26), calls=%async_computation | async-start | bytes 2621440 | tf_op jit(solution)/shard_map/all_to_all | solution.py:427
  12.2 12.8 %collective-permute-start.2 = (bf16[16,7296]{1,0:T(8,128)(2,1)S(1)}, bf16[16,7296]{1,0:T(8,128)(2,1)S(1)}, u32[]{:S(2)}, u32[]{:S(2)}) collective-permute-start(bf16[16,7296]{1,0:T(8,128)(2,1)S(1)} %pad_maximum_fusion.x0_ref), channel_id=1, source_target_pairs={{0,6},{1,7},{2,0},{3,1},{4,2},{5,3},{6,4},{7,5},{8,14},{9,15},{10,... | collective-permute-start | bytes 700424 | tf_op jit(solution)/shard_map/ppermute | solution.py:417
  15.3 10.2 %collective-permute-start.1 = (bf16[16,7296]{1,0:T(8,128)(2,1)S(1)}, bf16[16,7296]{1,0:T(8,128)(2,1)S(1)}, u32[]{:S(2)}, u32[]{:S(2)}) collective-permute-start(bf16[16,7296]{1,0:T(8,128)(2,1)S(1)} %pad_maximum_fusion.x0_ref), channel_id=1, source_target_pairs={{0,4},{1,5},{2,6},{3,7},{4,0},{5,1},{6,2},{7,3},{8,12},{9,13},{10,... | collective-permute-start | bytes 700424 | tf_op jit(solution)/shard_map/ppermute | solution.py:417
  16.0 12.7 %collective-permute-start = (bf16[16,7296]{1,0:T(8,128)(2,1)S(1)}, bf16[16,7296]{1,0:T(8,128)(2,1)S(1)}, u32[]{:S(2)}, u32[]{:S(2)}) collective-permute-start(bf16[16,7296]{1,0:T(8,128)(2,1)S(1)} %pad_maximum_fusion.x0_ref), channel_id=1, source_target_pairs={{0,2},{1,3},{2,4},{3,5},{4,6},{5,7},{6,0},{7,1},{8,10},{9,11},{10,... | collective-permute-start | bytes 700424 | tf_op jit(solution)/shard_map/ppermute | solution.py:417
  30.5 1.5 %copy-start = (bf16[384,3584]{1,0:T(8,128)(2,1)}, bf16[384,3584]{1,0:T(8,128)(2,1)S(1)}, u32[]{:S(2)}) copy-start(bf16[384,3584]{1,0:T(8,128)(2,1)S(1)} %send_x.1) | copy-start | bytes 8257540
  32.7 49.2 %all-to-all-start.1 = ((bf16[16,24,3584]{2,1,0:T(8,128)(2,1)}), bf16[16,24,3584]{2,1,0:T(8,128)(2,1)}, u32[]{:S(2)}, u32[]{:S(2)}) async-start(bf16[16,24,3584]{2,1,0:T(8,128)(2,1)} %bitcast.18), calls=%async_computation.1 | async-start | bytes 5505024 | tf_op jit(solution)/shard_map/all_to_all | solution.py:427
  41.7 33.1 %collective-permute-start.3 = (bf16[48,7168]{1,0:T(8,128)(2,1)S(1)}, bf16[48,7168]{1,0:T(8,128)(2,1)S(1)}, u32[]{:S(2)}, u32[]{:S(2)}) collective-permute-start(bf16[48,7168]{1,0:T(8,128)(2,1)S(1)} %get-tuple-element.42), channel_id=1, source_target_pairs={{0,2},{1,3},{2,4},{3,5},{4,6},{5,7},{6,0},{7,1},{8,10},{9,11},{10,... | collective-permute-start | bytes 2064392 | tf_op jit(solution)/shard_map/ppermute | solution.py:417
  41.7 33.0 %collective-permute-start.4 = (bf16[48,7168]{1,0:T(8,128)(2,1)S(1)}, bf16[48,7168]{1,0:T(8,128)(2,1)S(1)}, u32[]{:S(2)}, u32[]{:S(2)}) collective-permute-start(bf16[48,7168]{1,0:T(8,128)(2,1)S(1)} %get-tuple-element.43), channel_id=1, source_target_pairs={{0,4},{1,5},{2,6},{3,7},{4,0},{5,1},{6,2},{7,3},{8,12},{9,13},{10,... | collective-permute-start | bytes 2064392 | tf_op jit(solution)/shard_map/ppermute | solution.py:417
  44.4 31.0 %collective-permute-start.5 = (bf16[48,7168]{1,0:T(8,128)(2,1)S(1)}, bf16[48,7168]{1,0:T(8,128)(2,1)S(1)}, u32[]{:S(2)}, u32[]{:S(2)}) collective-permute-start(bf16[48,7168]{1,0:T(8,128)(2,1)S(1)} %get-tuple-element.44), channel_id=1, source_target_pairs={{0,6},{1,7},{2,0},{3,1},{4,2},{5,3},{6,4},{7,5},{8,14},{9,15},{10,... | collective-permute-start | bytes 2064392 | tf_op jit(solution)/shard_map/ppermute | solution.py:417
  45.7 3.1 %copy-start.1 = (bf16[1,512,7168]{2,1,0:T(8,128)(2,1)S(1)}, bf16[1,512,7168]{2,1,0:T(8,128)(2,1)}, u32[]{:S(2)}) copy-start(bf16[1,512,7168]{2,1,0:T(8,128)(2,1)} %param.13) | copy-start | bytes 22020100
  52.9 22.5 %collective-permute-start.6 = (bf16[48,7168]{1,0:T(8,128)(2,1)S(1)}, bf16[48,7168]{1,0:T(8,128)(2,1)S(1)}, u32[]{:S(2)}, u32[]{:S(2)}) collective-permute-start(bf16[48,7168]{1,0:T(8,128)(2,1)S(1)} %get-tuple-element.41.refs_0_), channel_id=1, source_target_pairs={{0,1},{1,0},{2,3},{3,2},{4,5},{5,4},{6,7},{7,6},{8,9},{9,8},{10,11... | collective-permute-start | bytes 2064392 | tf_op jit(solution)/shard_map/ppermute | solution.py:421
  74.8 2.1 %collective-permute-start.7 = (bf16[48,7168]{1,0:T(8,128)(2,1)S(1)}, bf16[48,7168]{1,0:T(8,128)(2,1)S(1)}, u32[]{:S(2)}, u32[]{:S(2)}) collective-permute-start(bf16[48,7168]{1,0:T(8,128)(2,1)S(1)} %collective-permute-done.3.refs_1_), channel_id=1, source_target_pairs={{0,1},{1,0},{2,3},{3,2},{4,5},{5,4},{6,7},{7,6},{8,9},{9,8},{10,11... | collective-permute-start | bytes 2064392 | tf_op jit(solution)/shard_map/ppermute | solution.py:421
  74.8 3.1 %collective-permute-start.8 = (bf16[48,7168]{1,0:T(8,128)(2,1)S(1)}, bf16[48,7168]{1,0:T(8,128)(2,1)S(1)}, u32[]{:S(2)}, u32[]{:S(2)}) collective-permute-start(bf16[48,7168]{1,0:T(8,128)(2,1)S(1)} %collective-permute-done.4.refs_2_), channel_id=1, source_target_pairs={{0,1},{1,0},{2,3},{3,2},{4,5},{5,4},{6,7},{7,6},{8,9},{9,8},{10,11... | collective-permute-start | bytes 2064392 | tf_op jit(solution)/shard_map/ppermute | solution.py:421
  75.4 3.5 %collective-permute-start.9 = (bf16[48,7168]{1,0:T(8,128)(2,1)S(1)}, bf16[48,7168]{1,0:T(8,128)(2,1)S(1)}, u32[]{:S(2)}, u32[]{:S(2)}) collective-permute-start(bf16[48,7168]{1,0:T(8,128)(2,1)S(1)} %collective-permute-done.5.refs_3_), channel_id=1, source_target_pairs={{0,1},{1,0},{2,3},{3,2},{4,5},{5,4},{6,7},{7,6},{8,9},{9,8},{10,11... | collective-permute-start | bytes 2064392 | tf_op jit(solution)/shard_map/ppermute | solution.py:421
  81.9 8.8 %collective-permute-start.10 = (bf16[384,3584]{1,0:T(8,128)(2,1)}, bf16[384,3584]{1,0:T(8,128)(2,1)S(1)}, u32[]{:S(2)}, u32[]{:S(2)}) collective-permute-start(bf16[384,3584]{1,0:T(8,128)(2,1)} %bitcast.7.x_ref), channel_id=1, source_target_pairs={{0,1},{1,0},{2,3},{3,2},{4,5},{5,4},{6,7},{7,6},{8,9},{9,8},{10,11... | collective-permute-start | bytes 8257544 | tf_op jit(solution)/shard_map/ppermute | solution.py:421
  98.9 3.7 %collective-permute-start.12 = (bf16[192,3968]{1,0:T(8,128)(2,1)S(1)}, bf16[192,3968]{1,0:T(8,128)(2,1)S(1)}, u32[]{:S(2)}, u32[]{:S(2)}) collective-permute-start(bf16[192,3968]{1,0:T(8,128)(2,1)S(1)} %get-tuple-element.58), channel_id=1, source_target_pairs={{0,1},{1,0},{2,3},{3,2},{4,5},{5,4},{6,7},{7,6},{8,9},{9,8},{10,11... | collective-permute-start | bytes 4571144 | tf_op jit(solution)/shard_map/ppermute | solution.py:421
  102.2 3.9 %collective-permute-start.11 = (bf16[192,3328]{1,0:T(8,128)(2,1)S(1)}, bf16[192,3328]{1,0:T(8,128)(2,1)S(1)}, u32[]{:S(2)}, u32[]{:S(2)}) collective-permute-start(bf16[192,3328]{1,0:T(8,128)(2,1)S(1)} %get-tuple-element.56), channel_id=1, source_target_pairs={{0,1},{1,0},{2,3},{3,2},{4,5},{5,4},{6,7},{7,6},{8,9},{9,8},{10,11... | collective-permute-start | bytes 3833864 | tf_op jit(solution)/shard_map/ppermute | solution.py:421
  104.0 12.1 %collective-permute-start.13 = (bf16[48,3968]{1,0:T(8,128)(2,1)}, bf16[48,3968]{1,0:T(8,128)(2,1)}, u32[]{:S(2)}, u32[]{:S(2)}) collective-permute-start(bf16[48,3968]{1,0:T(8,128)(2,1)} %get-tuple-element.62), channel_id=1, source_target_pairs={{0,6},{1,7},{2,0},{3,1},{4,2},{5,3},{6,4},{7,5},{8,14},{9,15},{10,... | collective-permute-start | bytes 1142792 | tf_op jit(solution)/shard_map/ppermute | solution.py:417
  105.1 13.6 %collective-permute-start.14 = (bf16[48,3968]{1,0:T(8,128)(2,1)}, bf16[48,3968]{1,0:T(8,128)(2,1)}, u32[]{:S(2)}, u32[]{:S(2)}) collective-permute-start(bf16[48,3968]{1,0:T(8,128)(2,1)} %get-tuple-element.63), channel_id=1, source_target_pairs={{0,4},{1,5},{2,6},{3,7},{4,0},{5,1},{6,2},{7,3},{8,12},{9,13},{10,... | collective-permute-start | bytes 1142792 | tf_op jit(solution)/shard_map/ppermute | solution.py:417
  105.1 20.8 %collective-permute-start.15 = (bf16[48,3968]{1,0:T(8,128)(2,1)}, bf16[48,3968]{1,0:T(8,128)(2,1)}, u32[]{:S(2)}, u32[]{:S(2)}) collective-permute-start(bf16[48,3968]{1,0:T(8,128)(2,1)} %get-tuple-element.64), channel_id=1, source_target_pairs={{0,2},{1,3},{2,4},{3,5},{4,6},{5,7},{6,0},{7,1},{8,10},{9,11},{10,... | collective-permute-start | bytes 1142792 | tf_op jit(solution)/shard_map/ppermute | solution.py:417
  108.2 27.3 %all-to-all-start.2 = ((bf16[16,24,1664]{2,1,0:T(8,128)(2,1)}), bf16[16,24,1664]{2,1,0:T(8,128)(2,1)S(1)}, u32[]{:S(2)}, u32[]{:S(2)}) async-start(bf16[16,24,1664]{2,1,0:T(8,128)(2,1)} %bitcast.11), calls=%async_computation.2 | async-start | bytes 2555904 | tf_op jit(solution)/shard_map/all_to_all | solution.py:427
  135.5 15.3 %all-to-all-start.3 = ((bf16[16,80,256]{2,1,0:T(8,128)(2,1)}), bf16[16,80,256]{2,1,0:T(8,128)(2,1)S(1)}, u32[]{:S(2)}, u32[]{:S(2)}) async-start(bf16[16,80,256]{2,1,0:T(8,128)(2,1)} %bitcast.13), calls=%async_computation.3 | async-start | bytes 1310720 | tf_op jit(solution)/shard_map/all_to_all | solution.py:427
  140.6 5.3 %collective-permute-start.16 = (bf16[16,3328]{1,0:T(8,128)(2,1)S(1)}, bf16[16,3328]{1,0:T(8,128)(2,1)S(1)}, u32[]{:S(2)}, u32[]{:S(2)}) collective-permute-start(bf16[16,3328]{1,0:T(8,128)(2,1)S(1)} %get-tuple-element.69), channel_id=1, source_target_pairs={{0,6},{1,7},{2,0},{3,1},{4,2},{5,3},{6,4},{7,5},{8,14},{9,15},{10,... | collective-permute-start | bytes 319496 | tf_op jit(solution)/shard_map/ppermute | solution.py:417
  143.3 6.2 %collective-permute-start.17 = (bf16[16,3328]{1,0:T(8,128)(2,1)S(1)}, bf16[16,3328]{1,0:T(8,128)(2,1)S(1)}, u32[]{:S(2)}, u32[]{:S(2)}) collective-permute-start(bf16[16,3328]{1,0:T(8,128)(2,1)S(1)} %get-tuple-element.70), channel_id=1, source_target_pairs={{0,4},{1,5},{2,6},{3,7},{4,0},{5,1},{6,2},{7,3},{8,12},{9,13},{10,... | collective-permute-start | bytes 319496 | tf_op jit(solution)/shard_map/ppermute | solution.py:417
  144.9 5.9 %collective-permute-start.18 = (bf16[16,3328]{1,0:T(8,128)(2,1)S(1)}, bf16[16,3328]{1,0:T(8,128)(2,1)S(1)}, u32[]{:S(2)}, u32[]{:S(2)}) collective-permute-start(bf16[16,3328]{1,0:T(8,128)(2,1)S(1)} %get-tuple-element.71), channel_id=1, source_target_pairs={{0,2},{1,3},{2,4},{3,5},{4,6},{5,7},{6,0},{7,1},{8,10},{9,11},{10,... | collective-permute-start | bytes 319496 | tf_op jit(solution)/shard_map/ppermute | solution.py:417

commit v9 on v8

--- a/solution.py
+++ b/solution.py
@@ -194,7 +194,7 @@
 
 
 def back_kernel(*refs):
-    pieces, down_ref, out_ref = refs[:8], refs[8], refs[9]
+    pieces, down_ref, out_ref = refs[:4], refs[4], refs[5]
     rows = jnp.concatenate([p[...] for p in pieces], axis=0)
     out_ref[...] = dot_nt(rows, down_ref[...])
 
@@ -225,7 +225,7 @@
 
 
 def forward_kernel(
-    x_ref, gate_ref, up_ref, back_ref, pg_ref, pu_ref, dgate_ref, dup_ref, ext_ref
+    x_ref, gate_ref, up_ref, back_ref, back2_ref, pg_ref, pu_ref, dgate_ref, dup_ref, ext_ref
 ):
     pre_gate = jnp.zeros((SLOTS, HALF), F32)
     pre_up = jnp.zeros((SLOTS, HALF), F32)
@@ -236,7 +236,7 @@
         pre_up = pre_up + dot(rows, up_ref[at, :])
     pre_gate = jnp.concatenate([pg_ref[...], pre_gate], axis=0)
     pre_up = jnp.concatenate([pu_ref[...], pre_up], axis=0)
-    back = back_ref[...]
+    back = jnp.concatenate([back_ref[...], back2_ref[...]], axis=0)
     sig = jax.nn.sigmoid(pre_gate)
     act = pre_gate * sig
     hidden = (act * pre_up).astype(BF)
@@ -460,10 +460,10 @@
     x_mine = node_exchange(x_send)
     dy_mine = [dy_own] + [shift_y(dy_far[s - 1], s) for s in (1, 2, 3)]
     dy_other = [swap_core(v) for v in dy_mine]
-    back = whole(back_kernel, sds((2 * SLOTS, HALF), F32), [VM] * 9, "back")(
-        *dy_mine, *dy_other, down_near
-    )
-    x_mine, back = lax.optimization_barrier((x_mine, back))
+    back = whole(back_kernel, sds((SLOTS, HALF), F32), [VM] * 5, "back")
+    back_own = back(*dy_mine, down_near)
+    back_other = back(*dy_other, down_near)
+    x_mine, back_own, back_other = lax.optimization_barrier((x_mine, back_own, back_other))
     x_other = swap_core(x_mine)
     pre_gate, pre_up, gate_near, up_near = whole(
         forward_own_kernel,
@@ -471,13 +471,13 @@
         [VM, hbm, hbm, hbm],
         "forward_own",
         [pltpu.SemaphoreType.DMA((4, 4))],
-    )(x_mine, w_gate, w_up, back)
+    )(x_mine, w_gate, w_up, back_other)
     d_gate, d_up, ext = whole(
         forward_kernel,
         [sds((2 * SLOTS, HALF)), sds((2 * SLOTS, HALF)), sds((2 * SLOTS, EXT))],
-        [VM] * 6,
+        [VM] * 7,
         "forward",
-    )(x_other, gate_near, up_near, back, pre_gate, pre_up)
+    )(x_other, gate_near, up_near, back_own, back_other, pre_gate, pre_up)
 
     def dx(part, width):
         return whole(

time: 154 us -> 154 us (level)
  waiting for transfers between devices: 59.2 us -> 56.5 us
  Pallas kernels: 45.3 us -> 47.4 us
    ppermute x7, waiting for transfers between devices: 3.5 us -> 0.9 us  [swap_core(): return lax.ppermute(v, 'local', [(i, i ^ 1) for i in range(8)])]
    pallas_call x1 -> x2, Pallas kernels: 3.03 us -> 5.13 us  [the longest x1 2.57 us: on_device(): back_own = back(*dy_mine, down_near)]
  transfers between devices with their start and end apart: 23 -> 23, of which waited for: 14 -> 12; matrix products, arithmetic and copies ran while one was open for 0% -> 0% of each run, Pallas kernels for 21% -> 22%
where the time goes in v9:
time: 154 us; the launch traced here: 153 us
  waiting for transfers between devices  56.5 us (37%)
  Pallas kernels  47.4 us (31%)
  starting transfers between devices  43.3 us (28%)
  local copies, waits for them, and re-layouts  4.79 us (3%)
    ppermute x12, waiting for transfers between devices, shift_y(): return lax.ppermute(v, 'local', [(i, (i + 2 * s) % 8) for i in range(8)])  48.1 us
    all_to_all x4, starting transfers between devices, node_exchange(): lax.all_to_all(v, 'node', split_axis=0, concat_axis=0, tiled=True)  24.9 us
    ppermute x12, starting transfers between devices, shift_y(): return lax.ppermute(v, 'local', [(i, (i + 2 * s) % 8) for i in range(8)])  16.5 us
    pallas_call x1, Pallas kernels, on_device(): whole(forward_own_kernel, [sds((SLOTS, HALF), F32)] * 2 + [sds((WIDTH, HA...  8.42 us
    all_to_all x4, waiting for transfers between devices, node_exchange(): lax.all_to_all(v, 'node', split_axis=0, concat_axis=0, tiled=True)  7.5 us
    pallas_call x2, Pallas kernels, dx(): whole(functools.partial(dx_kernel, part), [sds((SLOTS, width))] * 2, [VM]...  6.09 us
    pallas_call x1, Pallas kernels, on_device(): whole(forward_kernel, [sds((2 * SLOTS, HALF)), sds((2 * SLOTS, HALF)), sd...  4.81 us
    unnamed x10, local copies, waits for them, and re-layouts  4.62 us
  transfers between devices with their start and end apart: 23, of which 12 were waited for; matrix products, arithmetic and copies ran while one was open for 0% of the time, Pallas kernels for 22%

profile of v9, /device:TPU:0, one launch (start us, length us, event | category | flops | bytes accessed | tf_op | source)
XLA Modules:
  0.0 153.0 jit_solution(12348147880235105109)
XLA Ops:
  0.6 3.2 %send_dy.1 = bf16[640,1024]{1,0:T(8,128)(2,1)} custom-call(s32[8,16]{1,0:T(8,128)} %bitcast.22, f32[8,16]{1,0:T(8,128)} %bitcast.27, bf16[16,7168]{1,0:T(8,128)(2,1)} %dy_ref.1), custom_call_target="tpu_custom_call" | custom-call | tf_op jit(solution)/shard_map/send_dy/pallas_call | solution.py:436
  3.8 8.1 %all-to-all-start = ((bf16[16,40,1024]{2,1,0:T(8,128)(2,1)}), bf16[16,40,1024]{2,1,0:T(8,128)(2,1)S(1)}, u32[]{:S(2)}, u32[]{:S(2)}) async-start(bf16[16,40,1024]{2,1,0:T(8,128)(2,1)} %bitcast.26), calls=%async_computation | async-start | bytes 2621440 | tf_op jit(solution)/shard_map/all_to_all | solution.py:427
  12.2 3.1 %collective-permute-start.2 = (bf16[16,7296]{1,0:T(8,128)(2,1)S(1)}, bf16[16,7296]{1,0:T(8,128)(2,1)S(1)}, u32[]{:S(2)}, u32[]{:S(2)}) collective-permute-start(bf16[16,7296]{1,0:T(8,128)(2,1)S(1)} %pad_maximum_fusion.x0_ref), channel_id=1, source_target_pairs={{0,6},{1,7},{2,0},{3,1},{4,2},{5,3},{6,4},{7,5},{8,14},{9,15},{10,... | collective-permute-start | bytes 700424 | tf_op jit(solution)/shard_map/ppermute | solution.py:417
  17.0 8.0 %collective-permute-done.2.x3_ref = bf16[16,7296]{1,0:T(8,128)(2,1)S(1)} collective-permute-done((bf16[16,7296]{1,0:T(8,128)(2,1)S(1)}, bf16[16,7296]{1,0:T(8,128)(2,1)S(1)}, u32[]{:S(2)}, u32[]{:S(2)}) %collective-permute-start.2) | collective-permute-done | bytes 233504 | tf_op jit(solution)/shard_map/ppermute | solution.py:417
  25.5 3.2 %collective-permute-done.x1_ref = bf16[16,7296]{1,0:T(8,128)(2,1)S(1)} collective-permute-done((bf16[16,7296]{1,0:T(8,128)(2,1)S(1)}, bf16[16,7296]{1,0:T(8,128)(2,1)S(1)}, u32[]{:S(2)}, u32[]{:S(2)}) %collective-permute-start) | collective-permute-done | bytes 233504 | tf_op jit(solution)/shard_map/ppermute | solution.py:417
  28.7 1.8 %send_x.1 = bf16[384,3584]{1,0:T(8,128)(2,1)S(1)} custom-call(s32[2]{0:T(128)S(1)} %pad_add_fusion.place_ref, bf16[16,7296]{1,0:T(8,128)(2,1)S(1)} %pad_maximum_fusion.x0_ref, bf16[16,7296]{1,0:T(8,128)(2,1)S(1)} %collective-permute-done.x1_ref, bf16[16,7296]{1,0:T(8,128)(2,1)S(1)} %collective-permute-done.1.x2_ref, ...), custom_call_target="tpu_custom_call" | custom-call | tf_op jit(solution)/shard_map/send_x/pallas_call | solution.py:445
  30.5 1.5 copy-done
  32.7 6.3 %all-to-all-start.1 = ((bf16[16,24,3584]{2,1,0:T(8,128)(2,1)}), bf16[16,24,3584]{2,1,0:T(8,128)(2,1)}, u32[]{:S(2)}, u32[]{:S(2)}) async-start(bf16[16,24,3584]{2,1,0:T(8,128)(2,1)} %bitcast.18), calls=%async_computation.1 | async-start | bytes 5505024 | tf_op jit(solution)/shard_map/all_to_all | solution.py:427
  39.0 2.6 %regroup.1 = (bf16[48,7168]{1,0:T(8,128)(2,1)S(1)}, bf16[48,7168]{1,0:T(8,128)(2,1)S(1)}, bf16[48,7168]{1,0:T(8,128)(2,1)S(1)}, bf16[640,256]{1,0:T(8,128)(2,1)S(1)}) custom-call(s32[2]{0:T(128)S(1)} %pad_add_fusion.place_ref, bf16[640,1024]{1,0:T(8,128)(2,1)S(1)} %bitcast.16), custom_call_target="tpu_custom_call" | custom-call | tf_op jit(solution)/shard_map/regroup/pallas_call | solution.py:447
  41.7 2.6 %collective-permute-start.4 = (bf16[48,7168]{1,0:T(8,128)(2,1)S(1)}, bf16[48,7168]{1,0:T(8,128)(2,1)S(1)}, u32[]{:S(2)}, u32[]{:S(2)}) collective-permute-start(bf16[48,7168]{1,0:T(8,128)(2,1)S(1)} %get-tuple-element.44), channel_id=1, source_target_pairs={{0,4},{1,5},{2,6},{3,7},{4,0},{5,1},{6,2},{7,3},{8,12},{9,13},{10,... | collective-permute-start | bytes 2064392 | tf_op jit(solution)/shard_map/ppermute | solution.py:417
  45.7 3.1 %copy-done.1 = bf16[1,512,7168]{2,1,0:T(8,128)(2,1)S(1)} copy-done((bf16[1,512,7168]{2,1,0:T(8,128)(2,1)S(1)}, bf16[1,512,7168]{2,1,0:T(8,128)(2,1)}, u32[]{:S(2)}) %copy-start.1) | copy-done | bytes 7340056
  48.8 4.1 %regroup_own.1 = (bf16[48,7168]{1,0:T(8,128)(2,1)S(1)}, bf16[512,7168]{1,0:T(8,128)(2,1)S(1)}) custom-call(s32[2]{0:T(128)S(1)} %pad_add_fusion.place_ref, bf16[640,1024]{1,0:T(8,128)(2,1)S(1)} %bitcast.17, bf16[512,7168]{1,0:T(8,128)(2,1)S(1)} %bitcast.19), custom_call_target="tpu_custom_call" | custom-call | tf_op jit(solution)/shard_map/regroup_own/pallas_call | solution.py:453
  53.0 21.8 %collective-permute-done.3.refs_1_ = bf16[48,7168]{1,0:T(8,128)(2,1)S(1)} collective-permute-done((bf16[48,7168]{1,0:T(8,128)(2,1)S(1)}, bf16[48,7168]{1,0:T(8,128)(2,1)S(1)}, u32[]{:S(2)}, u32[]{:S(2)}) %collective-permute-start.3) | collective-permute-done | bytes 688160 | tf_op jit(solution)/shard_map/ppermute | solution.py:417
  75.4 2.6 %back.2.back_ref = f32[192,512]{1,0:T(8,128)S(1)} custom-call(bf16[48,7168]{1,0:T(8,128)(2,1)S(1)} %get-tuple-element.42.refs_0_, bf16[48,7168]{1,0:T(8,128)(2,1)S(1)} %collective-permute-done.3.refs_1_, bf16[48,7168]{1,0:T(8,128)(2,1)S(1)} %collective-permute-done.4.refs_2_, bf16[48,7168]{1,0:T(8,128)(2,1)S(1)} %collective-permute-done.5.refs_3_, ...), custom_call_target="tpu_custom_call" | custom-call | tf_op jit(solution)/shard_map/back/pallas_call | solution.py:464
  78.9 2.6 %back.3.mark_ref.back2_ref = f32[192,512]{1,0:T(8,128)S(1)} custom-call(bf16[48,7168]{1,0:T(8,128)(2,1)S(1)} %collective-permute-done.6.refs_0_, bf16[48,7168]{1,0:T(8,128)(2,1)S(1)} %collective-permute-done.7.refs_1_, bf16[48,7168]{1,0:T(8,128)(2,1)S(1)} %collective-permute-done.8.refs_2_, bf16[48,7168]{1,0:T(8,128)(2,1)S(1)} %collective-permute-done.9.refs_3_, ...), custom_call_target="tpu_custom_call" | custom-call | tf_op jit(solution)/shard_map/back/pallas_call | solution.py:465
  81.9 8.4 %forward_own.1 = (f32[192,512]{1,0:T(8,128)S(1)}, f32[192,512]{1,0:T(8,128)S(1)}, bf16[7168,512]{1,0:T(8,128)(2,1)S(1)}, bf16[7168,512]{1,0:T(8,128)(2,1)S(1)}) custom-call(bf16[384,3584]{1,0:T(8,128)(2,1)} %bitcast.7.x_ref, bf16[7168,512]{1,0:T(8,128)(2,1)} %bitcast.24, bf16[7168,512]{1,0:T(8,128)(2,1)} %bitcast.25, f32[192,512]{1,0:T(8,128)S(1)} %back.3.mark_ref.back2_ref), custom_call_target="tpu_custom_call" | custom-call | tf_op jit(solution)/shard_map/forward_own/pallas_call | solution.py:468
  90.3 4.8 %forward.1 = (bf16[384,512]{1,0:T(8,128)(2,1)S(1)}, bf16[384,512]{1,0:T(8,128)(2,1)S(1)}, bf16[384,128]{1,0:T(8,128)(2,1)S(1)}) custom-call(bf16[384,3584]{1,0:T(8,128)(2,1)S(1)} %collective-permute-done.10.x_ref, bf16[7168,512]{1,0:T(8,128)(2,1)S(1)} %get-tuple-element.49.gate_ref, bf16[7168,512]{1,0:T(8,128)(2,1)S(1)} %get-tuple-element.50.up_ref, ...), custom_call_target="tpu_custom_call" | custom-call | tf_op jit(solution)/shard_map/forward/pallas_call | solution.py:475
  95.1 3.3 %dx.3 = (bf16[192,3968]{1,0:T(8,128)(2,1)S(1)}, bf16[192,3968]{1,0:T(8,128)(2,1)S(1)}) custom-call(bf16[384,512]{1,0:T(8,128)(2,1)S(1)} %get-tuple-element.54.dgate_ref, bf16[384,512]{1,0:T(8,128)(2,1)S(1)} %get-tuple-element.55.dup_ref, bf16[7168,512]{1,0:T(8,128)(2,1)S(1)} %get-tuple-element.49.gate_ref, bf16[7168,512]{1,0:T(8,128)(2,1)S(1)} %get-tuple-element.50.up_ref, ...), custom_call_target="tpu_custom_call" | custom-call | tf_op jit(solution)/shard_map/dx/pallas_call | solution.py:483
  98.8 2.8 %dx.2 = (bf16[192,3328]{1,0:T(8,128)(2,1)S(1)}, bf16[192,3328]{1,0:T(8,128)(2,1)S(1)}) custom-call(bf16[384,512]{1,0:T(8,128)(2,1)S(1)} %get-tuple-element.54.dgate_ref, bf16[384,512]{1,0:T(8,128)(2,1)S(1)} %get-tuple-element.55.dup_ref, bf16[7168,512]{1,0:T(8,128)(2,1)S(1)} %get-tuple-element.49.gate_ref, bf16[7168,512]{1,0:T(8,128)(2,1)S(1)} %get-tuple-element.50.up_ref, ...), custom_call_target="tpu_custom_call" | custom-call | tf_op jit(solution)/shard_map/dx/pallas_call | solution.py:483
  103.6 1.8 %collective-permute-start.13 = (bf16[48,3968]{1,0:T(8,128)(2,1)}, bf16[48,3968]{1,0:T(8,128)(2,1)}, u32[]{:S(2)}, u32[]{:S(2)}) collective-permute-start(bf16[48,3968]{1,0:T(8,128)(2,1)} %get-tuple-element.64), channel_id=1, source_target_pairs={{0,6},{1,7},{2,0},{3,1},{4,2},{5,3},{6,4},{7,5},{8,14},{9,15},{10,... | collective-permute-start | bytes 1142792 | tf_op jit(solution)/shard_map/ppermute | solution.py:417
  106.3 2.1 %add_to_nodes.1 = (bf16[384,1664]{1,0:T(8,128)(2,1)}, f32[8,128]{1,0:T(8,128)S(1)}) custom-call(bf16[192,3328]{1,0:T(8,128)(2,1)S(1)} %get-tuple-element.57.own_ref, bf16[192,3328]{1,0:T(8,128)(2,1)S(1)} %collective-permute-done.11.got_ref, f32[8,128]{1,0:T(8,128)S(1)} %get-tuple-element.61.mark_ref), custom_call_target="tpu_custom_call" | custom-call | tf_op jit(solution)/shard_map/add_to_nodes/pallas_call | solution.py:501
  108.4 6.9 %all-to-all-start.2 = ((bf16[16,24,1664]{2,1,0:T(8,128)(2,1)}), bf16[16,24,1664]{2,1,0:T(8,128)(2,1)S(1)}, u32[]{:S(2)}, u32[]{:S(2)}) async-start(bf16[16,24,1664]{2,1,0:T(8,128)(2,1)} %bitcast.11), calls=%async_computation.2 | async-start | bytes 2555904 | tf_op jit(solution)/shard_map/all_to_all | solution.py:427
  116.3 2.7 %collective-permute-done.14.p2_ref = bf16[48,3968]{1,0:T(8,128)(2,1)} collective-permute-done((bf16[48,3968]{1,0:T(8,128)(2,1)}, bf16[48,3968]{1,0:T(8,128)(2,1)}, u32[]{:S(2)}, u32[]{:S(2)}) %collective-permute-start.14) | collective-permute-done | bytes 380960 | tf_op jit(solution)/shard_map/ppermute | solution.py:417
  119.0 6.6 %collective-permute-done.15.p3_ref = bf16[48,3968]{1,0:T(8,128)(2,1)} collective-permute-done((bf16[48,3968]{1,0:T(8,128)(2,1)}, bf16[48,3968]{1,0:T(8,128)(2,1)}, u32[]{:S(2)}, u32[]{:S(2)}) %collective-permute-start.15) | collective-permute-done | bytes 380960 | tf_op jit(solution)/shard_map/ppermute | solution.py:417
  125.6 2.8 %combine.1 = bf16[1280,256]{1,0:T(8,128)(2,1)} custom-call(f32[128,128]{1,0:T(8,128)S(1)} %table.1.table_ref, bf16[48,3968]{1,0:T(8,128)(2,1)S(1)} %get-tuple-element.63.p0_ref, bf16[48,3968]{1,0:T(8,128)(2,1)} %collective-permute-done.13.p1_ref, bf16[48,3968]{1,0:T(8,128)(2,1)} %collective-permute-done.14.p2_ref, ...), custom_call_target="tpu_custom_call" | custom-call | flops 20000000000 | bytes 70000000 | tf_op jit(solution)/shard_map/combine/pallas_call | solution.py:506
  128.4 6.8 %all-to-all-done.2 = bf16[16,24,1664]{2,1,0:T(8,128)(2,1)S(1)} async-done(((bf16[16,24,1664]{2,1,0:T(8,128)(2,1)}), bf16[16,24,1664]{2,1,0:T(8,128)(2,1)S(1)}, u32[]{:S(2)}, u32[]{:S(2)}) %all-to-all-start.2) | async-done | bytes 1277984 | tf_op jit(solution)/shard_map/all_to_all | solution.py:427
  135.3 3.6 %all-to-all-start.3 = ((bf16[16,80,256]{2,1,0:T(8,128)(2,1)}), bf16[16,80,256]{2,1,0:T(8,128)(2,1)S(1)}, u32[]{:S(2)}, u32[]{:S(2)}) async-start(bf16[16,80,256]{2,1,0:T(8,128)(2,1)} %bitcast.13), calls=%async_computation.3 | async-start | bytes 1310720 | tf_op jit(solution)/shard_map/all_to_all | solution.py:427
  140.4 2.4 %collective-permute-start.16 = (bf16[16,3328]{1,0:T(8,128)(2,1)S(1)}, bf16[16,3328]{1,0:T(8,128)(2,1)S(1)}, u32[]{:S(2)}, u32[]{:S(2)}) collective-permute-start(bf16[16,3328]{1,0:T(8,128)(2,1)S(1)} %get-tuple-element.71), channel_id=1, source_target_pairs={{0,6},{1,7},{2,0},{3,1},{4,2},{5,3},{6,4},{7,5},{8,14},{9,15},{10,... | collective-permute-start | bytes 319496 | tf_op jit(solution)/shard_map/ppermute | solution.py:417
  142.8 1.9 %collective-permute-start.17 = (bf16[16,3328]{1,0:T(8,128)(2,1)S(1)}, bf16[16,3328]{1,0:T(8,128)(2,1)S(1)}, u32[]{:S(2)}, u32[]{:S(2)}) collective-permute-start(bf16[16,3328]{1,0:T(8,128)(2,1)S(1)} %get-tuple-element.72), channel_id=1, source_target_pairs={{0,4},{1,5},{2,6},{3,7},{4,0},{5,1},{6,2},{7,3},{8,12},{9,13},{10,... | collective-permute-start | bytes 319496 | tf_op jit(solution)/shard_map/ppermute | solution.py:417
  145.4 3.6 %collective-permute-done.17.b2_ref = bf16[16,3328]{1,0:T(8,128)(2,1)S(1)} collective-permute-done((bf16[16,3328]{1,0:T(8,128)(2,1)S(1)}, bf16[16,3328]{1,0:T(8,128)(2,1)S(1)}, u32[]{:S(2)}, u32[]{:S(2)}) %collective-permute-start.17) | collective-permute-done | bytes 106528 | tf_op jit(solution)/shard_map/ppermute | solution.py:417
  149.0 1.6 %collective-permute-done.18.b3_ref = bf16[16,3328]{1,0:T(8,128)(2,1)S(1)} collective-permute-done((bf16[16,3328]{1,0:T(8,128)(2,1)S(1)}, bf16[16,3328]{1,0:T(8,128)(2,1)S(1)}, u32[]{:S(2)}, u32[]{:S(2)}) %collective-permute-start.18) | collective-permute-done | bytes 106528 | tf_op jit(solution)/shard_map/ppermute | solution.py:417
  150.6 2.4 %finish.1 = (bf16[16,7168]{1,0:T(8,128)(2,1)}, f32[8,16]{1,0:T(8,128)}) custom-call(s32[2]{0:T(128)S(1)} %pad_add_fusion.place_ref, s32[8,16]{1,0:T(8,128)S(1)} %bitcast.23, bf16[1280,256]{1,0:T(8,128)(2,1)S(1)} %bitcast.21, bf16[16,3328]{1,0:T(8,128)(2,1)S(1)} %get-tuple-element.70.b0_ref, bf16[16,3328]{1,0:T(8,128)(2,1)S(1)} %collective-permute-done.16.b1_ref, ...), custom_call_target="tpu_custom_call" | custom-call | tf_op jit(solution)/shard_map/finish/pallas_call | solution.py:520
  (47 shorter events, 13.0 us)
Async XLA Ops:
  3.8 8.1 %copy-start.2 = (s32[16,8]{0,1:T(8,128)S(1)}, s32[16,8]{0,1:T(8,128)}, u32[]{:S(2)}) copy-start(s32[16,8]{0,1:T(8,128)} %param.9) | copy-start | bytes 1540
  3.8 8.1 %copy-start.4 = (f32[16,8]{0,1:T(8,128)S(1)}, f32[16,8]{0,1:T(8,128)}, u32[]{:S(2)}) copy-start(f32[16,8]{0,1:T(8,128)} %param.10) | copy-start | bytes 1540
  3.8 8.4 %copy-start.3 = (bf16[16,7168]{1,0:T(8,128)(2,1)S(1)}, bf16[16,7168]{1,0:T(8,128)(2,1)}, u32[]{:S(2)}) copy-start(bf16[16,7168]{1,0:T(8,128)(2,1)} %param.7) | copy-start | bytes 688132
  3.8 28.9 %all-to-all-start = ((bf16[16,40,1024]{2,1,0:T(8,128)(2,1)}), bf16[16,40,1024]{2,1,0:T(8,128)(2,1)S(1)}, u32[]{:S(2)}, u32[]{:S(2)}) async-start(bf16[16,40,1024]{2,1,0:T(8,128)(2,1)} %bitcast.26), calls=%async_computation | async-start | bytes 2621440 | tf_op jit(solution)/shard_map/all_to_all | solution.py:427
  12.2 12.8 %collective-permute-start.2 = (bf16[16,7296]{1,0:T(8,128)(2,1)S(1)}, bf16[16,7296]{1,0:T(8,128)(2,1)S(1)}, u32[]{:S(2)}, u32[]{:S(2)}) collective-permute-start(bf16[16,7296]{1,0:T(8,128)(2,1)S(1)} %pad_maximum_fusion.x0_ref), channel_id=1, source_target_pairs={{0,6},{1,7},{2,0},{3,1},{4,2},{5,3},{6,4},{7,5},{8,14},{9,15},{10,... | collective-permute-start | bytes 700424 | tf_op jit(solution)/shard_map/ppermute | solution.py:417
  15.3 10.2 %collective-permute-start.1 = (bf16[16,7296]{1,0:T(8,128)(2,1)S(1)}, bf16[16,7296]{1,0:T(8,128)(2,1)S(1)}, u32[]{:S(2)}, u32[]{:S(2)}) collective-permute-start(bf16[16,7296]{1,0:T(8,128)(2,1)S(1)} %pad_maximum_fusion.x0_ref), channel_id=1, source_target_pairs={{0,4},{1,5},{2,6},{3,7},{4,0},{5,1},{6,2},{7,3},{8,12},{9,13},{10,... | collective-permute-start | bytes 700424 | tf_op jit(solution)/shard_map/ppermute | solution.py:417
  16.0 12.7 %collective-permute-start = (bf16[16,7296]{1,0:T(8,128)(2,1)S(1)}, bf16[16,7296]{1,0:T(8,128)(2,1)S(1)}, u32[]{:S(2)}, u32[]{:S(2)}) collective-permute-start(bf16[16,7296]{1,0:T(8,128)(2,1)S(1)} %pad_maximum_fusion.x0_ref), channel_id=1, source_target_pairs={{0,2},{1,3},{2,4},{3,5},{4,6},{5,7},{6,0},{7,1},{8,10},{9,11},{10,... | collective-permute-start | bytes 700424 | tf_op jit(solution)/shard_map/ppermute | solution.py:417
  30.5 1.5 %copy-start = (bf16[384,3584]{1,0:T(8,128)(2,1)}, bf16[384,3584]{1,0:T(8,128)(2,1)S(1)}, u32[]{:S(2)}) copy-start(bf16[384,3584]{1,0:T(8,128)(2,1)S(1)} %send_x.1) | copy-start | bytes 8257540
  32.7 48.7 %all-to-all-start.1 = ((bf16[16,24,3584]{2,1,0:T(8,128)(2,1)}), bf16[16,24,3584]{2,1,0:T(8,128)(2,1)}, u32[]{:S(2)}, u32[]{:S(2)}) async-start(bf16[16,24,3584]{2,1,0:T(8,128)(2,1)} %bitcast.18), calls=%async_computation.1 | async-start | bytes 5505024 | tf_op jit(solution)/shard_map/all_to_all | solution.py:427
  41.7 33.1 %collective-permute-start.3 = (bf16[48,7168]{1,0:T(8,128)(2,1)S(1)}, bf16[48,7168]{1,0:T(8,128)(2,1)S(1)}, u32[]{:S(2)}, u32[]{:S(2)}) collective-permute-start(bf16[48,7168]{1,0:T(8,128)(2,1)S(1)} %get-tuple-element.43), channel_id=1, source_target_pairs={{0,2},{1,3},{2,4},{3,5},{4,6},{5,7},{6,0},{7,1},{8,10},{9,11},{10,... | collective-permute-start | bytes 2064392 | tf_op jit(solution)/shard_map/ppermute | solution.py:417
  41.7 33.0 %collective-permute-start.4 = (bf16[48,7168]{1,0:T(8,128)(2,1)S(1)}, bf16[48,7168]{1,0:T(8,128)(2,1)S(1)}, u32[]{:S(2)}, u32[]{:S(2)}) collective-permute-start(bf16[48,7168]{1,0:T(8,128)(2,1)S(1)} %get-tuple-element.44), channel_id=1, source_target_pairs={{0,4},{1,5},{2,6},{3,7},{4,0},{5,1},{6,2},{7,3},{8,12},{9,13},{10,... | collective-permute-start | bytes 2064392 | tf_op jit(solution)/shard_map/ppermute | solution.py:417
  44.4 31.0 %collective-permute-start.5 = (bf16[48,7168]{1,0:T(8,128)(2,1)S(1)}, bf16[48,7168]{1,0:T(8,128)(2,1)S(1)}, u32[]{:S(2)}, u32[]{:S(2)}) collective-permute-start(bf16[48,7168]{1,0:T(8,128)(2,1)S(1)} %get-tuple-element.45), channel_id=1, source_target_pairs={{0,6},{1,7},{2,0},{3,1},{4,2},{5,3},{6,4},{7,5},{8,14},{9,15},{10,... | collective-permute-start | bytes 2064392 | tf_op jit(solution)/shard_map/ppermute | solution.py:417
  45.7 3.1 %copy-start.1 = (bf16[1,512,7168]{2,1,0:T(8,128)(2,1)S(1)}, bf16[1,512,7168]{2,1,0:T(8,128)(2,1)}, u32[]{:S(2)}) copy-start(bf16[1,512,7168]{2,1,0:T(8,128)(2,1)} %param.13) | copy-start | bytes 22020100
  52.9 25.0 %collective-permute-start.6 = (bf16[48,7168]{1,0:T(8,128)(2,1)S(1)}, bf16[48,7168]{1,0:T(8,128)(2,1)S(1)}, u32[]{:S(2)}, u32[]{:S(2)}) collective-permute-start(bf16[48,7168]{1,0:T(8,128)(2,1)S(1)} %get-tuple-element.42.refs_0_), channel_id=1, source_target_pairs={{0,1},{1,0},{2,3},{3,2},{4,5},{5,4},{6,7},{7,6},{8,9},{9,8},{10,11... | collective-permute-start | bytes 2064392 | tf_op jit(solution)/shard_map/ppermute | solution.py:421
  74.8 3.2 %collective-permute-start.7 = (bf16[48,7168]{1,0:T(8,128)(2,1)S(1)}, bf16[48,7168]{1,0:T(8,128)(2,1)S(1)}, u32[]{:S(2)}, u32[]{:S(2)}) collective-permute-start(bf16[48,7168]{1,0:T(8,128)(2,1)S(1)} %collective-permute-done.3.refs_1_), channel_id=1, source_target_pairs={{0,1},{1,0},{2,3},{3,2},{4,5},{5,4},{6,7},{7,6},{8,9},{9,8},{10,11... | collective-permute-start | bytes 2064392 | tf_op jit(solution)/shard_map/ppermute | solution.py:421
  74.8 3.2 %collective-permute-start.8 = (bf16[48,7168]{1,0:T(8,128)(2,1)S(1)}, bf16[48,7168]{1,0:T(8,128)(2,1)S(1)}, u32[]{:S(2)}, u32[]{:S(2)}) collective-permute-start(bf16[48,7168]{1,0:T(8,128)(2,1)S(1)} %collective-permute-done.4.refs_2_), channel_id=1, source_target_pairs={{0,1},{1,0},{2,3},{3,2},{4,5},{5,4},{6,7},{7,6},{8,9},{9,8},{10,11... | collective-permute-start | bytes 2064392 | tf_op jit(solution)/shard_map/ppermute | solution.py:421
  75.4 3.5 %collective-permute-start.9 = (bf16[48,7168]{1,0:T(8,128)(2,1)S(1)}, bf16[48,7168]{1,0:T(8,128)(2,1)S(1)}, u32[]{:S(2)}, u32[]{:S(2)}) collective-permute-start(bf16[48,7168]{1,0:T(8,128)(2,1)S(1)} %collective-permute-done.5.refs_3_), channel_id=1, source_target_pairs={{0,1},{1,0},{2,3},{3,2},{4,5},{5,4},{6,7},{7,6},{8,9},{9,8},{10,11... | collective-permute-start | bytes 2064392 | tf_op jit(solution)/shard_map/ppermute | solution.py:421
  81.5 8.8 %collective-permute-start.10 = (bf16[384,3584]{1,0:T(8,128)(2,1)}, bf16[384,3584]{1,0:T(8,128)(2,1)S(1)}, u32[]{:S(2)}, u32[]{:S(2)}) collective-permute-start(bf16[384,3584]{1,0:T(8,128)(2,1)} %bitcast.7.x_ref), channel_id=1, source_target_pairs={{0,1},{1,0},{2,3},{3,2},{4,5},{5,4},{6,7},{7,6},{8,9},{9,8},{10,11... | collective-permute-start | bytes 8257544 | tf_op jit(solution)/shard_map/ppermute | solution.py:421
  98.4 3.7 %collective-permute-start.12 = (bf16[192,3968]{1,0:T(8,128)(2,1)S(1)}, bf16[192,3968]{1,0:T(8,128)(2,1)S(1)}, u32[]{:S(2)}, u32[]{:S(2)}) collective-permute-start(bf16[192,3968]{1,0:T(8,128)(2,1)S(1)} %get-tuple-element.60), channel_id=1, source_target_pairs={{0,1},{1,0},{2,3},{3,2},{4,5},{5,4},{6,7},{7,6},{8,9},{9,8},{10,11... | collective-permute-start | bytes 4571144 | tf_op jit(solution)/shard_map/ppermute | solution.py:421
  101.7 4.6 %collective-permute-start.11 = (bf16[192,3328]{1,0:T(8,128)(2,1)S(1)}, bf16[192,3328]{1,0:T(8,128)(2,1)S(1)}, u32[]{:S(2)}, u32[]{:S(2)}) collective-permute-start(bf16[192,3328]{1,0:T(8,128)(2,1)S(1)} %get-tuple-element.58), channel_id=1, source_target_pairs={{0,1},{1,0},{2,3},{3,2},{4,5},{5,4},{6,7},{7,6},{8,9},{9,8},{10,11... | collective-permute-start | bytes 3833864 | tf_op jit(solution)/shard_map/ppermute | solution.py:421
  103.6 12.7 %collective-permute-start.13 = (bf16[48,3968]{1,0:T(8,128)(2,1)}, bf16[48,3968]{1,0:T(8,128)(2,1)}, u32[]{:S(2)}, u32[]{:S(2)}) collective-permute-start(bf16[48,3968]{1,0:T(8,128)(2,1)} %get-tuple-element.64), channel_id=1, source_target_pairs={{0,6},{1,7},{2,0},{3,1},{4,2},{5,3},{6,4},{7,5},{8,14},{9,15},{10,... | collective-permute-start | bytes 1142792 | tf_op jit(solution)/shard_map/ppermute | solution.py:417
  105.4 13.6 %collective-permute-start.14 = (bf16[48,3968]{1,0:T(8,128)(2,1)}, bf16[48,3968]{1,0:T(8,128)(2,1)}, u32[]{:S(2)}, u32[]{:S(2)}) collective-permute-start(bf16[48,3968]{1,0:T(8,128)(2,1)} %get-tuple-element.65), channel_id=1, source_target_pairs={{0,4},{1,5},{2,6},{3,7},{4,0},{5,1},{6,2},{7,3},{8,12},{9,13},{10,... | collective-permute-start | bytes 1142792 | tf_op jit(solution)/shard_map/ppermute | solution.py:417
  105.4 20.2 %collective-permute-start.15 = (bf16[48,3968]{1,0:T(8,128)(2,1)}, bf16[48,3968]{1,0:T(8,128)(2,1)}, u32[]{:S(2)}, u32[]{:S(2)}) collective-permute-start(bf16[48,3968]{1,0:T(8,128)(2,1)} %get-tuple-element.66), channel_id=1, source_target_pairs={{0,2},{1,3},{2,4},{3,5},{4,6},{5,7},{6,0},{7,1},{8,10},{9,11},{10,... | collective-permute-start | bytes 1142792 | tf_op jit(solution)/shard_map/ppermute | solution.py:417
  108.4 26.9 %all-to-all-start.2 = ((bf16[16,24,1664]{2,1,0:T(8,128)(2,1)}), bf16[16,24,1664]{2,1,0:T(8,128)(2,1)S(1)}, u32[]{:S(2)}, u32[]{:S(2)}) async-start(bf16[16,24,1664]{2,1,0:T(8,128)(2,1)} %bitcast.11), calls=%async_computation.2 | async-start | bytes 2555904 | tf_op jit(solution)/shard_map/all_to_all | solution.py:427
  135.3 15.4 %all-to-all-start.3 = ((bf16[16,80,256]{2,1,0:T(8,128)(2,1)}), bf16[16,80,256]{2,1,0:T(8,128)(2,1)S(1)}, u32[]{:S(2)}, u32[]{:S(2)}) async-start(bf16[16,80,256]{2,1,0:T(8,128)(2,1)} %bitcast.13), calls=%async_computation.3 | async-start | bytes 1310720 | tf_op jit(solution)/shard_map/all_to_all | solution.py:427
  140.4 5.1 %collective-permute-start.16 = (bf16[16,3328]{1,0:T(8,128)(2,1)S(1)}, bf16[16,3328]{1,0:T(8,128)(2,1)S(1)}, u32[]{:S(2)}, u32[]{:S(2)}) collective-permute-start(bf16[16,3328]{1,0:T(8,128)(2,1)S(1)} %get-tuple-element.71), channel_id=1, source_target_pairs={{0,6},{1,7},{2,0},{3,1},{4,2},{5,3},{6,4},{7,5},{8,14},{9,15},{10,... | collective-permute-start | bytes 319496 | tf_op jit(solution)/shard_map/ppermute | solution.py:417
  142.8 6.2 %collective-permute-start.17 = (bf16[16,3328]{1,0:T(8,128)(2,1)S(1)}, bf16[16,3328]{1,0:T(8,128)(2,1)S(1)}, u32[]{:S(2)}, u32[]{:S(2)}) collective-permute-start(bf16[16,3328]{1,0:T(8,128)(2,1)S(1)} %get-tuple-element.72), channel_id=1, source_target_pairs={{0,4},{1,5},{2,6},{3,7},{4,0},{5,1},{6,2},{7,3},{8,12},{9,13},{10,... | collective-permute-start | bytes 319496 | tf_op jit(solution)/shard_map/ppermute | solution.py:417
  144.7 5.9 %collective-permute-start.18 = (bf16[16,3328]{1,0:T(8,128)(2,1)S(1)}, bf16[16,3328]{1,0:T(8,128)(2,1)S(1)}, u32[]{:S(2)}, u32[]{:S(2)}) collective-permute-start(bf16[16,3328]{1,0:T(8,128)(2,1)S(1)} %get-tuple-element.73), channel_id=1, source_target_pairs={{0,2},{1,3},{2,4},{3,5},{4,6},{5,7},{6,0},{7,1},{8,10},{9,11},{10,... | collective-permute-start | bytes 319496 | tf_op jit(solution)/shard_map/ppermute | solution.py:417
